TPU v7x, 512 devices: a whole 4x4x16 slice. The times are simulated.
512 devices in a mesh: gx: 32 (over z, core), gy: 16 (over x, y).
Axes of the slice: x: 4, y: 4, z: 16, core: 2. Of those that a mesh axis runs over, the one named last changes fastest.
Arguments:
- prior: float32 [3, 2, 4, 128, 128, 128], P(None, None, None, 'gx', 'gy'), may hold values from -1.25 to 1.25
- coefficient: float32 [128, 128, 128], P('gx', 'gy'), may hold values from 0.2 to 2
Outputs:
- new_blocks: float32 [2, 2, 4, 128, 128, 128], P(None, None, None, 'gx', 'gy')
All inputs are finite; a program needn't handle non-finite values.
Results may differ from a plain program's by a relative error of at most 0.0003.
Values sent between devices are 32-bit elements; how exact they have to be, the bound alone decides.
No kernel may reach another device: no remote copies, remote signals or barrier semaphores. Data moves between devices by JAX's collectives and lax.ppermute only.
A program may use at most 64 MiB of HBM per device.

v0:
```python
import jax
import jax.numpy as jnp
from jax import lax
from jax.sharding import PartitionSpec as P

ITERS = 2
SWEEPS = 4


HIGHEST = lax.Precision.HIGHEST


def with_halo(cells, sides, width):
    for axis, dim in sides:
        count = lax.axis_size(axis)
        ends = count - 1
        head = lax.slice_in_dim(cells, 0, width, axis=dim)
        tail = lax.slice_in_dim(cells, cells.shape[dim] - width, cells.shape[dim], axis=dim)
        cells = jnp.concatenate(
            [
                lax.ppermute(tail, axis, [(i, (i + 1) % count) for i in range(ends)]),
                cells,
                lax.ppermute(head, axis, [((i + 1) % count, i) for i in range(ends)]),
            ],
            axis=dim,
        )
    return cells


def flatten_fields(block):
    return block.reshape(block.shape[0] * block.shape[1] * block.shape[2], -1)


def real_gram(left, right):
    return lax.dot_general(
        flatten_fields(left), flatten_fields(right), (((1,), (1,)), ((), ())), precision=HIGHEST
    )


def to_complex(gram, left_count, right_count):
    sources = gram.shape[1] // (2 * right_count)
    grid = gram.reshape(left_count, 2, sources, right_count, 2, sources)
    real_part = grid[:, 0, :, :, 0, :] + grid[:, 1, :, :, 1, :]
    imag_part = grid[:, 0, :, :, 1, :] - grid[:, 1, :, :, 0, :]
    shape = (left_count * sources, right_count * sources)
    return (real_part.reshape(shape), imag_part.reshape(shape))


def combine(fields, real_coef, imag_coef):
    count = fields.shape[0]
    sources = real_coef.shape[1]
    upper = jnp.concatenate([real_coef, imag_coef], 1).reshape(count, 1, sources, 2 * sources)
    lower = jnp.concatenate([-imag_coef, real_coef], 1).reshape(count, 1, sources, 2 * sources)
    mapping = jnp.concatenate([upper, lower], 1).reshape(count * 2 * sources, 2 * sources)
    result = lax.dot_general(
        mapping, flatten_fields(fields), (((0,), (0,)), ((), ())), precision=HIGHEST
    )
    return result.reshape(fields.shape[1:])


def cholesky_inverse(gram_real, gram_imag):
    count = gram_real.shape[0]
    upper_re = [[None] * count for _ in range(count)]
    upper_im = [[None] * count for _ in range(count)]
    for s in range(count):
        pivot = gram_real[s, s]
        for k in range(s):
            pivot = pivot - upper_re[k][s] * upper_re[k][s] - upper_im[k][s] * upper_im[k][s]
        diagonal = jnp.sqrt(pivot)
        upper_re[s][s] = diagonal
        upper_im[s][s] = 0.0 * diagonal
        for t in range(s + 1, count):
            entry_re = gram_real[s, t]
            entry_im = gram_imag[s, t]
            for k in range(s):
                entry_re = entry_re - (
                    upper_re[k][s] * upper_re[k][t] + upper_im[k][s] * upper_im[k][t]
                )
                entry_im = entry_im - (
                    upper_re[k][s] * upper_im[k][t] - upper_im[k][s] * upper_re[k][t]
                )
            upper_re[s][t] = entry_re / diagonal
            upper_im[s][t] = entry_im / diagonal
    zero_value = 0.0 * gram_real[0, 0]
    inverse_re = [[zero_value] * count for _ in range(count)]
    inverse_im = [[zero_value] * count for _ in range(count)]
    for t in range(count):
        inverse_re[t][t] = 1.0 / upper_re[t][t]
        for s in range(t):
            accum_re = zero_value
            accum_im = zero_value
            for k in range(s, t):
                accum_re = (
                    accum_re + inverse_re[s][k] * upper_re[k][t] - inverse_im[s][k] * upper_im[k][t]
                )
                accum_im = (
                    accum_im + inverse_re[s][k] * upper_im[k][t] + inverse_im[s][k] * upper_re[k][t]
                )
            inverse_re[s][t] = -accum_re / upper_re[t][t]
            inverse_im[s][t] = -accum_im / upper_re[t][t]
    stacked_re = jnp.stack([jnp.stack(row) for row in inverse_re])
    stacked_im = jnp.stack([jnp.stack(row) for row in inverse_im])
    return (stacked_re, stacked_im)


def apply_inverse(field, coefficient):
    real_diag = 6.0 - coefficient
    imag_diag = 0.5 * coefficient
    denom = real_diag * real_diag + imag_diag * imag_diag
    out_real = (real_diag * field[0] + imag_diag * field[1]) / denom
    out_imag = (real_diag * field[1] - imag_diag * field[0]) / denom
    return jnp.stack([out_real, out_imag])


def depth_neighbours(field):
    padded = jnp.pad(field, [(0, 0)] * (field.ndim - 1) + [(1, 1)])
    return padded[..., 2:] + padded[..., :-2]


def shrink_sum(padded):
    inner = padded[..., 1:-1, 1:-1, :]
    total = padded[..., 2:, 1:-1, :] + padded[..., :-2, 1:-1, :]
    total = total + padded[..., 1:-1, 2:, :] + padded[..., 1:-1, :-2, :]
    return (total + depth_neighbours(inner), inner)


def widen(field):
    return with_halo(field, (("gx", 2), ("gy", 3)), 1)


def smoothed_image(block, coefficient):
    solution = 0.8 * apply_inverse(block, coefficient)
    for sweep in range(SWEEPS - 1):
        around, inner = shrink_sum(widen(solution))
        solution = 0.2 * inner + 0.8 * apply_inverse(block + around, coefficient)
    around, inner = shrink_sum(widen(solution))
    return (6.0 - coefficient) * inner - around


def orthogonalize(window, fresh, cells):
    count = window.shape[0]
    first = lax.psum(real_gram(window, fresh[None]), ("gx", "gy"))
    coef_re, coef_im = to_complex(first / cells, count, 1)
    once = fresh - combine(window, coef_re, coef_im)
    second = lax.psum(real_gram(window, once[None]), ("gx", "gy"))
    coef_re, coef_im = to_complex(second / cells, count, 1)
    twice = once - combine(window, coef_re, coef_im)
    norms = lax.psum(real_gram(twice[None], twice[None]), ("gx", "gy"))
    gram_re, gram_im = to_complex(norms / cells, 1, 1)
    inverse_re, inverse_im = cholesky_inverse(gram_re, gram_im)
    return combine(twice[None], inverse_re, inverse_im)


def per_device(prior, coefficient):
    cells = coefficient.size * lax.axis_size("gx") * lax.axis_size("gy")
    window = prior
    current = prior[2]
    results = []
    for step in range(ITERS):
        fresh = smoothed_image(current, coefficient)
        current = orthogonalize(window, fresh, cells)
        results.append(current)
        window = jnp.concatenate([window[1:], current[None]], 0)
    return jnp.stack(results)


def solution(mesh):
    in_specs = (P(None, None, None, "gx", "gy", None), P("gx", "gy", None))
    out_specs = P(None, None, None, "gx", "gy", None)
    return jax.shard_map(
        per_device, mesh=mesh, in_specs=in_specs, out_specs=out_specs, check_vma=False
    )
```

profile of v0, /device:TPU:1, one launch (start us, length us, event | category | flops | bytes accessed | tf_op | source)
XLA Modules:
  0.0 798.6 jit_solution(585211759212168028)
XLA Ops:
  1.8 8.9 %collective-permute-start = (f32[2,4,1,8,128]{4,1,3,2,0:T(4,128)S(1)}, f32[2,4,1,8,128]{4,1,3,2,0:T(4,128)S(1)}, u32[]{:S(2)}, u32[]{:S(2)}) collective-permute-start(f32[2,4,1,8,128]{4,1,3,2,0:T(4,128)S(1)} %get-tuple-element.64), channel_id=1, source_target_pairs={{16,0},{32,16},{48,32},{64,48},{80,64},{96,80},{112,96},{128,112},... | collective-permute-start | bytes 98312 | tf_op jit(solution)/shard_map/ppermute | solution.py:23
  10.7 1.9 collective-permute-start.1
  12.7 1.2 collective-permute-done.1
  13.8 1.3 collective-permute-start.2
  15.1 4.0 collective-permute-start.3
  20.4 3.2 collective-permute-start.4
  23.7 3.9 collective-permute-start.5
  27.6 1.0 collective-permute-done.5
  28.6 1.3 collective-permute-start.6
  29.9 4.6 collective-permute-start.7
  34.5 0.9 collective-permute-done.7
  35.8 1.9 collective-permute-start.8
  37.7 5.1 collective-permute-start.9
  42.8 1.0 collective-permute-done.9
  43.8 1.3 collective-permute-start.10
  45.1 4.6 collective-permute-start.11
  49.7 0.9 collective-permute-done.11
  51.1 1.9 collective-permute-start.12
  53.0 5.1 collective-permute-start.13
  58.1 1.0 collective-permute-done.13
  59.1 1.3 collective-permute-start.14
  60.4 4.6 collective-permute-start.15
  66.6 121.4 %psum.42 = f32[24,8]{0,1:T(8,128)S(1)} all-reduce(f32[24,8]{0,1:T(8,128)S(1)} %convolution_bitcast_fusion.2), channel_id=1, replica_groups=mesh['gx'=32,'gy'=16] {'gx','gy'}, use_global_device_ids=true, to_apply=%region_0.1 | all-reduce | flops 192 | bytes 1536 | tf_op jit(solution)/shard_map/psum | solution.py:142
  189.8 100.4 %psum.43 = f32[24,8]{0,1:T(8,128)S(1)} all-reduce(f32[24,8]{0,1:T(8,128)S(1)} %convolution_bitcast_fusion.1), channel_id=1, replica_groups=mesh['gx'=32,'gy'=16] {'gx','gy'}, use_global_device_ids=true, to_apply=%region_1.2 | all-reduce | flops 192 | bytes 1536 | tf_op jit(solution)/shard_map/psum | solution.py:145
  291.9 98.9 %psum.44 = f32[8,8]{1,0:T(8,128)S(1)} all-reduce(f32[8,8]{1,0:T(8,128)S(1)} %fusion.86), channel_id=1, replica_groups=mesh['gx'=32,'gy'=16] {'gx','gy'}, use_global_device_ids=true, to_apply=%region_2.3 | all-reduce | flops 64 | bytes 512 | tf_op jit(solution)/shard_map/psum | solution.py:148
  404.9 2.6 collective-permute-start.16
  407.5 3.4 collective-permute-start.17
  410.9 1.0 collective-permute-done.17
  411.9 1.3 collective-permute-start.18
  413.2 4.0 collective-permute-start.19
  418.5 1.9 collective-permute-start.20
  420.5 5.4 collective-permute-start.21
  425.8 1.0 collective-permute-done.21
  426.9 1.3 collective-permute-start.22
  428.2 4.6 collective-permute-start.23
  434.1 1.9 collective-permute-start.24
  436.0 5.1 collective-permute-start.25
  441.1 1.0 collective-permute-done.25
  442.1 1.3 collective-permute-start.26
  443.4 4.6 collective-permute-start.27
  449.4 1.9 collective-permute-start.28
  451.3 5.2 collective-permute-start.29
  456.5 1.0 collective-permute-done.29
  457.5 1.3 collective-permute-start.30
  458.8 4.6 collective-permute-start.31
  465.1 115.8 %psum.45 = f32[24,8]{0,1:T(8,128)S(1)} all-reduce(f32[24,8]{0,1:T(8,128)S(1)} %fusion.88), channel_id=1, replica_groups=mesh['gx'=32,'gy'=16] {'gx','gy'}, use_global_device_ids=true, to_apply=%region_3.4 | all-reduce | flops 192 | bytes 1536 | tf_op jit(solution)/shard_map/psum | solution.py:142
  582.7 100.3 %psum.46 = f32[24,8]{0,1:T(8,128)S(1)} all-reduce(f32[24,8]{0,1:T(8,128)S(1)} %fusion.89), channel_id=1, replica_groups=mesh['gx'=32,'gy'=16] {'gx','gy'}, use_global_device_ids=true, to_apply=%region_4.5 | all-reduce | flops 192 | bytes 1536 | tf_op jit(solution)/shard_map/psum | solution.py:145
  684.7 98.8 %psum.47 = f32[8,8]{1,0:T(8,128)S(1)} all-reduce(f32[8,8]{1,0:T(8,128)S(1)} %fusion.90), channel_id=1, replica_groups=mesh['gx'=32,'gy'=16] {'gx','gy'}, use_global_device_ids=true, to_apply=%region_5.6 | all-reduce | flops 64 | bytes 512 | tf_op jit(solution)/shard_map/psum | solution.py:148
  (181 shorter events, 23.4 us)
Async XLA Ops:
  1.7 17.4 %copy-start = (f32[3,2,4,4,8,128]{5,4,3,2,1,0:T(8,128)S(1)}, f32[3,2,4,4,8,128]{5,4,3,2,1,0:T(8,128)}, u32[]{:S(2)}) copy-start(f32[3,2,4,4,8,128]{5,4,3,2,1,0:T(8,128)} %param.2) | copy-start | bytes 1179652
  1.8 10.9 %collective-permute-start = (f32[2,4,1,8,128]{4,1,3,2,0:T(4,128)S(1)}, f32[2,4,1,8,128]{4,1,3,2,0:T(4,128)S(1)}, u32[]{:S(2)}, u32[]{:S(2)}) collective-permute-start(f32[2,4,1,8,128]{4,1,3,2,0:T(4,128)S(1)} %get-tuple-element.64), channel_id=1, source_target_pairs={{16,0},{32,16},{48,32},{64,48},{80,64},{96,80},{112,96},{128,112},... | collective-permute-start | bytes 98312 | tf_op jit(solution)/shard_map/ppermute | solution.py:23
  10.7 3.1 collective-permute-start.1
  13.8 5.3 collective-permute-start.2
  15.1 4.9 collective-permute-start.3
  20.4 7.1 collective-permute-start.4
  23.7 4.9 collective-permute-start.5
  28.6 5.9 collective-permute-start.6
  29.9 5.5 collective-permute-start.7
  35.8 7.0 collective-permute-start.8
  37.7 6.1 collective-permute-start.9
  43.8 5.9 collective-permute-start.10
  45.1 5.5 collective-permute-start.11
  51.1 7.0 collective-permute-start.12
  53.0 6.1 collective-permute-start.13
  59.1 6.0 collective-permute-start.14
  60.4 5.5 collective-permute-start.15
  404.9 6.0 collective-permute-start.16
  407.5 4.4 collective-permute-start.17
  411.9 5.3 collective-permute-start.18
  413.2 4.9 collective-permute-start.19
  418.5 7.3 collective-permute-start.20
  420.5 6.4 collective-permute-start.21
  426.9 5.9 collective-permute-start.22
  428.2 5.5 collective-permute-start.23
  434.1 7.0 collective-permute-start.24
  436.0 6.1 collective-permute-start.25
  442.1 5.9 collective-permute-start.26
  443.4 5.5 collective-permute-start.27
  449.4 7.2 collective-permute-start.28
  451.3 12.1 %slice-start = ((f32[3,2,4,4,8,128]{5,4,3,2,1,0:T(8,128)}), f32[2,2,4,4,8,128]{5,4,3,2,1,0:T(8,128)S(1)}, s32[]{:S(2)}) async-start(f32[3,2,4,4,8,128]{5,4,3,2,1,0:T(8,128)} %param.2), calls=%async_computation | async-start | bytes 524288 | tf_op jit(solution)/shard_map/slice | solution.py:163
  451.3 6.2 collective-permute-start.29
  457.5 6.2 collective-permute-start.30
  458.8 5.5 collective-permute-start.31
where the time goes:
time: 801 us; the launch traced here: 799 us
  blocking collectives  636 us (79%)
  starting transfers between devices  105 us (13%)
  between operations  24.5 us (3%)
  waiting for transfers between devices  15 us (2%)
    psum x2, blocking collectives, orthogonalize(): first = lax.psum(real_gram(window, fresh[None]), ('gx', 'gy'))  237 us
    psum x2, blocking collectives, orthogonalize(): second = lax.psum(real_gram(window, once[None]), ('gx', 'gy'))  201 us
    psum x2, blocking collectives, orthogonalize(): norms = lax.psum(real_gram(twice[None], twice[None]), ('gx', 'gy'))  198 us
    ppermute x16, starting transfers between devices, with_halo(): lax.ppermute(tail, axis, [(i, (i + 1) % count) for i in range(ends)])  70.4 us
    ppermute x16, starting transfers between devices, with_halo(): lax.ppermute(head, axis, [((i + 1) % count, i) for i in range(ends)])  34.6 us
  transfers between devices with their start and end apart: 32, of which 16 were waited for; matrix products, arithmetic and copies ran while one was open for 0% of the time, Pallas kernels for 0%

commit v1 on v0

v1 whole, which is shorter than its diff:
```python
import functools

import jax
import jax.numpy as jnp
import numpy as np
from jax import lax
from jax.experimental import pallas as pl
from jax.experimental.pallas import tpu as pltpu
from jax.sharding import Mesh, PartitionSpec as P

LX, LY, NZ = 4, 8, 128
HALO = 4
EX, EY = LX + 2 * HALO, LY + 2 * HALO
WIDTHS = [EX - 2 * d for d in range(1, HALO + 1)]
STARTS = [sum(WIDTHS[:d]) for d in range(HALO)]
RIM = sum(WIDTHS)
BLOCKS = 7
ROWS = 64
F32 = jnp.float32
BF16 = jnp.bfloat16
HIGHEST = lax.Precision.HIGHEST
VMEM = pl.BlockSpec(memory_space=pltpu.VMEM)


def plane_of(parts, index):
    low, own, high = parts
    if index < HALO:
        return low, index
    if index < HALO + LX:
        return own, index - HALO
    return high, index - HALO - LX


def rim_kernel(groups, with_coefficient, *refs):
    own, low, high, up, down = refs[:5]
    for group in range(groups):
        for d in range(1, HALO + 1):
            for i in range(WIDTHS[d - 1]):
                ref, x = plane_of((low, own, high), d + i)
                spot = group * RIM + STARTS[d - 1] + i
                up[spot] = ref[group * LX + x, pl.ds((LY - d) * 8, 8), :]
                down[spot] = ref[group * LX + x, pl.ds((d - 1) * 8, 8), :]
    if with_coefficient:
        up[RIM + 3] = jnp.zeros((8, NZ), F32)
        down[RIM + 3] = jnp.zeros((8, NZ), F32)
        for d in range(1, HALO + 1):
            for i in range(WIDTHS[d - 1]):
                ref, x = plane_of((low, own, high), d + i)
                spot = STARTS[d - 1] + i
                tile, row = RIM + spot // 8, spot % 8
                up[tile, pl.ds(row, 1), :] = ref[x, pl.ds(LY * 8 + LY - d, 1), :]
                down[tile, pl.ds(row, 1), :] = ref[x, pl.ds(LY * 8 + d - 1, 1), :]


def pack_rim(groups, with_coefficient, own, low, high):
    shape = jax.ShapeDtypeStruct((groups * RIM + (4 if with_coefficient else 0), 8, NZ), F32)
    return pl.pallas_call(
        functools.partial(rim_kernel, groups, with_coefficient),
        out_shape=(shape, shape),
        in_specs=[VMEM] * 3,
        out_specs=(VMEM, VMEM),
        name="pack_rim",
    )(own, low, high)


def fill_block(group, parts, from_low, from_high, wide):
    low, own, high = parts
    wide[...] = jnp.zeros(wide.shape, F32)
    for index in range(EX):
        ref, x = plane_of(parts, index)
        wide[index, HALO:HALO + LY] = ref[group * LX + x, pl.ds(0, LY * 8), :].reshape(LY, 8, NZ)
    for d in range(1, HALO + 1):
        spot = group * RIM + STARTS[d - 1]
        for i in range(WIDTHS[d - 1]):
            wide[d + i, HALO - d] = from_low[spot + i]
            wide[d + i, HALO + LY - 1 + d] = from_high[spot + i]


def fill_coefficient(parts, from_low, from_high, wide):
    wide[...] = jnp.zeros(wide.shape, F32)
    for index in range(EX):
        ref, x = plane_of(parts, index)
        wide[index, HALO:HALO + LY] = ref[x, pl.ds(LY * 8, LY), :]
    for d in range(1, HALO + 1):
        for i in range(WIDTHS[d - 1]):
            spot = STARTS[d - 1] + i
            tile, row = RIM + spot // 8, spot % 8
            wide[d + i, pl.ds(HALO - d, 1), :] = from_low[tile, pl.ds(row, 1), :]
            wide[d + i, pl.ds(HALO + LY - 1 + d, 1), :] = from_high[tile, pl.ds(row, 1), :]


def fill_tables(coef, table_re, table_im, diag_re, diag_im):
    value = coef[...]
    real = 6.0 - value
    imag = 0.5 * value
    scale = jnp.where(value > 0.0, 0.8 / (real * real + imag * imag), 0.0)
    diag_re[...] = real * scale
    diag_im[...] = imag * scale
    sign = jnp.where(lax.broadcasted_iota(jnp.int32, (8, NZ), 0) < 4, 1.0, -1.0)

    def body(x, carry):
        for y in range(EY):
            table_re[x, y] = jnp.broadcast_to(diag_re[x, pl.ds(y, 1), :], (8, NZ))
            table_im[x, y] = jnp.broadcast_to(diag_im[x, pl.ds(y, 1), :], (8, NZ)) * sign
        return carry

    lax.fori_loop(0, EX, body, 0)


def depth_sum(value):
    lane = lax.broadcasted_iota(jnp.int32, value.shape, 2)
    above = jnp.where(lane == 0, 0.0, pltpu.roll(value, 1, 2))
    below = jnp.where(lane == NZ - 1, 0.0, pltpu.roll(value, NZ - 1, 2))
    return above + below


def around(ref, x, low, high):
    total = ref[x - 1, low:high] + ref[x + 1, low:high]
    total = total + ref[x, low - 1:high - 1] + ref[x, low + 1:high + 1]
    return total + depth_sum(ref[x, low:high])


def smooth(block, coef, table_re, table_im, first, second, store):
    def solve(value, x, low, high):
        return (table_re[x, low:high] * value
                + table_im[x, low:high] * pltpu.roll(value, 4, 1))

    def start(x, carry):
        first[x] = solve(block[x], x, 0, EY)
        return carry

    lax.fori_loop(0, EX, start, 0)
    here, there = first, second
    for k in range(1, HALO):
        low, high = k, EY - k

        def sweep(x, carry, here=here, there=there, low=low, high=high):
            value = block[x, low:high] + around(here, x, low, high)
            there[x, low:high] = 0.2 * here[x, low:high] + solve(value, x, low, high)
            return carry

        lax.fori_loop(k, EX - k, sweep, 0)
        here, there = there, here

    def image(x, carry):
        low, high = HALO, HALO + LY
        for y in range(low, high):
            diag = 6.0 - coef[x, pl.ds(y, 1), :]
            total = here[x - 1, y] + here[x + 1, y] + here[x, y - 1] + here[x, y + 1]
            total = total + depth_sum(here[x, y:y + 1])[0]
            store(x - HALO, y - HALO, diag * here[x, y] - total)
        return carry

    lax.fori_loop(HALO, HALO + LX, image, 0)


BIG = pltpu.VMEM((EX, EY, 8, NZ), F32)
FLAT = pltpu.VMEM((EX, EY, NZ), F32)
SMOOTH_SCRATCH = [BIG, BIG, BIG, BIG, BIG, FLAT, FLAT]


def first_kernel(own, low, high, from_low, from_high, out, coef, block, first, second,
                 table_re, table_im, diag_re, diag_im):
    parts = (low, own, high)
    fill_block(0, parts, from_low, from_high, block)
    fill_coefficient(parts, from_low, from_high, coef)
    fill_tables(coef, table_re, table_im, diag_re, diag_im)

    def store(x, y, value):
        out[x, pl.ds(y * 8, 8), :] = value

    smooth(block, coef, table_re, table_im, first, second, store)


def first_image(*args):
    return pl.pallas_call(
        first_kernel,
        out_shape=(jax.ShapeDtypeStruct((LX, LY * 8, NZ), F32),
                   jax.ShapeDtypeStruct((EX, EY, NZ), F32)),
        in_specs=[VMEM] * 5,
        out_specs=(VMEM, VMEM),
        scratch_shapes=SMOOTH_SCRATCH,
        compiler_params=pltpu.CompilerParams(vmem_limit_bytes=24 << 20),
        cost_estimate=pl.CostEstimate(flops=6_000_000, bytes_accessed=2_000_000, transcendentals=0),
        name="first_image",
    )(*args)


def old_kernel(own, low, high, from_low, from_high, coef, out, block, first, second,
               table_re, table_im, diag_re, diag_im):
    fill_tables(coef, table_re, table_im, diag_re, diag_im)
    for group in range(2):
        fill_block(group, (low, own, high), from_low, from_high, block)

        def store(x, y, value, group=group):
            out[group * LX + x, pl.ds(y * 8, 8), :] = value

        smooth(block, coef, table_re, table_im, first, second, store)


def old_images(*args):
    return pl.pallas_call(
        old_kernel,
        out_shape=jax.ShapeDtypeStruct((2 * LX, LY * 8, NZ), F32),
        in_specs=[VMEM] * 6,
        out_specs=VMEM,
        scratch_shapes=SMOOTH_SCRATCH,
        compiler_params=pltpu.CompilerParams(vmem_limit_bytes=24 << 20),
        cost_estimate=pl.CostEstimate(flops=12_000_000, bytes_accessed=4_000_000, transcendentals=0),
        name="old_images",
    )(*args)


def split3(value):
    high = value.astype(BF16)
    rest = value - high.astype(F32)
    middle = rest.astype(BF16)
    low = (rest - middle.astype(F32)).astype(BF16)
    return high, middle, low


def basis_plane(old, recent, w, old_image, w_image, x):
    refs = [(old, x), (old, LX + x), (recent, x), (w, x), (old_image, x), (old_image, LX + x), (w_image, x)]
    rows = []
    for ref, index in refs:
        rows.append(jnp.concatenate([ref[index, pl.ds(y * 8, 8), :] for y in range(LY)], axis=1))
    rows.append(jnp.zeros((8, LY * NZ), F32))
    return jnp.concatenate(rows, axis=0)


def lane_roll(value, amount):
    return pltpu.roll(value, amount % NZ, 1)


SLOTS = [(0, 0), (0, 56), (1, 0), (1, 40), (1, 72), (1, 96), (0, 104)]


def pack_gram(gram):
    lane = lax.broadcasted_iota(jnp.int32, (8, NZ), 1)
    row = lax.broadcasted_iota(jnp.int32, (8, NZ), 0)
    packed = jnp.zeros((8, NZ), F32)
    for b in range(BLOCKS):
        rows = gram[8 * b:8 * b + 8]
        turned = jnp.where(lane % 8 < 4, lane_roll(rows, -4), -lane_roll(rows, 4))
        both = rows + pltpu.roll(turned, 4, 0)
        half, start = SLOTS[b]
        moved = lane_roll(both, start - 8 * b)
        if half:
            moved = pltpu.roll(moved, 4, 0)
        keep = (lane >= start) & (lane < start + 8 * (BLOCKS - b)) & (row // 4 == half)
        packed = packed + jnp.where(keep, moved, 0.0)
    return packed


def unpack_gram(packed):
    lane = lax.broadcasted_iota(jnp.int32, (8, NZ), 1)
    row = lax.broadcasted_iota(jnp.int32, (8, NZ), 0)
    rows = []
    for b in range(BLOCKS):
        half, start = SLOTS[b]
        moved = lane_roll(packed, 8 * b - start)
        if half:
            moved = pltpu.roll(moved, 4, 0)
        keep = (lane >= 8 * b) & (lane < 8 * BLOCKS) & (row < 4)
        moved = jnp.where(keep, moved, 0.0)
        turned = jnp.where(lane % 8 < 4, -lane_roll(moved, -4), lane_roll(moved, 4))
        rows.append(moved + pltpu.roll(turned, 4, 0))
    rows.append(jnp.zeros((NZ - 8 * BLOCKS, NZ), F32))
    upper = jnp.concatenate(rows, axis=0)
    tall = lax.broadcasted_iota(jnp.int32, (NZ, NZ), 0)
    wide = lax.broadcasted_iota(jnp.int32, (NZ, NZ), 1)
    return jnp.where(tall // 8 <= wide // 8, upper, upper.T)


def gram_kernel(peers, own, low, high, from_low, from_high, coef, old, recent, old_image, w_image, out,
                block, first, second, table_re, table_im, diag_re, diag_im):
    fill_tables(coef, table_re, table_im, diag_re, diag_im)
    fill_block(0, (low, own, high), from_low, from_high, block)

    def store(x, y, value):
        w_image[x, pl.ds(y * 8, 8), :] = value

    smooth(block, coef, table_re, table_im, first, second, store)

    def plane(x, total):
        stacked = jnp.concatenate(split3(basis_plane(old, recent, own, old_image, w_image, x)), axis=0)
        return total + lax.dot_general(stacked, stacked, (((1,), (1,)), ((), ())), preferred_element_type=F32)

    total = lax.fori_loop(0, LX, plane, jnp.zeros((3 * ROWS, 3 * ROWS), F32))
    tall = total[0:ROWS] + total[ROWS:2 * ROWS] + total[2 * ROWS:3 * ROWS]
    gram = tall[:, 0:ROWS] + tall[:, ROWS:2 * ROWS] + tall[:, 2 * ROWS:3 * ROWS]
    gram = jnp.concatenate([gram, jnp.zeros((ROWS, NZ - ROWS), F32)], axis=1)
    packed = pack_gram(gram)
    for peer in range(peers):
        out[peer] = packed


def image_and_gram(peers, *args):
    return pl.pallas_call(
        functools.partial(gram_kernel, peers),
        out_shape=(jax.ShapeDtypeStruct((LX, LY * 8, NZ), F32),
                   jax.ShapeDtypeStruct((peers, 8, NZ), F32)),
        in_specs=[VMEM] * 9,
        out_specs=(VMEM, VMEM),
        scratch_shapes=SMOOTH_SCRATCH,
        compiler_params=pltpu.CompilerParams(vmem_limit_bytes=32 << 20),
        name="image_and_gram",
    )(*args)


def sum_kernel(parts, out):
    total = jnp.sum(parts[...], axis=0)
    for peer in range(out.shape[0]):
        out[peer] = total


def sum_and_spread(parts, peers):
    return pl.pallas_call(
        sum_kernel,
        out_shape=jax.ShapeDtypeStruct((peers, 8, NZ), F32),
        in_specs=[VMEM],
        out_specs=VMEM,
        name="sum_and_spread",
    )(parts)


def mul(left, right):
    return lax.dot_general(left, right, (((1,), (0,)), ((), ())), precision=HIGHEST, preferred_element_type=F32)


def mul_t(left, right):
    return lax.dot_general(left, right, (((1,), (1,)), ((), ())), precision=HIGHEST, preferred_element_type=F32)


def inverse_factor(gram):
    lane = lax.broadcasted_iota(jnp.int32, (8, NZ), 1)
    row = lax.broadcasted_iota(jnp.int32, (8, NZ), 0)
    work = jnp.where(lane < 8, gram, jnp.where(lane == row + 8, 1.0, 0.0))
    rank = 2 * (row % 4) + row // 4
    for step in range(8):
        k = (step % 2) * 4 + step // 2
        line = work[k:k + 1, :]
        pivot = line[:, k:k + 1]
        column = work[:, k:k + 1]
        root = 1.0 / jnp.sqrt(pivot)
        line = line * root
        factor = column * root
        work = jnp.where(rank > step, work - factor * line, jnp.where(rank == step, line, work))
    return jnp.where(lane < 8, lane_roll(work, -8), 0.0)


def coefficients(gram):
    lane = lax.broadcasted_iota(jnp.int32, (8, NZ), 1)
    row = lax.broadcasted_iota(jnp.int32, (8, NZ), 0)
    tall = lax.broadcasted_iota(jnp.int32, (NZ, NZ), 0)
    wide = lax.broadcasted_iota(jnp.int32, (NZ, NZ), 1)

    def normalise(rows):
        small = mul_t(mul(rows, gram), rows_in(rows))
        return mul(inverse_factor(small)[:, 0:8], rows)

    def rows_in(rows):
        return jnp.concatenate([rows, jnp.zeros((NZ - 8, NZ), F32)], axis=0)

    once = jnp.where(lane < 24, gram[24:32], 0.0)
    again = jnp.where(lane < 24, mul(once, gram), 0.0)
    fresh = jnp.where(lane == row + 24, 1.0, 0.0)
    new = normalise(fresh - (2.0 * once - again))
    image = (jnp.where((lane >= 32) & (lane < 48), lane_roll(new, 32), 0.0)
             + jnp.where((lane >= 24) & (lane < 32), lane_roll(new, 8), 0.0)
             + jnp.where((lane >= 48) & (lane < 56), lane_roll(new, 24), 0.0))
    window = jnp.where((tall < 16) & (wide == tall + 8), 1.0, 0.0)
    window = jnp.concatenate([window[0:16], new, window[24:]], axis=0)

    def project(rows):
        return mul(mul_t(mul(rows, gram), window), window)

    once = project(image)
    again = project(once)
    newest = normalise(image - (2.0 * once - again))
    return new, newest


def final_kernel(cells, parts, old, recent, w, old_image, w_image, out):
    gram = unpack_gram(jnp.sum(parts[...], axis=0) * (1.0 / cells))
    new, newest = coefficients(gram)
    mapping = jnp.concatenate([new, newest], axis=0)[:, 0:ROWS]
    pieces = [jnp.concatenate([piece] * 3, axis=1) for piece in split3(mapping)]
    stacked_map = jnp.concatenate(pieces, axis=0)

    def plane(x, carry):
        stacked = jnp.concatenate(split3(basis_plane(old, recent, w, old_image, w_image, x)), axis=0)
        full = lax.dot_general(stacked_map, stacked, (((1,), (0,)), ((), ())), preferred_element_type=F32)
        result = full[32:48] + full[16:32] + full[0:16]
        for k in range(2):
            tiles = jnp.stack([result[8 * k:8 * k + 8, y * NZ:(y + 1) * NZ] for y in range(LY)])
            out[k, :, x] = jnp.swapaxes(tiles, 0, 1)
        return carry

    lax.fori_loop(0, LX, plane, 0)


def finish(cells, *args):
    return pl.pallas_call(
        functools.partial(final_kernel, cells),
        out_shape=jax.ShapeDtypeStruct((2, 8, LX, LY, NZ), F32),
        in_specs=[VMEM] * 6,
        out_specs=VMEM,
        compiler_params=pltpu.CompilerParams(vmem_limit_bytes=32 << 20),
        name="finish",
    )(*args)


GX = ("z", "core")


def from_both(axis, count, to_higher, to_lower):
    return (
        lax.ppermute(to_higher, axis, [(i, i + 1) for i in range(count - 1)]),
        lax.ppermute(to_lower, axis, [(i + 1, i) for i in range(count - 1)]),
    )


def per_device(nx, ny, nz, prior, coefficient):
    cells = coefficient.size * nx * ny
    by_cell = prior.transpose(0, 3, 4, 1, 2, 5).reshape(3, LX, LY * 8, NZ)
    recent = by_cell[2]
    old = by_cell[:2].reshape(2 * LX, LY * 8, NZ)

    start = jnp.concatenate([recent, coefficient], axis=1)
    low, high = from_both(GX, nx, start, start)
    up, down = pack_rim(1, True, start, low, high)
    below, above = from_both("gy", ny, up, down)
    w, coef = first_image(start, low, high, below, above)

    old_low, old_high = from_both(GX, nx, old, old)
    up, down = pack_rim(2, False, old, old_low, old_high)
    old_below, old_above = from_both("gy", ny, up, down)

    low, high = from_both(GX, nx, w, w)
    up, down = pack_rim(1, False, w, low, high)
    below, above = from_both("gy", ny, up, down)
    old_image = old_images(old, old_low, old_high, old_below, old_above, coef)

    w_image, spread = image_and_gram(2 * ny, w, low, high, below, above, coef, old, recent, old_image)
    got = lax.all_to_all(spread, ("core", "gy"), 0, 0)
    got = lax.all_to_all(sum_and_spread(got, nz), "z", 0, 0)
    out = finish(cells, got, old, recent, w, old_image, w_image)
    return out.reshape(2, 2, 4, LX, LY, NZ)


def solution(mesh):
    nx, ny = mesh.shape["gx"], mesh.shape["gy"]
    fine = Mesh(np.asarray(mesh.devices).reshape(nx // 2, 2, ny), ("z", "core", "gy"))
    in_specs = (P(None, None, None, GX, "gy", None), P(GX, "gy", None))
    out_specs = P(None, None, None, GX, "gy", None)
    return jax.shard_map(
        functools.partial(per_device, nx, ny, nx // 2),
        mesh=fine, in_specs=in_specs, out_specs=out_specs, check_vma=False,
    )
```

time: 801 us -> 126 us (0.16)
  blocking collectives: 636 us -> 48.4 us
  starting transfers between devices: 105 us -> 32.8 us
  Pallas kernels: 0 us -> 27.6 us
  between operations: 24.5 us -> 0.34 us
  waiting for transfers between devices: 15 us -> 6.03 us
    psum x6 -> x0, blocking collectives: 636 us -> none  [the longest x2 237 us: orthogonalize(): first = lax.psum(real_gram(window, fresh[None]), ('gx', 'gy'))]
    ppermute x32 -> x12, starting transfers between devices: 105 us -> 32.8 us  [the longest x6 19.5 us: from_both(): lax.ppermute(to_higher, axis, [(i, i + 1) for i in range(count - 1)])]
    all_to_all x0 -> x2, blocking collectives: none -> 48.4 us  [the longest x1 30.6 us: per_device(): got = lax.all_to_all(sum_and_spread(got, nz), 'z', 0, 0)]
    pallas_call x0 -> x8, Pallas kernels: none -> 27.6 us  [the longest x1 6.26 us: old_images(): pl.pallas_call(old_kernel, out_shape=jax.ShapeDtypeStruct((2 * LX, LY * 8...]
    ppermute x32 -> x12, waiting for transfers between devices: 15 us -> 6.03 us  [the longest x6 4.15 us: from_both(): lax.ppermute(to_lower, axis, [(i + 1, i) for i in range(count - 1)])]
  transfers between devices with their start and end apart: 32 -> 12, of which waited for: 16 -> 2; matrix products, arithmetic and copies ran while one was open for 0% -> 0% of each run, Pallas kernels for 0% -> 13%
where the time goes in v1:
time: 126 us; the launch traced here: 125 us
  blocking collectives  48.4 us (38%)
  starting transfers between devices  32.8 us (26%)
  Pallas kernels  27.6 us (22%)
  local copies, waits for them, and re-layouts  9.57 us (8%)
  waiting for transfers between devices  6.03 us (5%)
    all_to_all x1, blocking collectives, per_device(): got = lax.all_to_all(sum_and_spread(got, nz), 'z', 0, 0)  30.6 us
    ppermute x6, starting transfers between devices, from_both(): lax.ppermute(to_higher, axis, [(i, i + 1) for i in range(count - 1)])  19.5 us
    all_to_all x1, blocking collectives, per_device(): got = lax.all_to_all(spread, ('core', 'gy'), 0, 0)  17.8 us
    ppermute x6, starting transfers between devices, from_both(): lax.ppermute(to_lower, axis, [(i + 1, i) for i in range(count - 1)])  13.4 us
    unnamed x36, local copies, waits for them, and re-layouts  8.31 us
    pallas_call x1, Pallas kernels, old_images(): pl.pallas_call(old_kernel, out_shape=jax.ShapeDtypeStruct((2 * LX, LY * 8...  6.26 us
    pallas_call x1, Pallas kernels, finish(): pl.pallas_call(functools.partial(final_kernel, cells), out_shape=jax.Shap...  5.53 us
    pallas_call x3, Pallas kernels, pack_rim(): pl.pallas_call(functools.partial(rim_kernel, groups, with_coefficient), o...  5.45 us
  transfers between devices with their start and end apart: 12, of which 2 were waited for; matrix products, arithmetic and copies ran while one was open for 0% of the time, Pallas kernels for 13%

profile of v1, /device:TPU:1, one launch (start us, length us, event | category | flops | bytes accessed | tf_op | source)
XLA Modules:
  0.0 125.5 jit_solution(9912136795931741700)
XLA Ops:
  0.0 1.0 slice.10
  1.0 0.0 copy-start.17
  1.0 0.1 copy.3
  1.1 0.6 copy-done.17
  1.7 0.7 pad_maximum_fusion.refs_0_.own
  2.4 4.9 %collective-permute-start = (f32[4,72,128]{2,1,0:T(8,128)}, f32[4,72,128]{2,1,0:T(8,128)S(1)}, u32[]{:S(2)}, u32[]{:S(2)}) collective-permute-start(f32[4,72,128]{2,1,0:T(8,128)} %pad_maximum_fusion.refs_0_.own), channel_id=1, source_target_pairs={{0,16},{16,32},{32,48},{48,64},{64,80},{80,96},{96,112},{112,128},... | collective-permute-start | bytes 442376 | tf_op jit(solution)/shard_map/ppermute | solution.py:419
  7.3 5.1 %collective-permute-start.1 = (f32[4,72,128]{2,1,0:T(8,128)}, f32[4,72,128]{2,1,0:T(8,128)S(1)}, u32[]{:S(2)}, u32[]{:S(2)}) collective-permute-start(f32[4,72,128]{2,1,0:T(8,128)} %pad_maximum_fusion.refs_0_.own), channel_id=1, source_target_pairs={{16,0},{32,16},{48,32},{64,48},{80,64},{96,80},{112,96},{128,112},... | collective-permute-start | bytes 442376 | tf_op jit(solution)/shard_map/ppermute | solution.py:420
  12.5 0.2 copy.4
  12.7 0.0 copy-start
  12.7 1.9 %collective-permute-start.8 = (f32[8,64,128]{2,1,0:T(8,128)S(1)}, f32[8,64,128]{2,1,0:T(8,128)S(1)}, u32[]{:S(2)}, u32[]{:S(2)}) collective-permute-start(f32[8,64,128]{2,1,0:T(8,128)S(1)} %bitcast.4), channel_id=1, source_target_pairs={{0,16},{16,32},{32,48},{48,64},{64,80},{80,96},{96,112},{112,128},... | collective-permute-start | bytes 786440 | tf_op jit(solution)/shard_map/ppermute | solution.py:419
  14.6 2.4 %collective-permute-start.9 = (f32[8,64,128]{2,1,0:T(8,128)S(1)}, f32[8,64,128]{2,1,0:T(8,128)S(1)}, u32[]{:S(2)}, u32[]{:S(2)}) collective-permute-start(f32[8,64,128]{2,1,0:T(8,128)S(1)} %bitcast.5), channel_id=1, source_target_pairs={{16,0},{32,16},{48,32},{64,48},{80,64},{96,80},{112,96},{128,112},... | collective-permute-start | bytes 786440 | tf_op jit(solution)/shard_map/ppermute | solution.py:420
  17.0 0.0 collective-permute-done.refs_1_.low
  17.1 0.0 collective-permute-done.1.refs_2_.high
  17.1 0.6 copy-done.8
  17.7 0.7 copy-done.10
  18.4 1.8 %pack_rim.3 = (f32[32,8,128]{2,1,0:T(8,128)}, f32[32,8,128]{2,1,0:T(8,128)}) custom-call(f32[4,72,128]{2,1,0:T(8,128)} %pad_maximum_fusion.refs_0_.own, f32[4,72,128]{2,1,0:T(8,128)} %copy-done.8, f32[4,72,128]{2,1,0:T(8,128)} %copy-done.10), custom_call_target="tpu_custom_call" | custom-call | tf_op jit(solution)/shard_map/pack_rim/pallas_call | solution.py:57
  20.2 1.3 %collective-permute-start.2 = (f32[32,8,128]{2,1,0:T(8,128)}, f32[32,8,128]{2,1,0:T(8,128)S(1)}, u32[]{:S(2)}, u32[]{:S(2)}) collective-permute-start(f32[32,8,128]{2,1,0:T(8,128)} %get-tuple-element.15), channel_id=1, source_target_pairs={{0,1},{1,2},{2,3},{3,4},{4,5},{5,6},{6,7},{7,8},{8,9},{9,10},{10,1... | collective-permute-start | bytes 393224 | tf_op jit(solution)/shard_map/ppermute | solution.py:419
  21.5 1.3 %collective-permute-start.3 = (f32[32,8,128]{2,1,0:T(8,128)}, f32[32,8,128]{2,1,0:T(8,128)S(1)}, u32[]{:S(2)}, u32[]{:S(2)}) collective-permute-start(f32[32,8,128]{2,1,0:T(8,128)} %get-tuple-element.16), channel_id=1, source_target_pairs={{1,0},{2,1},{3,2},{4,3},{5,4},{6,5},{7,6},{8,7},{9,8},{10,9},{11,1... | collective-permute-start | bytes 393224 | tf_op jit(solution)/shard_map/ppermute | solution.py:420
  22.8 1.9 %collective-permute-done.2.from_low = f32[32,8,128]{2,1,0:T(8,128)S(1)} collective-permute-done((f32[32,8,128]{2,1,0:T(8,128)}, f32[32,8,128]{2,1,0:T(8,128)S(1)}, u32[]{:S(2)}, u32[]{:S(2)}) %collective-permute-start.2) | collective-permute-done | bytes 131104 | tf_op jit(solution)/shard_map/ppermute | solution.py:419
  24.6 4.1 %collective-permute-done.3.from_high = f32[32,8,128]{2,1,0:T(8,128)S(1)} collective-permute-done((f32[32,8,128]{2,1,0:T(8,128)}, f32[32,8,128]{2,1,0:T(8,128)S(1)}, u32[]{:S(2)}, u32[]{:S(2)}) %collective-permute-start.3) | collective-permute-done | bytes 131104 | tf_op jit(solution)/shard_map/ppermute | solution.py:420
  28.8 0.9 copy-done.9
  29.7 0.9 copy-done.11
  30.6 4.1 %first_image.1 = (f32[4,64,128]{2,1,0:T(8,128)S(1)}, f32[12,16,128]{2,1,0:T(8,128)S(1)}) custom-call(f32[4,72,128]{2,1,0:T(8,128)} %pad_maximum_fusion.refs_0_.own, f32[4,72,128]{2,1,0:T(8,128)S(1)} %copy-done.9, f32[4,72,128]{2,1,0:T(8,128)S(1)} %copy-done.11, f32[32,8,128]{2,1,0:T(8,128)S(1)} %collective-permute-done.2.from_low, ...), custom_call_target="tpu_custom_call" | custom-call | flops 6000000 | bytes 2000000 | tf_op jit(solution)/shard_map/first_image/pallas_call | solution.py:176
  34.8 4.0 %collective-permute-start.4 = (f32[4,64,128]{2,1,0:T(8,128)S(1)}, f32[4,64,128]{2,1,0:T(8,128)S(1)}, u32[]{:S(2)}, u32[]{:S(2)}) collective-permute-start(f32[4,64,128]{2,1,0:T(8,128)S(1)} %get-tuple-element.17.refs_0_.own.w), channel_id=1, source_target_pairs={{0,16},{16,32},{32,48},{48,64},{64,80},{80,96},{96,112},{112,128},... | collective-permute-start | bytes 393224 | tf_op jit(solution)/shard_map/ppermute | solution.py:419
  38.8 1.9 %collective-permute-start.5 = (f32[4,64,128]{2,1,0:T(8,128)S(1)}, f32[4,64,128]{2,1,0:T(8,128)S(1)}, u32[]{:S(2)}, u32[]{:S(2)}) collective-permute-start(f32[4,64,128]{2,1,0:T(8,128)S(1)} %get-tuple-element.17.refs_0_.own.w), channel_id=1, source_target_pairs={{16,0},{32,16},{48,32},{64,48},{80,64},{96,80},{112,96},{128,112},... | collective-permute-start | bytes 393224 | tf_op jit(solution)/shard_map/ppermute | solution.py:420
  40.7 0.0 collective-permute-done.8.refs_1_.low
  40.8 0.0 collective-permute-done.9.refs_2_.high
  40.8 0.7 copy-done.4
  41.4 0.7 copy-done.6
  42.1 1.9 %pack_rim.5 = (f32[56,8,128]{2,1,0:T(8,128)}, f32[56,8,128]{2,1,0:T(8,128)}) custom-call(f32[8,64,128]{2,1,0:T(8,128)} %bitcast.6, f32[8,64,128]{2,1,0:T(8,128)} %copy-done.4, f32[8,64,128]{2,1,0:T(8,128)} %copy-done.6), custom_call_target="tpu_custom_call" | custom-call | tf_op jit(solution)/shard_map/pack_rim/pallas_call | solution.py:57
  44.1 3.3 %collective-permute-start.10 = (f32[56,8,128]{2,1,0:T(8,128)}, f32[56,8,128]{2,1,0:T(8,128)S(1)}, u32[]{:S(2)}, u32[]{:S(2)}) collective-permute-start(f32[56,8,128]{2,1,0:T(8,128)} %get-tuple-element.21), channel_id=1, source_target_pairs={{0,1},{1,2},{2,3},{3,4},{4,5},{5,6},{6,7},{7,8},{8,9},{9,10},{10,1... | collective-permute-start | bytes 688136 | tf_op jit(solution)/shard_map/ppermute | solution.py:419
  47.4 1.3 %collective-permute-start.11 = (f32[56,8,128]{2,1,0:T(8,128)}, f32[56,8,128]{2,1,0:T(8,128)S(1)}, u32[]{:S(2)}, u32[]{:S(2)}) collective-permute-start(f32[56,8,128]{2,1,0:T(8,128)} %get-tuple-element.22), channel_id=1, source_target_pairs={{1,0},{2,1},{3,2},{4,3},{5,4},{6,5},{7,6},{8,7},{9,8},{10,9},{11,1... | collective-permute-start | bytes 688136 | tf_op jit(solution)/shard_map/ppermute | solution.py:420
  48.7 0.0 collective-permute-done.4.refs_1_.low
  48.7 0.0 collective-permute-done.5.refs_2_.high
  48.7 0.6 copy-done.12
  49.4 0.6 copy-done.14
  50.0 1.7 %pack_rim.4 = (f32[28,8,128]{2,1,0:T(8,128)}, f32[28,8,128]{2,1,0:T(8,128)}) custom-call(f32[4,64,128]{2,1,0:T(8,128)} %copy-done.2, f32[4,64,128]{2,1,0:T(8,128)} %copy-done.12, f32[4,64,128]{2,1,0:T(8,128)} %copy-done.14), custom_call_target="tpu_custom_call" | custom-call | tf_op jit(solution)/shard_map/pack_rim/pallas_call | solution.py:57
  51.7 4.0 %collective-permute-start.6 = (f32[28,8,128]{2,1,0:T(8,128)}, f32[28,8,128]{2,1,0:T(8,128)S(1)}, u32[]{:S(2)}, u32[]{:S(2)}) collective-permute-start(f32[28,8,128]{2,1,0:T(8,128)} %get-tuple-element.18), channel_id=1, source_target_pairs={{0,1},{1,2},{2,3},{3,4},{4,5},{5,6},{6,7},{7,8},{8,9},{9,10},{10,1... | collective-permute-start | bytes 344072 | tf_op jit(solution)/shard_map/ppermute | solution.py:419
  55.7 1.3 %collective-permute-start.7 = (f32[28,8,128]{2,1,0:T(8,128)}, f32[28,8,128]{2,1,0:T(8,128)S(1)}, u32[]{:S(2)}, u32[]{:S(2)}) collective-permute-start(f32[28,8,128]{2,1,0:T(8,128)} %get-tuple-element.19), channel_id=1, source_target_pairs={{1,0},{2,1},{3,2},{4,3},{5,4},{6,5},{7,6},{8,7},{9,8},{10,9},{11,1... | collective-permute-start | bytes 344072 | tf_op jit(solution)/shard_map/ppermute | solution.py:420
  57.0 0.0 collective-permute-done.10.from_low
  57.1 0.9 copy-done.5
  58.0 0.9 copy-done.7
  59.0 6.3 %old_images.1.old_image = f32[8,64,128]{2,1,0:T(8,128)S(1)} custom-call(f32[8,64,128]{2,1,0:T(8,128)S(1)} %bitcast.7, f32[8,64,128]{2,1,0:T(8,128)S(1)} %copy-done.5, f32[8,64,128]{2,1,0:T(8,128)S(1)} %copy-done.7, f32[56,8,128]{2,1,0:T(8,128)S(1)} %collective-permute-done.10.from_low, f32[56,8,128]{2,1,0:T(8,128)S(1)} %collective-permute-done.11.from_high, ...), custom_call_target="tpu_custom_call" | custom-call | flops 12000000 | bytes 4000000 | tf_op jit(solution)/shard_map/old_images/pallas_call | solution.py:202
  65.3 4.6 %image_and_gram.1 = (f32[4,64,128]{2,1,0:T(8,128)S(1)}, f32[32,8,128]{2,1,0:T(8,128)S(1)}) custom-call(f32[4,64,128]{2,1,0:T(8,128)S(1)} %copy-done.3, f32[4,64,128]{2,1,0:T(8,128)S(1)} %copy-done.13, f32[4,64,128]{2,1,0:T(8,128)S(1)} %copy-done.15, f32[28,8,128]{2,1,0:T(8,128)S(1)} %collective-permute-done.6.from_low, ...), custom_call_target="tpu_custom_call" | custom-call | tf_op jit(solution)/shard_map/image_and_gram/pallas_call | solution.py:299
  69.9 17.8 %all_to_all.10.parts = f32[32,8,128]{2,1,0:T(8,128)} all-to-all(f32[32,8,128]{2,1,0:T(8,128)S(1)} %get-tuple-element.23), channel_id=1, replica_groups=mesh['z'=16,'core'=2,'gy'=16] {'core','gy'}, dimensions={0} | all-to-all | bytes 262144 | tf_op jit(solution)/shard_map/all_to_all | solution.py:446
  87.8 1.6 %sum_and_spread.1 = f32[16,8,128]{2,1,0:T(8,128)} custom-call(f32[32,8,128]{2,1,0:T(8,128)} %all_to_all.10.parts), custom_call_target="tpu_custom_call" | custom-call | tf_op jit(solution)/shard_map/sum_and_spread/pallas_call | solution.py:318
  89.3 30.6 %all_to_all.11.parts = f32[16,8,128]{2,1,0:T(8,128)S(1)} all-to-all(f32[16,8,128]{2,1,0:T(8,128)} %sum_and_spread.1), channel_id=1, replica_groups=mesh['z'=16,'core'=2,'gy'=16] {'z'}, dimensions={0} | all-to-all | bytes 131072 | tf_op jit(solution)/shard_map/all_to_all | solution.py:447
  119.9 5.5 %finish.1 = f32[2,8,4,8,128]{4,3,2,1,0:T(8,128)} custom-call(f32[16,8,128]{2,1,0:T(8,128)S(1)} %all_to_all.11.parts, f32[8,64,128]{2,1,0:T(8,128)S(1)} %bitcast.9, f32[4,64,128]{2,1,0:T(8,128)S(1)} %bitcast.12, f32[4,64,128]{2,1,0:T(8,128)S(1)} %copy-done.3, f32[8,64,128]{2,1,0:T(8,128)S(1)} %old_images.1.old_image, f32[4,64,128]{2,1,0:T(8,128)S(1)} %get-tuple-element.24.w_image), custom_call_target="tpu_custom_call" | custom-call | tf_op jit(solution)/shard_map/finish/pallas_call | solution.py:404
  (27 shorter events, 0.1 us)
Async XLA Ops:
  0.0 12.5 %copy-start.16 = (f32[3,2,4,4,8,128]{5,4,3,2,1,0:T(8,128)S(1)}, f32[3,2,4,4,8,128]{5,4,3,2,1,0:T(8,128)}, u32[]{:S(2)}) copy-start(f32[3,2,4,4,8,128]{5,4,3,2,1,0:T(8,128)} %param.2) | copy-start | bytes 1179652
  1.0 0.7 copy-start.17
  2.4 14.7 %collective-permute-start = (f32[4,72,128]{2,1,0:T(8,128)}, f32[4,72,128]{2,1,0:T(8,128)S(1)}, u32[]{:S(2)}, u32[]{:S(2)}) collective-permute-start(f32[4,72,128]{2,1,0:T(8,128)} %pad_maximum_fusion.refs_0_.own), channel_id=1, source_target_pairs={{0,16},{16,32},{32,48},{48,64},{64,80},{80,96},{96,112},{112,128},... | collective-permute-start | bytes 442376 | tf_op jit(solution)/shard_map/ppermute | solution.py:419
  7.3 9.8 %collective-permute-start.1 = (f32[4,72,128]{2,1,0:T(8,128)}, f32[4,72,128]{2,1,0:T(8,128)S(1)}, u32[]{:S(2)}, u32[]{:S(2)}) collective-permute-start(f32[4,72,128]{2,1,0:T(8,128)} %pad_maximum_fusion.refs_0_.own), channel_id=1, source_target_pairs={{16,0},{32,16},{48,32},{64,48},{80,64},{96,80},{112,96},{128,112},... | collective-permute-start | bytes 442376 | tf_op jit(solution)/shard_map/ppermute | solution.py:420
  12.7 22.1 %copy-start = (f32[2,4,8,2,4,128]{5,4,3,2,1,0:T(4,128)}, f32[2,4,8,2,4,128]{5,4,3,2,1,0:T(4,128)S(1)}, u32[]{:S(2)}) copy-start(f32[2,4,8,2,4,128]{5,4,3,2,1,0:T(4,128)S(1)} %copy.4) | copy-start | bytes 786436
  12.7 28.0 %collective-permute-start.8 = (f32[8,64,128]{2,1,0:T(8,128)S(1)}, f32[8,64,128]{2,1,0:T(8,128)S(1)}, u32[]{:S(2)}, u32[]{:S(2)}) collective-permute-start(f32[8,64,128]{2,1,0:T(8,128)S(1)} %bitcast.4), channel_id=1, source_target_pairs={{0,16},{16,32},{32,48},{48,64},{64,80},{80,96},{96,112},{112,128},... | collective-permute-start | bytes 786440 | tf_op jit(solution)/shard_map/ppermute | solution.py:419
  14.6 26.1 %collective-permute-start.9 = (f32[8,64,128]{2,1,0:T(8,128)S(1)}, f32[8,64,128]{2,1,0:T(8,128)S(1)}, u32[]{:S(2)}, u32[]{:S(2)}) collective-permute-start(f32[8,64,128]{2,1,0:T(8,128)S(1)} %bitcast.5), channel_id=1, source_target_pairs={{16,0},{32,16},{48,32},{64,48},{80,64},{96,80},{112,96},{128,112},... | collective-permute-start | bytes 786440 | tf_op jit(solution)/shard_map/ppermute | solution.py:420
  17.1 0.7 copy-start.8
  17.7 0.7 copy-start.10
  20.2 4.5 %collective-permute-start.2 = (f32[32,8,128]{2,1,0:T(8,128)}, f32[32,8,128]{2,1,0:T(8,128)S(1)}, u32[]{:S(2)}, u32[]{:S(2)}) collective-permute-start(f32[32,8,128]{2,1,0:T(8,128)} %get-tuple-element.15), channel_id=1, source_target_pairs={{0,1},{1,2},{2,3},{3,4},{4,5},{5,6},{6,7},{7,8},{8,9},{9,10},{10,1... | collective-permute-start | bytes 393224 | tf_op jit(solution)/shard_map/ppermute | solution.py:419
  21.5 7.3 %collective-permute-start.3 = (f32[32,8,128]{2,1,0:T(8,128)}, f32[32,8,128]{2,1,0:T(8,128)S(1)}, u32[]{:S(2)}, u32[]{:S(2)}) collective-permute-start(f32[32,8,128]{2,1,0:T(8,128)} %get-tuple-element.16), channel_id=1, source_target_pairs={{1,0},{2,1},{3,2},{4,3},{5,4},{6,5},{7,6},{8,7},{9,8},{10,9},{11,1... | collective-permute-start | bytes 393224 | tf_op jit(solution)/shard_map/ppermute | solution.py:420
  28.8 0.9 copy-start.9
  29.7 0.9 copy-start.11
  34.7 9.3 %copy-start.2 = (f32[4,64,128]{2,1,0:T(8,128)}, f32[4,64,128]{2,1,0:T(8,128)S(1)}, u32[]{:S(2)}) copy-start(f32[4,64,128]{2,1,0:T(8,128)S(1)} %get-tuple-element.17.refs_0_.own.w) | copy-start | bytes 393220
  34.8 14.0 %collective-permute-start.4 = (f32[4,64,128]{2,1,0:T(8,128)S(1)}, f32[4,64,128]{2,1,0:T(8,128)S(1)}, u32[]{:S(2)}, u32[]{:S(2)}) collective-permute-start(f32[4,64,128]{2,1,0:T(8,128)S(1)} %get-tuple-element.17.refs_0_.own.w), channel_id=1, source_target_pairs={{0,16},{16,32},{32,48},{48,64},{64,80},{80,96},{96,112},{112,128},... | collective-permute-start | bytes 393224 | tf_op jit(solution)/shard_map/ppermute | solution.py:419
  38.8 9.9 %collective-permute-start.5 = (f32[4,64,128]{2,1,0:T(8,128)S(1)}, f32[4,64,128]{2,1,0:T(8,128)S(1)}, u32[]{:S(2)}, u32[]{:S(2)}) collective-permute-start(f32[4,64,128]{2,1,0:T(8,128)S(1)} %get-tuple-element.17.refs_0_.own.w), channel_id=1, source_target_pairs={{16,0},{32,16},{48,32},{64,48},{80,64},{96,80},{112,96},{128,112},... | collective-permute-start | bytes 393224 | tf_op jit(solution)/shard_map/ppermute | solution.py:420
  40.7 0.7 copy-start.4
  41.4 0.7 copy-start.6
  44.1 13.0 %copy-start.1 = (f32[2,4,8,2,4,128]{5,4,3,2,1,0:T(4,128)S(1)}, f32[2,4,8,2,4,128]{5,4,3,2,1,0:T(4,128)}, u32[]{:S(2)}) copy-start(f32[2,4,8,2,4,128]{5,4,3,2,1,0:T(4,128)} %copy-done) | copy-start | bytes 786436
  44.1 13.0 %collective-permute-start.10 = (f32[56,8,128]{2,1,0:T(8,128)}, f32[56,8,128]{2,1,0:T(8,128)S(1)}, u32[]{:S(2)}, u32[]{:S(2)}) collective-permute-start(f32[56,8,128]{2,1,0:T(8,128)} %get-tuple-element.21), channel_id=1, source_target_pairs={{0,1},{1,2},{2,3},{3,4},{4,5},{5,6},{6,7},{7,8},{8,9},{9,10},{10,1... | collective-permute-start | bytes 688136 | tf_op jit(solution)/shard_map/ppermute | solution.py:419
  47.4 9.6 %collective-permute-start.11 = (f32[56,8,128]{2,1,0:T(8,128)}, f32[56,8,128]{2,1,0:T(8,128)S(1)}, u32[]{:S(2)}, u32[]{:S(2)}) collective-permute-start(f32[56,8,128]{2,1,0:T(8,128)} %get-tuple-element.22), channel_id=1, source_target_pairs={{1,0},{2,1},{3,2},{4,3},{5,4},{6,5},{7,6},{8,7},{9,8},{10,9},{11,1... | collective-permute-start | bytes 688136 | tf_op jit(solution)/shard_map/ppermute | solution.py:420
  48.7 0.7 copy-start.12
  49.4 0.6 copy-start.14
  51.7 13.5 %collective-permute-start.6 = (f32[28,8,128]{2,1,0:T(8,128)}, f32[28,8,128]{2,1,0:T(8,128)S(1)}, u32[]{:S(2)}, u32[]{:S(2)}) collective-permute-start(f32[28,8,128]{2,1,0:T(8,128)} %get-tuple-element.18), channel_id=1, source_target_pairs={{0,1},{1,2},{2,3},{3,4},{4,5},{5,6},{6,7},{7,8},{8,9},{9,10},{10,1... | collective-permute-start | bytes 344072 | tf_op jit(solution)/shard_map/ppermute | solution.py:419
  55.7 9.5 %collective-permute-start.7 = (f32[28,8,128]{2,1,0:T(8,128)}, f32[28,8,128]{2,1,0:T(8,128)S(1)}, u32[]{:S(2)}, u32[]{:S(2)}) collective-permute-start(f32[28,8,128]{2,1,0:T(8,128)} %get-tuple-element.19), channel_id=1, source_target_pairs={{1,0},{2,1},{3,2},{4,3},{5,4},{6,5},{7,6},{8,7},{9,8},{10,9},{11,1... | collective-permute-start | bytes 344072 | tf_op jit(solution)/shard_map/ppermute | solution.py:420
  57.1 1.0 copy-start.5
  58.0 0.9 copy-start.7
  59.0 6.3 %copy-start.3 = (f32[4,64,128]{2,1,0:T(8,128)S(1)}, f32[4,64,128]{2,1,0:T(8,128)}, u32[]{:S(2)}) copy-start(f32[4,64,128]{2,1,0:T(8,128)} %copy-done.2) | copy-start | bytes 393220
  59.0 6.3 %copy-start.13 = (f32[4,64,128]{2,1,0:T(8,128)S(1)}, f32[4,64,128]{2,1,0:T(8,128)}, u32[]{:S(2)}) copy-start(f32[4,64,128]{2,1,0:T(8,128)} %copy-done.12) | copy-start | bytes 393220
  59.0 6.3 %copy-start.15 = (f32[4,64,128]{2,1,0:T(8,128)S(1)}, f32[4,64,128]{2,1,0:T(8,128)}, u32[]{:S(2)}) copy-start(f32[4,64,128]{2,1,0:T(8,128)} %copy-done.14) | copy-start | bytes 393220

commit v2 on v1

--- a/solution.py
+++ b/solution.py
@@ -38,18 +38,19 @@
             for i in range(WIDTHS[d - 1]):
                 ref, x = plane_of((low, own, high), d + i)
                 spot = group * RIM + STARTS[d - 1] + i
-                up[spot] = ref[group * LX + x, pl.ds((LY - d) * 8, 8), :]
-                down[spot] = ref[group * LX + x, pl.ds((d - 1) * 8, 8), :]
+                up[spot] = ref[x, pl.ds((group * LY + LY - d) * 8, 8), :]
+                down[spot] = ref[x, pl.ds((group * LY + d - 1) * 8, 8), :]
     if with_coefficient:
-        up[RIM + 3] = jnp.zeros((8, NZ), F32)
-        down[RIM + 3] = jnp.zeros((8, NZ), F32)
+        base, line = groups * RIM, groups * LY * 8
+        up[base + 3] = jnp.zeros((8, NZ), F32)
+        down[base + 3] = jnp.zeros((8, NZ), F32)
         for d in range(1, HALO + 1):
             for i in range(WIDTHS[d - 1]):
                 ref, x = plane_of((low, own, high), d + i)
                 spot = STARTS[d - 1] + i
-                tile, row = RIM + spot // 8, spot % 8
-                up[tile, pl.ds(row, 1), :] = ref[x, pl.ds(LY * 8 + LY - d, 1), :]
-                down[tile, pl.ds(row, 1), :] = ref[x, pl.ds(LY * 8 + d - 1, 1), :]
+                tile, row = base + spot // 8, spot % 8
+                up[tile, pl.ds(row, 1), :] = ref[x, pl.ds(line + LY - d, 1), :]
+                down[tile, pl.ds(row, 1), :] = ref[x, pl.ds(line + d - 1, 1), :]
 
 
 def pack_rim(groups, with_coefficient, own, low, high):
@@ -59,16 +60,16 @@
         out_shape=(shape, shape),
         in_specs=[VMEM] * 3,
         out_specs=(VMEM, VMEM),
+        compiler_params=pltpu.CompilerParams(vmem_limit_bytes=1 << 20),
         name="pack_rim",
     )(own, low, high)
 
 
 def fill_block(group, parts, from_low, from_high, wide):
-    low, own, high = parts
     wide[...] = jnp.zeros(wide.shape, F32)
     for index in range(EX):
         ref, x = plane_of(parts, index)
-        wide[index, HALO:HALO + LY] = ref[group * LX + x, pl.ds(0, LY * 8), :].reshape(LY, 8, NZ)
+        wide[index, HALO:HALO + LY] = ref[x, pl.ds(group * LY * 8, LY * 8), :].reshape(LY, 8, NZ)
     for d in range(1, HALO + 1):
         spot = group * RIM + STARTS[d - 1]
         for i in range(WIDTHS[d - 1]):
@@ -76,15 +77,15 @@
             wide[d + i, HALO + LY - 1 + d] = from_high[spot + i]
 
 
-def fill_coefficient(parts, from_low, from_high, wide):
+def fill_coefficient(groups, parts, from_low, from_high, wide):
     wide[...] = jnp.zeros(wide.shape, F32)
     for index in range(EX):
         ref, x = plane_of(parts, index)
-        wide[index, HALO:HALO + LY] = ref[x, pl.ds(LY * 8, LY), :]
+        wide[index, HALO:HALO + LY] = ref[x, pl.ds(groups * LY * 8, LY), :]
     for d in range(1, HALO + 1):
         for i in range(WIDTHS[d - 1]):
             spot = STARTS[d - 1] + i
-            tile, row = RIM + spot // 8, spot % 8
+            tile, row = groups * RIM + spot // 8, spot % 8
             wide[d + i, pl.ds(HALO - d, 1), :] = from_low[tile, pl.ds(row, 1), :]
             wide[d + i, pl.ds(HALO + LY - 1 + d, 1), :] = from_high[tile, pl.ds(row, 1), :]
 
@@ -162,8 +163,8 @@
 def first_kernel(own, low, high, from_low, from_high, out, coef, block, first, second,
                  table_re, table_im, diag_re, diag_im):
     parts = (low, own, high)
-    fill_block(0, parts, from_low, from_high, block)
-    fill_coefficient(parts, from_low, from_high, coef)
+    fill_block(2, parts, from_low, from_high, block)
+    fill_coefficient(3, parts, from_low, from_high, coef)
     fill_tables(coef, table_re, table_im, diag_re, diag_im)
 
     def store(x, y, value):
@@ -186,28 +187,27 @@
     )(*args)
 
 
-def old_kernel(own, low, high, from_low, from_high, coef, out, block, first, second,
+def old_kernel(group, own, low, high, from_low, from_high, coef, out, block, first, second,
                table_re, table_im, diag_re, diag_im):
     fill_tables(coef, table_re, table_im, diag_re, diag_im)
-    for group in range(2):
-        fill_block(group, (low, own, high), from_low, from_high, block)
-
-        def store(x, y, value, group=group):
-            out[group * LX + x, pl.ds(y * 8, 8), :] = value
-
-        smooth(block, coef, table_re, table_im, first, second, store)
-
-
-def old_images(*args):
-    return pl.pallas_call(
-        old_kernel,
-        out_shape=jax.ShapeDtypeStruct((2 * LX, LY * 8, NZ), F32),
+    fill_block(group, (low, own, high), from_low, from_high, block)
+
+    def store(x, y, value):
+        out[x, pl.ds(y * 8, 8), :] = value
+
+    smooth(block, coef, table_re, table_im, first, second, store)
+
+
+def old_image(group, *args):
+    return pl.pallas_call(
+        functools.partial(old_kernel, group),
+        out_shape=jax.ShapeDtypeStruct((LX, LY * 8, NZ), F32),
         in_specs=[VMEM] * 6,
         out_specs=VMEM,
         scratch_shapes=SMOOTH_SCRATCH,
         compiler_params=pltpu.CompilerParams(vmem_limit_bytes=24 << 20),
-        cost_estimate=pl.CostEstimate(flops=12_000_000, bytes_accessed=4_000_000, transcendentals=0),
-        name="old_images",
+        cost_estimate=pl.CostEstimate(flops=6_000_000, bytes_accessed=12_000_000, transcendentals=0),
+        name="old_image",
     )(*args)
 
 
@@ -219,11 +219,11 @@
     return high, middle, low
 
 
-def basis_plane(old, recent, w, old_image, w_image, x):
-    refs = [(old, x), (old, LX + x), (recent, x), (w, x), (old_image, x), (old_image, LX + x), (w_image, x)]
+def basis_plane(start, w, image0, image1, w_image, x):
+    refs = [(start, 0), (start, LY), (start, 2 * LY), (w, 0), (image0, 0), (image1, 0), (w_image, 0)]
     rows = []
-    for ref, index in refs:
-        rows.append(jnp.concatenate([ref[index, pl.ds(y * 8, 8), :] for y in range(LY)], axis=1))
+    for ref, first in refs:
+        rows.append(jnp.concatenate([ref[x, pl.ds((first + y) * 8, 8), :] for y in range(LY)], axis=1))
     rows.append(jnp.zeros((8, LY * NZ), F32))
     return jnp.concatenate(rows, axis=0)
 
@@ -272,7 +272,7 @@
     return jnp.where(tall // 8 <= wide // 8, upper, upper.T)
 
 
-def gram_kernel(peers, own, low, high, from_low, from_high, coef, old, recent, old_image, w_image, out,
+def gram_kernel(peers, own, low, high, from_low, from_high, coef, start, image0, image1, w_image, out,
                 block, first, second, table_re, table_im, diag_re, diag_im):
     fill_tables(coef, table_re, table_im, diag_re, diag_im)
     fill_block(0, (low, own, high), from_low, from_high, block)
@@ -283,7 +283,7 @@
     smooth(block, coef, table_re, table_im, first, second, store)
 
     def plane(x, total):
-        stacked = jnp.concatenate(split3(basis_plane(old, recent, own, old_image, w_image, x)), axis=0)
+        stacked = jnp.concatenate(split3(basis_plane(start, own, image0, image1, w_image, x)), axis=0)
         return total + lax.dot_general(stacked, stacked, (((1,), (1,)), ((), ())), preferred_element_type=F32)
 
     total = lax.fori_loop(0, LX, plane, jnp.zeros((3 * ROWS, 3 * ROWS), F32))
@@ -320,6 +320,7 @@
         out_shape=jax.ShapeDtypeStruct((peers, 8, NZ), F32),
         in_specs=[VMEM],
         out_specs=VMEM,
+        compiler_params=pltpu.CompilerParams(vmem_limit_bytes=1 << 20),
         name="sum_and_spread",
     )(parts)
 
@@ -381,7 +382,7 @@
     return new, newest
 
 
-def final_kernel(cells, parts, old, recent, w, old_image, w_image, out):
+def final_kernel(cells, parts, start, w, image0, image1, w_image, out):
     gram = unpack_gram(jnp.sum(parts[...], axis=0) * (1.0 / cells))
     new, newest = coefficients(gram)
     mapping = jnp.concatenate([new, newest], axis=0)[:, 0:ROWS]
@@ -389,7 +390,7 @@
     stacked_map = jnp.concatenate(pieces, axis=0)
 
     def plane(x, carry):
-        stacked = jnp.concatenate(split3(basis_plane(old, recent, w, old_image, w_image, x)), axis=0)
+        stacked = jnp.concatenate(split3(basis_plane(start, w, image0, image1, w_image, x)), axis=0)
         full = lax.dot_general(stacked_map, stacked, (((1,), (0,)), ((), ())), preferred_element_type=F32)
         result = full[32:48] + full[16:32] + full[0:16]
         for k in range(2):
@@ -423,29 +424,23 @@
 
 def per_device(nx, ny, nz, prior, coefficient):
     cells = coefficient.size * nx * ny
-    by_cell = prior.transpose(0, 3, 4, 1, 2, 5).reshape(3, LX, LY * 8, NZ)
-    recent = by_cell[2]
-    old = by_cell[:2].reshape(2 * LX, LY * 8, NZ)
-
-    start = jnp.concatenate([recent, coefficient], axis=1)
-    low, high = from_both(GX, nx, start, start)
-    up, down = pack_rim(1, True, start, low, high)
-    below, above = from_both("gy", ny, up, down)
-    w, coef = first_image(start, low, high, below, above)
-
-    old_low, old_high = from_both(GX, nx, old, old)
-    up, down = pack_rim(2, False, old, old_low, old_high)
-    old_below, old_above = from_both("gy", ny, up, down)
-
-    low, high = from_both(GX, nx, w, w)
-    up, down = pack_rim(1, False, w, low, high)
-    below, above = from_both("gy", ny, up, down)
-    old_image = old_images(old, old_low, old_high, old_below, old_above, coef)
-
-    w_image, spread = image_and_gram(2 * ny, w, low, high, below, above, coef, old, recent, old_image)
+    by_cell = prior.transpose(3, 0, 4, 1, 2, 5).reshape(LX, 3 * LY * 8, NZ)
+    start = jnp.concatenate([by_cell, coefficient], axis=1)
+    sides = from_both(GX, nx, start, start)
+    up, down = pack_rim(3, True, start, *sides)
+    rims = from_both("gy", ny, up, down)
+    w, coef = first_image(start, *sides, *rims)
+
+    w_sides = from_both(GX, nx, w, w)
+    up, down = pack_rim(1, False, w, *w_sides)
+    w_rims = from_both("gy", ny, up, down)
+    image0 = old_image(0, start, *sides, *rims, coef)
+    image1 = old_image(1, start, *sides, *rims, coef)
+
+    w_image, spread = image_and_gram(2 * ny, w, *w_sides, *w_rims, coef, start, image0, image1)
     got = lax.all_to_all(spread, ("core", "gy"), 0, 0)
     got = lax.all_to_all(sum_and_spread(got, nz), "z", 0, 0)
-    out = finish(cells, got, old, recent, w, old_image, w_image)
+    out = finish(cells, got, start, w, image0, image1, w_image)
     return out.reshape(2, 2, 4, LX, LY, NZ)
 
 

time: 126 us -> 107 us (0.85)
  waiting for transfers between devices: 6.03 us -> 15 us
  local copies, waits for them, and re-layouts: 9.57 us -> 1.27 us
  starting transfers between devices: 32.8 us -> 24.5 us
  Pallas kernels: 27.6 us -> 20.1 us
  blocking collectives: 48.4 us -> 46 us
    ppermute x6 -> x4, starting transfers between devices: 19.5 us -> 11.2 us  [from_both(): lax.ppermute(to_higher, axis, [(i, i + 1) for i in range(count - 1)])]
    unnamed x36 -> x2, local copies, waits for them, and re-layouts: 8.31 us -> 0.01 us
    ppermute x6 -> x4, waiting for transfers between devices: 1.88 us -> 10.1 us  [from_both(): lax.ppermute(to_higher, axis, [(i, i + 1) for i in range(count - 1)])]
    pallas_call x3 -> x2, Pallas kernels: 5.45 us -> 0.08 us  [pack_rim(): pl.pallas_call(functools.partial(rim_kernel, groups, with_coefficient), o...]
    pallas_call x1, Pallas kernels: 1.57 us -> 0.04 us  [sum_and_spread(): pl.pallas_call(sum_kernel, out_shape=jax.ShapeDtypeStruct((peers, 8, NZ),...]
    all_to_all x1, blocking collectives: 17.8 us -> 16.5 us  [per_device(): got = lax.all_to_all(spread, ('core', 'gy'), 0, 0)]
    transpose x0 -> x1, local copies, waits for them, and re-layouts: none -> 1.26 us  [per_device(): by_cell = prior.transpose(3, 0, 4, 1, 2, 5).reshape(LX, 3 * LY * 8, NZ)]
    slice x4 -> x0, local copies, waits for them, and re-layouts: 1.26 us -> none  [the longest x2 1.07 us: per_device(): recent = by_cell[2]]
  transfers between devices with their start and end apart: 12 -> 8, of which waited for: 2 -> 5; matrix products, arithmetic and copies ran while one was open for 0% -> 0% of each run, Pallas kernels for 13% -> 6%
where the time goes in v2:
time: 107 us
  blocking collectives  46 us (43%)
  starting transfers between devices  24.5 us (23%)
  Pallas kernels  20.1 us (19%)
  waiting for transfers between devices  15 us (14%)
  local copies, waits for them, and re-layouts  1.27 us (1%)
    all_to_all x1, blocking collectives, per_device(): got = lax.all_to_all(sum_and_spread(got, nz), 'z', 0, 0)  29.5 us
    all_to_all x1, blocking collectives, per_device(): got = lax.all_to_all(spread, ('core', 'gy'), 0, 0)  16.5 us
    ppermute x4, starting transfers between devices, from_both(): lax.ppermute(to_lower, axis, [(i + 1, i) for i in range(count - 1)])  13.3 us
    ppermute x4, starting transfers between devices, from_both(): lax.ppermute(to_higher, axis, [(i, i + 1) for i in range(count - 1)])  11.2 us
    ppermute x4, waiting for transfers between devices, from_both(): lax.ppermute(to_higher, axis, [(i, i + 1) for i in range(count - 1)])  10.1 us
    pallas_call x2, Pallas kernels, old_image(): pl.pallas_call(functools.partial(old_kernel, group), out_shape=jax.ShapeD...  6.5 us
    pallas_call x1, Pallas kernels, finish(): pl.pallas_call(functools.partial(final_kernel, cells), out_shape=jax.Shap...  5.54 us
    ppermute x4, waiting for transfers between devices, from_both(): lax.ppermute(to_lower, axis, [(i + 1, i) for i in range(count - 1)])  4.83 us
  transfers between devices with their start and end apart: 8, of which 5 were waited for; matrix products, arithmetic and copies ran while one was open for 0% of the time, Pallas kernels for 6%

profile of v2, /device:TPU:1, one launch (start us, length us, event | category | flops | bytes accessed | tf_op | source)
XLA Modules:
  0.0 106.9 jit_solution(11439326832910798931)
XLA Ops:
  0.0 0.0 copy-start
  0.0 1.3 %copy.3 = f32[4,3,8,2,4,128]{5,4,3,2,1,0:T(4,128)S(1)} copy(f32[4,3,8,2,4,128]{5,2,0,4,3,1:T(8,128)} %bitcast.4) | data formatting | bytes 786432 | tf_op jit(solution)/shard_map/transpose | solution.py:427
  1.3 0.0 copy-done
  1.3 8.8 %collective-permute-start.1 = (f32[4,200,128]{2,1,0:T(8,128)S(1)}, f32[4,200,128]{2,1,0:T(8,128)S(1)}, u32[]{:S(2)}, u32[]{:S(2)}) collective-permute-start(f32[4,200,128]{2,1,0:T(8,128)S(1)} %pad_maximum_fusion.refs_0_.own.start), channel_id=1, source_target_pairs={{16,0},{32,16},{48,32},{64,48},{80,64},{96,80},{112,96},{128,112},... | collective-permute-start | bytes 1228808 | tf_op jit(solution)/shard_map/ppermute | solution.py:421
  10.1 1.9 %collective-permute-start = (f32[4,200,128]{2,1,0:T(8,128)S(1)}, f32[4,200,128]{2,1,0:T(8,128)S(1)}, u32[]{:S(2)}, u32[]{:S(2)}) collective-permute-start(f32[4,200,128]{2,1,0:T(8,128)S(1)} %pad_maximum_fusion.refs_0_.own.start), channel_id=1, source_target_pairs={{0,16},{16,32},{32,48},{48,64},{64,80},{80,96},{96,112},{112,128},... | collective-permute-start | bytes 1228808 | tf_op jit(solution)/shard_map/ppermute | solution.py:420
  12.0 0.0 collective-permute-done.1.refs_2_.high
  12.1 4.9 %collective-permute-done.refs_1_.low = f32[4,200,128]{2,1,0:T(8,128)S(1)} collective-permute-done((f32[4,200,128]{2,1,0:T(8,128)S(1)}, f32[4,200,128]{2,1,0:T(8,128)S(1)}, u32[]{:S(2)}, u32[]{:S(2)}) %collective-permute-start) | collective-permute-done | bytes 409632 | tf_op jit(solution)/shard_map/ppermute | solution.py:420
  16.9 0.1 pack_rim.2
  17.0 1.3 %collective-permute-start.2 = (f32[88,8,128]{2,1,0:T(8,128)S(1)}, f32[88,8,128]{2,1,0:T(8,128)S(1)}, u32[]{:S(2)}, u32[]{:S(2)}) collective-permute-start(f32[88,8,128]{2,1,0:T(8,128)S(1)} %get-tuple-element.13), channel_id=1, source_target_pairs={{0,1},{1,2},{2,3},{3,4},{4,5},{5,6},{6,7},{7,8},{8,9},{9,10},{10,1... | collective-permute-start | bytes 1081352 | tf_op jit(solution)/shard_map/ppermute | solution.py:420
  18.3 1.3 %collective-permute-start.3 = (f32[88,8,128]{2,1,0:T(8,128)S(1)}, f32[88,8,128]{2,1,0:T(8,128)S(1)}, u32[]{:S(2)}, u32[]{:S(2)}) collective-permute-start(f32[88,8,128]{2,1,0:T(8,128)S(1)} %get-tuple-element.14), channel_id=1, source_target_pairs={{1,0},{2,1},{3,2},{4,3},{5,4},{6,5},{7,6},{8,7},{9,8},{10,9},{11,1... | collective-permute-start | bytes 1081352 | tf_op jit(solution)/shard_map/ppermute | solution.py:421
  19.6 4.0 %collective-permute-done.2.from_low = f32[88,8,128]{2,1,0:T(8,128)S(1)} collective-permute-done((f32[88,8,128]{2,1,0:T(8,128)S(1)}, f32[88,8,128]{2,1,0:T(8,128)S(1)}, u32[]{:S(2)}, u32[]{:S(2)}) %collective-permute-start.2) | collective-permute-done | bytes 360480 | tf_op jit(solution)/shard_map/ppermute | solution.py:420
  23.7 4.1 %collective-permute-done.3.from_high = f32[88,8,128]{2,1,0:T(8,128)S(1)} collective-permute-done((f32[88,8,128]{2,1,0:T(8,128)S(1)}, f32[88,8,128]{2,1,0:T(8,128)S(1)}, u32[]{:S(2)}, u32[]{:S(2)}) %collective-permute-start.3) | collective-permute-done | bytes 360480 | tf_op jit(solution)/shard_map/ppermute | solution.py:421
  27.8 3.2 %first_image.1 = (f32[4,64,128]{2,1,0:T(8,128)S(1)}, f32[12,16,128]{2,1,0:T(8,128)S(1)}) custom-call(f32[4,200,128]{2,1,0:T(8,128)S(1)} %pad_maximum_fusion.refs_0_.own.start, f32[4,200,128]{2,1,0:T(8,128)S(1)} %collective-permute-done.refs_1_.low, f32[4,200,128]{2,1,0:T(8,128)S(1)} %collective-permute-done.1.refs_2_.high, ...), custom_call_target="tpu_custom_call" | custom-call | flops 6000000 | bytes 2000000 | tf_op jit(solution)/shard_map/first_image/pallas_call | solution.py:177
  31.0 1.9 %collective-permute-start.5 = (f32[4,64,128]{2,1,0:T(8,128)S(1)}, f32[4,64,128]{2,1,0:T(8,128)S(1)}, u32[]{:S(2)}, u32[]{:S(2)}) collective-permute-start(f32[4,64,128]{2,1,0:T(8,128)S(1)} %get-tuple-element.15.refs_0_.own.w), channel_id=1, source_target_pairs={{16,0},{32,16},{48,32},{64,48},{80,64},{96,80},{112,96},{128,112},... | collective-permute-start | bytes 393224 | tf_op jit(solution)/shard_map/ppermute | solution.py:421
  32.9 4.7 %collective-permute-start.4 = (f32[4,64,128]{2,1,0:T(8,128)S(1)}, f32[4,64,128]{2,1,0:T(8,128)S(1)}, u32[]{:S(2)}, u32[]{:S(2)}) collective-permute-start(f32[4,64,128]{2,1,0:T(8,128)S(1)} %get-tuple-element.15.refs_0_.own.w), channel_id=1, source_target_pairs={{0,16},{16,32},{32,48},{48,64},{64,80},{80,96},{96,112},{112,128},... | collective-permute-start | bytes 393224 | tf_op jit(solution)/shard_map/ppermute | solution.py:420
  37.7 0.7 collective-permute-done.5.refs_2_.high
  38.4 1.2 %collective-permute-done.4.refs_1_.low = f32[4,64,128]{2,1,0:T(8,128)S(1)} collective-permute-done((f32[4,64,128]{2,1,0:T(8,128)S(1)}, f32[4,64,128]{2,1,0:T(8,128)S(1)}, u32[]{:S(2)}, u32[]{:S(2)}) %collective-permute-start.4) | collective-permute-done | bytes 131104 | tf_op jit(solution)/shard_map/ppermute | solution.py:420
  39.6 3.2 %collective-permute-start.6 = (f32[28,8,128]{2,1,0:T(8,128)S(1)}, f32[28,8,128]{2,1,0:T(8,128)S(1)}, u32[]{:S(2)}, u32[]{:S(2)}) collective-permute-start(f32[28,8,128]{2,1,0:T(8,128)S(1)} %get-tuple-element.16), channel_id=1, source_target_pairs={{0,1},{1,2},{2,3},{3,4},{4,5},{5,6},{6,7},{7,8},{8,9},{9,10},{10,1... | collective-permute-start | bytes 344072 | tf_op jit(solution)/shard_map/ppermute | solution.py:420
  42.8 1.3 %collective-permute-start.7 = (f32[28,8,128]{2,1,0:T(8,128)S(1)}, f32[28,8,128]{2,1,0:T(8,128)S(1)}, u32[]{:S(2)}, u32[]{:S(2)}) collective-permute-start(f32[28,8,128]{2,1,0:T(8,128)S(1)} %get-tuple-element.17), channel_id=1, source_target_pairs={{1,0},{2,1},{3,2},{4,3},{5,4},{6,5},{7,6},{8,7},{9,8},{10,9},{11,1... | collective-permute-start | bytes 344072 | tf_op jit(solution)/shard_map/ppermute | solution.py:421
  44.1 3.2 %old_image.3.image1 = f32[4,64,128]{2,1,0:T(8,128)S(1)} custom-call(f32[4,200,128]{2,1,0:T(8,128)S(1)} %pad_maximum_fusion.refs_0_.own.start, f32[4,200,128]{2,1,0:T(8,128)S(1)} %collective-permute-done.refs_1_.low, f32[4,200,128]{2,1,0:T(8,128)S(1)} %collective-permute-done.1.refs_2_.high, f32[88,8,128]{2,1,0:T(8,128)S(1)} %collective-permute-done.2.from_low, ...), custom_call_target="tpu_custom_call" | custom-call | flops 6000000 | bytes 12000000 | tf_op jit(solution)/shard_map/old_image/pallas_call | solution.py:202
  47.4 3.2 %old_image.2.image0 = f32[4,64,128]{2,1,0:T(8,128)S(1)} custom-call(f32[4,200,128]{2,1,0:T(8,128)S(1)} %pad_maximum_fusion.refs_0_.own.start, f32[4,200,128]{2,1,0:T(8,128)S(1)} %collective-permute-done.refs_1_.low, f32[4,200,128]{2,1,0:T(8,128)S(1)} %collective-permute-done.1.refs_2_.high, f32[88,8,128]{2,1,0:T(8,128)S(1)} %collective-permute-done.2.from_low, ...), custom_call_target="tpu_custom_call" | custom-call | flops 6000000 | bytes 12000000 | tf_op jit(solution)/shard_map/old_image/pallas_call | solution.py:202
  50.6 0.0 collective-permute-done.6.from_low
  50.7 0.0 collective-permute-done.7.from_high
  50.7 4.7 %image_and_gram.1 = (f32[4,64,128]{2,1,0:T(8,128)S(1)}, f32[32,8,128]{2,1,0:T(8,128)S(1)}) custom-call(f32[4,64,128]{2,1,0:T(8,128)S(1)} %get-tuple-element.15.refs_0_.own.w, f32[4,64,128]{2,1,0:T(8,128)S(1)} %collective-permute-done.4.refs_1_.low, f32[4,64,128]{2,1,0:T(8,128)S(1)} %collective-permute-done.5.refs_2_.high, ...), custom_call_target="tpu_custom_call" | custom-call | tf_op jit(solution)/shard_map/image_and_gram/pallas_call | solution.py:299
  55.3 16.5 %all_to_all.10.parts = f32[32,8,128]{2,1,0:T(8,128)S(1)} all-to-all(f32[32,8,128]{2,1,0:T(8,128)S(1)} %get-tuple-element.19), channel_id=1, replica_groups=mesh['z'=16,'core'=2,'gy'=16] {'core','gy'}, dimensions={0} | all-to-all | bytes 262144 | tf_op jit(solution)/shard_map/all_to_all | solution.py:441
  71.9 29.5 %all_to_all.11.parts = f32[16,8,128]{2,1,0:T(8,128)S(1)} all-to-all(f32[16,8,128]{2,1,0:T(8,128)S(1)} %sum_and_spread.1), channel_id=1, replica_groups=mesh['z'=16,'core'=2,'gy'=16] {'z'}, dimensions={0} | all-to-all | bytes 131072 | tf_op jit(solution)/shard_map/all_to_all | solution.py:442
  101.4 5.5 %finish.1 = f32[2,8,4,8,128]{4,3,2,1,0:T(8,128)} custom-call(f32[16,8,128]{2,1,0:T(8,128)S(1)} %all_to_all.11.parts, f32[4,200,128]{2,1,0:T(8,128)S(1)} %pad_maximum_fusion.refs_0_.own.start, f32[4,64,128]{2,1,0:T(8,128)S(1)} %get-tuple-element.15.refs_0_.own.w, f32[4,64,128]{2,1,0:T(8,128)S(1)} %old_image.2.image0, f32[4,64,128]{2,1,0:T(8,128)S(1)} %old_image.3.image1, ...), custom_call_target="tpu_custom_call" | custom-call | tf_op jit(solution)/shard_map/finish/pallas_call | solution.py:405
  (3 shorter events, 0.1 us)
Async XLA Ops:
  0.0 1.3 %copy-start = (f32[4,8,128]{2,1,0:T(8,128)S(1)}, f32[4,8,128]{2,1,0:T(8,128)}, u32[]{:S(2)}) copy-start(f32[4,8,128]{2,1,0:T(8,128)} %param.3) | copy-start | bytes 49156
  1.3 10.7 %collective-permute-start.1 = (f32[4,200,128]{2,1,0:T(8,128)S(1)}, f32[4,200,128]{2,1,0:T(8,128)S(1)}, u32[]{:S(2)}, u32[]{:S(2)}) collective-permute-start(f32[4,200,128]{2,1,0:T(8,128)S(1)} %pad_maximum_fusion.refs_0_.own.start), channel_id=1, source_target_pairs={{16,0},{32,16},{48,32},{64,48},{80,64},{96,80},{112,96},{128,112},... | collective-permute-start | bytes 1228808 | tf_op jit(solution)/shard_map/ppermute | solution.py:421
  10.1 6.8 %collective-permute-start = (f32[4,200,128]{2,1,0:T(8,128)S(1)}, f32[4,200,128]{2,1,0:T(8,128)S(1)}, u32[]{:S(2)}, u32[]{:S(2)}) collective-permute-start(f32[4,200,128]{2,1,0:T(8,128)S(1)} %pad_maximum_fusion.refs_0_.own.start), channel_id=1, source_target_pairs={{0,16},{16,32},{32,48},{48,64},{64,80},{80,96},{96,112},{112,128},... | collective-permute-start | bytes 1228808 | tf_op jit(solution)/shard_map/ppermute | solution.py:420
  17.0 6.7 %collective-permute-start.2 = (f32[88,8,128]{2,1,0:T(8,128)S(1)}, f32[88,8,128]{2,1,0:T(8,128)S(1)}, u32[]{:S(2)}, u32[]{:S(2)}) collective-permute-start(f32[88,8,128]{2,1,0:T(8,128)S(1)} %get-tuple-element.13), channel_id=1, source_target_pairs={{0,1},{1,2},{2,3},{3,4},{4,5},{5,6},{6,7},{7,8},{8,9},{9,10},{10,1... | collective-permute-start | bytes 1081352 | tf_op jit(solution)/shard_map/ppermute | solution.py:420
  18.3 9.5 %collective-permute-start.3 = (f32[88,8,128]{2,1,0:T(8,128)S(1)}, f32[88,8,128]{2,1,0:T(8,128)S(1)}, u32[]{:S(2)}, u32[]{:S(2)}) collective-permute-start(f32[88,8,128]{2,1,0:T(8,128)S(1)} %get-tuple-element.14), channel_id=1, source_target_pairs={{1,0},{2,1},{3,2},{4,3},{5,4},{6,5},{7,6},{8,7},{9,8},{10,9},{11,1... | collective-permute-start | bytes 1081352 | tf_op jit(solution)/shard_map/ppermute | solution.py:421
  31.0 7.4 %collective-permute-start.5 = (f32[4,64,128]{2,1,0:T(8,128)S(1)}, f32[4,64,128]{2,1,0:T(8,128)S(1)}, u32[]{:S(2)}, u32[]{:S(2)}) collective-permute-start(f32[4,64,128]{2,1,0:T(8,128)S(1)} %get-tuple-element.15.refs_0_.own.w), channel_id=1, source_target_pairs={{16,0},{32,16},{48,32},{64,48},{80,64},{96,80},{112,96},{128,112},... | collective-permute-start | bytes 393224 | tf_op jit(solution)/shard_map/ppermute | solution.py:421
  32.9 6.7 %collective-permute-start.4 = (f32[4,64,128]{2,1,0:T(8,128)S(1)}, f32[4,64,128]{2,1,0:T(8,128)S(1)}, u32[]{:S(2)}, u32[]{:S(2)}) collective-permute-start(f32[4,64,128]{2,1,0:T(8,128)S(1)} %get-tuple-element.15.refs_0_.own.w), channel_id=1, source_target_pairs={{0,16},{16,32},{32,48},{48,64},{64,80},{80,96},{96,112},{112,128},... | collective-permute-start | bytes 393224 | tf_op jit(solution)/shard_map/ppermute | solution.py:420
  39.6 11.0 %collective-permute-start.6 = (f32[28,8,128]{2,1,0:T(8,128)S(1)}, f32[28,8,128]{2,1,0:T(8,128)S(1)}, u32[]{:S(2)}, u32[]{:S(2)}) collective-permute-start(f32[28,8,128]{2,1,0:T(8,128)S(1)} %get-tuple-element.16), channel_id=1, source_target_pairs={{0,1},{1,2},{2,3},{3,4},{4,5},{5,6},{6,7},{7,8},{8,9},{9,10},{10,1... | collective-permute-start | bytes 344072 | tf_op jit(solution)/shard_map/ppermute | solution.py:420
  42.8 7.8 %collective-permute-start.7 = (f32[28,8,128]{2,1,0:T(8,128)S(1)}, f32[28,8,128]{2,1,0:T(8,128)S(1)}, u32[]{:S(2)}, u32[]{:S(2)}) collective-permute-start(f32[28,8,128]{2,1,0:T(8,128)S(1)} %get-tuple-element.17), channel_id=1, source_target_pairs={{1,0},{2,1},{3,2},{4,3},{5,4},{6,5},{7,6},{8,7},{9,8},{10,9},{11,1... | collective-permute-start | bytes 344072 | tf_op jit(solution)/shard_map/ppermute | solution.py:421

commit v3 on v2

--- a/solution.py
+++ b/solution.py
@@ -31,8 +31,7 @@
     return high, index - HALO - LX
 
 
-def rim_kernel(groups, with_coefficient, *refs):
-    own, low, high, up, down = refs[:5]
+def rim_kernel(groups, with_coefficient, own, low, high, up, down):
     for group in range(groups):
         for d in range(1, HALO + 1):
             for i in range(WIDTHS[d - 1]):
@@ -53,7 +52,7 @@
                 down[tile, pl.ds(row, 1), :] = ref[x, pl.ds(line + d - 1, 1), :]
 
 
-def pack_rim(groups, with_coefficient, own, low, high):
+def pack_rim(groups, with_coefficient, own, sides):
     shape = jax.ShapeDtypeStruct((groups * RIM + (4 if with_coefficient else 0), 8, NZ), F32)
     return pl.pallas_call(
         functools.partial(rim_kernel, groups, with_coefficient),
@@ -62,7 +61,27 @@
         out_specs=(VMEM, VMEM),
         compiler_params=pltpu.CompilerParams(vmem_limit_bytes=1 << 20),
         name="pack_rim",
-    )(own, low, high)
+    )(own, *sides)
+
+
+def turn_kernel(prior, after, old):
+    del after
+    for k in range(2):
+        for x in range(LX):
+            fields = prior[k, :, :, x].reshape(8, LY, NZ)
+            old[x, pl.ds(k * LY * 8, LY * 8), :] = jnp.swapaxes(fields, 0, 1).reshape(LY * 8, NZ)
+
+
+def turn_old(prior, after):
+    return pl.pallas_call(
+        turn_kernel,
+        out_shape=jax.ShapeDtypeStruct((LX, 2 * LY * 8, NZ), F32),
+        in_specs=[VMEM, pl.BlockSpec(memory_space=pl.ANY)],
+        out_specs=VMEM,
+        compiler_params=pltpu.CompilerParams(vmem_limit_bytes=1 << 20),
+        cost_estimate=pl.CostEstimate(flops=6_000_000, bytes_accessed=12_000_000, transcendentals=0),
+        name="turn_old",
+    )(prior, after)
 
 
 def fill_block(group, parts, from_low, from_high, wide):
@@ -163,8 +182,8 @@
 def first_kernel(own, low, high, from_low, from_high, out, coef, block, first, second,
                  table_re, table_im, diag_re, diag_im):
     parts = (low, own, high)
-    fill_block(2, parts, from_low, from_high, block)
-    fill_coefficient(3, parts, from_low, from_high, coef)
+    fill_block(0, parts, from_low, from_high, block)
+    fill_coefficient(1, parts, from_low, from_high, coef)
     fill_tables(coef, table_re, table_im, diag_re, diag_im)
 
     def store(x, y, value):
@@ -219,8 +238,8 @@
     return high, middle, low
 
 
-def basis_plane(start, w, image0, image1, w_image, x):
-    refs = [(start, 0), (start, LY), (start, 2 * LY), (w, 0), (image0, 0), (image1, 0), (w_image, 0)]
+def basis_plane(start, old, w, image0, image1, w_image, x):
+    refs = [(old, 0), (old, LY), (start, 0), (w, 0), (image0, 0), (image1, 0), (w_image, 0)]
     rows = []
     for ref, first in refs:
         rows.append(jnp.concatenate([ref[x, pl.ds((first + y) * 8, 8), :] for y in range(LY)], axis=1))
@@ -272,7 +291,7 @@
     return jnp.where(tall // 8 <= wide // 8, upper, upper.T)
 
 
-def gram_kernel(peers, own, low, high, from_low, from_high, coef, start, image0, image1, w_image, out,
+def gram_kernel(peers, own, low, high, from_low, from_high, coef, start, old, image0, image1, w_image, out,
                 block, first, second, table_re, table_im, diag_re, diag_im):
     fill_tables(coef, table_re, table_im, diag_re, diag_im)
     fill_block(0, (low, own, high), from_low, from_high, block)
@@ -283,7 +302,7 @@
     smooth(block, coef, table_re, table_im, first, second, store)
 
     def plane(x, total):
-        stacked = jnp.concatenate(split3(basis_plane(start, own, image0, image1, w_image, x)), axis=0)
+        stacked = jnp.concatenate(split3(basis_plane(start, old, own, image0, image1, w_image, x)), axis=0)
         return total + lax.dot_general(stacked, stacked, (((1,), (1,)), ((), ())), preferred_element_type=F32)
 
     total = lax.fori_loop(0, LX, plane, jnp.zeros((3 * ROWS, 3 * ROWS), F32))
@@ -300,7 +319,7 @@
         functools.partial(gram_kernel, peers),
         out_shape=(jax.ShapeDtypeStruct((LX, LY * 8, NZ), F32),
                    jax.ShapeDtypeStruct((peers, 8, NZ), F32)),
-        in_specs=[VMEM] * 9,
+        in_specs=[VMEM] * 10,
         out_specs=(VMEM, VMEM),
         scratch_shapes=SMOOTH_SCRATCH,
         compiler_params=pltpu.CompilerParams(vmem_limit_bytes=32 << 20),
@@ -382,7 +401,7 @@
     return new, newest
 
 
-def final_kernel(cells, parts, start, w, image0, image1, w_image, out):
+def final_kernel(cells, parts, start, old, w, image0, image1, w_image, out):
     gram = unpack_gram(jnp.sum(parts[...], axis=0) * (1.0 / cells))
     new, newest = coefficients(gram)
     mapping = jnp.concatenate([new, newest], axis=0)[:, 0:ROWS]
@@ -390,7 +409,7 @@
     stacked_map = jnp.concatenate(pieces, axis=0)
 
     def plane(x, carry):
-        stacked = jnp.concatenate(split3(basis_plane(start, w, image0, image1, w_image, x)), axis=0)
+        stacked = jnp.concatenate(split3(basis_plane(start, old, w, image0, image1, w_image, x)), axis=0)
         full = lax.dot_general(stacked_map, stacked, (((1,), (0,)), ((), ())), preferred_element_type=F32)
         result = full[32:48] + full[16:32] + full[0:16]
         for k in range(2):
@@ -405,7 +424,7 @@
     return pl.pallas_call(
         functools.partial(final_kernel, cells),
         out_shape=jax.ShapeDtypeStruct((2, 8, LX, LY, NZ), F32),
-        in_specs=[VMEM] * 6,
+        in_specs=[VMEM] * 7,
         out_specs=VMEM,
         compiler_params=pltpu.CompilerParams(vmem_limit_bytes=32 << 20),
         name="finish",
@@ -424,23 +443,25 @@
 
 def per_device(nx, ny, nz, prior, coefficient):
     cells = coefficient.size * nx * ny
-    by_cell = prior.transpose(3, 0, 4, 1, 2, 5).reshape(LX, 3 * LY * 8, NZ)
-    start = jnp.concatenate([by_cell, coefficient], axis=1)
+    recent = prior[2].transpose(2, 3, 0, 1, 4).reshape(LX, LY * 8, NZ)
+    start = jnp.concatenate([recent, coefficient], axis=1)
     sides = from_both(GX, nx, start, start)
-    up, down = pack_rim(3, True, start, *sides)
+    up, down = pack_rim(1, True, start, sides)
     rims = from_both("gy", ny, up, down)
+    old = turn_old(prior, rims[0])
     w, coef = first_image(start, *sides, *rims)
 
+    old_sides = from_both(GX, nx, old, old)
+    old_rims = from_both("gy", ny, *pack_rim(2, False, old, old_sides))
     w_sides = from_both(GX, nx, w, w)
-    up, down = pack_rim(1, False, w, *w_sides)
-    w_rims = from_both("gy", ny, up, down)
-    image0 = old_image(0, start, *sides, *rims, coef)
-    image1 = old_image(1, start, *sides, *rims, coef)
-
-    w_image, spread = image_and_gram(2 * ny, w, *w_sides, *w_rims, coef, start, image0, image1)
+    w_rims = from_both("gy", ny, *pack_rim(1, False, w, w_sides))
+    image0 = old_image(0, old, *old_sides, *old_rims, coef)
+    image1 = old_image(1, old, *old_sides, *old_rims, coef)
+
+    w_image, spread = image_and_gram(2 * ny, w, *w_sides, *w_rims, coef, start, old, image0, image1)
     got = lax.all_to_all(spread, ("core", "gy"), 0, 0)
     got = lax.all_to_all(sum_and_spread(got, nz), "z", 0, 0)
-    out = finish(cells, got, start, w, image0, image1, w_image)
+    out = finish(cells, got, start, old, w, image0, image1, w_image)
     return out.reshape(2, 2, 4, LX, LY, NZ)
 
 

time: 107 us -> 117 us (1.093)
  starting transfers between devices: 24.5 us -> 36.3 us
  waiting for transfers between devices: 15 us -> 8.87 us
  blocking collectives: 46 us -> 49.6 us
    ppermute x4 -> x6, starting transfers between devices: 11.2 us -> 23.5 us  [from_both(): lax.ppermute(to_higher, axis, [(i, i + 1) for i in range(count - 1)])]
    ppermute x4 -> x6, waiting for transfers between devices: 10.1 us -> 1.94 us  [from_both(): lax.ppermute(to_higher, axis, [(i, i + 1) for i in range(count - 1)])]
    all_to_all x1, blocking collectives: 16.5 us -> 18.9 us  [per_device(): got = lax.all_to_all(spread, ('core', 'gy'), 0, 0)]
    ppermute x4 -> x6, waiting for transfers between devices: 4.83 us -> 6.94 us  [from_both(): lax.ppermute(to_lower, axis, [(i + 1, i) for i in range(count - 1)])]
    all_to_all x1, blocking collectives: 29.5 us -> 30.7 us  [per_device(): got = lax.all_to_all(sum_and_spread(got, nz), 'z', 0, 0)]
    ppermute x4 -> x6, starting transfers between devices: 13.3 us -> 12.9 us  [from_both(): lax.ppermute(to_lower, axis, [(i + 1, i) for i in range(count - 1)])]
  transfers between devices with their start and end apart: 8 -> 12, of which waited for: 5 -> 4; matrix products, arithmetic and copies ran while one was open for 0% -> 0% of each run, Pallas kernels for 6% -> 8%
where the time goes in v3:
time: 117 us
  blocking collectives  49.6 us (42%)
  starting transfers between devices  36.3 us (31%)
  Pallas kernels  20.1 us (17%)
  waiting for transfers between devices  8.87 us (8%)
  local copies, waits for them, and re-layouts  1.61 us (1%)
    all_to_all x1, blocking collectives, per_device(): got = lax.all_to_all(sum_and_spread(got, nz), 'z', 0, 0)  30.7 us
    ppermute x6, starting transfers between devices, from_both(): lax.ppermute(to_higher, axis, [(i, i + 1) for i in range(count - 1)])  23.5 us
    all_to_all x1, blocking collectives, per_device(): got = lax.all_to_all(spread, ('core', 'gy'), 0, 0)  18.9 us
    ppermute x6, starting transfers between devices, from_both(): lax.ppermute(to_lower, axis, [(i + 1, i) for i in range(count - 1)])  12.9 us
    ppermute x6, waiting for transfers between devices, from_both(): lax.ppermute(to_lower, axis, [(i + 1, i) for i in range(count - 1)])  6.94 us
    pallas_call x2, Pallas kernels, old_image(): pl.pallas_call(functools.partial(old_kernel, group), out_shape=jax.ShapeD...  6.49 us
    pallas_call x1, Pallas kernels, finish(): pl.pallas_call(functools.partial(final_kernel, cells), out_shape=jax.Shap...  5.54 us
    pallas_call x1, Pallas kernels, image_and_gram(): pl.pallas_call(functools.partial(gram_kernel, peers), out_shape=(jax.Shap...  4.65 us
  transfers between devices with their start and end apart: 12, of which 4 were waited for; matrix products, arithmetic and copies ran while one was open for 0% of the time, Pallas kernels for 8%

profile of v3, /device:TPU:1, one launch (start us, length us, event | category | flops | bytes accessed | tf_op | source)
XLA Modules:
  0.0 116.8 jit_solution(4605922295949369032)
XLA Ops:
  0.0 0.9 slice_bitcast_fusion
  0.9 0.0 copy-start.1
  0.9 0.1 copy.3
  1.0 0.0 copy-start
  1.0 0.6 copy-done.1
  1.7 4.9 %collective-permute-start = (f32[4,72,128]{2,1,0:T(8,128)S(1)}, f32[4,72,128]{2,1,0:T(8,128)S(1)}, u32[]{:S(2)}, u32[]{:S(2)}) collective-permute-start(f32[4,72,128]{2,1,0:T(8,128)S(1)} %pad_maximum_fusion.own.start), channel_id=1, source_target_pairs={{0,16},{16,32},{32,48},{48,64},{64,80},{80,96},{96,112},{112,128},... | collective-permute-start | bytes 442376 | tf_op jit(solution)/shard_map/ppermute | solution.py:439
  6.6 5.1 %collective-permute-start.1 = (f32[4,72,128]{2,1,0:T(8,128)S(1)}, f32[4,72,128]{2,1,0:T(8,128)S(1)}, u32[]{:S(2)}, u32[]{:S(2)}) collective-permute-start(f32[4,72,128]{2,1,0:T(8,128)S(1)} %pad_maximum_fusion.own.start), channel_id=1, source_target_pairs={{16,0},{32,16},{48,32},{64,48},{80,64},{96,80},{112,96},{128,112},... | collective-permute-start | bytes 442376 | tf_op jit(solution)/shard_map/ppermute | solution.py:440
  11.8 0.0 collective-permute-done.low
  11.8 1.3 %collective-permute-done.1.high = f32[4,72,128]{2,1,0:T(8,128)S(1)} collective-permute-done((f32[4,72,128]{2,1,0:T(8,128)S(1)}, f32[4,72,128]{2,1,0:T(8,128)S(1)}, u32[]{:S(2)}, u32[]{:S(2)}) %collective-permute-start.1) | collective-permute-done | bytes 147488 | tf_op jit(solution)/shard_map/ppermute | solution.py:440
  13.1 3.2 %collective-permute-start.2 = (f32[32,8,128]{2,1,0:T(8,128)S(1)}, f32[32,8,128]{2,1,0:T(8,128)S(1)}, u32[]{:S(2)}, u32[]{:S(2)}) collective-permute-start(f32[32,8,128]{2,1,0:T(8,128)S(1)} %get-tuple-element.15), channel_id=1, source_target_pairs={{0,1},{1,2},{2,3},{3,4},{4,5},{5,6},{6,7},{7,8},{8,9},{9,10},{10,1... | collective-permute-start | bytes 393224 | tf_op jit(solution)/shard_map/ppermute | solution.py:439
  16.3 1.9 %collective-permute-done.2.from_low.after = f32[32,8,128]{2,1,0:T(8,128)S(1)} collective-permute-done((f32[32,8,128]{2,1,0:T(8,128)S(1)}, f32[32,8,128]{2,1,0:T(8,128)S(1)}, u32[]{:S(2)}, u32[]{:S(2)}) %collective-permute-start.2) | collective-permute-done | bytes 131104 | tf_op jit(solution)/shard_map/ppermute | solution.py:439
  18.2 0.0 copy-done
  18.2 0.1 turn_old.1.own.old
  18.3 2.7 %collective-permute-start.8 = (f32[4,128,128]{2,1,0:T(8,128)S(1)}, f32[4,128,128]{2,1,0:T(8,128)S(1)}, u32[]{:S(2)}, u32[]{:S(2)}) collective-permute-start(f32[4,128,128]{2,1,0:T(8,128)S(1)} %turn_old.1.own.old), channel_id=1, source_target_pairs={{0,16},{16,32},{32,48},{48,64},{64,80},{80,96},{96,112},{112,128},... | collective-permute-start | bytes 786440 | tf_op jit(solution)/shard_map/ppermute | solution.py:439
  21.0 1.9 %collective-permute-start.9 = (f32[4,128,128]{2,1,0:T(8,128)S(1)}, f32[4,128,128]{2,1,0:T(8,128)S(1)}, u32[]{:S(2)}, u32[]{:S(2)}) collective-permute-start(f32[4,128,128]{2,1,0:T(8,128)S(1)} %turn_old.1.own.old), channel_id=1, source_target_pairs={{16,0},{32,16},{48,32},{64,48},{80,64},{96,80},{112,96},{128,112},... | collective-permute-start | bytes 786440 | tf_op jit(solution)/shard_map/ppermute | solution.py:440
  23.0 1.3 %collective-permute-start.3 = (f32[32,8,128]{2,1,0:T(8,128)S(1)}, f32[32,8,128]{2,1,0:T(8,128)S(1)}, u32[]{:S(2)}, u32[]{:S(2)}) collective-permute-start(f32[32,8,128]{2,1,0:T(8,128)S(1)} %get-tuple-element.16), channel_id=1, source_target_pairs={{1,0},{2,1},{3,2},{4,3},{5,4},{6,5},{7,6},{8,7},{9,8},{10,9},{11,1... | collective-permute-start | bytes 393224 | tf_op jit(solution)/shard_map/ppermute | solution.py:440
  24.3 5.5 %collective-permute-done.3.from_high = f32[32,8,128]{2,1,0:T(8,128)S(1)} collective-permute-done((f32[32,8,128]{2,1,0:T(8,128)S(1)}, f32[32,8,128]{2,1,0:T(8,128)S(1)}, u32[]{:S(2)}, u32[]{:S(2)}) %collective-permute-start.3) | collective-permute-done | bytes 131104 | tf_op jit(solution)/shard_map/ppermute | solution.py:440
  29.7 3.2 %first_image.1 = (f32[4,64,128]{2,1,0:T(8,128)S(1)}, f32[12,16,128]{2,1,0:T(8,128)S(1)}) custom-call(f32[4,72,128]{2,1,0:T(8,128)S(1)} %pad_maximum_fusion.own.start, f32[4,72,128]{2,1,0:T(8,128)S(1)} %collective-permute-done.low, f32[4,72,128]{2,1,0:T(8,128)S(1)} %collective-permute-done.1.high, f32[32,8,128]{2,1,0:T(8,128)S(1)} %collective-permute-done.2.from_low.after, ...), custom_call_target="tpu_custom_call" | custom-call | flops 6000000 | bytes 2000000 | tf_op jit(solution)/shard_map/first_image/pallas_call | solution.py:196
  33.0 5.2 %collective-permute-start.4 = (f32[4,64,128]{2,1,0:T(8,128)S(1)}, f32[4,64,128]{2,1,0:T(8,128)S(1)}, u32[]{:S(2)}, u32[]{:S(2)}) collective-permute-start(f32[4,64,128]{2,1,0:T(8,128)S(1)} %get-tuple-element.17.own.w), channel_id=1, source_target_pairs={{0,16},{16,32},{32,48},{48,64},{64,80},{80,96},{96,112},{112,128},... | collective-permute-start | bytes 393224 | tf_op jit(solution)/shard_map/ppermute | solution.py:439
  38.2 1.9 %collective-permute-start.5 = (f32[4,64,128]{2,1,0:T(8,128)S(1)}, f32[4,64,128]{2,1,0:T(8,128)S(1)}, u32[]{:S(2)}, u32[]{:S(2)}) collective-permute-start(f32[4,64,128]{2,1,0:T(8,128)S(1)} %get-tuple-element.17.own.w), channel_id=1, source_target_pairs={{16,0},{32,16},{48,32},{64,48},{80,64},{96,80},{112,96},{128,112},... | collective-permute-start | bytes 393224 | tf_op jit(solution)/shard_map/ppermute | solution.py:440
  40.1 0.0 collective-permute-done.8.low
  40.1 0.0 collective-permute-done.9.high
  40.2 3.4 %collective-permute-start.10 = (f32[56,8,128]{2,1,0:T(8,128)S(1)}, f32[56,8,128]{2,1,0:T(8,128)S(1)}, u32[]{:S(2)}, u32[]{:S(2)}) collective-permute-start(f32[56,8,128]{2,1,0:T(8,128)S(1)} %get-tuple-element.21), channel_id=1, source_target_pairs={{0,1},{1,2},{2,3},{3,4},{4,5},{5,6},{6,7},{7,8},{8,9},{9,10},{10,1... | collective-permute-start | bytes 688136 | tf_op jit(solution)/shard_map/ppermute | solution.py:439
  43.6 1.3 %collective-permute-start.11 = (f32[56,8,128]{2,1,0:T(8,128)S(1)}, f32[56,8,128]{2,1,0:T(8,128)S(1)}, u32[]{:S(2)}, u32[]{:S(2)}) collective-permute-start(f32[56,8,128]{2,1,0:T(8,128)S(1)} %get-tuple-element.22), channel_id=1, source_target_pairs={{1,0},{2,1},{3,2},{4,3},{5,4},{6,5},{7,6},{8,7},{9,8},{10,9},{11,1... | collective-permute-start | bytes 688136 | tf_op jit(solution)/shard_map/ppermute | solution.py:440
  44.9 0.0 collective-permute-done.4.low
  44.9 0.0 collective-permute-done.5.high
  44.9 4.0 %collective-permute-start.6 = (f32[28,8,128]{2,1,0:T(8,128)S(1)}, f32[28,8,128]{2,1,0:T(8,128)S(1)}, u32[]{:S(2)}, u32[]{:S(2)}) collective-permute-start(f32[28,8,128]{2,1,0:T(8,128)S(1)} %get-tuple-element.18), channel_id=1, source_target_pairs={{0,1},{1,2},{2,3},{3,4},{4,5},{5,6},{6,7},{7,8},{8,9},{9,10},{10,1... | collective-permute-start | bytes 344072 | tf_op jit(solution)/shard_map/ppermute | solution.py:439
  48.9 1.3 %collective-permute-start.7 = (f32[28,8,128]{2,1,0:T(8,128)S(1)}, f32[28,8,128]{2,1,0:T(8,128)S(1)}, u32[]{:S(2)}, u32[]{:S(2)}) collective-permute-start(f32[28,8,128]{2,1,0:T(8,128)S(1)} %get-tuple-element.19), channel_id=1, source_target_pairs={{1,0},{2,1},{3,2},{4,3},{5,4},{6,5},{7,6},{8,7},{9,8},{10,9},{11,1... | collective-permute-start | bytes 344072 | tf_op jit(solution)/shard_map/ppermute | solution.py:440
  50.2 0.0 collective-permute-done.10.from_low
  50.2 0.2 collective-permute-done.11.from_high
  50.4 3.2 %old_image.3.image1 = f32[4,64,128]{2,1,0:T(8,128)S(1)} custom-call(f32[4,128,128]{2,1,0:T(8,128)S(1)} %turn_old.1.own.old, f32[4,128,128]{2,1,0:T(8,128)S(1)} %collective-permute-done.8.low, f32[4,128,128]{2,1,0:T(8,128)S(1)} %collective-permute-done.9.high, f32[56,8,128]{2,1,0:T(8,128)S(1)} %collective-permute-done.10.from_low, ...), custom_call_target="tpu_custom_call" | custom-call | flops 6000000 | bytes 12000000 | tf_op jit(solution)/shard_map/old_image/pallas_call | solution.py:221
  53.6 3.2 %old_image.2.image0 = f32[4,64,128]{2,1,0:T(8,128)S(1)} custom-call(f32[4,128,128]{2,1,0:T(8,128)S(1)} %turn_old.1.own.old, f32[4,128,128]{2,1,0:T(8,128)S(1)} %collective-permute-done.8.low, f32[4,128,128]{2,1,0:T(8,128)S(1)} %collective-permute-done.9.high, f32[56,8,128]{2,1,0:T(8,128)S(1)} %collective-permute-done.10.from_low, ...), custom_call_target="tpu_custom_call" | custom-call | flops 6000000 | bytes 12000000 | tf_op jit(solution)/shard_map/old_image/pallas_call | solution.py:221
  56.9 0.0 collective-permute-done.6.from_low
  56.9 0.0 collective-permute-done.7.from_high
  56.9 4.6 %image_and_gram.1 = (f32[4,64,128]{2,1,0:T(8,128)S(1)}, f32[32,8,128]{2,1,0:T(8,128)S(1)}) custom-call(f32[4,64,128]{2,1,0:T(8,128)S(1)} %get-tuple-element.17.own.w, f32[4,64,128]{2,1,0:T(8,128)S(1)} %collective-permute-done.4.low, f32[4,64,128]{2,1,0:T(8,128)S(1)} %collective-permute-done.5.high, f32[28,8,128]{2,1,0:T(8,128)S(1)} %collective-permute-done.6.from_low, ...), custom_call_target="tpu_custom_call" | custom-call | tf_op jit(solution)/shard_map/image_and_gram/pallas_call | solution.py:318
  61.6 18.9 %all_to_all.10.parts = f32[32,8,128]{2,1,0:T(8,128)S(1)} all-to-all(f32[32,8,128]{2,1,0:T(8,128)S(1)} %get-tuple-element.23), channel_id=1, replica_groups=mesh['z'=16,'core'=2,'gy'=16] {'core','gy'}, dimensions={0} | all-to-all | bytes 262144 | tf_op jit(solution)/shard_map/all_to_all | solution.py:462
  80.5 30.7 %all_to_all.11.parts = f32[16,8,128]{2,1,0:T(8,128)S(1)} all-to-all(f32[16,8,128]{2,1,0:T(8,128)S(1)} %sum_and_spread.1), channel_id=1, replica_groups=mesh['z'=16,'core'=2,'gy'=16] {'z'}, dimensions={0} | all-to-all | bytes 131072 | tf_op jit(solution)/shard_map/all_to_all | solution.py:463
  111.2 5.5 %finish.1 = f32[2,8,4,8,128]{4,3,2,1,0:T(8,128)} custom-call(f32[16,8,128]{2,1,0:T(8,128)S(1)} %all_to_all.11.parts, f32[4,72,128]{2,1,0:T(8,128)S(1)} %pad_maximum_fusion.own.start, f32[4,128,128]{2,1,0:T(8,128)S(1)} %turn_old.1.own.old, f32[4,64,128]{2,1,0:T(8,128)S(1)} %get-tuple-element.17.own.w, f32[4,64,128]{2,1,0:T(8,128)S(1)} %old_image.2.image0, ...), custom_call_target="tpu_custom_call" | custom-call | tf_op jit(solution)/shard_map/finish/pallas_call | solution.py:424
  (5 shorter events, 0.1 us)
Async XLA Ops:
  0.9 0.7 copy-start.1
  1.0 17.2 %copy-start = (f32[3,2,4,4,8,128]{5,4,3,2,1,0:T(8,128)S(1)}, f32[3,2,4,4,8,128]{5,4,3,2,1,0:T(8,128)}, u32[]{:S(2)}) copy-start(f32[3,2,4,4,8,128]{5,4,3,2,1,0:T(8,128)} %prior.1) | copy-start | bytes 1179652
  1.7 10.1 %collective-permute-start = (f32[4,72,128]{2,1,0:T(8,128)S(1)}, f32[4,72,128]{2,1,0:T(8,128)S(1)}, u32[]{:S(2)}, u32[]{:S(2)}) collective-permute-start(f32[4,72,128]{2,1,0:T(8,128)S(1)} %pad_maximum_fusion.own.start), channel_id=1, source_target_pairs={{0,16},{16,32},{32,48},{48,64},{64,80},{80,96},{96,112},{112,128},... | collective-permute-start | bytes 442376 | tf_op jit(solution)/shard_map/ppermute | solution.py:439
  6.6 6.5 %collective-permute-start.1 = (f32[4,72,128]{2,1,0:T(8,128)S(1)}, f32[4,72,128]{2,1,0:T(8,128)S(1)}, u32[]{:S(2)}, u32[]{:S(2)}) collective-permute-start(f32[4,72,128]{2,1,0:T(8,128)S(1)} %pad_maximum_fusion.own.start), channel_id=1, source_target_pairs={{16,0},{32,16},{48,32},{64,48},{80,64},{96,80},{112,96},{128,112},... | collective-permute-start | bytes 442376 | tf_op jit(solution)/shard_map/ppermute | solution.py:440
  13.1 5.1 %collective-permute-start.2 = (f32[32,8,128]{2,1,0:T(8,128)S(1)}, f32[32,8,128]{2,1,0:T(8,128)S(1)}, u32[]{:S(2)}, u32[]{:S(2)}) collective-permute-start(f32[32,8,128]{2,1,0:T(8,128)S(1)} %get-tuple-element.15), channel_id=1, source_target_pairs={{0,1},{1,2},{2,3},{3,4},{4,5},{5,6},{6,7},{7,8},{8,9},{9,10},{10,1... | collective-permute-start | bytes 393224 | tf_op jit(solution)/shard_map/ppermute | solution.py:439
  18.3 21.8 %collective-permute-start.8 = (f32[4,128,128]{2,1,0:T(8,128)S(1)}, f32[4,128,128]{2,1,0:T(8,128)S(1)}, u32[]{:S(2)}, u32[]{:S(2)}) collective-permute-start(f32[4,128,128]{2,1,0:T(8,128)S(1)} %turn_old.1.own.old), channel_id=1, source_target_pairs={{0,16},{16,32},{32,48},{48,64},{64,80},{80,96},{96,112},{112,128},... | collective-permute-start | bytes 786440 | tf_op jit(solution)/shard_map/ppermute | solution.py:439
  21.0 19.1 %collective-permute-start.9 = (f32[4,128,128]{2,1,0:T(8,128)S(1)}, f32[4,128,128]{2,1,0:T(8,128)S(1)}, u32[]{:S(2)}, u32[]{:S(2)}) collective-permute-start(f32[4,128,128]{2,1,0:T(8,128)S(1)} %turn_old.1.own.old), channel_id=1, source_target_pairs={{16,0},{32,16},{48,32},{64,48},{80,64},{96,80},{112,96},{128,112},... | collective-permute-start | bytes 786440 | tf_op jit(solution)/shard_map/ppermute | solution.py:440
  23.0 6.8 %collective-permute-start.3 = (f32[32,8,128]{2,1,0:T(8,128)S(1)}, f32[32,8,128]{2,1,0:T(8,128)S(1)}, u32[]{:S(2)}, u32[]{:S(2)}) collective-permute-start(f32[32,8,128]{2,1,0:T(8,128)S(1)} %get-tuple-element.16), channel_id=1, source_target_pairs={{1,0},{2,1},{3,2},{4,3},{5,4},{6,5},{7,6},{8,7},{9,8},{10,9},{11,1... | collective-permute-start | bytes 393224 | tf_op jit(solution)/shard_map/ppermute | solution.py:440
  33.0 11.9 %collective-permute-start.4 = (f32[4,64,128]{2,1,0:T(8,128)S(1)}, f32[4,64,128]{2,1,0:T(8,128)S(1)}, u32[]{:S(2)}, u32[]{:S(2)}) collective-permute-start(f32[4,64,128]{2,1,0:T(8,128)S(1)} %get-tuple-element.17.own.w), channel_id=1, source_target_pairs={{0,16},{16,32},{32,48},{48,64},{64,80},{80,96},{96,112},{112,128},... | collective-permute-start | bytes 393224 | tf_op jit(solution)/shard_map/ppermute | solution.py:439
  38.2 6.7 %collective-permute-start.5 = (f32[4,64,128]{2,1,0:T(8,128)S(1)}, f32[4,64,128]{2,1,0:T(8,128)S(1)}, u32[]{:S(2)}, u32[]{:S(2)}) collective-permute-start(f32[4,64,128]{2,1,0:T(8,128)S(1)} %get-tuple-element.17.own.w), channel_id=1, source_target_pairs={{16,0},{32,16},{48,32},{64,48},{80,64},{96,80},{112,96},{128,112},... | collective-permute-start | bytes 393224 | tf_op jit(solution)/shard_map/ppermute | solution.py:440
  40.2 10.0 %collective-permute-start.10 = (f32[56,8,128]{2,1,0:T(8,128)S(1)}, f32[56,8,128]{2,1,0:T(8,128)S(1)}, u32[]{:S(2)}, u32[]{:S(2)}) collective-permute-start(f32[56,8,128]{2,1,0:T(8,128)S(1)} %get-tuple-element.21), channel_id=1, source_target_pairs={{0,1},{1,2},{2,3},{3,4},{4,5},{5,6},{6,7},{7,8},{8,9},{9,10},{10,1... | collective-permute-start | bytes 688136 | tf_op jit(solution)/shard_map/ppermute | solution.py:439
  43.6 6.8 %collective-permute-start.11 = (f32[56,8,128]{2,1,0:T(8,128)S(1)}, f32[56,8,128]{2,1,0:T(8,128)S(1)}, u32[]{:S(2)}, u32[]{:S(2)}) collective-permute-start(f32[56,8,128]{2,1,0:T(8,128)S(1)} %get-tuple-element.22), channel_id=1, source_target_pairs={{1,0},{2,1},{3,2},{4,3},{5,4},{6,5},{7,6},{8,7},{9,8},{10,9},{11,1... | collective-permute-start | bytes 688136 | tf_op jit(solution)/shard_map/ppermute | solution.py:440
  44.9 12.0 %collective-permute-start.6 = (f32[28,8,128]{2,1,0:T(8,128)S(1)}, f32[28,8,128]{2,1,0:T(8,128)S(1)}, u32[]{:S(2)}, u32[]{:S(2)}) collective-permute-start(f32[28,8,128]{2,1,0:T(8,128)S(1)} %get-tuple-element.18), channel_id=1, source_target_pairs={{0,1},{1,2},{2,3},{3,4},{4,5},{5,6},{6,7},{7,8},{8,9},{9,10},{10,1... | collective-permute-start | bytes 344072 | tf_op jit(solution)/shard_map/ppermute | solution.py:439
  48.9 8.0 %collective-permute-start.7 = (f32[28,8,128]{2,1,0:T(8,128)S(1)}, f32[28,8,128]{2,1,0:T(8,128)S(1)}, u32[]{:S(2)}, u32[]{:S(2)}) collective-permute-start(f32[28,8,128]{2,1,0:T(8,128)S(1)} %get-tuple-element.19), channel_id=1, source_target_pairs={{1,0},{2,1},{3,2},{4,3},{5,4},{6,5},{7,6},{8,7},{9,8},{10,9},{11,1... | collective-permute-start | bytes 344072 | tf_op jit(solution)/shard_map/ppermute | solution.py:440

commit v4 on v2

--- a/solution.py
+++ b/solution.py
@@ -31,47 +31,55 @@
     return high, index - HALO - LX
 
 
-def rim_kernel(groups, with_coefficient, *refs):
-    own, low, high, up, down = refs[:5]
-    for group in range(groups):
-        for d in range(1, HALO + 1):
-            for i in range(WIDTHS[d - 1]):
-                ref, x = plane_of((low, own, high), d + i)
-                spot = group * RIM + STARTS[d - 1] + i
-                up[spot] = ref[x, pl.ds((group * LY + LY - d) * 8, 8), :]
-                down[spot] = ref[x, pl.ds((group * LY + d - 1) * 8, 8), :]
-    if with_coefficient:
-        base, line = groups * RIM, groups * LY * 8
-        up[base + 3] = jnp.zeros((8, NZ), F32)
-        down[base + 3] = jnp.zeros((8, NZ), F32)
-        for d in range(1, HALO + 1):
-            for i in range(WIDTHS[d - 1]):
-                ref, x = plane_of((low, own, high), d + i)
-                spot = STARTS[d - 1] + i
-                tile, row = base + spot // 8, spot % 8
-                up[tile, pl.ds(row, 1), :] = ref[x, pl.ds(line + LY - d, 1), :]
-                down[tile, pl.ds(row, 1), :] = ref[x, pl.ds(line + d - 1, 1), :]
-
-
-def pack_rim(groups, with_coefficient, own, low, high):
-    shape = jax.ShapeDtypeStruct((groups * RIM + (4 if with_coefficient else 0), 8, NZ), F32)
-    return pl.pallas_call(
-        functools.partial(rim_kernel, groups, with_coefficient),
-        out_shape=(shape, shape),
+def fill_rim(parts, group, up, down, slot):
+    for d in range(1, HALO + 1):
+        for i in range(WIDTHS[d - 1]):
+            ref, x = plane_of(parts, d + i)
+            spot = slot * RIM + STARTS[d - 1] + i
+            up[spot] = ref[x, pl.ds((group * LY + LY - d) * 8, 8), :]
+            down[spot] = ref[x, pl.ds((group * LY + d - 1) * 8, 8), :]
+
+
+def first_rim_kernel(own, low, high, up, down, old_up, old_down):
+    parts = (low, own, high)
+    fill_rim(parts, 2, up, down, 0)
+    line = 3 * LY * 8
+    up[RIM + 3] = jnp.zeros((8, NZ), F32)
+    down[RIM + 3] = jnp.zeros((8, NZ), F32)
+    for d in range(1, HALO + 1):
+        for i in range(WIDTHS[d - 1]):
+            ref, x = plane_of(parts, d + i)
+            spot = STARTS[d - 1] + i
+            tile, row = RIM + spot // 8, spot % 8
+            up[tile, pl.ds(row, 1), :] = ref[x, pl.ds(line + LY - d, 1), :]
+            down[tile, pl.ds(row, 1), :] = ref[x, pl.ds(line + d - 1, 1), :]
+    fill_rim(parts, 0, old_up, old_down, 0)
+    fill_rim(parts, 1, old_up, old_down, 1)
+
+
+def rim_kernel(own, low, high, up, down):
+    fill_rim((low, own, high), 0, up, down, 0)
+
+
+def pack_rim(kernel, sizes, own, sides):
+    shapes = tuple(jax.ShapeDtypeStruct((size, 8, NZ), F32) for size in sizes)
+    return pl.pallas_call(
+        kernel,
+        out_shape=shapes,
         in_specs=[VMEM] * 3,
-        out_specs=(VMEM, VMEM),
+        out_specs=(VMEM,) * len(shapes),
         compiler_params=pltpu.CompilerParams(vmem_limit_bytes=1 << 20),
         name="pack_rim",
-    )(own, low, high)
-
-
-def fill_block(group, parts, from_low, from_high, wide):
+    )(own, *sides)
+
+
+def fill_block(group, slot, parts, from_low, from_high, wide):
     wide[...] = jnp.zeros(wide.shape, F32)
     for index in range(EX):
         ref, x = plane_of(parts, index)
         wide[index, HALO:HALO + LY] = ref[x, pl.ds(group * LY * 8, LY * 8), :].reshape(LY, 8, NZ)
     for d in range(1, HALO + 1):
-        spot = group * RIM + STARTS[d - 1]
+        spot = slot * RIM + STARTS[d - 1]
         for i in range(WIDTHS[d - 1]):
             wide[d + i, HALO - d] = from_low[spot + i]
             wide[d + i, HALO + LY - 1 + d] = from_high[spot + i]
@@ -85,7 +93,7 @@
     for d in range(1, HALO + 1):
         for i in range(WIDTHS[d - 1]):
             spot = STARTS[d - 1] + i
-            tile, row = groups * RIM + spot // 8, spot % 8
+            tile, row = RIM + spot // 8, spot % 8
             wide[d + i, pl.ds(HALO - d, 1), :] = from_low[tile, pl.ds(row, 1), :]
             wide[d + i, pl.ds(HALO + LY - 1 + d, 1), :] = from_high[tile, pl.ds(row, 1), :]
 
@@ -163,7 +171,7 @@
 def first_kernel(own, low, high, from_low, from_high, out, coef, block, first, second,
                  table_re, table_im, diag_re, diag_im):
     parts = (low, own, high)
-    fill_block(2, parts, from_low, from_high, block)
+    fill_block(2, 0, parts, from_low, from_high, block)
     fill_coefficient(3, parts, from_low, from_high, coef)
     fill_tables(coef, table_re, table_im, diag_re, diag_im)
 
@@ -190,7 +198,7 @@
 def old_kernel(group, own, low, high, from_low, from_high, coef, out, block, first, second,
                table_re, table_im, diag_re, diag_im):
     fill_tables(coef, table_re, table_im, diag_re, diag_im)
-    fill_block(group, (low, own, high), from_low, from_high, block)
+    fill_block(group, group, (low, own, high), from_low, from_high, block)
 
     def store(x, y, value):
         out[x, pl.ds(y * 8, 8), :] = value
@@ -275,7 +283,7 @@
 def gram_kernel(peers, own, low, high, from_low, from_high, coef, start, image0, image1, w_image, out,
                 block, first, second, table_re, table_im, diag_re, diag_im):
     fill_tables(coef, table_re, table_im, diag_re, diag_im)
-    fill_block(0, (low, own, high), from_low, from_high, block)
+    fill_block(0, 0, (low, own, high), from_low, from_high, block)
 
     def store(x, y, value):
         w_image[x, pl.ds(y * 8, 8), :] = value
@@ -427,15 +435,15 @@
     by_cell = prior.transpose(3, 0, 4, 1, 2, 5).reshape(LX, 3 * LY * 8, NZ)
     start = jnp.concatenate([by_cell, coefficient], axis=1)
     sides = from_both(GX, nx, start, start)
-    up, down = pack_rim(3, True, start, *sides)
+    up, down, old_up, old_down = pack_rim(first_rim_kernel, [RIM + 4] * 2 + [2 * RIM] * 2, start, sides)
     rims = from_both("gy", ny, up, down)
+    old_rims = from_both("gy", ny, old_up, old_down)
     w, coef = first_image(start, *sides, *rims)
 
     w_sides = from_both(GX, nx, w, w)
-    up, down = pack_rim(1, False, w, *w_sides)
-    w_rims = from_both("gy", ny, up, down)
-    image0 = old_image(0, start, *sides, *rims, coef)
-    image1 = old_image(1, start, *sides, *rims, coef)
+    w_rims = from_both("gy", ny, *pack_rim(rim_kernel, [RIM] * 2, w, w_sides))
+    image0 = old_image(0, start, *sides, *old_rims, coef)
+    image1 = old_image(1, start, *sides, *old_rims, coef)
 
     w_image, spread = image_and_gram(2 * ny, w, *w_sides, *w_rims, coef, start, image0, image1)
     got = lax.all_to_all(spread, ("core", "gy"), 0, 0)

time: 107 us -> 108 us (level)
  starting transfers between devices: 24.5 us -> 29.8 us
  waiting for transfers between devices: 15 us -> 10.4 us
    ppermute x4 -> x5, waiting for transfers between devices: 10.1 us -> 0.63 us  [from_both(): lax.ppermute(to_higher, axis, [(i, i + 1) for i in range(count - 1)])]
    ppermute x4 -> x5, starting transfers between devices: 11.2 us -> 18.9 us  [from_both(): lax.ppermute(to_higher, axis, [(i, i + 1) for i in range(count - 1)])]
    ppermute x4 -> x5, waiting for transfers between devices: 4.83 us -> 9.76 us  [from_both(): lax.ppermute(to_lower, axis, [(i + 1, i) for i in range(count - 1)])]
    ppermute x4 -> x5, starting transfers between devices: 13.3 us -> 11 us  [from_both(): lax.ppermute(to_lower, axis, [(i + 1, i) for i in range(count - 1)])]
  transfers between devices with their start and end apart: 8 -> 10, of which waited for: 5 -> 4; matrix products, arithmetic and copies ran while one was open for 0% -> 0% of each run, Pallas kernels for 6% -> 6%
where the time goes in v4:
time: 108 us; the launch traced here: 107 us
  blocking collectives  45.4 us (42%)
  starting transfers between devices  29.8 us (28%)
  Pallas kernels  20.1 us (19%)
  waiting for transfers between devices  10.4 us (10%)
  local copies, waits for them, and re-layouts  1.27 us (1%)
    all_to_all x1, blocking collectives, per_device(): got = lax.all_to_all(sum_and_spread(got, nz), 'z', 0, 0)  29.4 us
    ppermute x5, starting transfers between devices, from_both(): lax.ppermute(to_higher, axis, [(i, i + 1) for i in range(count - 1)])  18.9 us
    all_to_all x1, blocking collectives, per_device(): got = lax.all_to_all(spread, ('core', 'gy'), 0, 0)  16 us
    ppermute x5, starting transfers between devices, from_both(): lax.ppermute(to_lower, axis, [(i + 1, i) for i in range(count - 1)])  11 us
    ppermute x5, waiting for transfers between devices, from_both(): lax.ppermute(to_lower, axis, [(i + 1, i) for i in range(count - 1)])  9.76 us
    pallas_call x2, Pallas kernels, old_image(): pl.pallas_call(functools.partial(old_kernel, group), out_shape=jax.ShapeD...  6.49 us
    pallas_call x1, Pallas kernels, finish(): pl.pallas_call(functools.partial(final_kernel, cells), out_shape=jax.Shap...  5.54 us
    pallas_call x1, Pallas kernels, image_and_gram(): pl.pallas_call(functools.partial(gram_kernel, peers), out_shape=(jax.Shap...  4.67 us
  transfers between devices with their start and end apart: 10, of which 4 were waited for; matrix products, arithmetic and copies ran while one was open for 0% of the time, Pallas kernels for 6%

profile of v4, /device:TPU:1, one launch (start us, length us, event | category | flops | bytes accessed | tf_op | source)
XLA Modules:
  0.0 107.2 jit_solution(71526171825666051)
XLA Ops:
  0.0 0.0 copy-start
  0.0 1.3 %copy.3 = f32[4,3,8,2,4,128]{5,4,3,2,1,0:T(4,128)S(1)} copy(f32[4,3,8,2,4,128]{5,2,0,4,3,1:T(8,128)} %bitcast.4) | data formatting | bytes 786432 | tf_op jit(solution)/shard_map/transpose | solution.py:435
  1.3 0.0 copy-done
  1.3 4.9 %collective-permute-start = (f32[4,200,128]{2,1,0:T(8,128)S(1)}, f32[4,200,128]{2,1,0:T(8,128)S(1)}, u32[]{:S(2)}, u32[]{:S(2)}) collective-permute-start(f32[4,200,128]{2,1,0:T(8,128)S(1)} %pad_maximum_fusion.own.start), channel_id=1, source_target_pairs={{0,16},{16,32},{32,48},{48,64},{64,80},{80,96},{96,112},{112,128},... | collective-permute-start | bytes 1228808 | tf_op jit(solution)/shard_map/ppermute | solution.py:428
  6.3 5.2 %collective-permute-start.1 = (f32[4,200,128]{2,1,0:T(8,128)S(1)}, f32[4,200,128]{2,1,0:T(8,128)S(1)}, u32[]{:S(2)}, u32[]{:S(2)}) collective-permute-start(f32[4,200,128]{2,1,0:T(8,128)S(1)} %pad_maximum_fusion.own.start), channel_id=1, source_target_pairs={{16,0},{32,16},{48,32},{64,48},{80,64},{96,80},{112,96},{128,112},... | collective-permute-start | bytes 1228808 | tf_op jit(solution)/shard_map/ppermute | solution.py:429
  11.4 0.0 collective-permute-done.low
  11.4 4.1 %collective-permute-done.1.high = f32[4,200,128]{2,1,0:T(8,128)S(1)} collective-permute-done((f32[4,200,128]{2,1,0:T(8,128)S(1)}, f32[4,200,128]{2,1,0:T(8,128)S(1)}, u32[]{:S(2)}, u32[]{:S(2)}) %collective-permute-start.1) | collective-permute-done | bytes 409632 | tf_op jit(solution)/shard_map/ppermute | solution.py:429
  15.5 0.1 pack_rim.2
  15.6 3.2 %collective-permute-start.2 = (f32[32,8,128]{2,1,0:T(8,128)S(1)}, f32[32,8,128]{2,1,0:T(8,128)S(1)}, u32[]{:S(2)}, u32[]{:S(2)}) collective-permute-start(f32[32,8,128]{2,1,0:T(8,128)S(1)} %get-tuple-element.15), channel_id=1, source_target_pairs={{0,1},{1,2},{2,3},{3,4},{4,5},{5,6},{6,7},{7,8},{8,9},{9,10},{10,1... | collective-permute-start | bytes 393224 | tf_op jit(solution)/shard_map/ppermute | solution.py:428
  18.8 1.3 %collective-permute-start.3 = (f32[32,8,128]{2,1,0:T(8,128)S(1)}, f32[32,8,128]{2,1,0:T(8,128)S(1)}, u32[]{:S(2)}, u32[]{:S(2)}) collective-permute-start(f32[32,8,128]{2,1,0:T(8,128)S(1)} %get-tuple-element.16), channel_id=1, source_target_pairs={{1,0},{2,1},{3,2},{4,3},{5,4},{6,5},{7,6},{8,7},{9,8},{10,9},{11,1... | collective-permute-start | bytes 393224 | tf_op jit(solution)/shard_map/ppermute | solution.py:429
  20.1 0.6 collective-permute-done.2.from_low
  20.7 3.9 %collective-permute-done.3.from_high = f32[32,8,128]{2,1,0:T(8,128)S(1)} collective-permute-done((f32[32,8,128]{2,1,0:T(8,128)S(1)}, f32[32,8,128]{2,1,0:T(8,128)S(1)}, u32[]{:S(2)}, u32[]{:S(2)}) %collective-permute-start.3) | collective-permute-done | bytes 131104 | tf_op jit(solution)/shard_map/ppermute | solution.py:429
  24.7 3.2 %first_image.1 = (f32[4,64,128]{2,1,0:T(8,128)S(1)}, f32[12,16,128]{2,1,0:T(8,128)S(1)}) custom-call(f32[4,200,128]{2,1,0:T(8,128)S(1)} %pad_maximum_fusion.own.start, f32[4,200,128]{2,1,0:T(8,128)S(1)} %collective-permute-done.low, f32[4,200,128]{2,1,0:T(8,128)S(1)} %collective-permute-done.1.high, f32[32,8,128]{2,1,0:T(8,128)S(1)} %collective-permute-done.2.from_low, ...), custom_call_target="tpu_custom_call" | custom-call | flops 6000000 | bytes 2000000 | tf_op jit(solution)/shard_map/first_image/pallas_call | solution.py:185
  27.9 3.5 %collective-permute-start.4 = (f32[4,64,128]{2,1,0:T(8,128)S(1)}, f32[4,64,128]{2,1,0:T(8,128)S(1)}, u32[]{:S(2)}, u32[]{:S(2)}) collective-permute-start(f32[4,64,128]{2,1,0:T(8,128)S(1)} %get-tuple-element.17.own.w), channel_id=1, source_target_pairs={{0,16},{16,32},{32,48},{48,64},{64,80},{80,96},{96,112},{112,128},... | collective-permute-start | bytes 393224 | tf_op jit(solution)/shard_map/ppermute | solution.py:428
  31.4 1.9 %collective-permute-start.5 = (f32[4,64,128]{2,1,0:T(8,128)S(1)}, f32[4,64,128]{2,1,0:T(8,128)S(1)}, u32[]{:S(2)}, u32[]{:S(2)}) collective-permute-start(f32[4,64,128]{2,1,0:T(8,128)S(1)} %get-tuple-element.17.own.w), channel_id=1, source_target_pairs={{16,0},{32,16},{48,32},{64,48},{80,64},{96,80},{112,96},{128,112},... | collective-permute-start | bytes 393224 | tf_op jit(solution)/shard_map/ppermute | solution.py:429
  33.3 3.2 %collective-permute-start.8 = (f32[56,8,128]{2,1,0:T(8,128)S(1)}, f32[56,8,128]{2,1,0:T(8,128)S(1)}, u32[]{:S(2)}, u32[]{:S(2)}) collective-permute-start(f32[56,8,128]{2,1,0:T(8,128)S(1)} %get-tuple-element.21), channel_id=1, source_target_pairs={{0,1},{1,2},{2,3},{3,4},{4,5},{5,6},{6,7},{7,8},{8,9},{9,10},{10,1... | collective-permute-start | bytes 688136 | tf_op jit(solution)/shard_map/ppermute | solution.py:428
  36.6 1.3 %collective-permute-start.9 = (f32[56,8,128]{2,1,0:T(8,128)S(1)}, f32[56,8,128]{2,1,0:T(8,128)S(1)}, u32[]{:S(2)}, u32[]{:S(2)}) collective-permute-start(f32[56,8,128]{2,1,0:T(8,128)S(1)} %get-tuple-element.22), channel_id=1, source_target_pairs={{1,0},{2,1},{3,2},{4,3},{5,4},{6,5},{7,6},{8,7},{9,8},{10,9},{11,1... | collective-permute-start | bytes 688136 | tf_op jit(solution)/shard_map/ppermute | solution.py:429
  37.9 0.0 collective-permute-done.4.low
  37.9 0.0 collective-permute-done.5.high
  37.9 4.0 %collective-permute-start.6 = (f32[28,8,128]{2,1,0:T(8,128)S(1)}, f32[28,8,128]{2,1,0:T(8,128)S(1)}, u32[]{:S(2)}, u32[]{:S(2)}) collective-permute-start(f32[28,8,128]{2,1,0:T(8,128)S(1)} %get-tuple-element.18), channel_id=1, source_target_pairs={{0,1},{1,2},{2,3},{3,4},{4,5},{5,6},{6,7},{7,8},{8,9},{9,10},{10,1... | collective-permute-start | bytes 344072 | tf_op jit(solution)/shard_map/ppermute | solution.py:428
  41.9 1.3 %collective-permute-start.7 = (f32[28,8,128]{2,1,0:T(8,128)S(1)}, f32[28,8,128]{2,1,0:T(8,128)S(1)}, u32[]{:S(2)}, u32[]{:S(2)}) collective-permute-start(f32[28,8,128]{2,1,0:T(8,128)S(1)} %get-tuple-element.19), channel_id=1, source_target_pairs={{1,0},{2,1},{3,2},{4,3},{5,4},{6,5},{7,6},{8,7},{9,8},{10,9},{11,1... | collective-permute-start | bytes 344072 | tf_op jit(solution)/shard_map/ppermute | solution.py:429
  43.2 0.0 collective-permute-done.8.from_low
  43.2 1.8 %collective-permute-done.9.from_high = f32[56,8,128]{2,1,0:T(8,128)S(1)} collective-permute-done((f32[56,8,128]{2,1,0:T(8,128)S(1)}, f32[56,8,128]{2,1,0:T(8,128)S(1)}, u32[]{:S(2)}, u32[]{:S(2)}) %collective-permute-start.9) | collective-permute-done | bytes 229408 | tf_op jit(solution)/shard_map/ppermute | solution.py:429
  45.0 3.2 %old_image.3.image1 = f32[4,64,128]{2,1,0:T(8,128)S(1)} custom-call(f32[4,200,128]{2,1,0:T(8,128)S(1)} %pad_maximum_fusion.own.start, f32[4,200,128]{2,1,0:T(8,128)S(1)} %collective-permute-done.low, f32[4,200,128]{2,1,0:T(8,128)S(1)} %collective-permute-done.1.high, f32[56,8,128]{2,1,0:T(8,128)S(1)} %collective-permute-done.8.from_low, ...), custom_call_target="tpu_custom_call" | custom-call | flops 6000000 | bytes 12000000 | tf_op jit(solution)/shard_map/old_image/pallas_call | solution.py:210
  48.2 3.2 %old_image.2.image0 = f32[4,64,128]{2,1,0:T(8,128)S(1)} custom-call(f32[4,200,128]{2,1,0:T(8,128)S(1)} %pad_maximum_fusion.own.start, f32[4,200,128]{2,1,0:T(8,128)S(1)} %collective-permute-done.low, f32[4,200,128]{2,1,0:T(8,128)S(1)} %collective-permute-done.1.high, f32[56,8,128]{2,1,0:T(8,128)S(1)} %collective-permute-done.8.from_low, ...), custom_call_target="tpu_custom_call" | custom-call | flops 6000000 | bytes 12000000 | tf_op jit(solution)/shard_map/old_image/pallas_call | solution.py:210
  51.5 0.0 collective-permute-done.6.from_low
  51.5 0.0 collective-permute-done.7.from_high
  51.5 4.7 %image_and_gram.1 = (f32[4,64,128]{2,1,0:T(8,128)S(1)}, f32[32,8,128]{2,1,0:T(8,128)S(1)}) custom-call(f32[4,64,128]{2,1,0:T(8,128)S(1)} %get-tuple-element.17.own.w, f32[4,64,128]{2,1,0:T(8,128)S(1)} %collective-permute-done.4.low, f32[4,64,128]{2,1,0:T(8,128)S(1)} %collective-permute-done.5.high, f32[28,8,128]{2,1,0:T(8,128)S(1)} %collective-permute-done.6.from_low, ...), custom_call_target="tpu_custom_call" | custom-call | tf_op jit(solution)/shard_map/image_and_gram/pallas_call | solution.py:307
  56.2 16.0 %all_to_all.10.parts = f32[32,8,128]{2,1,0:T(8,128)S(1)} all-to-all(f32[32,8,128]{2,1,0:T(8,128)S(1)} %get-tuple-element.23), channel_id=1, replica_groups=mesh['z'=16,'core'=2,'gy'=16] {'core','gy'}, dimensions={0} | all-to-all | bytes 262144 | tf_op jit(solution)/shard_map/all_to_all | solution.py:449
  72.2 29.4 %all_to_all.11.parts = f32[16,8,128]{2,1,0:T(8,128)S(1)} all-to-all(f32[16,8,128]{2,1,0:T(8,128)S(1)} %sum_and_spread.1), channel_id=1, replica_groups=mesh['z'=16,'core'=2,'gy'=16] {'z'}, dimensions={0} | all-to-all | bytes 131072 | tf_op jit(solution)/shard_map/all_to_all | solution.py:450
  101.6 5.5 %finish.1 = f32[2,8,4,8,128]{4,3,2,1,0:T(8,128)} custom-call(f32[16,8,128]{2,1,0:T(8,128)S(1)} %all_to_all.11.parts, f32[4,200,128]{2,1,0:T(8,128)S(1)} %pad_maximum_fusion.own.start, f32[4,64,128]{2,1,0:T(8,128)S(1)} %get-tuple-element.17.own.w, f32[4,64,128]{2,1,0:T(8,128)S(1)} %old_image.2.image0, f32[4,64,128]{2,1,0:T(8,128)S(1)} %old_image.3.image1, ...), custom_call_target="tpu_custom_call" | custom-call | tf_op jit(solution)/shard_map/finish/pallas_call | solution.py:413
  (3 shorter events, 0.1 us)
Async XLA Ops:
  0.0 1.3 %copy-start = (f32[4,8,128]{2,1,0:T(8,128)S(1)}, f32[4,8,128]{2,1,0:T(8,128)}, u32[]{:S(2)}) copy-start(f32[4,8,128]{2,1,0:T(8,128)} %param.3) | copy-start | bytes 49156
  1.3 10.1 %collective-permute-start = (f32[4,200,128]{2,1,0:T(8,128)S(1)}, f32[4,200,128]{2,1,0:T(8,128)S(1)}, u32[]{:S(2)}, u32[]{:S(2)}) collective-permute-start(f32[4,200,128]{2,1,0:T(8,128)S(1)} %pad_maximum_fusion.own.start), channel_id=1, source_target_pairs={{0,16},{16,32},{32,48},{48,64},{64,80},{80,96},{96,112},{112,128},... | collective-permute-start | bytes 1228808 | tf_op jit(solution)/shard_map/ppermute | solution.py:428
  6.3 9.3 %collective-permute-start.1 = (f32[4,200,128]{2,1,0:T(8,128)S(1)}, f32[4,200,128]{2,1,0:T(8,128)S(1)}, u32[]{:S(2)}, u32[]{:S(2)}) collective-permute-start(f32[4,200,128]{2,1,0:T(8,128)S(1)} %pad_maximum_fusion.own.start), channel_id=1, source_target_pairs={{16,0},{32,16},{48,32},{64,48},{80,64},{96,80},{112,96},{128,112},... | collective-permute-start | bytes 1228808 | tf_op jit(solution)/shard_map/ppermute | solution.py:429
  15.6 5.1 %collective-permute-start.2 = (f32[32,8,128]{2,1,0:T(8,128)S(1)}, f32[32,8,128]{2,1,0:T(8,128)S(1)}, u32[]{:S(2)}, u32[]{:S(2)}) collective-permute-start(f32[32,8,128]{2,1,0:T(8,128)S(1)} %get-tuple-element.15), channel_id=1, source_target_pairs={{0,1},{1,2},{2,3},{3,4},{4,5},{5,6},{6,7},{7,8},{8,9},{9,10},{10,1... | collective-permute-start | bytes 393224 | tf_op jit(solution)/shard_map/ppermute | solution.py:428
  18.8 5.8 %collective-permute-start.3 = (f32[32,8,128]{2,1,0:T(8,128)S(1)}, f32[32,8,128]{2,1,0:T(8,128)S(1)}, u32[]{:S(2)}, u32[]{:S(2)}) collective-permute-start(f32[32,8,128]{2,1,0:T(8,128)S(1)} %get-tuple-element.16), channel_id=1, source_target_pairs={{1,0},{2,1},{3,2},{4,3},{5,4},{6,5},{7,6},{8,7},{9,8},{10,9},{11,1... | collective-permute-start | bytes 393224 | tf_op jit(solution)/shard_map/ppermute | solution.py:429
  27.9 10.0 %collective-permute-start.4 = (f32[4,64,128]{2,1,0:T(8,128)S(1)}, f32[4,64,128]{2,1,0:T(8,128)S(1)}, u32[]{:S(2)}, u32[]{:S(2)}) collective-permute-start(f32[4,64,128]{2,1,0:T(8,128)S(1)} %get-tuple-element.17.own.w), channel_id=1, source_target_pairs={{0,16},{16,32},{32,48},{48,64},{64,80},{80,96},{96,112},{112,128},... | collective-permute-start | bytes 393224 | tf_op jit(solution)/shard_map/ppermute | solution.py:428
  31.4 6.5 %collective-permute-start.5 = (f32[4,64,128]{2,1,0:T(8,128)S(1)}, f32[4,64,128]{2,1,0:T(8,128)S(1)}, u32[]{:S(2)}, u32[]{:S(2)}) collective-permute-start(f32[4,64,128]{2,1,0:T(8,128)S(1)} %get-tuple-element.17.own.w), channel_id=1, source_target_pairs={{16,0},{32,16},{48,32},{64,48},{80,64},{96,80},{112,96},{128,112},... | collective-permute-start | bytes 393224 | tf_op jit(solution)/shard_map/ppermute | solution.py:429
  33.3 9.9 %collective-permute-start.8 = (f32[56,8,128]{2,1,0:T(8,128)S(1)}, f32[56,8,128]{2,1,0:T(8,128)S(1)}, u32[]{:S(2)}, u32[]{:S(2)}) collective-permute-start(f32[56,8,128]{2,1,0:T(8,128)S(1)} %get-tuple-element.21), channel_id=1, source_target_pairs={{0,1},{1,2},{2,3},{3,4},{4,5},{5,6},{6,7},{7,8},{8,9},{9,10},{10,1... | collective-permute-start | bytes 688136 | tf_op jit(solution)/shard_map/ppermute | solution.py:428
  36.6 8.4 %collective-permute-start.9 = (f32[56,8,128]{2,1,0:T(8,128)S(1)}, f32[56,8,128]{2,1,0:T(8,128)S(1)}, u32[]{:S(2)}, u32[]{:S(2)}) collective-permute-start(f32[56,8,128]{2,1,0:T(8,128)S(1)} %get-tuple-element.22), channel_id=1, source_target_pairs={{1,0},{2,1},{3,2},{4,3},{5,4},{6,5},{7,6},{8,7},{9,8},{10,9},{11,1... | collective-permute-start | bytes 688136 | tf_op jit(solution)/shard_map/ppermute | solution.py:429
  37.9 13.6 %collective-permute-start.6 = (f32[28,8,128]{2,1,0:T(8,128)S(1)}, f32[28,8,128]{2,1,0:T(8,128)S(1)}, u32[]{:S(2)}, u32[]{:S(2)}) collective-permute-start(f32[28,8,128]{2,1,0:T(8,128)S(1)} %get-tuple-element.18), channel_id=1, source_target_pairs={{0,1},{1,2},{2,3},{3,4},{4,5},{5,6},{6,7},{7,8},{8,9},{9,10},{10,1... | collective-permute-start | bytes 344072 | tf_op jit(solution)/shard_map/ppermute | solution.py:428
  41.9 9.6 %collective-permute-start.7 = (f32[28,8,128]{2,1,0:T(8,128)S(1)}, f32[28,8,128]{2,1,0:T(8,128)S(1)}, u32[]{:S(2)}, u32[]{:S(2)}) collective-permute-start(f32[28,8,128]{2,1,0:T(8,128)S(1)} %get-tuple-element.19), channel_id=1, source_target_pairs={{1,0},{2,1},{3,2},{4,3},{5,4},{6,5},{7,6},{8,7},{9,8},{10,9},{11,1... | collective-permute-start | bytes 344072 | tf_op jit(solution)/shard_map/ppermute | solution.py:429

commit v5 on v4

v5 whole, which is shorter than its diff:
```python
import functools

import jax
import jax.numpy as jnp
import numpy as np
from jax import lax
from jax.experimental import pallas as pl
from jax.experimental.pallas import tpu as pltpu
from jax.sharding import Mesh, PartitionSpec as P

LX, LY, NZ = 4, 8, 128
NEAR, FAR = 4, 8
BLOCKS = 7
ROWS = 64
F32 = jnp.float32
BF16 = jnp.bfloat16
HIGHEST = lax.Precision.HIGHEST
VMEM = pl.BlockSpec(memory_space=pltpu.VMEM)


def widths(halo):
    return [LX + 2 * (halo - d) for d in range(1, halo + 1)]


def rim_spots(halo):
    spots, place = [], 0
    for d, width in zip(range(1, halo + 1), widths(halo)):
        for i in range(width):
            spots.append((d, d + i, place))
            place += 1
    return spots


def plane_of(parts, index):
    ref, first = parts[index // LX]
    return ref, index % LX, first


def shifted(parts, rows):
    return [(ref, first + rows) for ref, first in parts]


def fill_rim(parts, halo, up, down, start):
    for d, plane, place in rim_spots(halo):
        ref, x, first = plane_of(parts, plane)
        up[start + place] = ref[x, pl.ds(first + (LY - d) * 8, 8), :]
        down[start + place] = ref[x, pl.ds(first + (d - 1) * 8, 8), :]


def fill_flat_rim(parts, halo, up, down, start):
    for d, plane, place in rim_spots(halo):
        ref, x, first = plane_of(parts, plane)
        tile, row = start + place // 8, place % 8
        up[tile, pl.ds(row, 1), :] = ref[x, pl.ds(first + LY - d, 1), :]
        down[tile, pl.ds(row, 1), :] = ref[x, pl.ds(first + d - 1, 1), :]


BLOCK = LY * 8
OLD_RIM = sum(widths(NEAR))
FAR_RIM = sum(widths(FAR))


def recent_parts(far_low, low, own, high, far_high):
    return [(far_low, 0), (low, 2 * BLOCK), (own, 2 * BLOCK), (high, 2 * BLOCK), (far_high, 0)]


def rim_kernel(own, low, high, far_low, far_high, up, down, old_up, old_down):
    parts = [(low, 0), (own, 0), (high, 0)]
    wide = recent_parts(far_low, low, own, high, far_high)
    for group in range(2):
        fill_rim(shifted(parts, group * BLOCK), NEAR, old_up, old_down, group * OLD_RIM)
    fill_flat_rim(shifted(wide, BLOCK), FAR, old_up, old_down, 2 * OLD_RIM)
    fill_rim(wide, FAR, up, down, 0)


def pack_rims(*args):
    sizes = [FAR_RIM] * 2 + [2 * OLD_RIM + FAR_RIM // 8] * 2
    shapes = tuple(jax.ShapeDtypeStruct((size, 8, NZ), F32) for size in sizes)
    return pl.pallas_call(
        rim_kernel,
        out_shape=shapes,
        in_specs=[VMEM] * 5,
        out_specs=(VMEM,) * 4,
        compiler_params=pltpu.CompilerParams(vmem_limit_bytes=1 << 20),
        name="pack_rims",
    )(*args)


def fill_block(parts, halo, from_low, from_high, start, wide):
    wide[...] = jnp.zeros(wide.shape, F32)
    for index in range(LX + 2 * halo):
        ref, x, first = plane_of(parts, index)
        wide[index, halo:halo + LY] = ref[x, pl.ds(first, BLOCK), :].reshape(LY, 8, NZ)
    for d, plane, place in rim_spots(halo):
        wide[plane, halo - d] = from_low[start + place]
        wide[plane, halo + LY - 1 + d] = from_high[start + place]


def fill_flat(parts, halo, from_low, from_high, start, wide):
    wide[...] = jnp.zeros(wide.shape, F32)
    for index in range(LX + 2 * halo):
        ref, x, first = plane_of(parts, index)
        wide[index, halo:halo + LY] = ref[x, pl.ds(first, LY), :]
    for d, plane, place in rim_spots(halo):
        tile, row = start + place // 8, place % 8
        wide[plane, pl.ds(halo - d, 1), :] = from_low[tile, pl.ds(row, 1), :]
        wide[plane, pl.ds(halo + LY - 1 + d, 1), :] = from_high[tile, pl.ds(row, 1), :]


def fill_tables(coef, skip, table_re, table_im, diag_re, diag_im):
    value = coef[...]
    real = 6.0 - value
    imag = 0.5 * value
    scale = jnp.where(value > 0.0, 0.8 / (real * real + imag * imag), 0.0)
    diag_re[...] = real * scale
    diag_im[...] = imag * scale
    sign = jnp.where(lax.broadcasted_iota(jnp.int32, (8, NZ), 0) < 4, 1.0, -1.0)
    size_x, size_y = table_re.shape[:2]

    def body(x, carry):
        for y in range(size_y):
            spot = pl.ds(y + skip, 1)
            table_re[x, y] = jnp.broadcast_to(diag_re[x + skip, spot, :], (8, NZ))
            table_im[x, y] = jnp.broadcast_to(diag_im[x + skip, spot, :], (8, NZ)) * sign
        return carry

    lax.fori_loop(0, size_x, body, 0)


def depth_sum(value):
    lane = lax.broadcasted_iota(jnp.int32, value.shape, 1)
    above = jnp.where(lane == 0, 0.0, pltpu.roll(value, 1, 1))
    below = jnp.where(lane == NZ - 1, 0.0, pltpu.roll(value, NZ - 1, 1))
    return above + below


def smooth(block, coef, skip, reach, table_re, table_im, first, second, store):
    size_x, size_y = block.shape[:2]

    def solve(value, x, y):
        return table_re[x, y] * value + table_im[x, y] * pltpu.roll(value, 4, 0)

    def sections(k):
        low, high = k, size_y - k
        if reach == 0:
            return [((k, size_x - k), (low, high))]
        return [((k, 4), (low + 5, high - 5)), ((4, size_x - 4), (low, high)),
                ((size_x - 4, size_x - k), (low + 5, high - 5))]

    def planes(k, body):
        for (begin, end), (low, high) in sections(k):
            if begin < end:
                lax.fori_loop(begin, end, functools.partial(body, low, high), 0)

    def start(low, high, x, carry):
        for y in range(low, high):
            first[x, y] = solve(block[x, y], x, y)
        return carry

    def around(ref, x, low, high):
        line = [ref[x, y] for y in range(low - 1, high + 1)]
        for y in range(low, high):
            mid = line[y - low + 1]
            total = ref[x - 1, y] + ref[x + 1, y] + line[y - low] + line[y - low + 2]
            yield y, mid, total + depth_sum(mid)

    if reach:
        first[...] = jnp.zeros(first.shape, F32)
        second[...] = jnp.zeros(second.shape, F32)
    planes(0, start)
    here, there = first, second
    for k in range(1, 4):
        def sweep(low, high, x, carry, here=here, there=there):
            for y, mid, total in around(here, x, low, high):
                there[x, y] = 0.2 * mid + solve(block[x, y] + total, x, y)
            return carry

        planes(k, sweep)
        here, there = there, here

    def image(x, carry):
        for y, mid, total in around(here, x, 4, size_y - 4):
            diag = 6.0 - coef[x + skip, pl.ds(y + skip, 1), :]
            store(x - 4, y - 4, diag * mid - total)
        return carry

    lax.fori_loop(4, size_x - 4, image, 0)


def wide_shape(halo):
    return (LX + 2 * halo, LY + 2 * halo)


FLAT = pltpu.VMEM((*wide_shape(FAR), NZ), F32)


def smooth_scratch(halo):
    return [pltpu.VMEM((*wide_shape(halo), 8, NZ), F32)] * 5 + [FLAT] * 2


def old_kernel(own, low, high, far_low, far_high, from_low, from_high, out, coef, block, first, second,
               table_re, table_im, diag_re, diag_im):
    wide = recent_parts(far_low, low, own, high, far_high)
    fill_flat(shifted(wide, BLOCK), FAR, from_low, from_high, 2 * OLD_RIM, coef)
    fill_tables(coef, FAR - NEAR, table_re, table_im, diag_re, diag_im)
    for group in range(2):
        parts = [(low, group * BLOCK), (own, group * BLOCK), (high, group * BLOCK)]
        fill_block(parts, NEAR, from_low, from_high, group * OLD_RIM, block)

        def store(x, y, value, group=group):
            out[x, pl.ds(group * BLOCK + y * 8, 8), :] = value

        smooth(block, coef, FAR - NEAR, 0, table_re, table_im, first, second, store)


def old_images(*args):
    return pl.pallas_call(
        old_kernel,
        out_shape=(jax.ShapeDtypeStruct((LX, 2 * BLOCK, NZ), F32),
                   jax.ShapeDtypeStruct((*wide_shape(FAR), NZ), F32)),
        in_specs=[VMEM] * 7,
        out_specs=(VMEM, VMEM),
        scratch_shapes=smooth_scratch(NEAR),
        compiler_params=pltpu.CompilerParams(vmem_limit_bytes=16 << 20),
        cost_estimate=pl.CostEstimate(flops=12_000_000, bytes_accessed=24_000_000, transcendentals=0),
        name="old_images",
    )(*args)


def first_kernel(own, low, high, far_low, far_high, from_low, from_high, coef, out, block, first, second,
                 table_re, table_im, diag_re, diag_im):
    fill_tables(coef, 0, table_re, table_im, diag_re, diag_im)
    fill_block(recent_parts(far_low, low, own, high, far_high), FAR, from_low, from_high, 0, block)

    def store(x, y, value):
        out[x, y] = value

    smooth(block, coef, 0, NEAR, table_re, table_im, first, second, store)


def first_image(*args):
    return pl.pallas_call(
        first_kernel,
        out_shape=jax.ShapeDtypeStruct((*wide_shape(NEAR), 8, NZ), F32),
        in_specs=[VMEM] * 8,
        out_specs=VMEM,
        scratch_shapes=smooth_scratch(FAR),
        compiler_params=pltpu.CompilerParams(vmem_limit_bytes=24 << 20),
        name="first_image",
    )(*args)


def split3(value):
    high = value.astype(BF16)
    rest = value - high.astype(F32)
    middle = rest.astype(BF16)
    low = (rest - middle.astype(F32)).astype(BF16)
    return high, middle, low


def basis_plane(start, w, old_image, w_image, x):
    refs = [(start, 0), (start, LY), (start, 2 * LY), (w, None), (old_image, 0), (old_image, LY), (w_image, 0)]
    rows = []
    for ref, first in refs:
        if first is None:
            tiles = [ref[x + NEAR, NEAR + y] for y in range(LY)]
        else:
            tiles = [ref[x, pl.ds((first + y) * 8, 8), :] for y in range(LY)]
        rows.append(jnp.concatenate(tiles, axis=1))
    rows.append(jnp.zeros((8, LY * NZ), F32))
    return jnp.concatenate(rows, axis=0)


def lane_roll(value, amount):
    return pltpu.roll(value, amount % NZ, 1)


SLOTS = [(0, 0), (0, 56), (1, 0), (1, 40), (1, 72), (1, 96), (0, 104)]


def pack_gram(gram):
    lane = lax.broadcasted_iota(jnp.int32, (8, NZ), 1)
    row = lax.broadcasted_iota(jnp.int32, (8, NZ), 0)
    packed = jnp.zeros((8, NZ), F32)
    for b in range(BLOCKS):
        rows = gram[8 * b:8 * b + 8]
        turned = jnp.where(lane % 8 < 4, lane_roll(rows, -4), -lane_roll(rows, 4))
        both = rows + pltpu.roll(turned, 4, 0)
        half, start = SLOTS[b]
        moved = lane_roll(both, start - 8 * b)
        if half:
            moved = pltpu.roll(moved, 4, 0)
        keep = (lane >= start) & (lane < start + 8 * (BLOCKS - b)) & (row // 4 == half)
        packed = packed + jnp.where(keep, moved, 0.0)
    return packed


def unpack_gram(packed):
    lane = lax.broadcasted_iota(jnp.int32, (8, NZ), 1)
    row = lax.broadcasted_iota(jnp.int32, (8, NZ), 0)
    rows = []
    for b in range(BLOCKS):
        half, start = SLOTS[b]
        moved = lane_roll(packed, 8 * b - start)
        if half:
            moved = pltpu.roll(moved, 4, 0)
        keep = (lane >= 8 * b) & (lane < 8 * BLOCKS) & (row < 4)
        moved = jnp.where(keep, moved, 0.0)
        turned = jnp.where(lane % 8 < 4, -lane_roll(moved, -4), lane_roll(moved, 4))
        rows.append(moved + pltpu.roll(turned, 4, 0))
    rows.append(jnp.zeros((NZ - 8 * BLOCKS, NZ), F32))
    upper = jnp.concatenate(rows, axis=0)
    tall = lax.broadcasted_iota(jnp.int32, (NZ, NZ), 0)
    wide = lax.broadcasted_iota(jnp.int32, (NZ, NZ), 1)
    return jnp.where(tall // 8 <= wide // 8, upper, upper.T)


def gram_kernel(peers, w, coef, start, old_image, w_image, out,
                first, second, table_re, table_im, diag_re, diag_im):
    fill_tables(coef, FAR - NEAR, table_re, table_im, diag_re, diag_im)

    def store(x, y, value):
        w_image[x, pl.ds(y * 8, 8), :] = value

    smooth(w, coef, FAR - NEAR, 0, table_re, table_im, first, second, store)

    def plane(x, total):
        stacked = jnp.concatenate(split3(basis_plane(start, w, old_image, w_image, x)), axis=0)
        return total + lax.dot_general(stacked, stacked, (((1,), (1,)), ((), ())), preferred_element_type=F32)

    total = lax.fori_loop(0, LX, plane, jnp.zeros((3 * ROWS, 3 * ROWS), F32))
    tall = total[0:ROWS] + total[ROWS:2 * ROWS] + total[2 * ROWS:3 * ROWS]
    gram = tall[:, 0:ROWS] + tall[:, ROWS:2 * ROWS] + tall[:, 2 * ROWS:3 * ROWS]
    gram = jnp.concatenate([gram, jnp.zeros((ROWS, NZ - ROWS), F32)], axis=1)
    packed = pack_gram(gram)
    for peer in range(peers):
        out[peer] = packed


def image_and_gram(peers, *args):
    return pl.pallas_call(
        functools.partial(gram_kernel, peers),
        out_shape=(jax.ShapeDtypeStruct((LX, LY * 8, NZ), F32),
                   jax.ShapeDtypeStruct((peers, 8, NZ), F32)),
        in_specs=[VMEM] * 4,
        out_specs=(VMEM, VMEM),
        scratch_shapes=smooth_scratch(NEAR)[1:],
        compiler_params=pltpu.CompilerParams(vmem_limit_bytes=32 << 20),
        name="image_and_gram",
    )(*args)


def sum_kernel(parts, out):
    total = jnp.sum(parts[...], axis=0)
    for peer in range(out.shape[0]):
        out[peer] = total


def sum_and_spread(parts, peers):
    return pl.pallas_call(
        sum_kernel,
        out_shape=jax.ShapeDtypeStruct((peers, 8, NZ), F32),
        in_specs=[VMEM],
        out_specs=VMEM,
        compiler_params=pltpu.CompilerParams(vmem_limit_bytes=1 << 20),
        name="sum_and_spread",
    )(parts)


def mul(left, right):
    return lax.dot_general(left, right, (((1,), (0,)), ((), ())), precision=HIGHEST, preferred_element_type=F32)


def mul_t(left, right):
    return lax.dot_general(left, right, (((1,), (1,)), ((), ())), precision=HIGHEST, preferred_element_type=F32)


def inverse_factor(gram):
    lane = lax.broadcasted_iota(jnp.int32, (8, NZ), 1)
    row = lax.broadcasted_iota(jnp.int32, (8, NZ), 0)
    work = jnp.where(lane < 8, gram, jnp.where(lane == row + 8, 1.0, 0.0))
    rank = 2 * (row % 4) + row // 4
    for step in range(8):
        k = (step % 2) * 4 + step // 2
        line = work[k:k + 1, :]
        pivot = line[:, k:k + 1]
        column = work[:, k:k + 1]
        root = 1.0 / jnp.sqrt(pivot)
        line = line * root
        factor = column * root
        work = jnp.where(rank > step, work - factor * line, jnp.where(rank == step, line, work))
    return jnp.where(lane < 8, lane_roll(work, -8), 0.0)


def coefficients(gram):
    lane = lax.broadcasted_iota(jnp.int32, (8, NZ), 1)
    row = lax.broadcasted_iota(jnp.int32, (8, NZ), 0)
    tall = lax.broadcasted_iota(jnp.int32, (NZ, NZ), 0)
    wide = lax.broadcasted_iota(jnp.int32, (NZ, NZ), 1)

    def normalise(rows):
        small = mul_t(mul(rows, gram), rows_in(rows))
        return mul(inverse_factor(small)[:, 0:8], rows)

    def rows_in(rows):
        return jnp.concatenate([rows, jnp.zeros((NZ - 8, NZ), F32)], axis=0)

    once = jnp.where(lane < 24, gram[24:32], 0.0)
    again = jnp.where(lane < 24, mul(once, gram), 0.0)
    fresh = jnp.where(lane == row + 24, 1.0, 0.0)
    new = normalise(fresh - (2.0 * once - again))
    image = (jnp.where((lane >= 32) & (lane < 48), lane_roll(new, 32), 0.0)
             + jnp.where((lane >= 24) & (lane < 32), lane_roll(new, 8), 0.0)
             + jnp.where((lane >= 48) & (lane < 56), lane_roll(new, 24), 0.0))
    window = jnp.where((tall < 16) & (wide == tall + 8), 1.0, 0.0)
    window = jnp.concatenate([window[0:16], new, window[24:]], axis=0)

    def project(rows):
        return mul(mul_t(mul(rows, gram), window), window)

    once = project(image)
    again = project(once)
    newest = normalise(image - (2.0 * once - again))
    return new, newest


def final_kernel(cells, parts, start, w, old_image, w_image, out):
    gram = unpack_gram(jnp.sum(parts[...], axis=0) * (1.0 / cells))
    new, newest = coefficients(gram)
    mapping = jnp.concatenate([new, newest], axis=0)[:, 0:ROWS]
    pieces = [jnp.concatenate([piece] * 3, axis=1) for piece in split3(mapping)]
    stacked_map = jnp.concatenate(pieces, axis=0)

    def plane(x, carry):
        stacked = jnp.concatenate(split3(basis_plane(start, w, old_image, w_image, x)), axis=0)
        full = lax.dot_general(stacked_map, stacked, (((1,), (0,)), ((), ())), preferred_element_type=F32)
        result = full[32:48] + full[16:32] + full[0:16]
        for k in range(2):
            tiles = jnp.stack([result[8 * k:8 * k + 8, y * NZ:(y + 1) * NZ] for y in range(LY)])
            out[k, :, x] = jnp.swapaxes(tiles, 0, 1)
        return carry

    lax.fori_loop(0, LX, plane, 0)


def finish(cells, *args):
    return pl.pallas_call(
        functools.partial(final_kernel, cells),
        out_shape=jax.ShapeDtypeStruct((2, 8, LX, LY, NZ), F32),
        in_specs=[VMEM] * 5,
        out_specs=VMEM,
        compiler_params=pltpu.CompilerParams(vmem_limit_bytes=32 << 20),
        name="finish",
    )(*args)


GX = ("z", "core")


def from_both(axis, count, to_higher, to_lower, step=1):
    return (
        lax.ppermute(to_higher, axis, [(i, i + step) for i in range(count - step)]),
        lax.ppermute(to_lower, axis, [(i + step, i) for i in range(count - step)]),
    )


def per_device(nx, ny, nz, prior, coefficient):
    cells = coefficient.size * nx * ny
    by_cell = prior.transpose(3, 0, 4, 1, 2, 5).reshape(LX, 3 * LY * 8, NZ)
    start = jnp.concatenate([by_cell, coefficient], axis=1)
    far = start[:, 2 * BLOCK:]
    sides = from_both(GX, nx, start, start) + from_both(GX, nx, far, far, 2)
    up, down, old_up, old_down = pack_rims(start, *sides)
    old_rims = from_both("gy", ny, old_up, old_down)
    rims = from_both("gy", ny, up, down)
    old_image, coef = old_images(start, *sides, *old_rims)
    w = first_image(start, *sides, *rims, coef)

    w_image, spread = image_and_gram(2 * ny, w, coef, start, old_image)
    got = lax.all_to_all(spread, ("core", "gy"), 0, 0)
    got = lax.all_to_all(sum_and_spread(got, nz), "z", 0, 0)
    out = finish(cells, got, start, w, old_image, w_image)
    return out.reshape(2, 2, 4, LX, LY, NZ)


def solution(mesh):
    nx, ny = mesh.shape["gx"], mesh.shape["gy"]
    fine = Mesh(np.asarray(mesh.devices).reshape(nx // 2, 2, ny), ("z", "core", "gy"))
    in_specs = (P(None, None, None, GX, "gy", None), P(GX, "gy", None))
    out_specs = P(None, None, None, GX, "gy", None)
    return jax.shard_map(
        functools.partial(per_device, nx, ny, nx // 2),
        mesh=fine, in_specs=in_specs, out_specs=out_specs, check_vma=False,
    )
```

time: 108 us -> 107 us (level)
  starting transfers between devices: 29.8 us -> 23.9 us
  Pallas kernels: 20.1 us -> 24.3 us
  waiting for transfers between devices: 10.4 us -> 11.7 us
    ppermute x10 -> x8, starting transfers between devices: 29.8 us -> 23.9 us  [the longest x4 12.7 us: from_both(): lax.ppermute(to_lower, axis, [(i + step, i) for i in range(count - step)])]
    pallas_call x5 -> x3, Pallas kernels: 9.8 us -> 14.2 us  [the longest x1 7.74 us: first_image(): pl.pallas_call(first_kernel, out_shape=jax.ShapeDtypeStruct((*wide_shape(...]
    all_to_all x1, blocking collectives: 29.4 us -> 27.6 us  [per_device(): got = lax.all_to_all(sum_and_spread(got, nz), 'z', 0, 0)]
    ppermute x10 -> x8, waiting for transfers between devices: 10.4 us -> 11.7 us  [the longest x4 6.39 us: from_both(): lax.ppermute(to_higher, axis, [(i, i + step) for i in range(count - step)])]
    all_to_all x1, blocking collectives: 16 us -> 17.3 us  [per_device(): got = lax.all_to_all(spread, ('core', 'gy'), 0, 0)]
  transfers between devices with their start and end apart: 10 -> 8, of which waited for: 4 -> 4; matrix products, arithmetic and copies ran while one was open for 0% -> 0% of each run, Pallas kernels for 6% -> 6%
where the time goes in v5:
time: 107 us; the launch traced here: 106 us
  blocking collectives  44.9 us (42%)
  Pallas kernels  24.3 us (23%)
  starting transfers between devices  23.9 us (22%)
  waiting for transfers between devices  11.7 us (11%)
  local copies, waits for them, and re-layouts  1.27 us (1%)
    all_to_all x1, blocking collectives, per_device(): got = lax.all_to_all(sum_and_spread(got, nz), 'z', 0, 0)  27.6 us
    all_to_all x1, blocking collectives, per_device(): got = lax.all_to_all(spread, ('core', 'gy'), 0, 0)  17.3 us
    ppermute x4, starting transfers between devices, from_both(): lax.ppermute(to_lower, axis, [(i + step, i) for i in range(count - step)])  12.7 us
    ppermute x4, starting transfers between devices, from_both(): lax.ppermute(to_higher, axis, [(i, i + step) for i in range(count - step)])  11.2 us
    pallas_call x1, Pallas kernels, first_image(): pl.pallas_call(first_kernel, out_shape=jax.ShapeDtypeStruct((*wide_shape(...  7.74 us
    ppermute x4, waiting for transfers between devices, from_both(): lax.ppermute(to_higher, axis, [(i, i + step) for i in range(count - step)])  6.39 us
    pallas_call x1, Pallas kernels, old_images(): pl.pallas_call(old_kernel, out_shape=(jax.ShapeDtypeStruct((LX, 2 * BLOCK...  6.31 us
    pallas_call x1, Pallas kernels, finish(): pl.pallas_call(functools.partial(final_kernel, cells), out_shape=jax.Shap...  5.54 us
  transfers between devices with their start and end apart: 8, of which 4 were waited for; matrix products, arithmetic and copies ran while one was open for 0% of the time, Pallas kernels for 6%

profile of v5, /device:TPU:1, one launch (start us, length us, event | category | flops | bytes accessed | tf_op | source)
XLA Modules:
  0.0 106.3 jit_solution(8479474930995501859)
XLA Ops:
  0.0 0.0 copy-start
  0.0 1.3 %copy.3 = f32[4,3,8,2,4,128]{5,4,3,2,1,0:T(4,128)S(1)} copy(f32[4,3,8,2,4,128]{5,2,0,4,3,1:T(8,128)} %bitcast.5) | data formatting | bytes 786432 | tf_op jit(solution)/shard_map/transpose | solution.py:469
  1.3 0.0 copy-done
  1.3 8.8 %collective-permute-start.1 = (f32[4,200,128]{2,1,0:T(8,128)S(1)}, f32[4,200,128]{2,1,0:T(8,128)S(1)}, u32[]{:S(2)}, u32[]{:S(2)}) collective-permute-start(f32[4,200,128]{2,1,0:T(8,128)S(1)} %pad_maximum_fusion.own.start), channel_id=1, source_target_pairs={{16,0},{32,16},{48,32},{64,48},{80,64},{96,80},{112,96},{128,112},... | collective-permute-start | bytes 1228808 | tf_op jit(solution)/shard_map/ppermute | solution.py:463
  10.1 1.9 %collective-permute-start = (f32[4,200,128]{2,1,0:T(8,128)S(1)}, f32[4,200,128]{2,1,0:T(8,128)S(1)}, u32[]{:S(2)}, u32[]{:S(2)}) collective-permute-start(f32[4,200,128]{2,1,0:T(8,128)S(1)} %pad_maximum_fusion.own.start), channel_id=1, source_target_pairs={{0,16},{16,32},{32,48},{48,64},{64,80},{80,96},{96,112},{112,128},... | collective-permute-start | bytes 1228808 | tf_op jit(solution)/shard_map/ppermute | solution.py:462
  12.1 1.3 %collective-permute-start.3 = (f32[4,72,128]{2,1,0:T(8,128)S(1)}, f32[4,72,128]{2,1,0:T(8,128)S(1)}, u32[]{:S(2)}, u32[]{:S(2)}) collective-permute-start(f32[4,72,128]{2,1,0:T(8,128)S(1)} %fusion), channel_id=1, source_target_pairs={{32,0},{48,16},{64,32},{80,48},{96,64},{112,80},{128,96},{144,112}... | collective-permute-start | bytes 442376 | tf_op jit(solution)/shard_map/ppermute | solution.py:463
  13.4 4.0 %collective-permute-start.2 = (f32[4,72,128]{2,1,0:T(8,128)S(1)}, f32[4,72,128]{2,1,0:T(8,128)S(1)}, u32[]{:S(2)}, u32[]{:S(2)}) collective-permute-start(f32[4,72,128]{2,1,0:T(8,128)S(1)} %fusion), channel_id=1, source_target_pairs={{0,32},{16,48},{32,64},{48,80},{64,96},{80,112},{96,128},{112,144}... | collective-permute-start | bytes 442376 | tf_op jit(solution)/shard_map/ppermute | solution.py:462
  17.4 1.5 %collective-permute-done.3.far_high = f32[4,72,128]{2,1,0:T(8,128)S(1)} collective-permute-done((f32[4,72,128]{2,1,0:T(8,128)S(1)}, f32[4,72,128]{2,1,0:T(8,128)S(1)}, u32[]{:S(2)}, u32[]{:S(2)}) %collective-permute-start.3) | collective-permute-done | bytes 147488 | tf_op jit(solution)/shard_map/ppermute | solution.py:463
  18.8 0.9 collective-permute-done.2.far_low
  19.7 0.0 collective-permute-done.1.high
  19.7 0.0 collective-permute-done.low
  19.7 0.1 pack_rims.1
  19.9 1.3 %collective-permute-start.4 = (f32[88,8,128]{2,1,0:T(8,128)S(1)}, f32[88,8,128]{2,1,0:T(8,128)S(1)}, u32[]{:S(2)}, u32[]{:S(2)}) collective-permute-start(f32[88,8,128]{2,1,0:T(8,128)S(1)} %get-tuple-element.13), channel_id=1, source_target_pairs={{0,1},{1,2},{2,3},{3,4},{4,5},{5,6},{6,7},{7,8},{8,9},{9,10},{10,1... | collective-permute-start | bytes 1081352 | tf_op jit(solution)/shard_map/ppermute | solution.py:462
  21.2 1.3 %collective-permute-start.5 = (f32[88,8,128]{2,1,0:T(8,128)S(1)}, f32[88,8,128]{2,1,0:T(8,128)S(1)}, u32[]{:S(2)}, u32[]{:S(2)}) collective-permute-start(f32[88,8,128]{2,1,0:T(8,128)S(1)} %get-tuple-element.14), channel_id=1, source_target_pairs={{1,0},{2,1},{3,2},{4,3},{5,4},{6,5},{7,6},{8,7},{9,8},{10,9},{11,1... | collective-permute-start | bytes 1081352 | tf_op jit(solution)/shard_map/ppermute | solution.py:463
  22.5 4.0 %collective-permute-start.6 = (f32[67,8,128]{2,1,0:T(8,128)S(1)}, f32[67,8,128]{2,1,0:T(8,128)S(1)}, u32[]{:S(2)}, u32[]{:S(2)}) collective-permute-start(f32[67,8,128]{2,1,0:T(8,128)S(1)} %get-tuple-element.15), channel_id=1, source_target_pairs={{0,1},{1,2},{2,3},{3,4},{4,5},{5,6},{6,7},{7,8},{8,9},{9,10},{10,1... | collective-permute-start | bytes 823304 | tf_op jit(solution)/shard_map/ppermute | solution.py:462
  26.5 1.3 %collective-permute-start.7 = (f32[67,8,128]{2,1,0:T(8,128)S(1)}, f32[67,8,128]{2,1,0:T(8,128)S(1)}, u32[]{:S(2)}, u32[]{:S(2)}) collective-permute-start(f32[67,8,128]{2,1,0:T(8,128)S(1)} %get-tuple-element.16), channel_id=1, source_target_pairs={{1,0},{2,1},{3,2},{4,3},{5,4},{6,5},{7,6},{8,7},{9,8},{10,9},{11,1... | collective-permute-start | bytes 823304 | tf_op jit(solution)/shard_map/ppermute | solution.py:463
  27.8 5.5 %collective-permute-done.6.from_low = f32[67,8,128]{2,1,0:T(8,128)S(1)} collective-permute-done((f32[67,8,128]{2,1,0:T(8,128)S(1)}, f32[67,8,128]{2,1,0:T(8,128)S(1)}, u32[]{:S(2)}, u32[]{:S(2)}) %collective-permute-start.6) | collective-permute-done | bytes 274464 | tf_op jit(solution)/shard_map/ppermute | solution.py:462
  33.3 3.9 %collective-permute-done.7.from_high = f32[67,8,128]{2,1,0:T(8,128)S(1)} collective-permute-done((f32[67,8,128]{2,1,0:T(8,128)S(1)}, f32[67,8,128]{2,1,0:T(8,128)S(1)}, u32[]{:S(2)}, u32[]{:S(2)}) %collective-permute-start.7) | collective-permute-done | bytes 274464 | tf_op jit(solution)/shard_map/ppermute | solution.py:463
  37.2 6.3 %old_images.1 = (f32[4,128,128]{2,1,0:T(8,128)S(1)}, f32[20,24,128]{2,1,0:T(8,128)S(1)}) custom-call(f32[4,200,128]{2,1,0:T(8,128)S(1)} %pad_maximum_fusion.own.start, f32[4,200,128]{2,1,0:T(8,128)S(1)} %collective-permute-done.low, f32[4,200,128]{2,1,0:T(8,128)S(1)} %collective-permute-done.1.high, f32[4,72,128]{2,1,0:T(8,128)S(1)} %collective-permute-done.2.far_low, ...), custom_call_target="tpu_custom_call" | custom-call | flops 12000000 | bytes 24000000 | tf_op jit(solution)/shard_map/old_images/pallas_call | solution.py:217
  43.5 0.0 collective-permute-done.4.from_low
  43.5 0.0 collective-permute-done.5.from_high
  43.5 7.7 %first_image.1.w = f32[12,16,8,128]{3,2,1,0:T(8,128)S(1)} custom-call(f32[4,200,128]{2,1,0:T(8,128)S(1)} %pad_maximum_fusion.own.start, f32[4,200,128]{2,1,0:T(8,128)S(1)} %collective-permute-done.low, f32[4,200,128]{2,1,0:T(8,128)S(1)} %collective-permute-done.1.high, f32[4,72,128]{2,1,0:T(8,128)S(1)} %collective-permute-done.2.far_low, ...), custom_call_target="tpu_custom_call" | custom-call | tf_op jit(solution)/shard_map/first_image/pallas_call | solution.py:242
  51.2 4.6 %image_and_gram.1 = (f32[4,64,128]{2,1,0:T(8,128)S(1)}, f32[32,8,128]{2,1,0:T(8,128)S(1)}) custom-call(f32[12,16,8,128]{3,2,1,0:T(8,128)S(1)} %first_image.1.w, f32[20,24,128]{2,1,0:T(8,128)S(1)} %get-tuple-element.17.coef, f32[4,200,128]{2,1,0:T(8,128)S(1)} %pad_maximum_fusion.own.start, f32[4,128,128]{2,1,0:T(8,128)S(1)} %get-tuple-element.18.old_image), custom_call_target="tpu_custom_call" | custom-call | tf_op jit(solution)/shard_map/image_and_gram/pallas_call | solution.py:341
  55.8 17.3 %all_to_all.10.parts = f32[32,8,128]{2,1,0:T(8,128)S(1)} all-to-all(f32[32,8,128]{2,1,0:T(8,128)S(1)} %get-tuple-element.19), channel_id=1, replica_groups=mesh['z'=16,'core'=2,'gy'=16] {'core','gy'}, dimensions={0} | all-to-all | bytes 262144 | tf_op jit(solution)/shard_map/all_to_all | solution.py:480
  73.2 27.6 %all_to_all.11.parts = f32[16,8,128]{2,1,0:T(8,128)S(1)} all-to-all(f32[16,8,128]{2,1,0:T(8,128)S(1)} %sum_and_spread.1), channel_id=1, replica_groups=mesh['z'=16,'core'=2,'gy'=16] {'z'}, dimensions={0} | all-to-all | bytes 131072 | tf_op jit(solution)/shard_map/all_to_all | solution.py:481
  100.8 5.5 %finish.1 = f32[2,8,4,8,128]{4,3,2,1,0:T(8,128)} custom-call(f32[16,8,128]{2,1,0:T(8,128)S(1)} %all_to_all.11.parts, f32[4,200,128]{2,1,0:T(8,128)S(1)} %pad_maximum_fusion.own.start, f32[12,16,8,128]{3,2,1,0:T(8,128)S(1)} %first_image.1.w, f32[4,128,128]{2,1,0:T(8,128)S(1)} %get-tuple-element.18.old_image, f32[4,64,128]{2,1,0:T(8,128)S(1)} %get-tuple-element.20.w_image), custom_call_target="tpu_custom_call" | custom-call | tf_op jit(solution)/shard_map/finish/pallas_call | solution.py:447
  (3 shorter events, 0.1 us)
Async XLA Ops:
  0.0 1.3 %copy-start = (f32[4,8,128]{2,1,0:T(8,128)S(1)}, f32[4,8,128]{2,1,0:T(8,128)}, u32[]{:S(2)}) copy-start(f32[4,8,128]{2,1,0:T(8,128)} %param.3) | copy-start | bytes 49156
  1.3 18.4 %collective-permute-start.1 = (f32[4,200,128]{2,1,0:T(8,128)S(1)}, f32[4,200,128]{2,1,0:T(8,128)S(1)}, u32[]{:S(2)}, u32[]{:S(2)}) collective-permute-start(f32[4,200,128]{2,1,0:T(8,128)S(1)} %pad_maximum_fusion.own.start), channel_id=1, source_target_pairs={{16,0},{32,16},{48,32},{64,48},{80,64},{96,80},{112,96},{128,112},... | collective-permute-start | bytes 1228808 | tf_op jit(solution)/shard_map/ppermute | solution.py:463
  10.1 9.6 %collective-permute-start = (f32[4,200,128]{2,1,0:T(8,128)S(1)}, f32[4,200,128]{2,1,0:T(8,128)S(1)}, u32[]{:S(2)}, u32[]{:S(2)}) collective-permute-start(f32[4,200,128]{2,1,0:T(8,128)S(1)} %pad_maximum_fusion.own.start), channel_id=1, source_target_pairs={{0,16},{16,32},{32,48},{48,64},{64,80},{80,96},{96,112},{112,128},... | collective-permute-start | bytes 1228808 | tf_op jit(solution)/shard_map/ppermute | solution.py:462
  12.1 6.8 %collective-permute-start.3 = (f32[4,72,128]{2,1,0:T(8,128)S(1)}, f32[4,72,128]{2,1,0:T(8,128)S(1)}, u32[]{:S(2)}, u32[]{:S(2)}) collective-permute-start(f32[4,72,128]{2,1,0:T(8,128)S(1)} %fusion), channel_id=1, source_target_pairs={{32,0},{48,16},{64,32},{80,48},{96,64},{112,80},{128,96},{144,112}... | collective-permute-start | bytes 442376 | tf_op jit(solution)/shard_map/ppermute | solution.py:463
  13.4 6.3 %collective-permute-start.2 = (f32[4,72,128]{2,1,0:T(8,128)S(1)}, f32[4,72,128]{2,1,0:T(8,128)S(1)}, u32[]{:S(2)}, u32[]{:S(2)}) collective-permute-start(f32[4,72,128]{2,1,0:T(8,128)S(1)} %fusion), channel_id=1, source_target_pairs={{0,32},{16,48},{32,64},{48,80},{64,96},{80,112},{96,128},{112,144}... | collective-permute-start | bytes 442376 | tf_op jit(solution)/shard_map/ppermute | solution.py:462
  19.9 23.6 %collective-permute-start.4 = (f32[88,8,128]{2,1,0:T(8,128)S(1)}, f32[88,8,128]{2,1,0:T(8,128)S(1)}, u32[]{:S(2)}, u32[]{:S(2)}) collective-permute-start(f32[88,8,128]{2,1,0:T(8,128)S(1)} %get-tuple-element.13), channel_id=1, source_target_pairs={{0,1},{1,2},{2,3},{3,4},{4,5},{5,6},{6,7},{7,8},{8,9},{9,10},{10,1... | collective-permute-start | bytes 1081352 | tf_op jit(solution)/shard_map/ppermute | solution.py:462
  21.2 22.3 %collective-permute-start.5 = (f32[88,8,128]{2,1,0:T(8,128)S(1)}, f32[88,8,128]{2,1,0:T(8,128)S(1)}, u32[]{:S(2)}, u32[]{:S(2)}) collective-permute-start(f32[88,8,128]{2,1,0:T(8,128)S(1)} %get-tuple-element.14), channel_id=1, source_target_pairs={{1,0},{2,1},{3,2},{4,3},{5,4},{6,5},{7,6},{8,7},{9,8},{10,9},{11,1... | collective-permute-start | bytes 1081352 | tf_op jit(solution)/shard_map/ppermute | solution.py:463
  22.5 10.8 %collective-permute-start.6 = (f32[67,8,128]{2,1,0:T(8,128)S(1)}, f32[67,8,128]{2,1,0:T(8,128)S(1)}, u32[]{:S(2)}, u32[]{:S(2)}) collective-permute-start(f32[67,8,128]{2,1,0:T(8,128)S(1)} %get-tuple-element.15), channel_id=1, source_target_pairs={{0,1},{1,2},{2,3},{3,4},{4,5},{5,6},{6,7},{7,8},{8,9},{9,10},{10,1... | collective-permute-start | bytes 823304 | tf_op jit(solution)/shard_map/ppermute | solution.py:462
  26.5 10.7 %collective-permute-start.7 = (f32[67,8,128]{2,1,0:T(8,128)S(1)}, f32[67,8,128]{2,1,0:T(8,128)S(1)}, u32[]{:S(2)}, u32[]{:S(2)}) collective-permute-start(f32[67,8,128]{2,1,0:T(8,128)S(1)} %get-tuple-element.16), channel_id=1, source_target_pairs={{1,0},{2,1},{3,2},{4,3},{5,4},{6,5},{7,6},{8,7},{9,8},{10,9},{11,1... | collective-permute-start | bytes 823304 | tf_op jit(solution)/shard_map/ppermute | solution.py:463

commit v6 on v5

--- a/solution.py
+++ b/solution.py
@@ -40,8 +40,8 @@
     return [(ref, first + rows) for ref, first in parts]
 
 
-def fill_rim(parts, halo, up, down, start):
-    for d, plane, place in rim_spots(halo):
+def fill_rim(parts, halo, up, down, start, begin=0, end=None):
+    for d, plane, place in rim_spots(halo)[begin:end]:
         ref, x, first = plane_of(parts, plane)
         up[start + place] = ref[x, pl.ds(first + (LY - d) * 8, 8), :]
         down[start + place] = ref[x, pl.ds(first + (d - 1) * 8, 8), :]
@@ -58,6 +58,8 @@
 BLOCK = LY * 8
 OLD_RIM = sum(widths(NEAR))
 FAR_RIM = sum(widths(FAR))
+SPLIT = sum(widths(FAR)[:5])
+EARLY = 2 * OLD_RIM + FAR_RIM // 8
 
 
 def recent_parts(far_low, low, own, high, far_high):
@@ -70,11 +72,12 @@
     for group in range(2):
         fill_rim(shifted(parts, group * BLOCK), NEAR, old_up, old_down, group * OLD_RIM)
     fill_flat_rim(shifted(wide, BLOCK), FAR, old_up, old_down, 2 * OLD_RIM)
-    fill_rim(wide, FAR, up, down, 0)
+    fill_rim(wide, FAR, up, down, 0, 0, SPLIT)
+    fill_rim(wide, FAR, old_up, old_down, EARLY - SPLIT, SPLIT)
 
 
 def pack_rims(*args):
-    sizes = [FAR_RIM] * 2 + [2 * OLD_RIM + FAR_RIM // 8] * 2
+    sizes = [SPLIT] * 2 + [EARLY + FAR_RIM - SPLIT] * 2
     shapes = tuple(jax.ShapeDtypeStruct((size, 8, NZ), F32) for size in sizes)
     return pl.pallas_call(
         rim_kernel,
@@ -86,14 +89,15 @@
     )(*args)
 
 
-def fill_block(parts, halo, from_low, from_high, start, wide):
+def fill_block(parts, halo, find_rim, wide):
     wide[...] = jnp.zeros(wide.shape, F32)
     for index in range(LX + 2 * halo):
         ref, x, first = plane_of(parts, index)
         wide[index, halo:halo + LY] = ref[x, pl.ds(first, BLOCK), :].reshape(LY, 8, NZ)
     for d, plane, place in rim_spots(halo):
-        wide[plane, halo - d] = from_low[start + place]
-        wide[plane, halo + LY - 1 + d] = from_high[start + place]
+        from_low, from_high, spot = find_rim(place)
+        wide[plane, halo - d] = from_low[spot]
+        wide[plane, halo + LY - 1 + d] = from_high[spot]
 
 
 def fill_flat(parts, halo, from_low, from_high, start, wide):
@@ -205,7 +209,7 @@
     fill_tables(coef, FAR - NEAR, table_re, table_im, diag_re, diag_im)
     for group in range(2):
         parts = [(low, group * BLOCK), (own, group * BLOCK), (high, group * BLOCK)]
-        fill_block(parts, NEAR, from_low, from_high, group * OLD_RIM, block)
+        fill_block(parts, NEAR, lambda place, group=group: (from_low, from_high, group * OLD_RIM + place), block)
 
         def store(x, y, value, group=group):
             out[x, pl.ds(group * BLOCK + y * 8, 8), :] = value
@@ -227,10 +231,16 @@
     )(*args)
 
 
-def first_kernel(own, low, high, far_low, far_high, from_low, from_high, coef, out, block, first, second,
+def first_kernel(coef, own, low, high, far_low, far_high, from_low, from_high, early_low, early_high, out, block, first, second,
                  table_re, table_im, diag_re, diag_im):
     fill_tables(coef, 0, table_re, table_im, diag_re, diag_im)
-    fill_block(recent_parts(far_low, low, own, high, far_high), FAR, from_low, from_high, 0, block)
+
+    def find_rim(place):
+        if place < SPLIT:
+            return from_low, from_high, place
+        return early_low, early_high, EARLY + place - SPLIT
+
+    fill_block(recent_parts(far_low, low, own, high, far_high), FAR, find_rim, block)
 
     def store(x, y, value):
         out[x, y] = value
@@ -242,7 +252,7 @@
     return pl.pallas_call(
         first_kernel,
         out_shape=jax.ShapeDtypeStruct((*wide_shape(NEAR), 8, NZ), F32),
-        in_specs=[VMEM] * 8,
+        in_specs=[VMEM] * 10,
         out_specs=VMEM,
         scratch_shapes=smooth_scratch(FAR),
         compiler_params=pltpu.CompilerParams(vmem_limit_bytes=24 << 20),
@@ -471,10 +481,10 @@
     far = start[:, 2 * BLOCK:]
     sides = from_both(GX, nx, start, start) + from_both(GX, nx, far, far, 2)
     up, down, old_up, old_down = pack_rims(start, *sides)
+    rims = from_both("gy", ny, up, down)
     old_rims = from_both("gy", ny, old_up, old_down)
-    rims = from_both("gy", ny, up, down)
     old_image, coef = old_images(start, *sides, *old_rims)
-    w = first_image(start, *sides, *rims, coef)
+    w = first_image(coef, start, *sides, *rims, *old_rims)
 
     w_image, spread = image_and_gram(2 * ny, w, coef, start, old_image)
     got = lax.all_to_all(spread, ("core", "gy"), 0, 0)

time: 107 us -> 100 us (0.935)
  waiting for transfers between devices: 11.7 us -> 5.58 us
    ppermute x4, waiting for transfers between devices: 6.39 us -> 0.87 us  [from_both(): lax.ppermute(to_higher, axis, [(i, i + step) for i in range(count - step)])]
  transfers between devices with their start and end apart: 8 -> 8, of which waited for: 4 -> 3; matrix products, arithmetic and copies ran while one was open for 0% -> 0% of each run, Pallas kernels for 6% -> 6%
where the time goes in v6:
time: 100 us
  blocking collectives  44.8 us (45%)
  Pallas kernels  24.3 us (24%)
  starting transfers between devices  23.9 us (24%)
  waiting for transfers between devices  5.58 us (6%)
  local copies, waits for them, and re-layouts  1.27 us (1%)
    all_to_all x1, blocking collectives, per_device(): got = lax.all_to_all(sum_and_spread(got, nz), 'z', 0, 0)  27.5 us
    all_to_all x1, blocking collectives, per_device(): got = lax.all_to_all(spread, ('core', 'gy'), 0, 0)  17.3 us
    ppermute x4, starting transfers between devices, from_both(): lax.ppermute(to_lower, axis, [(i + step, i) for i in range(count - step)])  12.7 us
    ppermute x4, starting transfers between devices, from_both(): lax.ppermute(to_higher, axis, [(i, i + step) for i in range(count - step)])  11.2 us
    pallas_call x1, Pallas kernels, first_image(): pl.pallas_call(first_kernel, out_shape=jax.ShapeDtypeStruct((*wide_shape(...  7.74 us
    pallas_call x1, Pallas kernels, old_images(): pl.pallas_call(old_kernel, out_shape=(jax.ShapeDtypeStruct((LX, 2 * BLOCK...  6.3 us
    pallas_call x1, Pallas kernels, finish(): pl.pallas_call(functools.partial(final_kernel, cells), out_shape=jax.Shap...  5.54 us
    ppermute x4, waiting for transfers between devices, from_both(): lax.ppermute(to_lower, axis, [(i + step, i) for i in range(count - step)])  4.71 us
  transfers between devices with their start and end apart: 8, of which 3 were waited for; matrix products, arithmetic and copies ran while one was open for 0% of the time, Pallas kernels for 6%

profile of v6, /device:TPU:1, one launch (start us, length us, event | category | flops | bytes accessed | tf_op | source)
XLA Modules:
  0.0 100.1 jit_solution(3442161102942782316)
XLA Ops:
  0.0 0.0 copy-start
  0.0 1.3 %copy.3 = f32[4,3,8,2,4,128]{5,4,3,2,1,0:T(4,128)S(1)} copy(f32[4,3,8,2,4,128]{5,2,0,4,3,1:T(8,128)} %bitcast.5) | data formatting | bytes 786432 | tf_op jit(solution)/shard_map/transpose | solution.py:479
  1.3 0.0 copy-done
  1.3 8.8 %collective-permute-start.1 = (f32[4,200,128]{2,1,0:T(8,128)S(1)}, f32[4,200,128]{2,1,0:T(8,128)S(1)}, u32[]{:S(2)}, u32[]{:S(2)}) collective-permute-start(f32[4,200,128]{2,1,0:T(8,128)S(1)} %pad_maximum_fusion.own.start), channel_id=1, source_target_pairs={{16,0},{32,16},{48,32},{64,48},{80,64},{96,80},{112,96},{128,112},... | collective-permute-start | bytes 1228808 | tf_op jit(solution)/shard_map/ppermute | solution.py:473
  10.1 1.9 %collective-permute-start = (f32[4,200,128]{2,1,0:T(8,128)S(1)}, f32[4,200,128]{2,1,0:T(8,128)S(1)}, u32[]{:S(2)}, u32[]{:S(2)}) collective-permute-start(f32[4,200,128]{2,1,0:T(8,128)S(1)} %pad_maximum_fusion.own.start), channel_id=1, source_target_pairs={{0,16},{16,32},{32,48},{48,64},{64,80},{80,96},{96,112},{112,128},... | collective-permute-start | bytes 1228808 | tf_op jit(solution)/shard_map/ppermute | solution.py:472
  12.1 1.3 %collective-permute-start.3 = (f32[4,72,128]{2,1,0:T(8,128)S(1)}, f32[4,72,128]{2,1,0:T(8,128)S(1)}, u32[]{:S(2)}, u32[]{:S(2)}) collective-permute-start(f32[4,72,128]{2,1,0:T(8,128)S(1)} %fusion), channel_id=1, source_target_pairs={{32,0},{48,16},{64,32},{80,48},{96,64},{112,80},{128,96},{144,112}... | collective-permute-start | bytes 442376 | tf_op jit(solution)/shard_map/ppermute | solution.py:473
  13.4 4.0 %collective-permute-start.2 = (f32[4,72,128]{2,1,0:T(8,128)S(1)}, f32[4,72,128]{2,1,0:T(8,128)S(1)}, u32[]{:S(2)}, u32[]{:S(2)}) collective-permute-start(f32[4,72,128]{2,1,0:T(8,128)S(1)} %fusion), channel_id=1, source_target_pairs={{0,32},{16,48},{32,64},{48,80},{64,96},{80,112},{96,128},{112,144}... | collective-permute-start | bytes 442376 | tf_op jit(solution)/shard_map/ppermute | solution.py:472
  17.4 1.5 %collective-permute-done.3.far_high = f32[4,72,128]{2,1,0:T(8,128)S(1)} collective-permute-done((f32[4,72,128]{2,1,0:T(8,128)S(1)}, f32[4,72,128]{2,1,0:T(8,128)S(1)}, u32[]{:S(2)}, u32[]{:S(2)}) %collective-permute-start.3) | collective-permute-done | bytes 147488 | tf_op jit(solution)/shard_map/ppermute | solution.py:473
  18.8 0.9 collective-permute-done.2.far_low
  19.7 0.0 collective-permute-done.1.high
  19.7 0.0 collective-permute-done.low
  19.7 0.1 pack_rims.1
  19.9 1.3 %collective-permute-start.4 = (f32[85,8,128]{2,1,0:T(8,128)S(1)}, f32[85,8,128]{2,1,0:T(8,128)S(1)}, u32[]{:S(2)}, u32[]{:S(2)}) collective-permute-start(f32[85,8,128]{2,1,0:T(8,128)S(1)} %get-tuple-element.13), channel_id=1, source_target_pairs={{0,1},{1,2},{2,3},{3,4},{4,5},{5,6},{6,7},{7,8},{8,9},{9,10},{10,1... | collective-permute-start | bytes 1044488 | tf_op jit(solution)/shard_map/ppermute | solution.py:472
  21.2 1.3 %collective-permute-start.5 = (f32[85,8,128]{2,1,0:T(8,128)S(1)}, f32[85,8,128]{2,1,0:T(8,128)S(1)}, u32[]{:S(2)}, u32[]{:S(2)}) collective-permute-start(f32[85,8,128]{2,1,0:T(8,128)S(1)} %get-tuple-element.14), channel_id=1, source_target_pairs={{1,0},{2,1},{3,2},{4,3},{5,4},{6,5},{7,6},{8,7},{9,8},{10,9},{11,1... | collective-permute-start | bytes 1044488 | tf_op jit(solution)/shard_map/ppermute | solution.py:473
  22.5 4.0 %collective-permute-start.6 = (f32[70,8,128]{2,1,0:T(8,128)S(1)}, f32[70,8,128]{2,1,0:T(8,128)S(1)}, u32[]{:S(2)}, u32[]{:S(2)}) collective-permute-start(f32[70,8,128]{2,1,0:T(8,128)S(1)} %get-tuple-element.16), channel_id=1, source_target_pairs={{0,1},{1,2},{2,3},{3,4},{4,5},{5,6},{6,7},{7,8},{8,9},{9,10},{10,1... | collective-permute-start | bytes 860168 | tf_op jit(solution)/shard_map/ppermute | solution.py:472
  26.5 1.3 %collective-permute-start.7 = (f32[70,8,128]{2,1,0:T(8,128)S(1)}, f32[70,8,128]{2,1,0:T(8,128)S(1)}, u32[]{:S(2)}, u32[]{:S(2)}) collective-permute-start(f32[70,8,128]{2,1,0:T(8,128)S(1)} %get-tuple-element.17), channel_id=1, source_target_pairs={{1,0},{2,1},{3,2},{4,3},{5,4},{6,5},{7,6},{8,7},{9,8},{10,9},{11,1... | collective-permute-start | bytes 860168 | tf_op jit(solution)/shard_map/ppermute | solution.py:473
  27.8 0.0 collective-permute-done.4.from_low.early_low
  27.8 3.2 %collective-permute-done.5.from_high.early_high = f32[85,8,128]{2,1,0:T(8,128)S(1)} collective-permute-done((f32[85,8,128]{2,1,0:T(8,128)S(1)}, f32[85,8,128]{2,1,0:T(8,128)S(1)}, u32[]{:S(2)}, u32[]{:S(2)}) %collective-permute-start.5) | collective-permute-done | bytes 348192 | tf_op jit(solution)/shard_map/ppermute | solution.py:473
  31.0 6.3 %old_images.1 = (f32[4,128,128]{2,1,0:T(8,128)S(1)}, f32[20,24,128]{2,1,0:T(8,128)S(1)}) custom-call(f32[4,200,128]{2,1,0:T(8,128)S(1)} %pad_maximum_fusion.own.start, f32[4,200,128]{2,1,0:T(8,128)S(1)} %collective-permute-done.low, f32[4,200,128]{2,1,0:T(8,128)S(1)} %collective-permute-done.1.high, f32[4,72,128]{2,1,0:T(8,128)S(1)} %collective-permute-done.2.far_low, ...), custom_call_target="tpu_custom_call" | custom-call | flops 12000000 | bytes 24000000 | tf_op jit(solution)/shard_map/old_images/pallas_call | solution.py:221
  37.3 0.0 collective-permute-done.6.from_low
  37.3 0.0 collective-permute-done.7.from_high
  37.4 7.7 %first_image.1.w = f32[12,16,8,128]{3,2,1,0:T(8,128)S(1)} custom-call(f32[20,24,128]{2,1,0:T(8,128)S(1)} %get-tuple-element.15.coef, f32[4,200,128]{2,1,0:T(8,128)S(1)} %pad_maximum_fusion.own.start, f32[4,200,128]{2,1,0:T(8,128)S(1)} %collective-permute-done.low, f32[4,200,128]{2,1,0:T(8,128)S(1)} %collective-permute-done.1.high, ...), custom_call_target="tpu_custom_call" | custom-call | tf_op jit(solution)/shard_map/first_image/pallas_call | solution.py:252
  45.1 4.6 %image_and_gram.1 = (f32[4,64,128]{2,1,0:T(8,128)S(1)}, f32[32,8,128]{2,1,0:T(8,128)S(1)}) custom-call(f32[12,16,8,128]{3,2,1,0:T(8,128)S(1)} %first_image.1.w, f32[20,24,128]{2,1,0:T(8,128)S(1)} %get-tuple-element.15.coef, f32[4,200,128]{2,1,0:T(8,128)S(1)} %pad_maximum_fusion.own.start, f32[4,128,128]{2,1,0:T(8,128)S(1)} %get-tuple-element.18.old_image), custom_call_target="tpu_custom_call" | custom-call | tf_op jit(solution)/shard_map/image_and_gram/pallas_call | solution.py:351
  49.7 17.3 %all_to_all.10.parts = f32[32,8,128]{2,1,0:T(8,128)S(1)} all-to-all(f32[32,8,128]{2,1,0:T(8,128)S(1)} %get-tuple-element.19), channel_id=1, replica_groups=mesh['z'=16,'core'=2,'gy'=16] {'core','gy'}, dimensions={0} | all-to-all | bytes 262144 | tf_op jit(solution)/shard_map/all_to_all | solution.py:490
  67.0 27.5 %all_to_all.11.parts = f32[16,8,128]{2,1,0:T(8,128)S(1)} all-to-all(f32[16,8,128]{2,1,0:T(8,128)S(1)} %sum_and_spread.1), channel_id=1, replica_groups=mesh['z'=16,'core'=2,'gy'=16] {'z'}, dimensions={0} | all-to-all | bytes 131072 | tf_op jit(solution)/shard_map/all_to_all | solution.py:491
  94.5 5.5 %finish.1 = f32[2,8,4,8,128]{4,3,2,1,0:T(8,128)} custom-call(f32[16,8,128]{2,1,0:T(8,128)S(1)} %all_to_all.11.parts, f32[4,200,128]{2,1,0:T(8,128)S(1)} %pad_maximum_fusion.own.start, f32[12,16,8,128]{3,2,1,0:T(8,128)S(1)} %first_image.1.w, f32[4,128,128]{2,1,0:T(8,128)S(1)} %get-tuple-element.18.old_image, f32[4,64,128]{2,1,0:T(8,128)S(1)} %get-tuple-element.20.w_image), custom_call_target="tpu_custom_call" | custom-call | tf_op jit(solution)/shard_map/finish/pallas_call | solution.py:457
  (3 shorter events, 0.1 us)
Async XLA Ops:
  0.0 1.3 %copy-start = (f32[4,8,128]{2,1,0:T(8,128)S(1)}, f32[4,8,128]{2,1,0:T(8,128)}, u32[]{:S(2)}) copy-start(f32[4,8,128]{2,1,0:T(8,128)} %param.3) | copy-start | bytes 49156
  1.3 18.4 %collective-permute-start.1 = (f32[4,200,128]{2,1,0:T(8,128)S(1)}, f32[4,200,128]{2,1,0:T(8,128)S(1)}, u32[]{:S(2)}, u32[]{:S(2)}) collective-permute-start(f32[4,200,128]{2,1,0:T(8,128)S(1)} %pad_maximum_fusion.own.start), channel_id=1, source_target_pairs={{16,0},{32,16},{48,32},{64,48},{80,64},{96,80},{112,96},{128,112},... | collective-permute-start | bytes 1228808 | tf_op jit(solution)/shard_map/ppermute | solution.py:473
  10.1 9.6 %collective-permute-start = (f32[4,200,128]{2,1,0:T(8,128)S(1)}, f32[4,200,128]{2,1,0:T(8,128)S(1)}, u32[]{:S(2)}, u32[]{:S(2)}) collective-permute-start(f32[4,200,128]{2,1,0:T(8,128)S(1)} %pad_maximum_fusion.own.start), channel_id=1, source_target_pairs={{0,16},{16,32},{32,48},{48,64},{64,80},{80,96},{96,112},{112,128},... | collective-permute-start | bytes 1228808 | tf_op jit(solution)/shard_map/ppermute | solution.py:472
  12.1 6.8 %collective-permute-start.3 = (f32[4,72,128]{2,1,0:T(8,128)S(1)}, f32[4,72,128]{2,1,0:T(8,128)S(1)}, u32[]{:S(2)}, u32[]{:S(2)}) collective-permute-start(f32[4,72,128]{2,1,0:T(8,128)S(1)} %fusion), channel_id=1, source_target_pairs={{32,0},{48,16},{64,32},{80,48},{96,64},{112,80},{128,96},{144,112}... | collective-permute-start | bytes 442376 | tf_op jit(solution)/shard_map/ppermute | solution.py:473
  13.4 6.3 %collective-permute-start.2 = (f32[4,72,128]{2,1,0:T(8,128)S(1)}, f32[4,72,128]{2,1,0:T(8,128)S(1)}, u32[]{:S(2)}, u32[]{:S(2)}) collective-permute-start(f32[4,72,128]{2,1,0:T(8,128)S(1)} %fusion), channel_id=1, source_target_pairs={{0,32},{16,48},{32,64},{48,80},{64,96},{80,112},{96,128},{112,144}... | collective-permute-start | bytes 442376 | tf_op jit(solution)/shard_map/ppermute | solution.py:472
  19.9 7.9 %collective-permute-start.4 = (f32[85,8,128]{2,1,0:T(8,128)S(1)}, f32[85,8,128]{2,1,0:T(8,128)S(1)}, u32[]{:S(2)}, u32[]{:S(2)}) collective-permute-start(f32[85,8,128]{2,1,0:T(8,128)S(1)} %get-tuple-element.13), channel_id=1, source_target_pairs={{0,1},{1,2},{2,3},{3,4},{4,5},{5,6},{6,7},{7,8},{8,9},{9,10},{10,1... | collective-permute-start | bytes 1044488 | tf_op jit(solution)/shard_map/ppermute | solution.py:472
  21.2 9.8 %collective-permute-start.5 = (f32[85,8,128]{2,1,0:T(8,128)S(1)}, f32[85,8,128]{2,1,0:T(8,128)S(1)}, u32[]{:S(2)}, u32[]{:S(2)}) collective-permute-start(f32[85,8,128]{2,1,0:T(8,128)S(1)} %get-tuple-element.14), channel_id=1, source_target_pairs={{1,0},{2,1},{3,2},{4,3},{5,4},{6,5},{7,6},{8,7},{9,8},{10,9},{11,1... | collective-permute-start | bytes 1044488 | tf_op jit(solution)/shard_map/ppermute | solution.py:473
  22.5 14.9 %collective-permute-start.6 = (f32[70,8,128]{2,1,0:T(8,128)S(1)}, f32[70,8,128]{2,1,0:T(8,128)S(1)}, u32[]{:S(2)}, u32[]{:S(2)}) collective-permute-start(f32[70,8,128]{2,1,0:T(8,128)S(1)} %get-tuple-element.16), channel_id=1, source_target_pairs={{0,1},{1,2},{2,3},{3,4},{4,5},{5,6},{6,7},{7,8},{8,9},{9,10},{10,1... | collective-permute-start | bytes 860168 | tf_op jit(solution)/shard_map/ppermute | solution.py:472
  26.5 10.9 %collective-permute-start.7 = (f32[70,8,128]{2,1,0:T(8,128)S(1)}, f32[70,8,128]{2,1,0:T(8,128)S(1)}, u32[]{:S(2)}, u32[]{:S(2)}) collective-permute-start(f32[70,8,128]{2,1,0:T(8,128)S(1)} %get-tuple-element.17), channel_id=1, source_target_pairs={{1,0},{2,1},{3,2},{4,3},{5,4},{6,5},{7,6},{8,7},{9,8},{10,9},{11,1... | collective-permute-start | bytes 860168 | tf_op jit(solution)/shard_map/ppermute | solution.py:473

commit v7 on v5

--- a/solution.py
+++ b/solution.py
@@ -18,93 +18,112 @@
 VMEM = pl.BlockSpec(memory_space=pltpu.VMEM)
 
 
-def widths(halo):
-    return [LX + 2 * (halo - d) for d in range(1, halo + 1)]
-
-
-def rim_spots(halo):
-    spots, place = [], 0
-    for d, width in zip(range(1, halo + 1), widths(halo)):
-        for i in range(width):
-            spots.append((d, d + i, place))
-            place += 1
-    return spots
-
-
-def plane_of(parts, index):
-    ref, first = parts[index // LX]
-    return ref, index % LX, first
-
-
-def shifted(parts, rows):
-    return [(ref, first + rows) for ref, first in parts]
-
-
-def fill_rim(parts, halo, up, down, start):
-    for d, plane, place in rim_spots(halo):
-        ref, x, first = plane_of(parts, plane)
-        up[start + place] = ref[x, pl.ds(first + (LY - d) * 8, 8), :]
-        down[start + place] = ref[x, pl.ds(first + (d - 1) * 8, 8), :]
-
-
-def fill_flat_rim(parts, halo, up, down, start):
-    for d, plane, place in rim_spots(halo):
-        ref, x, first = plane_of(parts, plane)
-        tile, row = start + place // 8, place % 8
-        up[tile, pl.ds(row, 1), :] = ref[x, pl.ds(first + LY - d, 1), :]
-        down[tile, pl.ds(row, 1), :] = ref[x, pl.ds(first + d - 1, 1), :]
-
-
 BLOCK = LY * 8
-OLD_RIM = sum(widths(NEAR))
-FAR_RIM = sum(widths(FAR))
-
-
-def recent_parts(far_low, low, own, high, far_high):
-    return [(far_low, 0), (low, 2 * BLOCK), (own, 2 * BLOCK), (high, 2 * BLOCK), (far_high, 0)]
-
-
-def rim_kernel(own, low, high, far_low, far_high, up, down, old_up, old_down):
-    parts = [(low, 0), (own, 0), (high, 0)]
-    wide = recent_parts(far_low, low, own, high, far_high)
-    for group in range(2):
-        fill_rim(shifted(parts, group * BLOCK), NEAR, old_up, old_down, group * OLD_RIM)
-    fill_flat_rim(shifted(wide, BLOCK), FAR, old_up, old_down, 2 * OLD_RIM)
-    fill_rim(wide, FAR, up, down, 0)
-
-
-def pack_rims(*args):
-    sizes = [FAR_RIM] * 2 + [2 * OLD_RIM + FAR_RIM // 8] * 2
-    shapes = tuple(jax.ShapeDtypeStruct((size, 8, NZ), F32) for size in sizes)
+HALF = NEAR * 8
+
+
+def spans(halo, begin, end):
+    found, place = [], 0
+    for d in range(begin + 1, end + 1):
+        found.append((d, halo - d, place))
+        place += LY + 2 * (halo - d)
+    return found, place
+
+
+OLD_SPANS, OLD_SIZE = spans(NEAR, 0, LX)
+SIDE_SPANS, SIDE_SIZE = spans(FAR, 0, LX)
+FAR_SPANS, FAR_SIZE = spans(FAR, LX, 2 * LX)
+SIDE_TILES = 2 * OLD_SIZE + SIDE_SIZE + -(-SIDE_SIZE // 8)
+FAR_TILES = FAR_SIZE + -(-FAR_SIZE // 8)
+
+
+def pack_columns(out, start, found, to_higher, rows, reach):
+    (below, low_row), (own, own_row), (above, high_row) = rows
+    for d, more, place in found:
+        x = LX - 1 - (d - 1) % LX if to_higher else (d - 1) % LX
+        spot = start + place
+        size = more * 8
+        if more:
+            out[pl.ds(spot, more)] = below[x, pl.ds(low_row + reach * 8 - size, size), :].reshape(more, 8, NZ)
+            out[pl.ds(spot + more + LY, more)] = above[x, pl.ds(high_row, size), :].reshape(more, 8, NZ)
+        out[pl.ds(spot + more, LY)] = own[x, pl.ds(own_row, BLOCK), :].reshape(LY, 8, NZ)
+
+
+def pack_coefficient(out, start, found, to_higher, below, own, above):
+    for d, more, place in found:
+        x = LX - 1 - (d - 1) % LX if to_higher else (d - 1) % LX
+        for y in range(-more, LY + more):
+            if y < 0:
+                ref, row = below, 2 * HALF + BLOCK + LY + y
+            elif y < LY:
+                ref, row = own, 3 * BLOCK + y
+            else:
+                ref, row = above, 2 * HALF + BLOCK + y - LY
+            spot = place + more + y
+            out[start + spot // 8, pl.ds(spot % 8, 1), :] = ref[x, pl.ds(row, 1), :]
+
+
+def column_kernel(own, below, above, *outs):
+    for out, to_higher, found, size in (
+        (outs[0], True, SIDE_SPANS, SIDE_SIZE),
+        (outs[1], False, SIDE_SPANS, SIDE_SIZE),
+        (outs[2], True, FAR_SPANS, FAR_SIZE),
+        (outs[3], False, FAR_SPANS, FAR_SIZE),
+    ):
+        start = 0
+        if found is SIDE_SPANS:
+            for group in range(2):
+                rows = [(below, group * HALF), (own, group * BLOCK), (above, group * HALF)]
+                pack_columns(out, start, OLD_SPANS, to_higher, rows, NEAR)
+                start += OLD_SIZE
+        rows = [(below, 2 * HALF), (own, 2 * BLOCK), (above, 2 * HALF)]
+        pack_columns(out, start, found, to_higher, rows, FAR)
+        if size % 8:
+            out[out.shape[0] - 1] = jnp.zeros((8, NZ), F32)
+        pack_coefficient(out, start + size, found, to_higher, below, own, above)
+
+
+def pack_all(*args):
+    shapes = tuple(jax.ShapeDtypeStruct((size, 8, NZ), F32) for size in [SIDE_TILES] * 2 + [FAR_TILES] * 2)
     return pl.pallas_call(
-        rim_kernel,
+        column_kernel,
         out_shape=shapes,
-        in_specs=[VMEM] * 5,
+        in_specs=[VMEM] * 3,
         out_specs=(VMEM,) * 4,
         compiler_params=pltpu.CompilerParams(vmem_limit_bytes=1 << 20),
-        name="pack_rims",
+        name="pack_all",
     )(*args)
 
 
-def fill_block(parts, halo, from_low, from_high, start, wide):
+def fill_block(wide, halo, rows, reach, sides):
+    (below, low_row), (own, own_row), (above, high_row) = rows
     wide[...] = jnp.zeros(wide.shape, F32)
-    for index in range(LX + 2 * halo):
-        ref, x, first = plane_of(parts, index)
-        wide[index, halo:halo + LY] = ref[x, pl.ds(first, BLOCK), :].reshape(LY, 8, NZ)
-    for d, plane, place in rim_spots(halo):
-        wide[plane, halo - d] = from_low[start + place]
-        wide[plane, halo + LY - 1 + d] = from_high[start + place]
-
-
-def fill_flat(parts, halo, from_low, from_high, start, wide):
+    for x in range(LX):
+        size = halo * 8
+        wide[halo + x, 0:halo] = below[x, pl.ds(low_row + reach * 8 - size, size), :].reshape(halo, 8, NZ)
+        wide[halo + x, halo:halo + LY] = own[x, pl.ds(own_row, BLOCK), :].reshape(LY, 8, NZ)
+        wide[halo + x, halo + LY:] = above[x, pl.ds(high_row, size), :].reshape(halo, 8, NZ)
+    for low, high, start, found in sides:
+        for d, more, place in found:
+            count = LY + 2 * more
+            begin = halo - more
+            wide[halo - d, begin:begin + count] = low[pl.ds(start + place, count)]
+            wide[halo + LX - 1 + d, begin:begin + count] = high[pl.ds(start + place, count)]
+
+
+def fill_flat(wide, below, own, above, sides):
     wide[...] = jnp.zeros(wide.shape, F32)
-    for index in range(LX + 2 * halo):
-        ref, x, first = plane_of(parts, index)
-        wide[index, halo:halo + LY] = ref[x, pl.ds(first, LY), :]
-    for d, plane, place in rim_spots(halo):
-        tile, row = start + place // 8, place % 8
-        wide[plane, pl.ds(halo - d, 1), :] = from_low[tile, pl.ds(row, 1), :]
-        wide[plane, pl.ds(halo + LY - 1 + d, 1), :] = from_high[tile, pl.ds(row, 1), :]
+    for x in range(LX):
+        wide[FAR + x, 0:FAR] = below[x, pl.ds(2 * HALF + BLOCK, LY), :]
+        wide[FAR + x, FAR:FAR + LY] = own[x, pl.ds(3 * BLOCK, LY), :]
+        wide[FAR + x, FAR + LY:] = above[x, pl.ds(2 * HALF + BLOCK, LY), :]
+    for low, high, start, found in sides:
+        for d, more, place in found:
+            for i in range(LY + 2 * more):
+                tile, row = start + (place + i) // 8, (place + i) % 8
+                y = FAR - more + i
+                wide[FAR - d, pl.ds(y, 1), :] = low[tile, pl.ds(row, 1), :]
+                wide[FAR + LX - 1 + d, pl.ds(y, 1), :] = high[tile, pl.ds(row, 1), :]
 
 
 def fill_tables(coef, skip, table_re, table_im, diag_re, diag_im):
@@ -198,14 +217,17 @@
     return [pltpu.VMEM((*wide_shape(halo), 8, NZ), F32)] * 5 + [FLAT] * 2
 
 
-def old_kernel(own, low, high, far_low, far_high, from_low, from_high, out, coef, block, first, second,
-               table_re, table_im, diag_re, diag_im):
-    wide = recent_parts(far_low, low, own, high, far_high)
-    fill_flat(shifted(wide, BLOCK), FAR, from_low, from_high, 2 * OLD_RIM, coef)
+def side_coefficient(low, high):
+    return (low, high, 2 * OLD_SIZE + SIDE_SIZE, SIDE_SPANS)
+
+
+def old_kernel(own, below, above, low, high, out, block, first, second,
+               table_re, table_im, diag_re, diag_im, coef):
+    fill_flat(coef, below, own, above, [side_coefficient(low, high)])
     fill_tables(coef, FAR - NEAR, table_re, table_im, diag_re, diag_im)
     for group in range(2):
-        parts = [(low, group * BLOCK), (own, group * BLOCK), (high, group * BLOCK)]
-        fill_block(parts, NEAR, from_low, from_high, group * OLD_RIM, block)
+        rows = [(below, group * HALF), (own, group * BLOCK), (above, group * HALF)]
+        fill_block(block, NEAR, rows, NEAR, [(low, high, group * OLD_SIZE, OLD_SPANS)])
 
         def store(x, y, value, group=group):
             out[x, pl.ds(group * BLOCK + y * 8, 8), :] = value
@@ -216,21 +238,24 @@
 def old_images(*args):
     return pl.pallas_call(
         old_kernel,
-        out_shape=(jax.ShapeDtypeStruct((LX, 2 * BLOCK, NZ), F32),
-                   jax.ShapeDtypeStruct((*wide_shape(FAR), NZ), F32)),
-        in_specs=[VMEM] * 7,
-        out_specs=(VMEM, VMEM),
-        scratch_shapes=smooth_scratch(NEAR),
+        out_shape=jax.ShapeDtypeStruct((LX, 2 * BLOCK, NZ), F32),
+        in_specs=[VMEM] * 5,
+        out_specs=VMEM,
+        scratch_shapes=smooth_scratch(NEAR) + [FLAT],
         compiler_params=pltpu.CompilerParams(vmem_limit_bytes=16 << 20),
         cost_estimate=pl.CostEstimate(flops=12_000_000, bytes_accessed=24_000_000, transcendentals=0),
         name="old_images",
     )(*args)
 
 
-def first_kernel(own, low, high, far_low, far_high, from_low, from_high, coef, out, block, first, second,
+def first_kernel(own, below, above, low, high, far_low, far_high, after, out, coef, block, first, second,
                  table_re, table_im, diag_re, diag_im):
+    del after
+    fill_flat(coef, below, own, above, [side_coefficient(low, high), (far_low, far_high, FAR_SIZE, FAR_SPANS)])
     fill_tables(coef, 0, table_re, table_im, diag_re, diag_im)
-    fill_block(recent_parts(far_low, low, own, high, far_high), FAR, from_low, from_high, 0, block)
+    rows = [(below, 2 * HALF), (own, 2 * BLOCK), (above, 2 * HALF)]
+    fill_block(block, FAR, rows, FAR,
+               [(low, high, 2 * OLD_SIZE, SIDE_SPANS), (far_low, far_high, 0, FAR_SPANS)])
 
     def store(x, y, value):
         out[x, y] = value
@@ -241,9 +266,10 @@
 def first_image(*args):
     return pl.pallas_call(
         first_kernel,
-        out_shape=jax.ShapeDtypeStruct((*wide_shape(NEAR), 8, NZ), F32),
-        in_specs=[VMEM] * 8,
-        out_specs=VMEM,
+        out_shape=(jax.ShapeDtypeStruct((*wide_shape(NEAR), 8, NZ), F32),
+                   jax.ShapeDtypeStruct((*wide_shape(FAR), NZ), F32)),
+        in_specs=[VMEM] * 7 + [pl.BlockSpec(memory_space=pl.ANY)],
+        out_specs=(VMEM, VMEM),
         scratch_shapes=smooth_scratch(FAR),
         compiler_params=pltpu.CompilerParams(vmem_limit_bytes=24 << 20),
         name="first_image",
@@ -468,13 +494,14 @@
     cells = coefficient.size * nx * ny
     by_cell = prior.transpose(3, 0, 4, 1, 2, 5).reshape(LX, 3 * LY * 8, NZ)
     start = jnp.concatenate([by_cell, coefficient], axis=1)
-    far = start[:, 2 * BLOCK:]
-    sides = from_both(GX, nx, start, start) + from_both(GX, nx, far, far, 2)
-    up, down, old_up, old_down = pack_rims(start, *sides)
-    old_rims = from_both("gy", ny, old_up, old_down)
+    up = jnp.concatenate([start[:, HALF:BLOCK], start[:, BLOCK + HALF:]], axis=1)
+    down = jnp.concatenate([start[:, :HALF], start[:, BLOCK:BLOCK + HALF], start[:, 2 * BLOCK:]], axis=1)
     rims = from_both("gy", ny, up, down)
-    old_image, coef = old_images(start, *sides, *old_rims)
-    w = first_image(start, *sides, *rims, coef)
+    right, left, far_right, far_left = pack_all(start, *rims)
+    sides = from_both(GX, nx, right, left)
+    far_sides = from_both(GX, nx, far_right, far_left, 2)
+    old_image = old_images(start, *rims, *sides)
+    w, coef = first_image(start, *rims, *sides, *far_sides, old_image)
 
     w_image, spread = image_and_gram(2 * ny, w, coef, start, old_image)
     got = lax.all_to_all(spread, ("core", "gy"), 0, 0)

time: 107 us -> 102 us (0.953)
  starting transfers between devices: 23.9 us -> 19.2 us
  blocking collectives: 44.9 us -> 41.9 us
  waiting for transfers between devices: 11.7 us -> 13.9 us
    ppermute x4 -> x3, starting transfers between devices: 12.7 us -> 4.5 us  [from_both(): lax.ppermute(to_lower, axis, [(i + step, i) for i in range(count - step)])]
    ppermute x4 -> x3, waiting for transfers between devices: 5.34 us -> 9.06 us  [from_both(): lax.ppermute(to_lower, axis, [(i + step, i) for i in range(count - step)])]
    ppermute x4 -> x3, starting transfers between devices: 11.2 us -> 14.7 us  [from_both(): lax.ppermute(to_higher, axis, [(i, i + step) for i in range(count - step)])]
    all_to_all x1, blocking collectives: 17.3 us -> 15.7 us  [per_device(): got = lax.all_to_all(spread, ('core', 'gy'), 0, 0)]
    ppermute x4 -> x3, waiting for transfers between devices: 6.39 us -> 4.82 us  [from_both(): lax.ppermute(to_higher, axis, [(i, i + step) for i in range(count - step)])]
    all_to_all x1, blocking collectives: 27.6 us -> 26.1 us  [per_device(): got = lax.all_to_all(sum_and_spread(got, nz), 'z', 0, 0)]
  transfers between devices with their start and end apart: 8 -> 6, of which waited for: 4 -> 4; matrix products, arithmetic and copies ran while one was open for 0% -> 0% of each run, Pallas kernels for 6% -> 6%
where the time goes in v7:
time: 102 us; the launch traced here: 101 us
  blocking collectives  41.9 us (41%)
  Pallas kernels  24.3 us (24%)
  starting transfers between devices  19.2 us (19%)
  waiting for transfers between devices  13.9 us (14%)
  local copies, waits for them, and re-layouts  1.96 us (2%)
    all_to_all x1, blocking collectives, per_device(): got = lax.all_to_all(sum_and_spread(got, nz), 'z', 0, 0)  26.1 us
    all_to_all x1, blocking collectives, per_device(): got = lax.all_to_all(spread, ('core', 'gy'), 0, 0)  15.7 us
    ppermute x3, starting transfers between devices, from_both(): lax.ppermute(to_higher, axis, [(i, i + step) for i in range(count - step)])  14.7 us
    ppermute x3, waiting for transfers between devices, from_both(): lax.ppermute(to_lower, axis, [(i + step, i) for i in range(count - step)])  9.06 us
    pallas_call x1, Pallas kernels, first_image(): pl.pallas_call(first_kernel, out_shape=(jax.ShapeDtypeStruct((*wide_shape...  7.79 us
    pallas_call x1, Pallas kernels, old_images(): pl.pallas_call(old_kernel, out_shape=jax.ShapeDtypeStruct((LX, 2 * BLOCK,...  6.2 us
    pallas_call x1, Pallas kernels, finish(): pl.pallas_call(functools.partial(final_kernel, cells), out_shape=jax.Shap...  5.54 us
    ppermute x3, waiting for transfers between devices, from_both(): lax.ppermute(to_higher, axis, [(i, i + step) for i in range(count - step)])  4.82 us
  transfers between devices with their start and end apart: 6, of which 4 were waited for; matrix products, arithmetic and copies ran while one was open for 0% of the time, Pallas kernels for 6%

profile of v7, /device:TPU:1, one launch (start us, length us, event | category | flops | bytes accessed | tf_op | source)
XLA Modules:
  0.0 101.5 jit_solution(3036353657763973414)
XLA Ops:
  0.0 1.3 %copy.3 = f32[4,3,8,2,4,128]{5,4,3,2,1,0:T(4,128)S(1)} copy(f32[4,3,8,2,4,128]{5,2,0,4,3,1:T(8,128)} %bitcast.7) | data formatting | bytes 786432 | tf_op jit(solution)/shard_map/transpose | solution.py:495
  1.3 0.0 copy-start
  1.3 0.7 copy-done
  2.0 4.0 %collective-permute-start = (f32[4,136,128]{2,1,0:T(8,128)S(1)}, f32[4,136,128]{2,1,0:T(8,128)S(1)}, u32[]{:S(2)}, u32[]{:S(2)}) collective-permute-start(f32[4,136,128]{2,1,0:T(8,128)S(1)} %pad_maximum_fusion.1), channel_id=1, source_target_pairs={{0,1},{1,2},{2,3},{3,4},{4,5},{5,6},{6,7},{7,8},{8,9},{9,10},{10,1... | collective-permute-start | bytes 835592 | tf_op jit(solution)/shard_map/ppermute | solution.py:488
  6.1 1.3 %collective-permute-start.1 = (f32[4,136,128]{2,1,0:T(8,128)S(1)}, f32[4,136,128]{2,1,0:T(8,128)S(1)}, u32[]{:S(2)}, u32[]{:S(2)}) collective-permute-start(f32[4,136,128]{2,1,0:T(8,128)S(1)} %pad_maximum_fusion.2), channel_id=1, source_target_pairs={{1,0},{2,1},{3,2},{4,3},{5,4},{6,5},{7,6},{8,7},{9,8},{10,9},{11,1... | collective-permute-start | bytes 835592 | tf_op jit(solution)/shard_map/ppermute | solution.py:489
  7.5 2.1 %collective-permute-done.below = f32[4,136,128]{2,1,0:T(8,128)S(1)} collective-permute-done((f32[4,136,128]{2,1,0:T(8,128)S(1)}, f32[4,136,128]{2,1,0:T(8,128)S(1)}, u32[]{:S(2)}, u32[]{:S(2)}) %collective-permute-start) | collective-permute-done | bytes 278560 | tf_op jit(solution)/shard_map/ppermute | solution.py:488
  9.5 3.9 %collective-permute-done.1.above = f32[4,136,128]{2,1,0:T(8,128)S(1)} collective-permute-done((f32[4,136,128]{2,1,0:T(8,128)S(1)}, f32[4,136,128]{2,1,0:T(8,128)S(1)}, u32[]{:S(2)}, u32[]{:S(2)}) %collective-permute-start.1) | collective-permute-done | bytes 278560 | tf_op jit(solution)/shard_map/ppermute | solution.py:489
  13.4 0.2 pack_all.1
  13.6 7.1 %collective-permute-start.2 = (f32[174,8,128]{2,1,0:T(8,128)S(1)}, f32[174,8,128]{2,1,0:T(8,128)S(1)}, u32[]{:S(2)}, u32[]{:S(2)}) collective-permute-start(f32[174,8,128]{2,1,0:T(8,128)S(1)} %get-tuple-element.13), channel_id=1, source_target_pairs={{0,16},{16,32},{32,48},{48,64},{64,80},{80,96},{96,112},{112,128},... | collective-permute-start | bytes 2138120 | tf_op jit(solution)/shard_map/ppermute | solution.py:488
  20.7 1.9 %collective-permute-start.3 = (f32[174,8,128]{2,1,0:T(8,128)S(1)}, f32[174,8,128]{2,1,0:T(8,128)S(1)}, u32[]{:S(2)}, u32[]{:S(2)}) collective-permute-start(f32[174,8,128]{2,1,0:T(8,128)S(1)} %get-tuple-element.14), channel_id=1, source_target_pairs={{16,0},{32,16},{48,32},{64,48},{80,64},{96,80},{112,96},{128,112},... | collective-permute-start | bytes 2138120 | tf_op jit(solution)/shard_map/ppermute | solution.py:489
  22.6 3.6 %collective-permute-start.4 = (f32[50,8,128]{2,1,0:T(8,128)S(1)}, f32[50,8,128]{2,1,0:T(8,128)S(1)}, u32[]{:S(2)}, u32[]{:S(2)}) collective-permute-start(f32[50,8,128]{2,1,0:T(8,128)S(1)} %get-tuple-element.15), channel_id=1, source_target_pairs={{0,32},{16,48},{32,64},{48,80},{64,96},{80,112},{96,128},{112,144}... | collective-permute-start | bytes 614408 | tf_op jit(solution)/shard_map/ppermute | solution.py:488
  26.2 1.3 %collective-permute-start.5 = (f32[50,8,128]{2,1,0:T(8,128)S(1)}, f32[50,8,128]{2,1,0:T(8,128)S(1)}, u32[]{:S(2)}, u32[]{:S(2)}) collective-permute-start(f32[50,8,128]{2,1,0:T(8,128)S(1)} %get-tuple-element.16), channel_id=1, source_target_pairs={{32,0},{48,16},{64,32},{80,48},{96,64},{112,80},{128,96},{144,112}... | collective-permute-start | bytes 614408 | tf_op jit(solution)/shard_map/ppermute | solution.py:489
  27.5 2.7 %collective-permute-done.2.low = f32[174,8,128]{2,1,0:T(8,128)S(1)} collective-permute-done((f32[174,8,128]{2,1,0:T(8,128)S(1)}, f32[174,8,128]{2,1,0:T(8,128)S(1)}, u32[]{:S(2)}, u32[]{:S(2)}) %collective-permute-start.2) | collective-permute-done | bytes 712736 | tf_op jit(solution)/shard_map/ppermute | solution.py:488
  30.2 5.2 %collective-permute-done.3.high = f32[174,8,128]{2,1,0:T(8,128)S(1)} collective-permute-done((f32[174,8,128]{2,1,0:T(8,128)S(1)}, f32[174,8,128]{2,1,0:T(8,128)S(1)}, u32[]{:S(2)}, u32[]{:S(2)}) %collective-permute-start.3) | collective-permute-done | bytes 712736 | tf_op jit(solution)/shard_map/ppermute | solution.py:489
  35.4 6.2 %old_images.1.after.old_image = f32[4,128,128]{2,1,0:T(8,128)S(1)} custom-call(f32[4,200,128]{2,1,0:T(8,128)S(1)} %pad_maximum_fusion.own.start, f32[4,136,128]{2,1,0:T(8,128)S(1)} %collective-permute-done.below, f32[4,136,128]{2,1,0:T(8,128)S(1)} %collective-permute-done.1.above, f32[174,8,128]{2,1,0:T(8,128)S(1)} %collective-permute-done.2.low, ...), custom_call_target="tpu_custom_call" | custom-call | flops 12000000 | bytes 24000000 | tf_op jit(solution)/shard_map/old_images/pallas_call | solution.py:239
  41.6 0.0 collective-permute-done.4.far_low
  41.6 0.0 collective-permute-done.5.far_high
  41.6 7.8 %first_image.1 = (f32[12,16,8,128]{3,2,1,0:T(8,128)S(1)}, f32[20,24,128]{2,1,0:T(8,128)S(1)}) custom-call(f32[4,200,128]{2,1,0:T(8,128)S(1)} %pad_maximum_fusion.own.start, f32[4,136,128]{2,1,0:T(8,128)S(1)} %collective-permute-done.below, f32[4,136,128]{2,1,0:T(8,128)S(1)} %collective-permute-done.1.above, f32[174,8,128]{2,1,0:T(8,128)S(1)} %collective-permute-done.2.low, ...), custom_call_target="tpu_custom_call" | custom-call | tf_op jit(solution)/shard_map/first_image/pallas_call | solution.py:267
  49.4 4.6 %image_and_gram.1 = (f32[4,64,128]{2,1,0:T(8,128)S(1)}, f32[32,8,128]{2,1,0:T(8,128)S(1)}) custom-call(f32[12,16,8,128]{3,2,1,0:T(8,128)S(1)} %get-tuple-element.17.w, f32[20,24,128]{2,1,0:T(8,128)S(1)} %get-tuple-element.18.coef, f32[4,200,128]{2,1,0:T(8,128)S(1)} %pad_maximum_fusion.own.start, f32[4,128,128]{2,1,0:T(8,128)S(1)} %old_images.1.after.old_image), custom_call_target="tpu_custom_call" | custom-call | tf_op jit(solution)/shard_map/image_and_gram/pallas_call | solution.py:367
  54.0 15.7 %all_to_all.10.parts = f32[32,8,128]{2,1,0:T(8,128)S(1)} all-to-all(f32[32,8,128]{2,1,0:T(8,128)S(1)} %get-tuple-element.19), channel_id=1, replica_groups=mesh['z'=16,'core'=2,'gy'=16] {'core','gy'}, dimensions={0} | all-to-all | bytes 262144 | tf_op jit(solution)/shard_map/all_to_all | solution.py:507
  69.8 26.1 %all_to_all.11.parts = f32[16,8,128]{2,1,0:T(8,128)S(1)} all-to-all(f32[16,8,128]{2,1,0:T(8,128)S(1)} %sum_and_spread.1), channel_id=1, replica_groups=mesh['z'=16,'core'=2,'gy'=16] {'z'}, dimensions={0} | all-to-all | bytes 131072 | tf_op jit(solution)/shard_map/all_to_all | solution.py:508
  95.9 5.5 %finish.1 = f32[2,8,4,8,128]{4,3,2,1,0:T(8,128)} custom-call(f32[16,8,128]{2,1,0:T(8,128)S(1)} %all_to_all.11.parts, f32[4,200,128]{2,1,0:T(8,128)S(1)} %pad_maximum_fusion.own.start, f32[12,16,8,128]{3,2,1,0:T(8,128)S(1)} %get-tuple-element.17.w, f32[4,128,128]{2,1,0:T(8,128)S(1)} %old_images.1.after.old_image, f32[4,64,128]{2,1,0:T(8,128)S(1)} %get-tuple-element.20.w_image), custom_call_target="tpu_custom_call" | custom-call | tf_op jit(solution)/shard_map/finish/pallas_call | solution.py:473
  (7 shorter events, 0.2 us)
Async XLA Ops:
  1.3 0.7 copy-start
  2.0 7.5 %collective-permute-start = (f32[4,136,128]{2,1,0:T(8,128)S(1)}, f32[4,136,128]{2,1,0:T(8,128)S(1)}, u32[]{:S(2)}, u32[]{:S(2)}) collective-permute-start(f32[4,136,128]{2,1,0:T(8,128)S(1)} %pad_maximum_fusion.1), channel_id=1, source_target_pairs={{0,1},{1,2},{2,3},{3,4},{4,5},{5,6},{6,7},{7,8},{8,9},{9,10},{10,1... | collective-permute-start | bytes 835592 | tf_op jit(solution)/shard_map/ppermute | solution.py:488
  6.1 7.3 %collective-permute-start.1 = (f32[4,136,128]{2,1,0:T(8,128)S(1)}, f32[4,136,128]{2,1,0:T(8,128)S(1)}, u32[]{:S(2)}, u32[]{:S(2)}) collective-permute-start(f32[4,136,128]{2,1,0:T(8,128)S(1)} %pad_maximum_fusion.2), channel_id=1, source_target_pairs={{1,0},{2,1},{3,2},{4,3},{5,4},{6,5},{7,6},{8,7},{9,8},{10,9},{11,1... | collective-permute-start | bytes 835592 | tf_op jit(solution)/shard_map/ppermute | solution.py:489
  13.6 16.7 %collective-permute-start.2 = (f32[174,8,128]{2,1,0:T(8,128)S(1)}, f32[174,8,128]{2,1,0:T(8,128)S(1)}, u32[]{:S(2)}, u32[]{:S(2)}) collective-permute-start(f32[174,8,128]{2,1,0:T(8,128)S(1)} %get-tuple-element.13), channel_id=1, source_target_pairs={{0,16},{16,32},{32,48},{48,64},{64,80},{80,96},{96,112},{112,128},... | collective-permute-start | bytes 2138120 | tf_op jit(solution)/shard_map/ppermute | solution.py:488
  20.7 14.7 %collective-permute-start.3 = (f32[174,8,128]{2,1,0:T(8,128)S(1)}, f32[174,8,128]{2,1,0:T(8,128)S(1)}, u32[]{:S(2)}, u32[]{:S(2)}) collective-permute-start(f32[174,8,128]{2,1,0:T(8,128)S(1)} %get-tuple-element.14), channel_id=1, source_target_pairs={{16,0},{32,16},{48,32},{64,48},{80,64},{96,80},{112,96},{128,112},... | collective-permute-start | bytes 2138120 | tf_op jit(solution)/shard_map/ppermute | solution.py:489
  22.6 19.0 %collective-permute-start.4 = (f32[50,8,128]{2,1,0:T(8,128)S(1)}, f32[50,8,128]{2,1,0:T(8,128)S(1)}, u32[]{:S(2)}, u32[]{:S(2)}) collective-permute-start(f32[50,8,128]{2,1,0:T(8,128)S(1)} %get-tuple-element.15), channel_id=1, source_target_pairs={{0,32},{16,48},{32,64},{48,80},{64,96},{80,112},{96,128},{112,144}... | collective-permute-start | bytes 614408 | tf_op jit(solution)/shard_map/ppermute | solution.py:488
  26.2 15.4 %collective-permute-start.5 = (f32[50,8,128]{2,1,0:T(8,128)S(1)}, f32[50,8,128]{2,1,0:T(8,128)S(1)}, u32[]{:S(2)}, u32[]{:S(2)}) collective-permute-start(f32[50,8,128]{2,1,0:T(8,128)S(1)} %get-tuple-element.16), channel_id=1, source_target_pairs={{32,0},{48,16},{64,32},{80,48},{96,64},{112,80},{128,96},{144,112}... | collective-permute-start | bytes 614408 | tf_op jit(solution)/shard_map/ppermute | solution.py:489

commit v8 on v7

--- a/solution.py
+++ b/solution.py
@@ -30,11 +30,12 @@
     return found, place
 
 
-OLD_SPANS, OLD_SIZE = spans(NEAR, 0, LX)
+NEAR_SPANS, NEAR_SIZE = spans(NEAR, 0, LX)
 SIDE_SPANS, SIDE_SIZE = spans(FAR, 0, LX)
-FAR_SPANS, FAR_SIZE = spans(FAR, LX, 2 * LX)
-SIDE_TILES = 2 * OLD_SIZE + SIDE_SIZE + -(-SIDE_SIZE // 8)
-FAR_TILES = FAR_SIZE + -(-FAR_SIZE // 8)
+FLAT_TILES = -(-SIDE_SIZE // 8)
+SPLIT = NEAR_SPANS[-1][2]
+FIRST_TILES = SIDE_SIZE + FLAT_TILES + NEAR_SIZE - SPLIT
+SECOND_TILES = SPLIT + NEAR_SIZE
 
 
 def pack_columns(out, start, found, to_higher, rows, reach):
@@ -63,28 +64,22 @@
             out[start + spot // 8, pl.ds(spot % 8, 1), :] = ref[x, pl.ds(row, 1), :]
 
 
-def column_kernel(own, below, above, *outs):
-    for out, to_higher, found, size in (
-        (outs[0], True, SIDE_SPANS, SIDE_SIZE),
-        (outs[1], False, SIDE_SPANS, SIDE_SIZE),
-        (outs[2], True, FAR_SPANS, FAR_SIZE),
-        (outs[3], False, FAR_SPANS, FAR_SIZE),
-    ):
-        start = 0
-        if found is SIDE_SPANS:
-            for group in range(2):
-                rows = [(below, group * HALF), (own, group * BLOCK), (above, group * HALF)]
-                pack_columns(out, start, OLD_SPANS, to_higher, rows, NEAR)
-                start += OLD_SIZE
+def column_kernel(own, below, above, right, left, old_right, old_left):
+    for first, second, to_higher in ((right, old_right, True), (left, old_left, False)):
         rows = [(below, 2 * HALF), (own, 2 * BLOCK), (above, 2 * HALF)]
-        pack_columns(out, start, found, to_higher, rows, FAR)
-        if size % 8:
-            out[out.shape[0] - 1] = jnp.zeros((8, NZ), F32)
-        pack_coefficient(out, start + size, found, to_higher, below, own, above)
+        pack_columns(first, 0, SIDE_SPANS, to_higher, rows, FAR)
+        if SIDE_SIZE % 8:
+            first[SIDE_SIZE + FLAT_TILES - 1] = jnp.zeros((8, NZ), F32)
+        pack_coefficient(first, SIDE_SIZE, SIDE_SPANS, to_higher, below, own, above)
+        rows = [(below, 0), (own, 0), (above, 0)]
+        pack_columns(second, 0, NEAR_SPANS[:-1], to_higher, rows, NEAR)
+        pack_columns(first, SIDE_SIZE + FLAT_TILES - SPLIT, NEAR_SPANS[-1:], to_higher, rows, NEAR)
+        rows = [(below, HALF), (own, BLOCK), (above, HALF)]
+        pack_columns(second, SPLIT, NEAR_SPANS, to_higher, rows, NEAR)
 
 
 def pack_all(*args):
-    shapes = tuple(jax.ShapeDtypeStruct((size, 8, NZ), F32) for size in [SIDE_TILES] * 2 + [FAR_TILES] * 2)
+    shapes = tuple(jax.ShapeDtypeStruct((size, 8, NZ), F32) for size in [FIRST_TILES] * 2 + [SECOND_TILES] * 2)
     return pl.pallas_call(
         column_kernel,
         out_shape=shapes,
@@ -95,35 +90,38 @@
     )(*args)
 
 
+def fill_sides(wide, halo, sides):
+    for low, high, start, found in sides:
+        for d, more, place in found:
+            count = LY + 2 * more
+            begin = halo - more
+            wide[NEAR - d, begin:begin + count] = low[pl.ds(start + place, count)]
+            wide[NEAR + LX - 1 + d, begin:begin + count] = high[pl.ds(start + place, count)]
+
+
 def fill_block(wide, halo, rows, reach, sides):
     (below, low_row), (own, own_row), (above, high_row) = rows
     wide[...] = jnp.zeros(wide.shape, F32)
     for x in range(LX):
         size = halo * 8
-        wide[halo + x, 0:halo] = below[x, pl.ds(low_row + reach * 8 - size, size), :].reshape(halo, 8, NZ)
-        wide[halo + x, halo:halo + LY] = own[x, pl.ds(own_row, BLOCK), :].reshape(LY, 8, NZ)
-        wide[halo + x, halo + LY:] = above[x, pl.ds(high_row, size), :].reshape(halo, 8, NZ)
-    for low, high, start, found in sides:
-        for d, more, place in found:
-            count = LY + 2 * more
-            begin = halo - more
-            wide[halo - d, begin:begin + count] = low[pl.ds(start + place, count)]
-            wide[halo + LX - 1 + d, begin:begin + count] = high[pl.ds(start + place, count)]
-
-
-def fill_flat(wide, below, own, above, sides):
+        wide[NEAR + x, 0:halo] = below[x, pl.ds(low_row + reach * 8 - size, size), :].reshape(halo, 8, NZ)
+        wide[NEAR + x, halo:halo + LY] = own[x, pl.ds(own_row, BLOCK), :].reshape(LY, 8, NZ)
+        wide[NEAR + x, halo + LY:] = above[x, pl.ds(high_row, size), :].reshape(halo, 8, NZ)
+    fill_sides(wide, halo, sides)
+
+
+def fill_flat(wide, below, own, above, low, high):
     wide[...] = jnp.zeros(wide.shape, F32)
     for x in range(LX):
-        wide[FAR + x, 0:FAR] = below[x, pl.ds(2 * HALF + BLOCK, LY), :]
-        wide[FAR + x, FAR:FAR + LY] = own[x, pl.ds(3 * BLOCK, LY), :]
-        wide[FAR + x, FAR + LY:] = above[x, pl.ds(2 * HALF + BLOCK, LY), :]
-    for low, high, start, found in sides:
-        for d, more, place in found:
-            for i in range(LY + 2 * more):
-                tile, row = start + (place + i) // 8, (place + i) % 8
-                y = FAR - more + i
-                wide[FAR - d, pl.ds(y, 1), :] = low[tile, pl.ds(row, 1), :]
-                wide[FAR + LX - 1 + d, pl.ds(y, 1), :] = high[tile, pl.ds(row, 1), :]
+        wide[NEAR + x, 0:FAR] = below[x, pl.ds(2 * HALF + BLOCK, LY), :]
+        wide[NEAR + x, FAR:FAR + LY] = own[x, pl.ds(3 * BLOCK, LY), :]
+        wide[NEAR + x, FAR + LY:] = above[x, pl.ds(2 * HALF + BLOCK, LY), :]
+    for d, more, place in SIDE_SPANS:
+        for i in range(LY + 2 * more):
+            tile, row = SIDE_SIZE + (place + i) // 8, (place + i) % 8
+            y = FAR - more + i
+            wide[NEAR - d, pl.ds(y, 1), :] = low[tile, pl.ds(row, 1), :]
+            wide[NEAR + LX - 1 + d, pl.ds(y, 1), :] = high[tile, pl.ds(row, 1), :]
 
 
 def fill_tables(coef, skip, table_re, table_im, diag_re, diag_im):
@@ -139,8 +137,8 @@
     def body(x, carry):
         for y in range(size_y):
             spot = pl.ds(y + skip, 1)
-            table_re[x, y] = jnp.broadcast_to(diag_re[x + skip, spot, :], (8, NZ))
-            table_im[x, y] = jnp.broadcast_to(diag_im[x + skip, spot, :], (8, NZ)) * sign
+            table_re[x, y] = jnp.broadcast_to(diag_re[x, spot, :], (8, NZ))
+            table_im[x, y] = jnp.broadcast_to(diag_im[x, spot, :], (8, NZ)) * sign
         return carry
 
     lax.fori_loop(0, size_x, body, 0)
@@ -153,23 +151,14 @@
     return above + below
 
 
-def smooth(block, coef, skip, reach, table_re, table_im, first, second, store):
+def smooth(block, coef, skip, table_re, table_im, first, second, store):
     size_x, size_y = block.shape[:2]
 
     def solve(value, x, y):
         return table_re[x, y] * value + table_im[x, y] * pltpu.roll(value, 4, 0)
 
-    def sections(k):
-        low, high = k, size_y - k
-        if reach == 0:
-            return [((k, size_x - k), (low, high))]
-        return [((k, 4), (low + 5, high - 5)), ((4, size_x - 4), (low, high)),
-                ((size_x - 4, size_x - k), (low + 5, high - 5))]
-
     def planes(k, body):
-        for (begin, end), (low, high) in sections(k):
-            if begin < end:
-                lax.fori_loop(begin, end, functools.partial(body, low, high), 0)
+        lax.fori_loop(k, size_x - k, functools.partial(body, k, size_y - k), 0)
 
     def start(low, high, x, carry):
         for y in range(low, high):
@@ -183,9 +172,6 @@
             total = ref[x - 1, y] + ref[x + 1, y] + line[y - low] + line[y - low + 2]
             yield y, mid, total + depth_sum(mid)
 
-    if reach:
-        first[...] = jnp.zeros(first.shape, F32)
-        second[...] = jnp.zeros(second.shape, F32)
     planes(0, start)
     here, there = first, second
     for k in range(1, 4):
@@ -199,7 +185,7 @@
 
     def image(x, carry):
         for y, mid, total in around(here, x, 4, size_y - 4):
-            diag = 6.0 - coef[x + skip, pl.ds(y + skip, 1), :]
+            diag = 6.0 - coef[x, pl.ds(y + skip, 1), :]
             store(x - 4, y - 4, diag * mid - total)
         return carry
 
@@ -207,7 +193,7 @@
 
 
 def wide_shape(halo):
-    return (LX + 2 * halo, LY + 2 * halo)
+    return (LX + 2 * NEAR, LY + 2 * halo)
 
 
 FLAT = pltpu.VMEM((*wide_shape(FAR), NZ), F32)
@@ -217,62 +203,66 @@
     return [pltpu.VMEM((*wide_shape(halo), 8, NZ), F32)] * 5 + [FLAT] * 2
 
 
-def side_coefficient(low, high):
-    return (low, high, 2 * OLD_SIZE + SIDE_SIZE, SIDE_SPANS)
-
-
-def old_kernel(own, below, above, low, high, out, block, first, second,
-               table_re, table_im, diag_re, diag_im, coef):
-    fill_flat(coef, below, own, above, [side_coefficient(low, high)])
+def first_kernel(own, below, above, low, high, w, coef, out_right, out_left, block, first, second,
+                 table_re, table_im, diag_re, diag_im):
+    fill_flat(coef, below, own, above, low, high)
+    fill_tables(coef, 0, table_re, table_im, diag_re, diag_im)
+    rows = [(below, 2 * HALF), (own, 2 * BLOCK), (above, 2 * HALF)]
+    fill_block(block, FAR, rows, FAR, [(low, high, 0, SIDE_SPANS)])
+
+    def store(x, y, value):
+        w[x, y] = value
+
+    smooth(block, coef, 0, table_re, table_im, first, second, store)
+    for d, more, place in NEAR_SPANS:
+        count = LY + 2 * more
+        out_right[pl.ds(place, count)] = w[LX - d, pl.ds(NEAR - more, count)]
+        out_left[pl.ds(place, count)] = w[d - 1, pl.ds(NEAR - more, count)]
+
+
+def first_image(*args):
+    side = jax.ShapeDtypeStruct((NEAR_SIZE, 8, NZ), F32)
+    return pl.pallas_call(
+        first_kernel,
+        out_shape=(jax.ShapeDtypeStruct((LX, LY + 2 * NEAR, 8, NZ), F32),
+                   jax.ShapeDtypeStruct((*wide_shape(FAR), NZ), F32), side, side),
+        in_specs=[VMEM] * 5,
+        out_specs=(VMEM,) * 4,
+        scratch_shapes=smooth_scratch(FAR),
+        compiler_params=pltpu.CompilerParams(vmem_limit_bytes=16 << 20),
+        cost_estimate=pl.CostEstimate(flops=12_000_000, bytes_accessed=18_000_000, transcendentals=0),
+        name="first_image",
+    )(*args)
+
+
+def old_kernel(coef, own, below, above, low, high, first_low, first_high, out, block, first, second,
+               table_re, table_im, diag_re, diag_im):
     fill_tables(coef, FAR - NEAR, table_re, table_im, diag_re, diag_im)
     for group in range(2):
         rows = [(below, group * HALF), (own, group * BLOCK), (above, group * HALF)]
-        fill_block(block, NEAR, rows, NEAR, [(low, high, group * OLD_SIZE, OLD_SPANS)])
+        if group == 0:
+            sides = [(low, high, 0, NEAR_SPANS[:-1]),
+                     (first_low, first_high, SIDE_SIZE + FLAT_TILES - SPLIT, NEAR_SPANS[-1:])]
+        else:
+            sides = [(low, high, SPLIT, NEAR_SPANS)]
+        fill_block(block, NEAR, rows, NEAR, sides)
 
         def store(x, y, value, group=group):
             out[x, pl.ds(group * BLOCK + y * 8, 8), :] = value
 
-        smooth(block, coef, FAR - NEAR, 0, table_re, table_im, first, second, store)
+        smooth(block, coef, FAR - NEAR, table_re, table_im, first, second, store)
 
 
 def old_images(*args):
     return pl.pallas_call(
         old_kernel,
         out_shape=jax.ShapeDtypeStruct((LX, 2 * BLOCK, NZ), F32),
-        in_specs=[VMEM] * 5,
+        in_specs=[VMEM] * 8,
         out_specs=VMEM,
-        scratch_shapes=smooth_scratch(NEAR) + [FLAT],
+        scratch_shapes=smooth_scratch(NEAR),
         compiler_params=pltpu.CompilerParams(vmem_limit_bytes=16 << 20),
         cost_estimate=pl.CostEstimate(flops=12_000_000, bytes_accessed=24_000_000, transcendentals=0),
         name="old_images",
-    )(*args)
-
-
-def first_kernel(own, below, above, low, high, far_low, far_high, after, out, coef, block, first, second,
-                 table_re, table_im, diag_re, diag_im):
-    del after
-    fill_flat(coef, below, own, above, [side_coefficient(low, high), (far_low, far_high, FAR_SIZE, FAR_SPANS)])
-    fill_tables(coef, 0, table_re, table_im, diag_re, diag_im)
-    rows = [(below, 2 * HALF), (own, 2 * BLOCK), (above, 2 * HALF)]
-    fill_block(block, FAR, rows, FAR,
-               [(low, high, 2 * OLD_SIZE, SIDE_SPANS), (far_low, far_high, 0, FAR_SPANS)])
-
-    def store(x, y, value):
-        out[x, y] = value
-
-    smooth(block, coef, 0, NEAR, table_re, table_im, first, second, store)
-
-
-def first_image(*args):
-    return pl.pallas_call(
-        first_kernel,
-        out_shape=(jax.ShapeDtypeStruct((*wide_shape(NEAR), 8, NZ), F32),
-                   jax.ShapeDtypeStruct((*wide_shape(FAR), NZ), F32)),
-        in_specs=[VMEM] * 7 + [pl.BlockSpec(memory_space=pl.ANY)],
-        out_specs=(VMEM, VMEM),
-        scratch_shapes=smooth_scratch(FAR),
-        compiler_params=pltpu.CompilerParams(vmem_limit_bytes=24 << 20),
-        name="first_image",
     )(*args)
 
 
@@ -289,7 +279,7 @@
     rows = []
     for ref, first in refs:
         if first is None:
-            tiles = [ref[x + NEAR, NEAR + y] for y in range(LY)]
+            tiles = [ref[x, NEAR + y] for y in range(LY)]
         else:
             tiles = [ref[x, pl.ds((first + y) * 8, 8), :] for y in range(LY)]
         rows.append(jnp.concatenate(tiles, axis=1))
@@ -341,14 +331,18 @@
     return jnp.where(tall // 8 <= wide // 8, upper, upper.T)
 
 
-def gram_kernel(peers, w, coef, start, old_image, w_image, out,
-                first, second, table_re, table_im, diag_re, diag_im):
+def gram_kernel(peers, w, coef, low, high, start, old_image, w_image, out,
+                block, first, second, table_re, table_im, diag_re, diag_im):
     fill_tables(coef, FAR - NEAR, table_re, table_im, diag_re, diag_im)
+    block[...] = jnp.zeros(block.shape, F32)
+    for x in range(LX):
+        block[NEAR + x] = w[x]
+    fill_sides(block, NEAR, [(low, high, 0, NEAR_SPANS)])
 
     def store(x, y, value):
         w_image[x, pl.ds(y * 8, 8), :] = value
 
-    smooth(w, coef, FAR - NEAR, 0, table_re, table_im, first, second, store)
+    smooth(block, coef, FAR - NEAR, table_re, table_im, first, second, store)
 
     def plane(x, total):
         stacked = jnp.concatenate(split3(basis_plane(start, w, old_image, w_image, x)), axis=0)
@@ -368,9 +362,9 @@
         functools.partial(gram_kernel, peers),
         out_shape=(jax.ShapeDtypeStruct((LX, LY * 8, NZ), F32),
                    jax.ShapeDtypeStruct((peers, 8, NZ), F32)),
-        in_specs=[VMEM] * 4,
+        in_specs=[VMEM] * 6,
         out_specs=(VMEM, VMEM),
-        scratch_shapes=smooth_scratch(NEAR)[1:],
+        scratch_shapes=smooth_scratch(NEAR),
         compiler_params=pltpu.CompilerParams(vmem_limit_bytes=32 << 20),
         name="image_and_gram",
     )(*args)
@@ -497,13 +491,14 @@
     up = jnp.concatenate([start[:, HALF:BLOCK], start[:, BLOCK + HALF:]], axis=1)
     down = jnp.concatenate([start[:, :HALF], start[:, BLOCK:BLOCK + HALF], start[:, 2 * BLOCK:]], axis=1)
     rims = from_both("gy", ny, up, down)
-    right, left, far_right, far_left = pack_all(start, *rims)
+    right, left, old_right, old_left = pack_all(start, *rims)
     sides = from_both(GX, nx, right, left)
-    far_sides = from_both(GX, nx, far_right, far_left, 2)
-    old_image = old_images(start, *rims, *sides)
-    w, coef = first_image(start, *rims, *sides, *far_sides, old_image)
-
-    w_image, spread = image_and_gram(2 * ny, w, coef, start, old_image)
+    old_sides = from_both(GX, nx, old_right, old_left)
+    w, coef, w_right, w_left = first_image(start, *rims, *sides)
+    w_sides = from_both(GX, nx, w_right, w_left)
+    old_image = old_images(coef, start, *rims, *old_sides, *sides)
+
+    w_image, spread = image_and_gram(2 * ny, w, coef, *w_sides, start, old_image)
     got = lax.all_to_all(spread, ("core", "gy"), 0, 0)
     got = lax.all_to_all(sum_and_spread(got, nz), "z", 0, 0)
     out = finish(cells, got, start, w, old_image, w_image)

time: 102 us -> 100 us (0.980)
  waiting for transfers between devices: 13.9 us -> 7.46 us
  starting transfers between devices: 19.2 us -> 24.3 us
  Pallas kernels: 24.3 us -> 20.3 us
  blocking collectives: 41.9 us -> 45.5 us
    pallas_call x1, Pallas kernels: 7.79 us -> 3.84 us  [first_image(): pl.pallas_call(first_kernel, out_shape=(jax.ShapeDtypeStruct((LX, LY + 2...]
    ppermute x3 -> x4, waiting for transfers between devices: 9.06 us -> 5.38 us  [from_both(): lax.ppermute(to_lower, axis, [(i + step, i) for i in range(count - step)])]
    all_to_all x1, blocking collectives: 26.1 us -> 29.8 us  [per_device(): got = lax.all_to_all(sum_and_spread(got, nz), 'z', 0, 0)]
    ppermute x3 -> x4, starting transfers between devices: 4.5 us -> 7.3 us  [from_both(): lax.ppermute(to_lower, axis, [(i + step, i) for i in range(count - step)])]
    ppermute x3 -> x4, waiting for transfers between devices: 4.82 us -> 2.08 us  [from_both(): lax.ppermute(to_higher, axis, [(i, i + step) for i in range(count - step)])]
    ppermute x3 -> x4, starting transfers between devices: 14.7 us -> 17 us  [from_both(): lax.ppermute(to_higher, axis, [(i, i + step) for i in range(count - step)])]
  transfers between devices with their start and end apart: 6 -> 8, of which waited for: 4 -> 3; matrix products, arithmetic and copies ran while one was open for 0% -> 0% of each run, Pallas kernels for 6% -> 10%
where the time goes in v8:
time: 100 us; the launch traced here: 99.8 us
  blocking collectives  45.5 us (46%)
  starting transfers between devices  24.3 us (24%)
  Pallas kernels  20.3 us (20%)
  waiting for transfers between devices  7.46 us (7%)
  local copies, waits for them, and re-layouts  1.96 us (2%)
    all_to_all x1, blocking collectives, per_device(): got = lax.all_to_all(sum_and_spread(got, nz), 'z', 0, 0)  29.8 us
    ppermute x4, starting transfers between devices, from_both(): lax.ppermute(to_higher, axis, [(i, i + step) for i in range(count - step)])  17 us
    all_to_all x1, blocking collectives, per_device(): got = lax.all_to_all(spread, ('core', 'gy'), 0, 0)  15.7 us
    ppermute x4, starting transfers between devices, from_both(): lax.ppermute(to_lower, axis, [(i + step, i) for i in range(count - step)])  7.3 us
    pallas_call x1, Pallas kernels, old_images(): pl.pallas_call(old_kernel, out_shape=jax.ShapeDtypeStruct((LX, 2 * BLOCK,...  6.18 us
    pallas_call x1, Pallas kernels, finish(): pl.pallas_call(functools.partial(final_kernel, cells), out_shape=jax.Shap...  5.54 us
    ppermute x4, waiting for transfers between devices, from_both(): lax.ppermute(to_lower, axis, [(i + step, i) for i in range(count - step)])  5.38 us
    pallas_call x1, Pallas kernels, image_and_gram(): pl.pallas_call(functools.partial(gram_kernel, peers), out_shape=(jax.Shap...  4.61 us
  transfers between devices with their start and end apart: 8, of which 3 were waited for; matrix products, arithmetic and copies ran while one was open for 0% of the time, Pallas kernels for 10%

profile of v8, /device:TPU:1, one launch (start us, length us, event | category | flops | bytes accessed | tf_op | source)
XLA Modules:
  0.0 99.8 jit_solution(17701235945971802148)
XLA Ops:
  0.0 1.3 %copy.3 = f32[4,3,8,2,4,128]{5,4,3,2,1,0:T(4,128)S(1)} copy(f32[4,3,8,2,4,128]{5,2,0,4,3,1:T(8,128)} %bitcast.7) | data formatting | bytes 786432 | tf_op jit(solution)/shard_map/transpose | solution.py:489
  1.3 0.0 copy-start
  1.3 0.7 copy-done
  2.0 4.0 %collective-permute-start = (f32[4,136,128]{2,1,0:T(8,128)S(1)}, f32[4,136,128]{2,1,0:T(8,128)S(1)}, u32[]{:S(2)}, u32[]{:S(2)}) collective-permute-start(f32[4,136,128]{2,1,0:T(8,128)S(1)} %pad_maximum_fusion.1), channel_id=1, source_target_pairs={{0,1},{1,2},{2,3},{3,4},{4,5},{5,6},{6,7},{7,8},{8,9},{9,10},{10,1... | collective-permute-start | bytes 835592 | tf_op jit(solution)/shard_map/ppermute | solution.py:482
  6.1 1.3 %collective-permute-start.1 = (f32[4,136,128]{2,1,0:T(8,128)S(1)}, f32[4,136,128]{2,1,0:T(8,128)S(1)}, u32[]{:S(2)}, u32[]{:S(2)}) collective-permute-start(f32[4,136,128]{2,1,0:T(8,128)S(1)} %pad_maximum_fusion.2), channel_id=1, source_target_pairs={{1,0},{2,1},{3,2},{4,3},{5,4},{6,5},{7,6},{8,7},{9,8},{10,9},{11,1... | collective-permute-start | bytes 835592 | tf_op jit(solution)/shard_map/ppermute | solution.py:483
  7.5 2.1 %collective-permute-done.below = f32[4,136,128]{2,1,0:T(8,128)S(1)} collective-permute-done((f32[4,136,128]{2,1,0:T(8,128)S(1)}, f32[4,136,128]{2,1,0:T(8,128)S(1)}, u32[]{:S(2)}, u32[]{:S(2)}) %collective-permute-start) | collective-permute-done | bytes 278560 | tf_op jit(solution)/shard_map/ppermute | solution.py:482
  9.5 3.9 %collective-permute-done.1.above = f32[4,136,128]{2,1,0:T(8,128)S(1)} collective-permute-done((f32[4,136,128]{2,1,0:T(8,128)S(1)}, f32[4,136,128]{2,1,0:T(8,128)S(1)}, u32[]{:S(2)}, u32[]{:S(2)}) %collective-permute-start.1) | collective-permute-done | bytes 278560 | tf_op jit(solution)/shard_map/ppermute | solution.py:483
  13.4 0.1 pack_all.1
  13.5 7.1 %collective-permute-start.2 = (f32[94,8,128]{2,1,0:T(8,128)S(1)}, f32[94,8,128]{2,1,0:T(8,128)S(1)}, u32[]{:S(2)}, u32[]{:S(2)}) collective-permute-start(f32[94,8,128]{2,1,0:T(8,128)S(1)} %get-tuple-element.15), channel_id=1, source_target_pairs={{0,16},{16,32},{32,48},{48,64},{64,80},{80,96},{96,112},{112,128},... | collective-permute-start | bytes 1155080 | tf_op jit(solution)/shard_map/ppermute | solution.py:482
  20.6 1.9 %collective-permute-start.3 = (f32[94,8,128]{2,1,0:T(8,128)S(1)}, f32[94,8,128]{2,1,0:T(8,128)S(1)}, u32[]{:S(2)}, u32[]{:S(2)}) collective-permute-start(f32[94,8,128]{2,1,0:T(8,128)S(1)} %get-tuple-element.16), channel_id=1, source_target_pairs={{16,0},{32,16},{48,32},{64,48},{80,64},{96,80},{112,96},{128,112},... | collective-permute-start | bytes 1155080 | tf_op jit(solution)/shard_map/ppermute | solution.py:483
  22.6 3.6 %collective-permute-start.6 = (f32[80,8,128]{2,1,0:T(8,128)S(1)}, f32[80,8,128]{2,1,0:T(8,128)S(1)}, u32[]{:S(2)}, u32[]{:S(2)}) collective-permute-start(f32[80,8,128]{2,1,0:T(8,128)S(1)} %get-tuple-element.21), channel_id=1, source_target_pairs={{0,16},{16,32},{32,48},{48,64},{64,80},{80,96},{96,112},{112,128},... | collective-permute-start | bytes 983048 | tf_op jit(solution)/shard_map/ppermute | solution.py:482
  26.2 1.9 %collective-permute-start.7 = (f32[80,8,128]{2,1,0:T(8,128)S(1)}, f32[80,8,128]{2,1,0:T(8,128)S(1)}, u32[]{:S(2)}, u32[]{:S(2)}) collective-permute-start(f32[80,8,128]{2,1,0:T(8,128)S(1)} %get-tuple-element.22), channel_id=1, source_target_pairs={{16,0},{32,16},{48,32},{64,48},{80,64},{96,80},{112,96},{128,112},... | collective-permute-start | bytes 983048 | tf_op jit(solution)/shard_map/ppermute | solution.py:483
  28.2 0.0 collective-permute-done.2.low.first_low
  28.2 1.5 %collective-permute-done.3.high.first_high = f32[94,8,128]{2,1,0:T(8,128)S(1)} collective-permute-done((f32[94,8,128]{2,1,0:T(8,128)S(1)}, f32[94,8,128]{2,1,0:T(8,128)S(1)}, u32[]{:S(2)}, u32[]{:S(2)}) %collective-permute-start.3) | collective-permute-done | bytes 385056 | tf_op jit(solution)/shard_map/ppermute | solution.py:483
  29.7 3.8 %first_image.1 = (f32[4,16,8,128]{3,2,1,0:T(8,128)S(1)}, f32[12,24,128]{2,1,0:T(8,128)S(1)}, f32[44,8,128]{2,1,0:T(8,128)S(1)}, f32[44,8,128]{2,1,0:T(8,128)S(1)}) custom-call(f32[4,200,128]{2,1,0:T(8,128)S(1)} %pad_maximum_fusion.own.start, f32[4,136,128]{2,1,0:T(8,128)S(1)} %collective-permute-done.below, f32[4,136,128]{2,1,0:T(8,128)S(1)} %collective-permute-done.1.above, ...), custom_call_target="tpu_custom_call" | custom-call | flops 12000000 | bytes 18000000 | tf_op jit(solution)/shard_map/first_image/pallas_call | solution.py:225
  33.5 2.2 %collective-permute-start.4 = (f32[44,8,128]{2,1,0:T(8,128)S(1)}, f32[44,8,128]{2,1,0:T(8,128)S(1)}, u32[]{:S(2)}, u32[]{:S(2)}) collective-permute-start(f32[44,8,128]{2,1,0:T(8,128)S(1)} %get-tuple-element.19), channel_id=1, source_target_pairs={{0,16},{16,32},{32,48},{48,64},{64,80},{80,96},{96,112},{112,128},... | collective-permute-start | bytes 540680 | tf_op jit(solution)/shard_map/ppermute | solution.py:482
  35.7 2.2 %collective-permute-start.5 = (f32[44,8,128]{2,1,0:T(8,128)S(1)}, f32[44,8,128]{2,1,0:T(8,128)S(1)}, u32[]{:S(2)}, u32[]{:S(2)}) collective-permute-start(f32[44,8,128]{2,1,0:T(8,128)S(1)} %get-tuple-element.20), channel_id=1, source_target_pairs={{16,0},{32,16},{48,32},{64,48},{80,64},{96,80},{112,96},{128,112},... | collective-permute-start | bytes 540680 | tf_op jit(solution)/shard_map/ppermute | solution.py:483
  37.9 0.0 collective-permute-done.6.low
  37.9 0.0 collective-permute-done.7.high
  37.9 6.2 %old_images.1.old_image = f32[4,128,128]{2,1,0:T(8,128)S(1)} custom-call(f32[12,24,128]{2,1,0:T(8,128)S(1)} %get-tuple-element.18.coef, f32[4,200,128]{2,1,0:T(8,128)S(1)} %pad_maximum_fusion.own.start, f32[4,136,128]{2,1,0:T(8,128)S(1)} %collective-permute-done.below, f32[4,136,128]{2,1,0:T(8,128)S(1)} %collective-permute-done.1.above, ...), custom_call_target="tpu_custom_call" | custom-call | flops 12000000 | bytes 24000000 | tf_op jit(solution)/shard_map/old_images/pallas_call | solution.py:257
  44.1 0.0 collective-permute-done.4.low
  44.1 0.0 collective-permute-done.5.high
  44.1 4.6 %image_and_gram.1 = (f32[4,64,128]{2,1,0:T(8,128)S(1)}, f32[32,8,128]{2,1,0:T(8,128)S(1)}) custom-call(f32[4,16,8,128]{3,2,1,0:T(8,128)S(1)} %get-tuple-element.17.w, f32[12,24,128]{2,1,0:T(8,128)S(1)} %get-tuple-element.18.coef, f32[44,8,128]{2,1,0:T(8,128)S(1)} %collective-permute-done.4.low, f32[44,8,128]{2,1,0:T(8,128)S(1)} %collective-permute-done.5.high, ...), custom_call_target="tpu_custom_call" | custom-call | tf_op jit(solution)/shard_map/image_and_gram/pallas_call | solution.py:361
  48.7 15.7 %all_to_all.10.parts = f32[32,8,128]{2,1,0:T(8,128)S(1)} all-to-all(f32[32,8,128]{2,1,0:T(8,128)S(1)} %get-tuple-element.23), channel_id=1, replica_groups=mesh['z'=16,'core'=2,'gy'=16] {'core','gy'}, dimensions={0} | all-to-all | bytes 262144 | tf_op jit(solution)/shard_map/all_to_all | solution.py:502
  64.5 29.8 %all_to_all.11.parts = f32[16,8,128]{2,1,0:T(8,128)S(1)} all-to-all(f32[16,8,128]{2,1,0:T(8,128)S(1)} %sum_and_spread.1), channel_id=1, replica_groups=mesh['z'=16,'core'=2,'gy'=16] {'z'}, dimensions={0} | all-to-all | bytes 131072 | tf_op jit(solution)/shard_map/all_to_all | solution.py:503
  94.2 5.5 %finish.1 = f32[2,8,4,8,128]{4,3,2,1,0:T(8,128)} custom-call(f32[16,8,128]{2,1,0:T(8,128)S(1)} %all_to_all.11.parts, f32[4,200,128]{2,1,0:T(8,128)S(1)} %pad_maximum_fusion.own.start, f32[4,16,8,128]{3,2,1,0:T(8,128)S(1)} %get-tuple-element.17.w, f32[4,128,128]{2,1,0:T(8,128)S(1)} %old_images.1.old_image, f32[4,64,128]{2,1,0:T(8,128)S(1)} %get-tuple-element.24.w_image), custom_call_target="tpu_custom_call" | custom-call | tf_op jit(solution)/shard_map/finish/pallas_call | solution.py:467
  (7 shorter events, 0.2 us)
Async XLA Ops:
  1.3 0.7 copy-start
  2.0 7.5 %collective-permute-start = (f32[4,136,128]{2,1,0:T(8,128)S(1)}, f32[4,136,128]{2,1,0:T(8,128)S(1)}, u32[]{:S(2)}, u32[]{:S(2)}) collective-permute-start(f32[4,136,128]{2,1,0:T(8,128)S(1)} %pad_maximum_fusion.1), channel_id=1, source_target_pairs={{0,1},{1,2},{2,3},{3,4},{4,5},{5,6},{6,7},{7,8},{8,9},{9,10},{10,1... | collective-permute-start | bytes 835592 | tf_op jit(solution)/shard_map/ppermute | solution.py:482
  6.1 7.3 %collective-permute-start.1 = (f32[4,136,128]{2,1,0:T(8,128)S(1)}, f32[4,136,128]{2,1,0:T(8,128)S(1)}, u32[]{:S(2)}, u32[]{:S(2)}) collective-permute-start(f32[4,136,128]{2,1,0:T(8,128)S(1)} %pad_maximum_fusion.2), channel_id=1, source_target_pairs={{1,0},{2,1},{3,2},{4,3},{5,4},{6,5},{7,6},{8,7},{9,8},{10,9},{11,1... | collective-permute-start | bytes 835592 | tf_op jit(solution)/shard_map/ppermute | solution.py:483
  13.5 14.6 %collective-permute-start.2 = (f32[94,8,128]{2,1,0:T(8,128)S(1)}, f32[94,8,128]{2,1,0:T(8,128)S(1)}, u32[]{:S(2)}, u32[]{:S(2)}) collective-permute-start(f32[94,8,128]{2,1,0:T(8,128)S(1)} %get-tuple-element.15), channel_id=1, source_target_pairs={{0,16},{16,32},{32,48},{48,64},{64,80},{80,96},{96,112},{112,128},... | collective-permute-start | bytes 1155080 | tf_op jit(solution)/shard_map/ppermute | solution.py:482
  20.6 9.0 %collective-permute-start.3 = (f32[94,8,128]{2,1,0:T(8,128)S(1)}, f32[94,8,128]{2,1,0:T(8,128)S(1)}, u32[]{:S(2)}, u32[]{:S(2)}) collective-permute-start(f32[94,8,128]{2,1,0:T(8,128)S(1)} %get-tuple-element.16), channel_id=1, source_target_pairs={{16,0},{32,16},{48,32},{64,48},{80,64},{96,80},{112,96},{128,112},... | collective-permute-start | bytes 1155080 | tf_op jit(solution)/shard_map/ppermute | solution.py:483
  22.6 15.3 %collective-permute-start.6 = (f32[80,8,128]{2,1,0:T(8,128)S(1)}, f32[80,8,128]{2,1,0:T(8,128)S(1)}, u32[]{:S(2)}, u32[]{:S(2)}) collective-permute-start(f32[80,8,128]{2,1,0:T(8,128)S(1)} %get-tuple-element.21), channel_id=1, source_target_pairs={{0,16},{16,32},{32,48},{48,64},{64,80},{80,96},{96,112},{112,128},... | collective-permute-start | bytes 983048 | tf_op jit(solution)/shard_map/ppermute | solution.py:482
  26.2 11.6 %collective-permute-start.7 = (f32[80,8,128]{2,1,0:T(8,128)S(1)}, f32[80,8,128]{2,1,0:T(8,128)S(1)}, u32[]{:S(2)}, u32[]{:S(2)}) collective-permute-start(f32[80,8,128]{2,1,0:T(8,128)S(1)} %get-tuple-element.22), channel_id=1, source_target_pairs={{16,0},{32,16},{48,32},{64,48},{80,64},{96,80},{112,96},{128,112},... | collective-permute-start | bytes 983048 | tf_op jit(solution)/shard_map/ppermute | solution.py:483
  33.5 10.6 %collective-permute-start.4 = (f32[44,8,128]{2,1,0:T(8,128)S(1)}, f32[44,8,128]{2,1,0:T(8,128)S(1)}, u32[]{:S(2)}, u32[]{:S(2)}) collective-permute-start(f32[44,8,128]{2,1,0:T(8,128)S(1)} %get-tuple-element.19), channel_id=1, source_target_pairs={{0,16},{16,32},{32,48},{48,64},{64,80},{80,96},{96,112},{112,128},... | collective-permute-start | bytes 540680 | tf_op jit(solution)/shard_map/ppermute | solution.py:482
  35.7 8.4 %collective-permute-start.5 = (f32[44,8,128]{2,1,0:T(8,128)S(1)}, f32[44,8,128]{2,1,0:T(8,128)S(1)}, u32[]{:S(2)}, u32[]{:S(2)}) collective-permute-start(f32[44,8,128]{2,1,0:T(8,128)S(1)} %get-tuple-element.20), channel_id=1, source_target_pairs={{16,0},{32,16},{48,32},{64,48},{80,64},{96,80},{112,96},{128,112},... | collective-permute-start | bytes 540680 | tf_op jit(solution)/shard_map/ppermute | solution.py:483

commit v9 on v8

--- a/solution.py
+++ b/solution.py
@@ -141,7 +141,7 @@
             table_im[x, y] = jnp.broadcast_to(diag_im[x, spot, :], (8, NZ)) * sign
         return carry
 
-    lax.fori_loop(0, size_x, body, 0)
+    lax.fori_loop(0, size_x, body, 0, unroll=True)
 
 
 def depth_sum(value):
@@ -158,7 +158,7 @@
         return table_re[x, y] * value + table_im[x, y] * pltpu.roll(value, 4, 0)
 
     def planes(k, body):
-        lax.fori_loop(k, size_x - k, functools.partial(body, k, size_y - k), 0)
+        lax.fori_loop(k, size_x - k, functools.partial(body, k, size_y - k), 0, unroll=True)
 
     def start(low, high, x, carry):
         for y in range(low, high):
@@ -189,7 +189,7 @@
             store(x - 4, y - 4, diag * mid - total)
         return carry
 
-    lax.fori_loop(4, size_x - 4, image, 0)
+    lax.fori_loop(4, size_x - 4, image, 0, unroll=True)
 
 
 def wide_shape(halo):
@@ -348,7 +348,7 @@
         stacked = jnp.concatenate(split3(basis_plane(start, w, old_image, w_image, x)), axis=0)
         return total + lax.dot_general(stacked, stacked, (((1,), (1,)), ((), ())), preferred_element_type=F32)
 
-    total = lax.fori_loop(0, LX, plane, jnp.zeros((3 * ROWS, 3 * ROWS), F32))
+    total = lax.fori_loop(0, LX, plane, jnp.zeros((3 * ROWS, 3 * ROWS), F32), unroll=True)
     tall = total[0:ROWS] + total[ROWS:2 * ROWS] + total[2 * ROWS:3 * ROWS]
     gram = tall[:, 0:ROWS] + tall[:, ROWS:2 * ROWS] + tall[:, 2 * ROWS:3 * ROWS]
     gram = jnp.concatenate([gram, jnp.zeros((ROWS, NZ - ROWS), F32)], axis=1)
@@ -460,7 +460,7 @@
             out[k, :, x] = jnp.swapaxes(tiles, 0, 1)
         return carry
 
-    lax.fori_loop(0, LX, plane, 0)
+    lax.fori_loop(0, LX, plane, 0, unroll=True)
 
 
 def finish(cells, *args):

time: 100 us -> 91.4 us (0.914)
  Pallas kernels: 20.3 us -> 9.58 us
  waiting for transfers between devices: 7.46 us -> 11 us
  blocking collectives: 45.5 us -> 44 us
    pallas_call x1, Pallas kernels: 6.18 us -> 1.42 us  [old_images(): pl.pallas_call(old_kernel, out_shape=jax.ShapeDtypeStruct((LX, 2 * BLOCK,...]
    ppermute x4, waiting for transfers between devices: 5.38 us -> 8.9 us  [from_both(): lax.ppermute(to_lower, axis, [(i + step, i) for i in range(count - step)])]
    pallas_call x1, Pallas kernels: 4.61 us -> 1.49 us  [image_and_gram(): pl.pallas_call(functools.partial(gram_kernel, peers), out_shape=(jax.Shap...]
    pallas_call x1, Pallas kernels: 3.84 us -> 1.41 us  [first_image(): pl.pallas_call(first_kernel, out_shape=(jax.ShapeDtypeStruct((LX, LY + 2...]
    all_to_all x1, blocking collectives: 29.8 us -> 28.2 us  [per_device(): got = lax.all_to_all(sum_and_spread(got, nz), 'z', 0, 0)]
  transfers between devices with their start and end apart: 8 -> 8, of which waited for: 3 -> 4; matrix products, arithmetic and copies ran while one was open for 0% -> 0% of each run, Pallas kernels for 10% -> 3%
where the time goes in v9:
time: 91.4 us; the launch traced here: 91 us
  blocking collectives  44 us (48%)
  starting transfers between devices  24.3 us (27%)
  waiting for transfers between devices  11 us (12%)
  Pallas kernels  9.58 us (10%)
  local copies, waits for them, and re-layouts  1.96 us (2%)
    all_to_all x1, blocking collectives, per_device(): got = lax.all_to_all(sum_and_spread(got, nz), 'z', 0, 0)  28.2 us
    ppermute x4, starting transfers between devices, from_both(): lax.ppermute(to_higher, axis, [(i, i + step) for i in range(count - step)])  17 us
    all_to_all x1, blocking collectives, per_device(): got = lax.all_to_all(spread, ('core', 'gy'), 0, 0)  15.7 us
    ppermute x4, waiting for transfers between devices, from_both(): lax.ppermute(to_lower, axis, [(i + step, i) for i in range(count - step)])  8.9 us
    ppermute x4, starting transfers between devices, from_both(): lax.ppermute(to_lower, axis, [(i + step, i) for i in range(count - step)])  7.3 us
    pallas_call x1, Pallas kernels, finish(): pl.pallas_call(functools.partial(final_kernel, cells), out_shape=jax.Shap...  5.11 us
    ppermute x4, waiting for transfers between devices, from_both(): lax.ppermute(to_higher, axis, [(i, i + step) for i in range(count - step)])  2.08 us
  transfers between devices with their start and end apart: 8, of which 4 were waited for; matrix products, arithmetic and copies ran while one was open for 0% of the time, Pallas kernels for 3%

profile of v9, /device:TPU:1, one launch (start us, length us, event | category | flops | bytes accessed | tf_op | source)
XLA Modules:
  0.0 91.0 jit_solution(703067259660957831)
XLA Ops:
  0.0 1.3 %copy.3 = f32[4,3,8,2,4,128]{5,4,3,2,1,0:T(4,128)S(1)} copy(f32[4,3,8,2,4,128]{5,2,0,4,3,1:T(8,128)} %bitcast.7) | data formatting | bytes 786432 | tf_op jit(solution)/shard_map/transpose | solution.py:489
  1.3 0.0 copy-start
  1.3 0.7 copy-done
  2.0 4.0 %collective-permute-start = (f32[4,136,128]{2,1,0:T(8,128)S(1)}, f32[4,136,128]{2,1,0:T(8,128)S(1)}, u32[]{:S(2)}, u32[]{:S(2)}) collective-permute-start(f32[4,136,128]{2,1,0:T(8,128)S(1)} %pad_maximum_fusion.1), channel_id=1, source_target_pairs={{0,1},{1,2},{2,3},{3,4},{4,5},{5,6},{6,7},{7,8},{8,9},{9,10},{10,1... | collective-permute-start | bytes 835592 | tf_op jit(solution)/shard_map/ppermute | solution.py:482
  6.1 1.3 %collective-permute-start.1 = (f32[4,136,128]{2,1,0:T(8,128)S(1)}, f32[4,136,128]{2,1,0:T(8,128)S(1)}, u32[]{:S(2)}, u32[]{:S(2)}) collective-permute-start(f32[4,136,128]{2,1,0:T(8,128)S(1)} %pad_maximum_fusion.2), channel_id=1, source_target_pairs={{1,0},{2,1},{3,2},{4,3},{5,4},{6,5},{7,6},{8,7},{9,8},{10,9},{11,1... | collective-permute-start | bytes 835592 | tf_op jit(solution)/shard_map/ppermute | solution.py:483
  7.5 2.1 %collective-permute-done.below = f32[4,136,128]{2,1,0:T(8,128)S(1)} collective-permute-done((f32[4,136,128]{2,1,0:T(8,128)S(1)}, f32[4,136,128]{2,1,0:T(8,128)S(1)}, u32[]{:S(2)}, u32[]{:S(2)}) %collective-permute-start) | collective-permute-done | bytes 278560 | tf_op jit(solution)/shard_map/ppermute | solution.py:482
  9.5 3.9 %collective-permute-done.1.above = f32[4,136,128]{2,1,0:T(8,128)S(1)} collective-permute-done((f32[4,136,128]{2,1,0:T(8,128)S(1)}, f32[4,136,128]{2,1,0:T(8,128)S(1)}, u32[]{:S(2)}, u32[]{:S(2)}) %collective-permute-start.1) | collective-permute-done | bytes 278560 | tf_op jit(solution)/shard_map/ppermute | solution.py:483
  13.4 0.1 pack_all.1
  13.5 7.1 %collective-permute-start.2 = (f32[94,8,128]{2,1,0:T(8,128)S(1)}, f32[94,8,128]{2,1,0:T(8,128)S(1)}, u32[]{:S(2)}, u32[]{:S(2)}) collective-permute-start(f32[94,8,128]{2,1,0:T(8,128)S(1)} %get-tuple-element.15), channel_id=1, source_target_pairs={{0,16},{16,32},{32,48},{48,64},{64,80},{80,96},{96,112},{112,128},... | collective-permute-start | bytes 1155080 | tf_op jit(solution)/shard_map/ppermute | solution.py:482
  20.6 1.9 %collective-permute-start.3 = (f32[94,8,128]{2,1,0:T(8,128)S(1)}, f32[94,8,128]{2,1,0:T(8,128)S(1)}, u32[]{:S(2)}, u32[]{:S(2)}) collective-permute-start(f32[94,8,128]{2,1,0:T(8,128)S(1)} %get-tuple-element.16), channel_id=1, source_target_pairs={{16,0},{32,16},{48,32},{64,48},{80,64},{96,80},{112,96},{128,112},... | collective-permute-start | bytes 1155080 | tf_op jit(solution)/shard_map/ppermute | solution.py:483
  22.6 3.6 %collective-permute-start.6 = (f32[80,8,128]{2,1,0:T(8,128)S(1)}, f32[80,8,128]{2,1,0:T(8,128)S(1)}, u32[]{:S(2)}, u32[]{:S(2)}) collective-permute-start(f32[80,8,128]{2,1,0:T(8,128)S(1)} %get-tuple-element.21), channel_id=1, source_target_pairs={{0,16},{16,32},{32,48},{48,64},{64,80},{80,96},{96,112},{112,128},... | collective-permute-start | bytes 983048 | tf_op jit(solution)/shard_map/ppermute | solution.py:482
  26.2 1.9 %collective-permute-start.7 = (f32[80,8,128]{2,1,0:T(8,128)S(1)}, f32[80,8,128]{2,1,0:T(8,128)S(1)}, u32[]{:S(2)}, u32[]{:S(2)}) collective-permute-start(f32[80,8,128]{2,1,0:T(8,128)S(1)} %get-tuple-element.22), channel_id=1, source_target_pairs={{16,0},{32,16},{48,32},{64,48},{80,64},{96,80},{112,96},{128,112},... | collective-permute-start | bytes 983048 | tf_op jit(solution)/shard_map/ppermute | solution.py:483
  28.2 0.0 collective-permute-done.2.low.first_low
  28.2 1.5 %collective-permute-done.3.high.first_high = f32[94,8,128]{2,1,0:T(8,128)S(1)} collective-permute-done((f32[94,8,128]{2,1,0:T(8,128)S(1)}, f32[94,8,128]{2,1,0:T(8,128)S(1)}, u32[]{:S(2)}, u32[]{:S(2)}) %collective-permute-start.3) | collective-permute-done | bytes 385056 | tf_op jit(solution)/shard_map/ppermute | solution.py:483
  29.7 1.4 %first_image.1 = (f32[4,16,8,128]{3,2,1,0:T(8,128)S(1)}, f32[12,24,128]{2,1,0:T(8,128)S(1)}, f32[44,8,128]{2,1,0:T(8,128)S(1)}, f32[44,8,128]{2,1,0:T(8,128)S(1)}) custom-call(f32[4,200,128]{2,1,0:T(8,128)S(1)} %pad_maximum_fusion.own.start, f32[4,136,128]{2,1,0:T(8,128)S(1)} %collective-permute-done.below, f32[4,136,128]{2,1,0:T(8,128)S(1)} %collective-permute-done.1.above, ...), custom_call_target="tpu_custom_call" | custom-call | flops 12000000 | bytes 18000000 | tf_op jit(solution)/shard_map/first_image/pallas_call | solution.py:225
  31.1 2.2 %collective-permute-start.4 = (f32[44,8,128]{2,1,0:T(8,128)S(1)}, f32[44,8,128]{2,1,0:T(8,128)S(1)}, u32[]{:S(2)}, u32[]{:S(2)}) collective-permute-start(f32[44,8,128]{2,1,0:T(8,128)S(1)} %get-tuple-element.19), channel_id=1, source_target_pairs={{0,16},{16,32},{32,48},{48,64},{64,80},{80,96},{96,112},{112,128},... | collective-permute-start | bytes 540680 | tf_op jit(solution)/shard_map/ppermute | solution.py:482
  33.2 2.2 %collective-permute-start.5 = (f32[44,8,128]{2,1,0:T(8,128)S(1)}, f32[44,8,128]{2,1,0:T(8,128)S(1)}, u32[]{:S(2)}, u32[]{:S(2)}) collective-permute-start(f32[44,8,128]{2,1,0:T(8,128)S(1)} %get-tuple-element.20), channel_id=1, source_target_pairs={{16,0},{32,16},{48,32},{64,48},{80,64},{96,80},{112,96},{128,112},... | collective-permute-start | bytes 540680 | tf_op jit(solution)/shard_map/ppermute | solution.py:483
  35.4 0.0 collective-permute-done.6.low
  35.4 0.0 collective-permute-done.7.high
  35.4 1.4 %old_images.1.old_image = f32[4,128,128]{2,1,0:T(8,128)S(1)} custom-call(f32[12,24,128]{2,1,0:T(8,128)S(1)} %get-tuple-element.18.coef, f32[4,200,128]{2,1,0:T(8,128)S(1)} %pad_maximum_fusion.own.start, f32[4,136,128]{2,1,0:T(8,128)S(1)} %collective-permute-done.below, f32[4,136,128]{2,1,0:T(8,128)S(1)} %collective-permute-done.1.above, ...), custom_call_target="tpu_custom_call" | custom-call | flops 12000000 | bytes 24000000 | tf_op jit(solution)/shard_map/old_images/pallas_call | solution.py:257
  36.9 0.0 collective-permute-done.4.low
  36.9 3.5 %collective-permute-done.5.high = f32[44,8,128]{2,1,0:T(8,128)S(1)} collective-permute-done((f32[44,8,128]{2,1,0:T(8,128)S(1)}, f32[44,8,128]{2,1,0:T(8,128)S(1)}, u32[]{:S(2)}, u32[]{:S(2)}) %collective-permute-start.5) | collective-permute-done | bytes 180256 | tf_op jit(solution)/shard_map/ppermute | solution.py:483
  40.4 1.5 %image_and_gram.1 = (f32[4,64,128]{2,1,0:T(8,128)S(1)}, f32[32,8,128]{2,1,0:T(8,128)S(1)}) custom-call(f32[4,16,8,128]{3,2,1,0:T(8,128)S(1)} %get-tuple-element.17.w, f32[12,24,128]{2,1,0:T(8,128)S(1)} %get-tuple-element.18.coef, f32[44,8,128]{2,1,0:T(8,128)S(1)} %collective-permute-done.4.low, f32[44,8,128]{2,1,0:T(8,128)S(1)} %collective-permute-done.5.high, ...), custom_call_target="tpu_custom_call" | custom-call | tf_op jit(solution)/shard_map/image_and_gram/pallas_call | solution.py:361
  41.9 15.7 %all_to_all.10.parts = f32[32,8,128]{2,1,0:T(8,128)S(1)} all-to-all(f32[32,8,128]{2,1,0:T(8,128)S(1)} %get-tuple-element.23), channel_id=1, replica_groups=mesh['z'=16,'core'=2,'gy'=16] {'core','gy'}, dimensions={0} | all-to-all | bytes 262144 | tf_op jit(solution)/shard_map/all_to_all | solution.py:502
  57.7 28.2 %all_to_all.11.parts = f32[16,8,128]{2,1,0:T(8,128)S(1)} all-to-all(f32[16,8,128]{2,1,0:T(8,128)S(1)} %sum_and_spread.1), channel_id=1, replica_groups=mesh['z'=16,'core'=2,'gy'=16] {'z'}, dimensions={0} | all-to-all | bytes 131072 | tf_op jit(solution)/shard_map/all_to_all | solution.py:503
  85.9 5.1 %finish.1 = f32[2,8,4,8,128]{4,3,2,1,0:T(8,128)} custom-call(f32[16,8,128]{2,1,0:T(8,128)S(1)} %all_to_all.11.parts, f32[4,200,128]{2,1,0:T(8,128)S(1)} %pad_maximum_fusion.own.start, f32[4,16,8,128]{3,2,1,0:T(8,128)S(1)} %get-tuple-element.17.w, f32[4,128,128]{2,1,0:T(8,128)S(1)} %old_images.1.old_image, f32[4,64,128]{2,1,0:T(8,128)S(1)} %get-tuple-element.24.w_image), custom_call_target="tpu_custom_call" | custom-call | tf_op jit(solution)/shard_map/finish/pallas_call | solution.py:467
  (7 shorter events, 0.2 us)
Async XLA Ops:
  1.3 0.7 copy-start
  2.0 7.5 %collective-permute-start = (f32[4,136,128]{2,1,0:T(8,128)S(1)}, f32[4,136,128]{2,1,0:T(8,128)S(1)}, u32[]{:S(2)}, u32[]{:S(2)}) collective-permute-start(f32[4,136,128]{2,1,0:T(8,128)S(1)} %pad_maximum_fusion.1), channel_id=1, source_target_pairs={{0,1},{1,2},{2,3},{3,4},{4,5},{5,6},{6,7},{7,8},{8,9},{9,10},{10,1... | collective-permute-start | bytes 835592 | tf_op jit(solution)/shard_map/ppermute | solution.py:482
  6.1 7.3 %collective-permute-start.1 = (f32[4,136,128]{2,1,0:T(8,128)S(1)}, f32[4,136,128]{2,1,0:T(8,128)S(1)}, u32[]{:S(2)}, u32[]{:S(2)}) collective-permute-start(f32[4,136,128]{2,1,0:T(8,128)S(1)} %pad_maximum_fusion.2), channel_id=1, source_target_pairs={{1,0},{2,1},{3,2},{4,3},{5,4},{6,5},{7,6},{8,7},{9,8},{10,9},{11,1... | collective-permute-start | bytes 835592 | tf_op jit(solution)/shard_map/ppermute | solution.py:483
  13.5 14.6 %collective-permute-start.2 = (f32[94,8,128]{2,1,0:T(8,128)S(1)}, f32[94,8,128]{2,1,0:T(8,128)S(1)}, u32[]{:S(2)}, u32[]{:S(2)}) collective-permute-start(f32[94,8,128]{2,1,0:T(8,128)S(1)} %get-tuple-element.15), channel_id=1, source_target_pairs={{0,16},{16,32},{32,48},{48,64},{64,80},{80,96},{96,112},{112,128},... | collective-permute-start | bytes 1155080 | tf_op jit(solution)/shard_map/ppermute | solution.py:482
  20.6 9.0 %collective-permute-start.3 = (f32[94,8,128]{2,1,0:T(8,128)S(1)}, f32[94,8,128]{2,1,0:T(8,128)S(1)}, u32[]{:S(2)}, u32[]{:S(2)}) collective-permute-start(f32[94,8,128]{2,1,0:T(8,128)S(1)} %get-tuple-element.16), channel_id=1, source_target_pairs={{16,0},{32,16},{48,32},{64,48},{80,64},{96,80},{112,96},{128,112},... | collective-permute-start | bytes 1155080 | tf_op jit(solution)/shard_map/ppermute | solution.py:483
  22.6 12.8 %collective-permute-start.6 = (f32[80,8,128]{2,1,0:T(8,128)S(1)}, f32[80,8,128]{2,1,0:T(8,128)S(1)}, u32[]{:S(2)}, u32[]{:S(2)}) collective-permute-start(f32[80,8,128]{2,1,0:T(8,128)S(1)} %get-tuple-element.21), channel_id=1, source_target_pairs={{0,16},{16,32},{32,48},{48,64},{64,80},{80,96},{96,112},{112,128},... | collective-permute-start | bytes 983048 | tf_op jit(solution)/shard_map/ppermute | solution.py:482
  26.2 9.2 %collective-permute-start.7 = (f32[80,8,128]{2,1,0:T(8,128)S(1)}, f32[80,8,128]{2,1,0:T(8,128)S(1)}, u32[]{:S(2)}, u32[]{:S(2)}) collective-permute-start(f32[80,8,128]{2,1,0:T(8,128)S(1)} %get-tuple-element.22), channel_id=1, source_target_pairs={{16,0},{32,16},{48,32},{64,48},{80,64},{96,80},{112,96},{128,112},... | collective-permute-start | bytes 983048 | tf_op jit(solution)/shard_map/ppermute | solution.py:483
  31.1 5.8 %collective-permute-start.4 = (f32[44,8,128]{2,1,0:T(8,128)S(1)}, f32[44,8,128]{2,1,0:T(8,128)S(1)}, u32[]{:S(2)}, u32[]{:S(2)}) collective-permute-start(f32[44,8,128]{2,1,0:T(8,128)S(1)} %get-tuple-element.19), channel_id=1, source_target_pairs={{0,16},{16,32},{32,48},{48,64},{64,80},{80,96},{96,112},{112,128},... | collective-permute-start | bytes 540680 | tf_op jit(solution)/shard_map/ppermute | solution.py:482
  33.2 7.2 %collective-permute-start.5 = (f32[44,8,128]{2,1,0:T(8,128)S(1)}, f32[44,8,128]{2,1,0:T(8,128)S(1)}, u32[]{:S(2)}, u32[]{:S(2)}) collective-permute-start(f32[44,8,128]{2,1,0:T(8,128)S(1)} %get-tuple-element.20), channel_id=1, source_target_pairs={{16,0},{32,16},{48,32},{64,48},{80,64},{96,80},{112,96},{128,112},... | collective-permute-start | bytes 540680 | tf_op jit(solution)/shard_map/ppermute | solution.py:483

commit v10 on v9

--- a/solution.py
+++ b/solution.py
@@ -14,7 +14,6 @@
 ROWS = 64
 F32 = jnp.float32
 BF16 = jnp.bfloat16
-HIGHEST = lax.Precision.HIGHEST
 VMEM = pl.BlockSpec(memory_space=pltpu.VMEM)
 
 
@@ -387,61 +386,76 @@
     )(parts)
 
 
+def exact(left, right, dims):
+    parts = [part.astype(F32) for part in split3(left)]
+    stacked = jnp.concatenate([*parts, jnp.zeros((8, NZ), F32)], axis=0).astype(BF16)
+    high, middle, low = (
+        lax.dot_general(stacked, part, (dims, ((), ())), preferred_element_type=F32) for part in split3(right)
+    )
+    small = low[0:8] + middle[8:16] + high[16:24]
+    return small + (middle[0:8] + high[8:16]) + high[0:8]
+
+
 def mul(left, right):
-    return lax.dot_general(left, right, (((1,), (0,)), ((), ())), precision=HIGHEST, preferred_element_type=F32)
+    return exact(left, right, ((1,), (0,)))
 
 
 def mul_t(left, right):
-    return lax.dot_general(left, right, (((1,), (1,)), ((), ())), precision=HIGHEST, preferred_element_type=F32)
+    return exact(left, right, ((1,), (1,)))
 
 
 def inverse_factor(gram):
     lane = lax.broadcasted_iota(jnp.int32, (8, NZ), 1)
     row = lax.broadcasted_iota(jnp.int32, (8, NZ), 0)
     work = jnp.where(lane < 8, gram, jnp.where(lane == row + 8, 1.0, 0.0))
-    rank = 2 * (row % 4) + row // 4
-    for step in range(8):
-        k = (step % 2) * 4 + step // 2
-        line = work[k:k + 1, :]
-        pivot = line[:, k:k + 1]
-        column = work[:, k:k + 1]
-        root = 1.0 / jnp.sqrt(pivot)
-        line = line * root
-        factor = column * root
-        work = jnp.where(rank > step, work - factor * line, jnp.where(rank == step, line, work))
-    return jnp.where(lane < 8, lane_roll(work, -8), 0.0)
+    pivots = jnp.ones((8, NZ), F32)
+    for s in range(4):
+        pivot = jnp.broadcast_to(work[s:s + 1, s:s + 1], (8, NZ))
+        pivots = jnp.where(row % 4 == s, pivot, pivots)
+        if s < 3:
+            change = work[:, s:s + 1] * work[s:s + 1, :] + work[:, 4 + s:5 + s] * work[4 + s:5 + s, :]
+            work = jnp.where(row % 4 > s, work - change / pivot, work)
+    return jnp.where(lane < 8, lane_roll(work, -8), 0.0) / jnp.sqrt(pivots)
+
+
+def at_row(rows, start):
+    parts = [rows, jnp.zeros((NZ - 8 - start, NZ), F32)]
+    if start:
+        parts.insert(0, jnp.zeros((start, NZ), F32))
+    return jnp.concatenate(parts, axis=0)
 
 
 def coefficients(gram):
     lane = lax.broadcasted_iota(jnp.int32, (8, NZ), 1)
     row = lax.broadcasted_iota(jnp.int32, (8, NZ), 0)
-    tall = lax.broadcasted_iota(jnp.int32, (NZ, NZ), 0)
-    wide = lax.broadcasted_iota(jnp.int32, (NZ, NZ), 1)
-
-    def normalise(rows):
-        small = mul_t(mul(rows, gram), rows_in(rows))
-        return mul(inverse_factor(small)[:, 0:8], rows)
-
-    def rows_in(rows):
-        return jnp.concatenate([rows, jnp.zeros((NZ - 8, NZ), F32)], axis=0)
+    new_at = 8 * BLOCKS
 
     once = jnp.where(lane < 24, gram[24:32], 0.0)
     again = jnp.where(lane < 24, mul(once, gram), 0.0)
-    fresh = jnp.where(lane == row + 24, 1.0, 0.0)
-    new = normalise(fresh - (2.0 * once - again))
+    rows = jnp.where(lane == row + 24, 1.0, 0.0) - (2.0 * once - again)
+    rows_gram = mul(rows, gram)
+    spread = at_row(rows, 0)
+    factor = inverse_factor(mul_t(rows_gram, spread))
+    new = mul(factor, spread)
+    new_gram = mul(factor, at_row(rows_gram, 0))
+    new_rows = at_row(new, new_at)
+    border = at_row(new_gram + mul_t(new_gram, new_rows), new_at)
+    body = jnp.concatenate([gram[0:new_at], new_gram, gram[new_at + 8:]], axis=0)
     image = (jnp.where((lane >= 32) & (lane < 48), lane_roll(new, 32), 0.0)
              + jnp.where((lane >= 24) & (lane < 32), lane_roll(new, 8), 0.0)
              + jnp.where((lane >= 48) & (lane < 56), lane_roll(new, 24), 0.0))
-    window = jnp.where((tall < 16) & (wide == tall + 8), 1.0, 0.0)
-    window = jnp.concatenate([window[0:16], new, window[24:]], axis=0)
-
-    def project(rows):
-        return mul(mul_t(mul(rows, gram), window), window)
-
-    once = project(image)
-    again = project(once)
-    newest = normalise(image - (2.0 * once - again))
-    return new, newest
+    inside = ((lane >= 8) & (lane < 24)) | ((lane >= new_at) & (lane < new_at + 8))
+
+    def times_gram(value):
+        return mul(value, body) + mul_t(value, border)
+
+    once = jnp.where(inside, times_gram(image), 0.0)
+    again = jnp.where(inside, times_gram(once), 0.0)
+    rows = image - (2.0 * once - again)
+    spread = at_row(rows, 0)
+    newest = mul(inverse_factor(mul_t(times_gram(rows), spread)), spread)
+    on_new = jnp.where((lane >= new_at) & (lane < new_at + 8), newest, 0.0)
+    return new, newest - on_new + mul(on_new, new_rows)
 
 
 def final_kernel(cells, parts, start, w, old_image, w_image, out):

time: 91.4 us -> 90.3 us (0.988)
  Pallas kernels: 9.58 us -> 8.4 us
    pallas_call x1, Pallas kernels: 5.11 us -> 3.93 us  [finish(): pl.pallas_call(functools.partial(final_kernel, cells), out_shape=jax.Shap...]
where the time goes in v10:
time: 90.3 us; the launch traced here: 89.8 us
  blocking collectives  44 us (49%)
  starting transfers between devices  24.3 us (27%)
  waiting for transfers between devices  11 us (12%)
  Pallas kernels  8.4 us (9%)
  local copies, waits for them, and re-layouts  1.96 us (2%)
    all_to_all x1, blocking collectives, per_device(): got = lax.all_to_all(sum_and_spread(got, nz), 'z', 0, 0)  28.2 us
    ppermute x4, starting transfers between devices, from_both(): lax.ppermute(to_higher, axis, [(i, i + step) for i in range(count - step)])  17 us
    all_to_all x1, blocking collectives, per_device(): got = lax.all_to_all(spread, ('core', 'gy'), 0, 0)  15.7 us
    ppermute x4, waiting for transfers between devices, from_both(): lax.ppermute(to_lower, axis, [(i + step, i) for i in range(count - step)])  8.9 us
    ppermute x4, starting transfers between devices, from_both(): lax.ppermute(to_lower, axis, [(i + step, i) for i in range(count - step)])  7.3 us
    pallas_call x1, Pallas kernels, finish(): pl.pallas_call(functools.partial(final_kernel, cells), out_shape=jax.Shap...  3.93 us
    ppermute x4, waiting for transfers between devices, from_both(): lax.ppermute(to_higher, axis, [(i, i + step) for i in range(count - step)])  2.08 us
  transfers between devices with their start and end apart: 8, of which 4 were waited for; matrix products, arithmetic and copies ran while one was open for 0% of the time, Pallas kernels for 3%

profile of v10, /device:TPU:1, one launch (start us, length us, event | category | flops | bytes accessed | tf_op | source)
XLA Modules:
  0.0 89.8 jit_solution(18212449244877924362)
XLA Ops:
  0.0 1.3 %copy.3 = f32[4,3,8,2,4,128]{5,4,3,2,1,0:T(4,128)S(1)} copy(f32[4,3,8,2,4,128]{5,2,0,4,3,1:T(8,128)} %bitcast.7) | data formatting | bytes 786432 | tf_op jit(solution)/shard_map/transpose | solution.py:503
  1.3 0.0 copy-start
  1.3 0.7 copy-done
  2.0 4.0 %collective-permute-start = (f32[4,136,128]{2,1,0:T(8,128)S(1)}, f32[4,136,128]{2,1,0:T(8,128)S(1)}, u32[]{:S(2)}, u32[]{:S(2)}) collective-permute-start(f32[4,136,128]{2,1,0:T(8,128)S(1)} %pad_maximum_fusion.1), channel_id=1, source_target_pairs={{0,1},{1,2},{2,3},{3,4},{4,5},{5,6},{6,7},{7,8},{8,9},{9,10},{10,1... | collective-permute-start | bytes 835592 | tf_op jit(solution)/shard_map/ppermute | solution.py:496
  6.1 1.3 %collective-permute-start.1 = (f32[4,136,128]{2,1,0:T(8,128)S(1)}, f32[4,136,128]{2,1,0:T(8,128)S(1)}, u32[]{:S(2)}, u32[]{:S(2)}) collective-permute-start(f32[4,136,128]{2,1,0:T(8,128)S(1)} %pad_maximum_fusion.2), channel_id=1, source_target_pairs={{1,0},{2,1},{3,2},{4,3},{5,4},{6,5},{7,6},{8,7},{9,8},{10,9},{11,1... | collective-permute-start | bytes 835592 | tf_op jit(solution)/shard_map/ppermute | solution.py:497
  7.5 2.1 %collective-permute-done.below = f32[4,136,128]{2,1,0:T(8,128)S(1)} collective-permute-done((f32[4,136,128]{2,1,0:T(8,128)S(1)}, f32[4,136,128]{2,1,0:T(8,128)S(1)}, u32[]{:S(2)}, u32[]{:S(2)}) %collective-permute-start) | collective-permute-done | bytes 278560 | tf_op jit(solution)/shard_map/ppermute | solution.py:496
  9.5 3.9 %collective-permute-done.1.above = f32[4,136,128]{2,1,0:T(8,128)S(1)} collective-permute-done((f32[4,136,128]{2,1,0:T(8,128)S(1)}, f32[4,136,128]{2,1,0:T(8,128)S(1)}, u32[]{:S(2)}, u32[]{:S(2)}) %collective-permute-start.1) | collective-permute-done | bytes 278560 | tf_op jit(solution)/shard_map/ppermute | solution.py:497
  13.4 0.1 pack_all.1
  13.5 7.1 %collective-permute-start.2 = (f32[94,8,128]{2,1,0:T(8,128)S(1)}, f32[94,8,128]{2,1,0:T(8,128)S(1)}, u32[]{:S(2)}, u32[]{:S(2)}) collective-permute-start(f32[94,8,128]{2,1,0:T(8,128)S(1)} %get-tuple-element.15), channel_id=1, source_target_pairs={{0,16},{16,32},{32,48},{48,64},{64,80},{80,96},{96,112},{112,128},... | collective-permute-start | bytes 1155080 | tf_op jit(solution)/shard_map/ppermute | solution.py:496
  20.6 1.9 %collective-permute-start.3 = (f32[94,8,128]{2,1,0:T(8,128)S(1)}, f32[94,8,128]{2,1,0:T(8,128)S(1)}, u32[]{:S(2)}, u32[]{:S(2)}) collective-permute-start(f32[94,8,128]{2,1,0:T(8,128)S(1)} %get-tuple-element.16), channel_id=1, source_target_pairs={{16,0},{32,16},{48,32},{64,48},{80,64},{96,80},{112,96},{128,112},... | collective-permute-start | bytes 1155080 | tf_op jit(solution)/shard_map/ppermute | solution.py:497
  22.6 3.6 %collective-permute-start.6 = (f32[80,8,128]{2,1,0:T(8,128)S(1)}, f32[80,8,128]{2,1,0:T(8,128)S(1)}, u32[]{:S(2)}, u32[]{:S(2)}) collective-permute-start(f32[80,8,128]{2,1,0:T(8,128)S(1)} %get-tuple-element.21), channel_id=1, source_target_pairs={{0,16},{16,32},{32,48},{48,64},{64,80},{80,96},{96,112},{112,128},... | collective-permute-start | bytes 983048 | tf_op jit(solution)/shard_map/ppermute | solution.py:496
  26.2 1.9 %collective-permute-start.7 = (f32[80,8,128]{2,1,0:T(8,128)S(1)}, f32[80,8,128]{2,1,0:T(8,128)S(1)}, u32[]{:S(2)}, u32[]{:S(2)}) collective-permute-start(f32[80,8,128]{2,1,0:T(8,128)S(1)} %get-tuple-element.22), channel_id=1, source_target_pairs={{16,0},{32,16},{48,32},{64,48},{80,64},{96,80},{112,96},{128,112},... | collective-permute-start | bytes 983048 | tf_op jit(solution)/shard_map/ppermute | solution.py:497
  28.2 0.0 collective-permute-done.2.low.first_low
  28.2 1.5 %collective-permute-done.3.high.first_high = f32[94,8,128]{2,1,0:T(8,128)S(1)} collective-permute-done((f32[94,8,128]{2,1,0:T(8,128)S(1)}, f32[94,8,128]{2,1,0:T(8,128)S(1)}, u32[]{:S(2)}, u32[]{:S(2)}) %collective-permute-start.3) | collective-permute-done | bytes 385056 | tf_op jit(solution)/shard_map/ppermute | solution.py:497
  29.7 1.4 %first_image.1 = (f32[4,16,8,128]{3,2,1,0:T(8,128)S(1)}, f32[12,24,128]{2,1,0:T(8,128)S(1)}, f32[44,8,128]{2,1,0:T(8,128)S(1)}, f32[44,8,128]{2,1,0:T(8,128)S(1)}) custom-call(f32[4,200,128]{2,1,0:T(8,128)S(1)} %pad_maximum_fusion.own.start, f32[4,136,128]{2,1,0:T(8,128)S(1)} %collective-permute-done.below, f32[4,136,128]{2,1,0:T(8,128)S(1)} %collective-permute-done.1.above, ...), custom_call_target="tpu_custom_call" | custom-call | flops 12000000 | bytes 18000000 | tf_op jit(solution)/shard_map/first_image/pallas_call | solution.py:224
  31.1 2.2 %collective-permute-start.4 = (f32[44,8,128]{2,1,0:T(8,128)S(1)}, f32[44,8,128]{2,1,0:T(8,128)S(1)}, u32[]{:S(2)}, u32[]{:S(2)}) collective-permute-start(f32[44,8,128]{2,1,0:T(8,128)S(1)} %get-tuple-element.19), channel_id=1, source_target_pairs={{0,16},{16,32},{32,48},{48,64},{64,80},{80,96},{96,112},{112,128},... | collective-permute-start | bytes 540680 | tf_op jit(solution)/shard_map/ppermute | solution.py:496
  33.2 2.2 %collective-permute-start.5 = (f32[44,8,128]{2,1,0:T(8,128)S(1)}, f32[44,8,128]{2,1,0:T(8,128)S(1)}, u32[]{:S(2)}, u32[]{:S(2)}) collective-permute-start(f32[44,8,128]{2,1,0:T(8,128)S(1)} %get-tuple-element.20), channel_id=1, source_target_pairs={{16,0},{32,16},{48,32},{64,48},{80,64},{96,80},{112,96},{128,112},... | collective-permute-start | bytes 540680 | tf_op jit(solution)/shard_map/ppermute | solution.py:497
  35.4 0.0 collective-permute-done.6.low
  35.4 0.0 collective-permute-done.7.high
  35.4 1.4 %old_images.1.old_image = f32[4,128,128]{2,1,0:T(8,128)S(1)} custom-call(f32[12,24,128]{2,1,0:T(8,128)S(1)} %get-tuple-element.18.coef, f32[4,200,128]{2,1,0:T(8,128)S(1)} %pad_maximum_fusion.own.start, f32[4,136,128]{2,1,0:T(8,128)S(1)} %collective-permute-done.below, f32[4,136,128]{2,1,0:T(8,128)S(1)} %collective-permute-done.1.above, ...), custom_call_target="tpu_custom_call" | custom-call | flops 12000000 | bytes 24000000 | tf_op jit(solution)/shard_map/old_images/pallas_call | solution.py:256
  36.9 0.0 collective-permute-done.4.low
  36.9 3.5 %collective-permute-done.5.high = f32[44,8,128]{2,1,0:T(8,128)S(1)} collective-permute-done((f32[44,8,128]{2,1,0:T(8,128)S(1)}, f32[44,8,128]{2,1,0:T(8,128)S(1)}, u32[]{:S(2)}, u32[]{:S(2)}) %collective-permute-start.5) | collective-permute-done | bytes 180256 | tf_op jit(solution)/shard_map/ppermute | solution.py:497
  40.4 1.5 %image_and_gram.1 = (f32[4,64,128]{2,1,0:T(8,128)S(1)}, f32[32,8,128]{2,1,0:T(8,128)S(1)}) custom-call(f32[4,16,8,128]{3,2,1,0:T(8,128)S(1)} %get-tuple-element.17.w, f32[12,24,128]{2,1,0:T(8,128)S(1)} %get-tuple-element.18.coef, f32[44,8,128]{2,1,0:T(8,128)S(1)} %collective-permute-done.4.low, f32[44,8,128]{2,1,0:T(8,128)S(1)} %collective-permute-done.5.high, ...), custom_call_target="tpu_custom_call" | custom-call | tf_op jit(solution)/shard_map/image_and_gram/pallas_call | solution.py:360
  41.9 15.7 %all_to_all.10.parts = f32[32,8,128]{2,1,0:T(8,128)S(1)} all-to-all(f32[32,8,128]{2,1,0:T(8,128)S(1)} %get-tuple-element.23), channel_id=1, replica_groups=mesh['z'=16,'core'=2,'gy'=16] {'core','gy'}, dimensions={0} | all-to-all | bytes 262144 | tf_op jit(solution)/shard_map/all_to_all | solution.py:516
  57.7 28.2 %all_to_all.11.parts = f32[16,8,128]{2,1,0:T(8,128)S(1)} all-to-all(f32[16,8,128]{2,1,0:T(8,128)S(1)} %sum_and_spread.1), channel_id=1, replica_groups=mesh['z'=16,'core'=2,'gy'=16] {'z'}, dimensions={0} | all-to-all | bytes 131072 | tf_op jit(solution)/shard_map/all_to_all | solution.py:517
  85.9 3.9 %finish.1 = f32[2,8,4,8,128]{4,3,2,1,0:T(8,128)} custom-call(f32[16,8,128]{2,1,0:T(8,128)S(1)} %all_to_all.11.parts, f32[4,200,128]{2,1,0:T(8,128)S(1)} %pad_maximum_fusion.own.start, f32[4,16,8,128]{3,2,1,0:T(8,128)S(1)} %get-tuple-element.17.w, f32[4,128,128]{2,1,0:T(8,128)S(1)} %old_images.1.old_image, f32[4,64,128]{2,1,0:T(8,128)S(1)} %get-tuple-element.24.w_image), custom_call_target="tpu_custom_call" | custom-call | tf_op jit(solution)/shard_map/finish/pallas_call | solution.py:481
  (7 shorter events, 0.2 us)
Async XLA Ops:
  1.3 0.7 copy-start
  2.0 7.5 %collective-permute-start = (f32[4,136,128]{2,1,0:T(8,128)S(1)}, f32[4,136,128]{2,1,0:T(8,128)S(1)}, u32[]{:S(2)}, u32[]{:S(2)}) collective-permute-start(f32[4,136,128]{2,1,0:T(8,128)S(1)} %pad_maximum_fusion.1), channel_id=1, source_target_pairs={{0,1},{1,2},{2,3},{3,4},{4,5},{5,6},{6,7},{7,8},{8,9},{9,10},{10,1... | collective-permute-start | bytes 835592 | tf_op jit(solution)/shard_map/ppermute | solution.py:496
  6.1 7.3 %collective-permute-start.1 = (f32[4,136,128]{2,1,0:T(8,128)S(1)}, f32[4,136,128]{2,1,0:T(8,128)S(1)}, u32[]{:S(2)}, u32[]{:S(2)}) collective-permute-start(f32[4,136,128]{2,1,0:T(8,128)S(1)} %pad_maximum_fusion.2), channel_id=1, source_target_pairs={{1,0},{2,1},{3,2},{4,3},{5,4},{6,5},{7,6},{8,7},{9,8},{10,9},{11,1... | collective-permute-start | bytes 835592 | tf_op jit(solution)/shard_map/ppermute | solution.py:497
  13.5 14.6 %collective-permute-start.2 = (f32[94,8,128]{2,1,0:T(8,128)S(1)}, f32[94,8,128]{2,1,0:T(8,128)S(1)}, u32[]{:S(2)}, u32[]{:S(2)}) collective-permute-start(f32[94,8,128]{2,1,0:T(8,128)S(1)} %get-tuple-element.15), channel_id=1, source_target_pairs={{0,16},{16,32},{32,48},{48,64},{64,80},{80,96},{96,112},{112,128},... | collective-permute-start | bytes 1155080 | tf_op jit(solution)/shard_map/ppermute | solution.py:496
  20.6 9.0 %collective-permute-start.3 = (f32[94,8,128]{2,1,0:T(8,128)S(1)}, f32[94,8,128]{2,1,0:T(8,128)S(1)}, u32[]{:S(2)}, u32[]{:S(2)}) collective-permute-start(f32[94,8,128]{2,1,0:T(8,128)S(1)} %get-tuple-element.16), channel_id=1, source_target_pairs={{16,0},{32,16},{48,32},{64,48},{80,64},{96,80},{112,96},{128,112},... | collective-permute-start | bytes 1155080 | tf_op jit(solution)/shard_map/ppermute | solution.py:497
  22.6 12.8 %collective-permute-start.6 = (f32[80,8,128]{2,1,0:T(8,128)S(1)}, f32[80,8,128]{2,1,0:T(8,128)S(1)}, u32[]{:S(2)}, u32[]{:S(2)}) collective-permute-start(f32[80,8,128]{2,1,0:T(8,128)S(1)} %get-tuple-element.21), channel_id=1, source_target_pairs={{0,16},{16,32},{32,48},{48,64},{64,80},{80,96},{96,112},{112,128},... | collective-permute-start | bytes 983048 | tf_op jit(solution)/shard_map/ppermute | solution.py:496
  26.2 9.2 %collective-permute-start.7 = (f32[80,8,128]{2,1,0:T(8,128)S(1)}, f32[80,8,128]{2,1,0:T(8,128)S(1)}, u32[]{:S(2)}, u32[]{:S(2)}) collective-permute-start(f32[80,8,128]{2,1,0:T(8,128)S(1)} %get-tuple-element.22), channel_id=1, source_target_pairs={{16,0},{32,16},{48,32},{64,48},{80,64},{96,80},{112,96},{128,112},... | collective-permute-start | bytes 983048 | tf_op jit(solution)/shard_map/ppermute | solution.py:497
  31.1 5.8 %collective-permute-start.4 = (f32[44,8,128]{2,1,0:T(8,128)S(1)}, f32[44,8,128]{2,1,0:T(8,128)S(1)}, u32[]{:S(2)}, u32[]{:S(2)}) collective-permute-start(f32[44,8,128]{2,1,0:T(8,128)S(1)} %get-tuple-element.19), channel_id=1, source_target_pairs={{0,16},{16,32},{32,48},{48,64},{64,80},{80,96},{96,112},{112,128},... | collective-permute-start | bytes 540680 | tf_op jit(solution)/shard_map/ppermute | solution.py:496
  33.2 7.2 %collective-permute-start.5 = (f32[44,8,128]{2,1,0:T(8,128)S(1)}, f32[44,8,128]{2,1,0:T(8,128)S(1)}, u32[]{:S(2)}, u32[]{:S(2)}) collective-permute-start(f32[44,8,128]{2,1,0:T(8,128)S(1)} %get-tuple-element.20), channel_id=1, source_target_pairs={{16,0},{32,16},{48,32},{64,48},{80,64},{96,80},{112,96},{128,112},... | collective-permute-start | bytes 540680 | tf_op jit(solution)/shard_map/ppermute | solution.py:497

commit v11 on v10

--- a/solution.py
+++ b/solution.py
@@ -32,9 +32,8 @@
 NEAR_SPANS, NEAR_SIZE = spans(NEAR, 0, LX)
 SIDE_SPANS, SIDE_SIZE = spans(FAR, 0, LX)
 FLAT_TILES = -(-SIDE_SIZE // 8)
-SPLIT = NEAR_SPANS[-1][2]
-FIRST_TILES = SIDE_SIZE + FLAT_TILES + NEAR_SIZE - SPLIT
-SECOND_TILES = SPLIT + NEAR_SIZE
+FIRST_TILES = SIDE_SIZE + FLAT_TILES
+SECOND_TILES = 3 * NEAR_SIZE
 
 
 def pack_columns(out, start, found, to_higher, rows, reach):
@@ -63,30 +62,29 @@
             out[start + spot // 8, pl.ds(spot % 8, 1), :] = ref[x, pl.ds(row, 1), :]
 
 
-def column_kernel(own, below, above, right, left, old_right, old_left):
-    for first, second, to_higher in ((right, old_right, True), (left, old_left, False)):
+def column_kernel(own, below, above, right, left):
+    for out, to_higher in ((right, True), (left, False)):
         rows = [(below, 2 * HALF), (own, 2 * BLOCK), (above, 2 * HALF)]
-        pack_columns(first, 0, SIDE_SPANS, to_higher, rows, FAR)
+        pack_columns(out, 0, SIDE_SPANS, to_higher, rows, FAR)
         if SIDE_SIZE % 8:
-            first[SIDE_SIZE + FLAT_TILES - 1] = jnp.zeros((8, NZ), F32)
-        pack_coefficient(first, SIDE_SIZE, SIDE_SPANS, to_higher, below, own, above)
-        rows = [(below, 0), (own, 0), (above, 0)]
-        pack_columns(second, 0, NEAR_SPANS[:-1], to_higher, rows, NEAR)
-        pack_columns(first, SIDE_SIZE + FLAT_TILES - SPLIT, NEAR_SPANS[-1:], to_higher, rows, NEAR)
-        rows = [(below, HALF), (own, BLOCK), (above, HALF)]
-        pack_columns(second, SPLIT, NEAR_SPANS, to_higher, rows, NEAR)
-
-
-def pack_all(*args):
-    shapes = tuple(jax.ShapeDtypeStruct((size, 8, NZ), F32) for size in [FIRST_TILES] * 2 + [SECOND_TILES] * 2)
+            out[SIDE_SIZE + FLAT_TILES - 1] = jnp.zeros((8, NZ), F32)
+        pack_coefficient(out, SIDE_SIZE, SIDE_SPANS, to_higher, below, own, above)
+
+
+def pack_recent(*args):
+    shape = jax.ShapeDtypeStruct((FIRST_TILES, 8, NZ), F32)
     return pl.pallas_call(
         column_kernel,
-        out_shape=shapes,
+        out_shape=(shape, shape),
         in_specs=[VMEM] * 3,
-        out_specs=(VMEM,) * 4,
+        out_specs=(VMEM, VMEM),
         compiler_params=pltpu.CompilerParams(vmem_limit_bytes=1 << 20),
-        name="pack_all",
+        name="pack_recent",
     )(*args)
+
+
+def old_rows(below, own, above, group):
+    return [(below, group * HALF), (own, group * BLOCK), (above, group * HALF)]
 
 
 def fill_sides(wide, halo, sides):
@@ -213,14 +211,18 @@
         w[x, y] = value
 
     smooth(block, coef, 0, table_re, table_im, first, second, store)
+    for group in range(2):
+        rows = old_rows(below, own, above, group)
+        pack_columns(out_right, group * NEAR_SIZE, NEAR_SPANS, True, rows, NEAR)
+        pack_columns(out_left, group * NEAR_SIZE, NEAR_SPANS, False, rows, NEAR)
     for d, more, place in NEAR_SPANS:
-        count = LY + 2 * more
-        out_right[pl.ds(place, count)] = w[LX - d, pl.ds(NEAR - more, count)]
-        out_left[pl.ds(place, count)] = w[d - 1, pl.ds(NEAR - more, count)]
+        count, spot = LY + 2 * more, 2 * NEAR_SIZE + place
+        out_right[pl.ds(spot, count)] = w[LX - d, pl.ds(NEAR - more, count)]
+        out_left[pl.ds(spot, count)] = w[d - 1, pl.ds(NEAR - more, count)]
 
 
 def first_image(*args):
-    side = jax.ShapeDtypeStruct((NEAR_SIZE, 8, NZ), F32)
+    side = jax.ShapeDtypeStruct((SECOND_TILES, 8, NZ), F32)
     return pl.pallas_call(
         first_kernel,
         out_shape=(jax.ShapeDtypeStruct((LX, LY + 2 * NEAR, 8, NZ), F32),
@@ -231,37 +233,6 @@
         compiler_params=pltpu.CompilerParams(vmem_limit_bytes=16 << 20),
         cost_estimate=pl.CostEstimate(flops=12_000_000, bytes_accessed=18_000_000, transcendentals=0),
         name="first_image",
-    )(*args)
-
-
-def old_kernel(coef, own, below, above, low, high, first_low, first_high, out, block, first, second,
-               table_re, table_im, diag_re, diag_im):
-    fill_tables(coef, FAR - NEAR, table_re, table_im, diag_re, diag_im)
-    for group in range(2):
-        rows = [(below, group * HALF), (own, group * BLOCK), (above, group * HALF)]
-        if group == 0:
-            sides = [(low, high, 0, NEAR_SPANS[:-1]),
-                     (first_low, first_high, SIDE_SIZE + FLAT_TILES - SPLIT, NEAR_SPANS[-1:])]
-        else:
-            sides = [(low, high, SPLIT, NEAR_SPANS)]
-        fill_block(block, NEAR, rows, NEAR, sides)
-
-        def store(x, y, value, group=group):
-            out[x, pl.ds(group * BLOCK + y * 8, 8), :] = value
-
-        smooth(block, coef, FAR - NEAR, table_re, table_im, first, second, store)
-
-
-def old_images(*args):
-    return pl.pallas_call(
-        old_kernel,
-        out_shape=jax.ShapeDtypeStruct((LX, 2 * BLOCK, NZ), F32),
-        in_specs=[VMEM] * 8,
-        out_specs=VMEM,
-        scratch_shapes=smooth_scratch(NEAR),
-        compiler_params=pltpu.CompilerParams(vmem_limit_bytes=16 << 20),
-        cost_estimate=pl.CostEstimate(flops=12_000_000, bytes_accessed=24_000_000, transcendentals=0),
-        name="old_images",
     )(*args)
 
 
@@ -330,13 +301,21 @@
     return jnp.where(tall // 8 <= wide // 8, upper, upper.T)
 
 
-def gram_kernel(peers, w, coef, low, high, start, old_image, w_image, out,
+def gram_kernel(peers, w, coef, low, high, start, below, above, old_image, w_image, out,
                 block, first, second, table_re, table_im, diag_re, diag_im):
     fill_tables(coef, FAR - NEAR, table_re, table_im, diag_re, diag_im)
+    for group in range(2):
+        rows = old_rows(below, start, above, group)
+        fill_block(block, NEAR, rows, NEAR, [(low, high, group * NEAR_SIZE, NEAR_SPANS)])
+
+        def store_old(x, y, value, group=group):
+            old_image[x, pl.ds(group * BLOCK + y * 8, 8), :] = value
+
+        smooth(block, coef, FAR - NEAR, table_re, table_im, first, second, store_old)
     block[...] = jnp.zeros(block.shape, F32)
     for x in range(LX):
         block[NEAR + x] = w[x]
-    fill_sides(block, NEAR, [(low, high, 0, NEAR_SPANS)])
+    fill_sides(block, NEAR, [(low, high, 2 * NEAR_SIZE, NEAR_SPANS)])
 
     def store(x, y, value):
         w_image[x, pl.ds(y * 8, 8), :] = value
@@ -356,16 +335,17 @@
         out[peer] = packed
 
 
-def image_and_gram(peers, *args):
+def images_and_gram(peers, *args):
     return pl.pallas_call(
         functools.partial(gram_kernel, peers),
-        out_shape=(jax.ShapeDtypeStruct((LX, LY * 8, NZ), F32),
+        out_shape=(jax.ShapeDtypeStruct((LX, 2 * BLOCK, NZ), F32),
+                   jax.ShapeDtypeStruct((LX, BLOCK, NZ), F32),
                    jax.ShapeDtypeStruct((peers, 8, NZ), F32)),
-        in_specs=[VMEM] * 6,
-        out_specs=(VMEM, VMEM),
+        in_specs=[VMEM] * 7,
+        out_specs=(VMEM,) * 3,
         scratch_shapes=smooth_scratch(NEAR),
-        compiler_params=pltpu.CompilerParams(vmem_limit_bytes=32 << 20),
-        name="image_and_gram",
+        compiler_params=pltpu.CompilerParams(vmem_limit_bytes=24 << 20),
+        name="images_and_gram",
     )(*args)
 
 
@@ -491,10 +471,10 @@
 GX = ("z", "core")
 
 
-def from_both(axis, count, to_higher, to_lower, step=1):
+def from_both(axis, count, to_higher, to_lower):
     return (
-        lax.ppermute(to_higher, axis, [(i, i + step) for i in range(count - step)]),
-        lax.ppermute(to_lower, axis, [(i + step, i) for i in range(count - step)]),
+        lax.ppermute(to_higher, axis, [(i, i + 1) for i in range(count - 1)]),
+        lax.ppermute(to_lower, axis, [(i + 1, i) for i in range(count - 1)]),
     )
 
 
@@ -505,14 +485,10 @@
     up = jnp.concatenate([start[:, HALF:BLOCK], start[:, BLOCK + HALF:]], axis=1)
     down = jnp.concatenate([start[:, :HALF], start[:, BLOCK:BLOCK + HALF], start[:, 2 * BLOCK:]], axis=1)
     rims = from_both("gy", ny, up, down)
-    right, left, old_right, old_left = pack_all(start, *rims)
+    sides = from_both(GX, nx, *pack_recent(start, *rims))
+    w, coef, right, left = first_image(start, *rims, *sides)
     sides = from_both(GX, nx, right, left)
-    old_sides = from_both(GX, nx, old_right, old_left)
-    w, coef, w_right, w_left = first_image(start, *rims, *sides)
-    w_sides = from_both(GX, nx, w_right, w_left)
-    old_image = old_images(coef, start, *rims, *old_sides, *sides)
-
-    w_image, spread = image_and_gram(2 * ny, w, coef, *w_sides, start, old_image)
+    old_image, w_image, spread = images_and_gram(2 * ny, w, coef, *sides, start, *rims)
     got = lax.all_to_all(spread, ("core", "gy"), 0, 0)
     got = lax.all_to_all(sum_and_spread(got, nz), "z", 0, 0)
     out = finish(cells, got, start, w, old_image, w_image)

time: 90.3 us -> 93.5 us (1.035)
  waiting for transfers between devices: 11 us -> 21.2 us
  starting transfers between devices: 24.3 us -> 18.7 us
  blocking collectives: 44 us -> 42.8 us
    ppermute x8 -> x6, waiting for transfers between devices: 11 us -> 21.2 us  [the longest x3 13 us: from_both(): lax.ppermute(to_lower, axis, [(i + 1, i) for i in range(count - 1)])]
    ppermute x8 -> x6, starting transfers between devices: 24.3 us -> 18.7 us  [the longest x3 13.1 us: from_both(): lax.ppermute(to_higher, axis, [(i, i + 1) for i in range(count - 1)])]
    all_to_all x1, blocking collectives: 28.2 us -> 27.1 us  [per_device(): got = lax.all_to_all(sum_and_spread(got, nz), 'z', 0, 0)]
    pallas_call x3 -> x2, Pallas kernels: 3.02 us -> 2.83 us  [the longest x1 2.75 us: images_and_gram(): pl.pallas_call(functools.partial(gram_kernel, peers), out_shape=(jax.Shap...]
  transfers between devices with their start and end apart: 8 -> 6, of which waited for: 4 -> 6; matrix products, arithmetic and copies ran while one was open for 0% -> 0% of each run, Pallas kernels for 3% -> 0%
where the time goes in v11:
time: 93.5 us; the launch traced here: 93.1 us
  blocking collectives  42.8 us (46%)
  waiting for transfers between devices  21.2 us (23%)
  starting transfers between devices  18.7 us (20%)
  Pallas kernels  8.24 us (9%)
  local copies, waits for them, and re-layouts  1.96 us (2%)
    all_to_all x1, blocking collectives, per_device(): got = lax.all_to_all(sum_and_spread(got, nz), 'z', 0, 0)  27.1 us
    all_to_all x1, blocking collectives, per_device(): got = lax.all_to_all(spread, ('core', 'gy'), 0, 0)  15.7 us
    ppermute x3, starting transfers between devices, from_both(): lax.ppermute(to_higher, axis, [(i, i + 1) for i in range(count - 1)])  13.1 us
    ppermute x3, waiting for transfers between devices, from_both(): lax.ppermute(to_lower, axis, [(i + 1, i) for i in range(count - 1)])  13 us
    ppermute x3, waiting for transfers between devices, from_both(): lax.ppermute(to_higher, axis, [(i, i + 1) for i in range(count - 1)])  8.24 us
    ppermute x3, starting transfers between devices, from_both(): lax.ppermute(to_lower, axis, [(i + 1, i) for i in range(count - 1)])  5.65 us
    pallas_call x1, Pallas kernels, finish(): pl.pallas_call(functools.partial(final_kernel, cells), out_shape=jax.Shap...  3.93 us
    pallas_call x1, Pallas kernels, images_and_gram(): pl.pallas_call(functools.partial(gram_kernel, peers), out_shape=(jax.Shap...  2.75 us
  transfers between devices with their start and end apart: 6, of which 6 were waited for; matrix products, arithmetic and copies ran while one was open for 0% of the time, Pallas kernels for 0%

profile of v11, /device:TPU:1, one launch (start us, length us, event | category | flops | bytes accessed | tf_op | source)
XLA Modules:
  0.0 93.1 jit_solution(18230822191317116989)
XLA Ops:
  0.0 1.3 %copy.3 = f32[4,3,8,2,4,128]{5,4,3,2,1,0:T(4,128)S(1)} copy(f32[4,3,8,2,4,128]{5,2,0,4,3,1:T(8,128)} %bitcast.7) | data formatting | bytes 786432 | tf_op jit(solution)/shard_map/transpose | solution.py:483
  1.3 0.0 copy-start
  1.3 0.7 copy-done
  2.0 4.0 %collective-permute-start = (f32[4,136,128]{2,1,0:T(8,128)S(1)}, f32[4,136,128]{2,1,0:T(8,128)S(1)}, u32[]{:S(2)}, u32[]{:S(2)}) collective-permute-start(f32[4,136,128]{2,1,0:T(8,128)S(1)} %pad_maximum_fusion.1), channel_id=1, source_target_pairs={{0,1},{1,2},{2,3},{3,4},{4,5},{5,6},{6,7},{7,8},{8,9},{9,10},{10,1... | collective-permute-start | bytes 835592 | tf_op jit(solution)/shard_map/ppermute | solution.py:476
  6.1 1.3 %collective-permute-start.1 = (f32[4,136,128]{2,1,0:T(8,128)S(1)}, f32[4,136,128]{2,1,0:T(8,128)S(1)}, u32[]{:S(2)}, u32[]{:S(2)}) collective-permute-start(f32[4,136,128]{2,1,0:T(8,128)S(1)} %pad_maximum_fusion.2), channel_id=1, source_target_pairs={{1,0},{2,1},{3,2},{4,3},{5,4},{6,5},{7,6},{8,7},{9,8},{10,9},{11,1... | collective-permute-start | bytes 835592 | tf_op jit(solution)/shard_map/ppermute | solution.py:477
  7.5 2.1 %collective-permute-done.below = f32[4,136,128]{2,1,0:T(8,128)S(1)} collective-permute-done((f32[4,136,128]{2,1,0:T(8,128)S(1)}, f32[4,136,128]{2,1,0:T(8,128)S(1)}, u32[]{:S(2)}, u32[]{:S(2)}) %collective-permute-start) | collective-permute-done | bytes 278560 | tf_op jit(solution)/shard_map/ppermute | solution.py:476
  9.5 3.9 %collective-permute-done.1.above = f32[4,136,128]{2,1,0:T(8,128)S(1)} collective-permute-done((f32[4,136,128]{2,1,0:T(8,128)S(1)}, f32[4,136,128]{2,1,0:T(8,128)S(1)}, u32[]{:S(2)}, u32[]{:S(2)}) %collective-permute-start.1) | collective-permute-done | bytes 278560 | tf_op jit(solution)/shard_map/ppermute | solution.py:477
  13.4 0.1 pack_recent.1
  13.5 7.1 %collective-permute-start.2 = (f32[86,8,128]{2,1,0:T(8,128)S(1)}, f32[86,8,128]{2,1,0:T(8,128)S(1)}, u32[]{:S(2)}, u32[]{:S(2)}) collective-permute-start(f32[86,8,128]{2,1,0:T(8,128)S(1)} %get-tuple-element.14), channel_id=1, source_target_pairs={{0,16},{16,32},{32,48},{48,64},{64,80},{80,96},{96,112},{112,128},... | collective-permute-start | bytes 1056776 | tf_op jit(solution)/shard_map/ppermute | solution.py:476
  20.6 1.9 %collective-permute-start.3 = (f32[86,8,128]{2,1,0:T(8,128)S(1)}, f32[86,8,128]{2,1,0:T(8,128)S(1)}, u32[]{:S(2)}, u32[]{:S(2)}) collective-permute-start(f32[86,8,128]{2,1,0:T(8,128)S(1)} %get-tuple-element.15), channel_id=1, source_target_pairs={{16,0},{32,16},{48,32},{64,48},{80,64},{96,80},{112,96},{128,112},... | collective-permute-start | bytes 1056776 | tf_op jit(solution)/shard_map/ppermute | solution.py:477
  22.5 2.3 %collective-permute-done.2.low = f32[86,8,128]{2,1,0:T(8,128)S(1)} collective-permute-done((f32[86,8,128]{2,1,0:T(8,128)S(1)}, f32[86,8,128]{2,1,0:T(8,128)S(1)}, u32[]{:S(2)}, u32[]{:S(2)}) %collective-permute-start.2) | collective-permute-done | bytes 352288 | tf_op jit(solution)/shard_map/ppermute | solution.py:476
  24.9 4.4 %collective-permute-done.3.high = f32[86,8,128]{2,1,0:T(8,128)S(1)} collective-permute-done((f32[86,8,128]{2,1,0:T(8,128)S(1)}, f32[86,8,128]{2,1,0:T(8,128)S(1)}, u32[]{:S(2)}, u32[]{:S(2)}) %collective-permute-start.3) | collective-permute-done | bytes 352288 | tf_op jit(solution)/shard_map/ppermute | solution.py:477
  29.3 1.4 %first_image.1 = (f32[4,16,8,128]{3,2,1,0:T(8,128)S(1)}, f32[12,24,128]{2,1,0:T(8,128)S(1)}, f32[132,8,128]{2,1,0:T(8,128)S(1)}, f32[132,8,128]{2,1,0:T(8,128)S(1)}) custom-call(f32[4,200,128]{2,1,0:T(8,128)S(1)} %pad_maximum_fusion.own.start, f32[4,136,128]{2,1,0:T(8,128)S(1)} %collective-permute-done.below, ...), custom_call_target="tpu_custom_call" | custom-call | flops 12000000 | bytes 18000000 | tf_op jit(solution)/shard_map/first_image/pallas_call | solution.py:226
  30.7 1.9 %collective-permute-start.4 = (f32[132,8,128]{2,1,0:T(8,128)S(1)}, f32[132,8,128]{2,1,0:T(8,128)S(1)}, u32[]{:S(2)}, u32[]{:S(2)}) collective-permute-start(f32[132,8,128]{2,1,0:T(8,128)S(1)} %get-tuple-element.18), channel_id=1, source_target_pairs={{0,16},{16,32},{32,48},{48,64},{64,80},{80,96},{96,112},{112,128},... | collective-permute-start | bytes 1622024 | tf_op jit(solution)/shard_map/ppermute | solution.py:476
  32.6 2.4 %collective-permute-start.5 = (f32[132,8,128]{2,1,0:T(8,128)S(1)}, f32[132,8,128]{2,1,0:T(8,128)S(1)}, u32[]{:S(2)}, u32[]{:S(2)}) collective-permute-start(f32[132,8,128]{2,1,0:T(8,128)S(1)} %get-tuple-element.19), channel_id=1, source_target_pairs={{16,0},{32,16},{48,32},{64,48},{80,64},{96,80},{112,96},{128,112},... | collective-permute-start | bytes 1622024 | tf_op jit(solution)/shard_map/ppermute | solution.py:477
  35.1 3.8 %collective-permute-done.4.low = f32[132,8,128]{2,1,0:T(8,128)S(1)} collective-permute-done((f32[132,8,128]{2,1,0:T(8,128)S(1)}, f32[132,8,128]{2,1,0:T(8,128)S(1)}, u32[]{:S(2)}, u32[]{:S(2)}) %collective-permute-start.4) | collective-permute-done | bytes 540704 | tf_op jit(solution)/shard_map/ppermute | solution.py:476
  38.9 4.7 %collective-permute-done.5.high = f32[132,8,128]{2,1,0:T(8,128)S(1)} collective-permute-done((f32[132,8,128]{2,1,0:T(8,128)S(1)}, f32[132,8,128]{2,1,0:T(8,128)S(1)}, u32[]{:S(2)}, u32[]{:S(2)}) %collective-permute-start.5) | collective-permute-done | bytes 540704 | tf_op jit(solution)/shard_map/ppermute | solution.py:477
  43.6 2.8 %images_and_gram.1 = (f32[4,128,128]{2,1,0:T(8,128)S(1)}, f32[4,64,128]{2,1,0:T(8,128)S(1)}, f32[32,8,128]{2,1,0:T(8,128)S(1)}) custom-call(f32[4,16,8,128]{3,2,1,0:T(8,128)S(1)} %get-tuple-element.16.w, f32[12,24,128]{2,1,0:T(8,128)S(1)} %get-tuple-element.17.coef, f32[132,8,128]{2,1,0:T(8,128)S(1)} %collective-permute-done.4.low, ...), custom_call_target="tpu_custom_call" | custom-call | tf_op jit(solution)/shard_map/images_and_gram/pallas_call | solution.py:339
  46.4 15.7 %all_to_all.10.parts = f32[32,8,128]{2,1,0:T(8,128)S(1)} all-to-all(f32[32,8,128]{2,1,0:T(8,128)S(1)} %get-tuple-element.20), channel_id=1, replica_groups=mesh['z'=16,'core'=2,'gy'=16] {'core','gy'}, dimensions={0} | all-to-all | bytes 262144 | tf_op jit(solution)/shard_map/all_to_all | solution.py:492
  62.1 27.1 %all_to_all.11.parts = f32[16,8,128]{2,1,0:T(8,128)S(1)} all-to-all(f32[16,8,128]{2,1,0:T(8,128)S(1)} %sum_and_spread.1), channel_id=1, replica_groups=mesh['z'=16,'core'=2,'gy'=16] {'z'}, dimensions={0} | all-to-all | bytes 131072 | tf_op jit(solution)/shard_map/all_to_all | solution.py:493
  89.2 3.9 %finish.1 = f32[2,8,4,8,128]{4,3,2,1,0:T(8,128)} custom-call(f32[16,8,128]{2,1,0:T(8,128)S(1)} %all_to_all.11.parts, f32[4,200,128]{2,1,0:T(8,128)S(1)} %pad_maximum_fusion.own.start, f32[4,16,8,128]{3,2,1,0:T(8,128)S(1)} %get-tuple-element.16.w, f32[4,128,128]{2,1,0:T(8,128)S(1)} %get-tuple-element.21.old_image, f32[4,64,128]{2,1,0:T(8,128)S(1)} %get-tuple-element.22.w_image), custom_call_target="tpu_custom_call" | custom-call | tf_op jit(solution)/shard_map/finish/pallas_call | solution.py:461
  (7 shorter events, 0.2 us)
Async XLA Ops:
  1.3 0.7 copy-start
  2.0 7.5 %collective-permute-start = (f32[4,136,128]{2,1,0:T(8,128)S(1)}, f32[4,136,128]{2,1,0:T(8,128)S(1)}, u32[]{:S(2)}, u32[]{:S(2)}) collective-permute-start(f32[4,136,128]{2,1,0:T(8,128)S(1)} %pad_maximum_fusion.1), channel_id=1, source_target_pairs={{0,1},{1,2},{2,3},{3,4},{4,5},{5,6},{6,7},{7,8},{8,9},{9,10},{10,1... | collective-permute-start | bytes 835592 | tf_op jit(solution)/shard_map/ppermute | solution.py:476
  6.1 7.3 %collective-permute-start.1 = (f32[4,136,128]{2,1,0:T(8,128)S(1)}, f32[4,136,128]{2,1,0:T(8,128)S(1)}, u32[]{:S(2)}, u32[]{:S(2)}) collective-permute-start(f32[4,136,128]{2,1,0:T(8,128)S(1)} %pad_maximum_fusion.2), channel_id=1, source_target_pairs={{1,0},{2,1},{3,2},{4,3},{5,4},{6,5},{7,6},{8,7},{9,8},{10,9},{11,1... | collective-permute-start | bytes 835592 | tf_op jit(solution)/shard_map/ppermute | solution.py:477
  13.5 11.4 %collective-permute-start.2 = (f32[86,8,128]{2,1,0:T(8,128)S(1)}, f32[86,8,128]{2,1,0:T(8,128)S(1)}, u32[]{:S(2)}, u32[]{:S(2)}) collective-permute-start(f32[86,8,128]{2,1,0:T(8,128)S(1)} %get-tuple-element.14), channel_id=1, source_target_pairs={{0,16},{16,32},{32,48},{48,64},{64,80},{80,96},{96,112},{112,128},... | collective-permute-start | bytes 1056776 | tf_op jit(solution)/shard_map/ppermute | solution.py:476
  20.6 8.7 %collective-permute-start.3 = (f32[86,8,128]{2,1,0:T(8,128)S(1)}, f32[86,8,128]{2,1,0:T(8,128)S(1)}, u32[]{:S(2)}, u32[]{:S(2)}) collective-permute-start(f32[86,8,128]{2,1,0:T(8,128)S(1)} %get-tuple-element.15), channel_id=1, source_target_pairs={{16,0},{32,16},{48,32},{64,48},{80,64},{96,80},{112,96},{128,112},... | collective-permute-start | bytes 1056776 | tf_op jit(solution)/shard_map/ppermute | solution.py:477
  30.7 8.2 %collective-permute-start.4 = (f32[132,8,128]{2,1,0:T(8,128)S(1)}, f32[132,8,128]{2,1,0:T(8,128)S(1)}, u32[]{:S(2)}, u32[]{:S(2)}) collective-permute-start(f32[132,8,128]{2,1,0:T(8,128)S(1)} %get-tuple-element.18), channel_id=1, source_target_pairs={{0,16},{16,32},{32,48},{48,64},{64,80},{80,96},{96,112},{112,128},... | collective-permute-start | bytes 1622024 | tf_op jit(solution)/shard_map/ppermute | solution.py:476
  32.6 11.0 %collective-permute-start.5 = (f32[132,8,128]{2,1,0:T(8,128)S(1)}, f32[132,8,128]{2,1,0:T(8,128)S(1)}, u32[]{:S(2)}, u32[]{:S(2)}) collective-permute-start(f32[132,8,128]{2,1,0:T(8,128)S(1)} %get-tuple-element.19), channel_id=1, source_target_pairs={{16,0},{32,16},{48,32},{64,48},{80,64},{96,80},{112,96},{128,112},... | collective-permute-start | bytes 1622024 | tf_op jit(solution)/shard_map/ppermute | solution.py:477

commit v12 on v10

--- a/solution.py
+++ b/solution.py
@@ -37,10 +37,22 @@
 SECOND_TILES = SPLIT + NEAR_SIZE
 
 
-def pack_columns(out, start, found, to_higher, rows, reach):
+def sent_plane(inner, d):
+    core = lax.axis_index("core")
+    far = core if inner else 1 - core
+    return (1 - far) * (LX - d) + far * (d - 1)
+
+
+def halo_plane(inner, d):
+    core = lax.axis_index("core")
+    far = core if inner else 1 - core
+    return (1 - far) * (NEAR + LX - 1 + d) + far * (NEAR - d)
+
+
+def pack_columns(out, start, found, inner, rows, reach):
     (below, low_row), (own, own_row), (above, high_row) = rows
     for d, more, place in found:
-        x = LX - 1 - (d - 1) % LX if to_higher else (d - 1) % LX
+        x = sent_plane(inner, d)
         spot = start + place
         size = more * 8
         if more:
@@ -49,9 +61,9 @@
         out[pl.ds(spot + more, LY)] = own[x, pl.ds(own_row, BLOCK), :].reshape(LY, 8, NZ)
 
 
-def pack_coefficient(out, start, found, to_higher, below, own, above):
+def pack_coefficient(out, start, found, inner, below, own, above):
     for d, more, place in found:
-        x = LX - 1 - (d - 1) % LX if to_higher else (d - 1) % LX
+        x = sent_plane(inner, d)
         for y in range(-more, LY + more):
             if y < 0:
                 ref, row = below, 2 * HALF + BLOCK + LY + y
@@ -63,18 +75,18 @@
             out[start + spot // 8, pl.ds(spot % 8, 1), :] = ref[x, pl.ds(row, 1), :]
 
 
-def column_kernel(own, below, above, right, left, old_right, old_left):
-    for first, second, to_higher in ((right, old_right, True), (left, old_left, False)):
+def column_kernel(own, below, above, outward, inward, old_outward, old_inward):
+    for first, second, inner in ((outward, old_outward, False), (inward, old_inward, True)):
         rows = [(below, 2 * HALF), (own, 2 * BLOCK), (above, 2 * HALF)]
-        pack_columns(first, 0, SIDE_SPANS, to_higher, rows, FAR)
+        pack_columns(first, 0, SIDE_SPANS, inner, rows, FAR)
         if SIDE_SIZE % 8:
             first[SIDE_SIZE + FLAT_TILES - 1] = jnp.zeros((8, NZ), F32)
-        pack_coefficient(first, SIDE_SIZE, SIDE_SPANS, to_higher, below, own, above)
+        pack_coefficient(first, SIDE_SIZE, SIDE_SPANS, inner, below, own, above)
         rows = [(below, 0), (own, 0), (above, 0)]
-        pack_columns(second, 0, NEAR_SPANS[:-1], to_higher, rows, NEAR)
-        pack_columns(first, SIDE_SIZE + FLAT_TILES - SPLIT, NEAR_SPANS[-1:], to_higher, rows, NEAR)
+        pack_columns(second, 0, NEAR_SPANS[:-1], inner, rows, NEAR)
+        pack_columns(first, SIDE_SIZE + FLAT_TILES - SPLIT, NEAR_SPANS[-1:], inner, rows, NEAR)
         rows = [(below, HALF), (own, BLOCK), (above, HALF)]
-        pack_columns(second, SPLIT, NEAR_SPANS, to_higher, rows, NEAR)
+        pack_columns(second, SPLIT, NEAR_SPANS, inner, rows, NEAR)
 
 
 def pack_all(*args):
@@ -90,12 +102,12 @@
 
 
 def fill_sides(wide, halo, sides):
-    for low, high, start, found in sides:
+    for outer, inner, start, found in sides:
         for d, more, place in found:
             count = LY + 2 * more
             begin = halo - more
-            wide[NEAR - d, begin:begin + count] = low[pl.ds(start + place, count)]
-            wide[NEAR + LX - 1 + d, begin:begin + count] = high[pl.ds(start + place, count)]
+            wide[halo_plane(False, d), begin:begin + count] = outer[pl.ds(start + place, count)]
+            wide[halo_plane(True, d), begin:begin + count] = inner[pl.ds(start + place, count)]
 
 
 def fill_block(wide, halo, rows, reach, sides):
@@ -109,7 +121,7 @@
     fill_sides(wide, halo, sides)
 
 
-def fill_flat(wide, below, own, above, low, high):
+def fill_flat(wide, below, own, above, outer, inner):
     wide[...] = jnp.zeros(wide.shape, F32)
     for x in range(LX):
         wide[NEAR + x, 0:FAR] = below[x, pl.ds(2 * HALF + BLOCK, LY), :]
@@ -119,8 +131,8 @@
         for i in range(LY + 2 * more):
             tile, row = SIDE_SIZE + (place + i) // 8, (place + i) % 8
             y = FAR - more + i
-            wide[NEAR - d, pl.ds(y, 1), :] = low[tile, pl.ds(row, 1), :]
-            wide[NEAR + LX - 1 + d, pl.ds(y, 1), :] = high[tile, pl.ds(row, 1), :]
+            wide[halo_plane(False, d), pl.ds(y, 1), :] = outer[tile, pl.ds(row, 1), :]
+            wide[halo_plane(True, d), pl.ds(y, 1), :] = inner[tile, pl.ds(row, 1), :]
 
 
 def fill_tables(coef, skip, table_re, table_im, diag_re, diag_im):
@@ -202,12 +214,12 @@
     return [pltpu.VMEM((*wide_shape(halo), 8, NZ), F32)] * 5 + [FLAT] * 2
 
 
-def first_kernel(own, below, above, low, high, w, coef, out_right, out_left, block, first, second,
+def first_kernel(own, below, above, outer, inner, w, coef, outward, inward, block, first, second,
                  table_re, table_im, diag_re, diag_im):
-    fill_flat(coef, below, own, above, low, high)
+    fill_flat(coef, below, own, above, outer, inner)
     fill_tables(coef, 0, table_re, table_im, diag_re, diag_im)
     rows = [(below, 2 * HALF), (own, 2 * BLOCK), (above, 2 * HALF)]
-    fill_block(block, FAR, rows, FAR, [(low, high, 0, SIDE_SPANS)])
+    fill_block(block, FAR, rows, FAR, [(outer, inner, 0, SIDE_SPANS)])
 
     def store(x, y, value):
         w[x, y] = value
@@ -215,8 +227,8 @@
     smooth(block, coef, 0, table_re, table_im, first, second, store)
     for d, more, place in NEAR_SPANS:
         count = LY + 2 * more
-        out_right[pl.ds(place, count)] = w[LX - d, pl.ds(NEAR - more, count)]
-        out_left[pl.ds(place, count)] = w[d - 1, pl.ds(NEAR - more, count)]
+        outward[pl.ds(place, count)] = w[sent_plane(False, d), pl.ds(NEAR - more, count)]
+        inward[pl.ds(place, count)] = w[sent_plane(True, d), pl.ds(NEAR - more, count)]
 
 
 def first_image(*args):
@@ -234,16 +246,16 @@
     )(*args)
 
 
-def old_kernel(coef, own, below, above, low, high, first_low, first_high, out, block, first, second,
+def old_kernel(coef, own, below, above, outer, inner, first_outer, first_inner, out, block, first, second,
                table_re, table_im, diag_re, diag_im):
     fill_tables(coef, FAR - NEAR, table_re, table_im, diag_re, diag_im)
     for group in range(2):
         rows = [(below, group * HALF), (own, group * BLOCK), (above, group * HALF)]
         if group == 0:
-            sides = [(low, high, 0, NEAR_SPANS[:-1]),
-                     (first_low, first_high, SIDE_SIZE + FLAT_TILES - SPLIT, NEAR_SPANS[-1:])]
+            sides = [(outer, inner, 0, NEAR_SPANS[:-1]),
+                     (first_outer, first_inner, SIDE_SIZE + FLAT_TILES - SPLIT, NEAR_SPANS[-1:])]
         else:
-            sides = [(low, high, SPLIT, NEAR_SPANS)]
+            sides = [(outer, inner, SPLIT, NEAR_SPANS)]
         fill_block(block, NEAR, rows, NEAR, sides)
 
         def store(x, y, value, group=group):
@@ -330,13 +342,13 @@
     return jnp.where(tall // 8 <= wide // 8, upper, upper.T)
 
 
-def gram_kernel(peers, w, coef, low, high, start, old_image, w_image, out,
+def gram_kernel(peers, w, coef, outer, inner, start, old_image, w_image, out,
                 block, first, second, table_re, table_im, diag_re, diag_im):
     fill_tables(coef, FAR - NEAR, table_re, table_im, diag_re, diag_im)
     block[...] = jnp.zeros(block.shape, F32)
     for x in range(LX):
         block[NEAR + x] = w[x]
-    fill_sides(block, NEAR, [(low, high, 0, NEAR_SPANS)])
+    fill_sides(block, NEAR, [(outer, inner, 0, NEAR_SPANS)])
 
     def store(x, y, value):
         w_image[x, pl.ds(y * 8, 8), :] = value
@@ -491,11 +503,17 @@
 GX = ("z", "core")
 
 
-def from_both(axis, count, to_higher, to_lower, step=1):
+def from_both(axis, count, to_higher, to_lower):
     return (
-        lax.ppermute(to_higher, axis, [(i, i + step) for i in range(count - step)]),
-        lax.ppermute(to_lower, axis, [(i + step, i) for i in range(count - step)]),
+        lax.ppermute(to_higher, axis, [(i, i + 1) for i in range(count - 1)]),
+        lax.ppermute(to_lower, axis, [(i + 1, i) for i in range(count - 1)]),
     )
+
+
+def exchange(count, outward, inward):
+    inner = [(i, i ^ 1) for i in range(count)]
+    outer = [(i, i + 1 if i % 2 else i - 1) for i in range(1, count - 1)]
+    return lax.ppermute(outward, GX, outer), lax.ppermute(inward, GX, inner)
 
 
 def per_device(nx, ny, nz, prior, coefficient):
@@ -505,11 +523,11 @@
     up = jnp.concatenate([start[:, HALF:BLOCK], start[:, BLOCK + HALF:]], axis=1)
     down = jnp.concatenate([start[:, :HALF], start[:, BLOCK:BLOCK + HALF], start[:, 2 * BLOCK:]], axis=1)
     rims = from_both("gy", ny, up, down)
-    right, left, old_right, old_left = pack_all(start, *rims)
-    sides = from_both(GX, nx, right, left)
-    old_sides = from_both(GX, nx, old_right, old_left)
-    w, coef, w_right, w_left = first_image(start, *rims, *sides)
-    w_sides = from_both(GX, nx, w_right, w_left)
+    outward, inward, old_outward, old_inward = pack_all(start, *rims)
+    sides = exchange(nx, outward, inward)
+    old_sides = exchange(nx, old_outward, old_inward)
+    w, coef, w_outward, w_inward = first_image(start, *rims, *sides)
+    w_sides = exchange(nx, w_outward, w_inward)
     old_image = old_images(coef, start, *rims, *old_sides, *sides)
 
     w_image, spread = image_and_gram(2 * ny, w, coef, *w_sides, start, old_image)

time: 90.3 us -> 85.4 us (0.946)
  waiting for transfers between devices: 11 us -> 5.97 us
  blocking collectives: 44 us -> 41.9 us
  starting transfers between devices: 24.3 us -> 26.1 us
    ppermute x8, waiting for transfers between devices: 11 us -> 5.97 us  [the longest x1 3.88 us: from_both(): lax.ppermute(to_lower, axis, [(i + 1, i) for i in range(count - 1)])]
    all_to_all x1, blocking collectives: 28.2 us -> 25.8 us  [per_device(): got = lax.all_to_all(sum_and_spread(got, nz), 'z', 0, 0)]
    ppermute x8, starting transfers between devices: 24.3 us -> 26.1 us  [the longest x6 20.7 us: exchange(): return (lax.ppermute(outward, GX, outer), lax.ppermute(inward, GX, inner))]
  transfers between devices with their start and end apart: 8 -> 8, of which waited for: 4 -> 2; matrix products, arithmetic and copies ran while one was open for 0% -> 0% of each run, Pallas kernels for 3% -> 4%
where the time goes in v12:
time: 85.4 us; the launch traced here: 84.9 us
  blocking collectives  41.9 us (49%)
  starting transfers between devices  26.1 us (31%)
  Pallas kernels  8.71 us (10%)
  waiting for transfers between devices  5.97 us (7%)
  local copies, waits for them, and re-layouts  1.96 us (2%)
    all_to_all x1, blocking collectives, per_device(): got = lax.all_to_all(sum_and_spread(got, nz), 'z', 0, 0)  25.8 us
    ppermute x6, starting transfers between devices, exchange(): return (lax.ppermute(outward, GX, outer), lax.ppermute(inward, GX, inner))  20.7 us
    all_to_all x1, blocking collectives, per_device(): got = lax.all_to_all(spread, ('core', 'gy'), 0, 0)  16.1 us
    ppermute x1, starting transfers between devices, from_both(): lax.ppermute(to_higher, axis, [(i, i + 1) for i in range(count - 1)])  4.05 us
    pallas_call x1, Pallas kernels, finish(): pl.pallas_call(functools.partial(final_kernel, cells), out_shape=jax.Shap...  3.93 us
    ppermute x1, waiting for transfers between devices, from_both(): lax.ppermute(to_lower, axis, [(i + 1, i) for i in range(count - 1)])  3.88 us
    ppermute x1, waiting for transfers between devices, from_both(): lax.ppermute(to_higher, axis, [(i, i + 1) for i in range(count - 1)])  2.07 us
  transfers between devices with their start and end apart: 8, of which 2 were waited for; matrix products, arithmetic and copies ran while one was open for 0% of the time, Pallas kernels for 4%

profile of v12, /device:TPU:1, one launch (start us, length us, event | category | flops | bytes accessed | tf_op | source)
XLA Modules:
  0.0 84.9 jit_solution(10151970975507716453)
XLA Ops:
  0.0 1.3 %copy.3 = f32[4,3,8,2,4,128]{5,4,3,2,1,0:T(4,128)S(1)} copy(f32[4,3,8,2,4,128]{5,2,0,4,3,1:T(8,128)} %bitcast.7) | data formatting | bytes 786432 | tf_op jit(solution)/shard_map/transpose | solution.py:521
  1.3 0.0 copy-start
  1.3 0.7 copy-done
  2.0 4.0 %collective-permute-start = (f32[4,136,128]{2,1,0:T(8,128)S(1)}, f32[4,136,128]{2,1,0:T(8,128)S(1)}, u32[]{:S(2)}, u32[]{:S(2)}) collective-permute-start(f32[4,136,128]{2,1,0:T(8,128)S(1)} %pad_maximum_fusion.1), channel_id=1, source_target_pairs={{0,1},{1,2},{2,3},{3,4},{4,5},{5,6},{6,7},{7,8},{8,9},{9,10},{10,1... | collective-permute-start | bytes 835592 | tf_op jit(solution)/shard_map/ppermute | solution.py:508
  6.1 1.3 %collective-permute-start.1 = (f32[4,136,128]{2,1,0:T(8,128)S(1)}, f32[4,136,128]{2,1,0:T(8,128)S(1)}, u32[]{:S(2)}, u32[]{:S(2)}) collective-permute-start(f32[4,136,128]{2,1,0:T(8,128)S(1)} %pad_maximum_fusion.2), channel_id=1, source_target_pairs={{1,0},{2,1},{3,2},{4,3},{5,4},{6,5},{7,6},{8,7},{9,8},{10,9},{11,1... | collective-permute-start | bytes 835592 | tf_op jit(solution)/shard_map/ppermute | solution.py:509
  7.5 2.1 %collective-permute-done.below = f32[4,136,128]{2,1,0:T(8,128)S(1)} collective-permute-done((f32[4,136,128]{2,1,0:T(8,128)S(1)}, f32[4,136,128]{2,1,0:T(8,128)S(1)}, u32[]{:S(2)}, u32[]{:S(2)}) %collective-permute-start) | collective-permute-done | bytes 278560 | tf_op jit(solution)/shard_map/ppermute | solution.py:508
  9.5 3.9 %collective-permute-done.1.above = f32[4,136,128]{2,1,0:T(8,128)S(1)} collective-permute-done((f32[4,136,128]{2,1,0:T(8,128)S(1)}, f32[4,136,128]{2,1,0:T(8,128)S(1)}, u32[]{:S(2)}, u32[]{:S(2)}) %collective-permute-start.1) | collective-permute-done | bytes 278560 | tf_op jit(solution)/shard_map/ppermute | solution.py:509
  13.4 0.1 pack_all.1
  13.5 7.1 %collective-permute-start.2 = (f32[94,8,128]{2,1,0:T(8,128)S(1)}, f32[94,8,128]{2,1,0:T(8,128)S(1)}, u32[]{:S(2)}, u32[]{:S(2)}) collective-permute-start(f32[94,8,128]{2,1,0:T(8,128)S(1)} %get-tuple-element.15), channel_id=1, source_target_pairs={{16,32},{32,16},{48,64},{64,48},{80,96},{96,80},{112,128},{128,112... | collective-permute-start | bytes 1155080 | tf_op jit(solution)/shard_map/ppermute | solution.py:516
  20.6 1.9 %collective-permute-start.3 = (f32[94,8,128]{2,1,0:T(8,128)S(1)}, f32[94,8,128]{2,1,0:T(8,128)S(1)}, u32[]{:S(2)}, u32[]{:S(2)}) collective-permute-start(f32[94,8,128]{2,1,0:T(8,128)S(1)} %get-tuple-element.16), channel_id=1, source_target_pairs={{0,16},{16,0},{32,48},{48,32},{64,80},{80,64},{96,112},{112,96},{1... | collective-permute-start | bytes 1155080 | tf_op jit(solution)/shard_map/ppermute | solution.py:516
  22.6 3.9 %collective-permute-start.6 = (f32[80,8,128]{2,1,0:T(8,128)S(1)}, f32[80,8,128]{2,1,0:T(8,128)S(1)}, u32[]{:S(2)}, u32[]{:S(2)}) collective-permute-start(f32[80,8,128]{2,1,0:T(8,128)S(1)} %get-tuple-element.21), channel_id=1, source_target_pairs={{16,32},{32,16},{48,64},{64,48},{80,96},{96,80},{112,128},{128,112... | collective-permute-start | bytes 983048 | tf_op jit(solution)/shard_map/ppermute | solution.py:516
  26.5 1.9 %collective-permute-start.7 = (f32[80,8,128]{2,1,0:T(8,128)S(1)}, f32[80,8,128]{2,1,0:T(8,128)S(1)}, u32[]{:S(2)}, u32[]{:S(2)}) collective-permute-start(f32[80,8,128]{2,1,0:T(8,128)S(1)} %get-tuple-element.22), channel_id=1, source_target_pairs={{0,16},{16,0},{32,48},{48,32},{64,80},{80,64},{96,112},{112,96},{1... | collective-permute-start | bytes 983048 | tf_op jit(solution)/shard_map/ppermute | solution.py:516
  28.4 0.0 collective-permute-done.2.outer.first_outer
  28.5 0.0 collective-permute-done.3.inner.first_inner
  28.5 1.6 %first_image.1 = (f32[4,16,8,128]{3,2,1,0:T(8,128)S(1)}, f32[12,24,128]{2,1,0:T(8,128)S(1)}, f32[44,8,128]{2,1,0:T(8,128)S(1)}, f32[44,8,128]{2,1,0:T(8,128)S(1)}) custom-call(f32[4,200,128]{2,1,0:T(8,128)S(1)} %pad_maximum_fusion.own.start, f32[4,136,128]{2,1,0:T(8,128)S(1)} %collective-permute-done.below, f32[4,136,128]{2,1,0:T(8,128)S(1)} %collective-permute-done.1.above, ...), custom_call_target="tpu_custom_call" | custom-call | flops 12000000 | bytes 18000000 | tf_op jit(solution)/shard_map/first_image/pallas_call | solution.py:236
  30.0 3.9 %collective-permute-start.4 = (f32[44,8,128]{2,1,0:T(8,128)S(1)}, f32[44,8,128]{2,1,0:T(8,128)S(1)}, u32[]{:S(2)}, u32[]{:S(2)}) collective-permute-start(f32[44,8,128]{2,1,0:T(8,128)S(1)} %get-tuple-element.19), channel_id=1, source_target_pairs={{16,32},{32,16},{48,64},{64,48},{80,96},{96,80},{112,128},{128,112... | collective-permute-start | bytes 540680 | tf_op jit(solution)/shard_map/ppermute | solution.py:516
  34.0 1.9 %collective-permute-start.5 = (f32[44,8,128]{2,1,0:T(8,128)S(1)}, f32[44,8,128]{2,1,0:T(8,128)S(1)}, u32[]{:S(2)}, u32[]{:S(2)}) collective-permute-start(f32[44,8,128]{2,1,0:T(8,128)S(1)} %get-tuple-element.20), channel_id=1, source_target_pairs={{0,16},{16,0},{32,48},{48,32},{64,80},{80,64},{96,112},{112,96},{1... | collective-permute-start | bytes 540680 | tf_op jit(solution)/shard_map/ppermute | solution.py:516
  35.9 0.0 collective-permute-done.6.outer
  35.9 0.0 collective-permute-done.7.inner
  35.9 1.5 %old_images.1.old_image = f32[4,128,128]{2,1,0:T(8,128)S(1)} custom-call(f32[12,24,128]{2,1,0:T(8,128)S(1)} %get-tuple-element.18.coef, f32[4,200,128]{2,1,0:T(8,128)S(1)} %pad_maximum_fusion.own.start, f32[4,136,128]{2,1,0:T(8,128)S(1)} %collective-permute-done.below, f32[4,136,128]{2,1,0:T(8,128)S(1)} %collective-permute-done.1.above, ...), custom_call_target="tpu_custom_call" | custom-call | flops 12000000 | bytes 24000000 | tf_op jit(solution)/shard_map/old_images/pallas_call | solution.py:268
  37.5 0.0 collective-permute-done.4.outer
  37.5 0.0 collective-permute-done.5.inner
  37.5 1.5 %image_and_gram.1 = (f32[4,64,128]{2,1,0:T(8,128)S(1)}, f32[32,8,128]{2,1,0:T(8,128)S(1)}) custom-call(f32[4,16,8,128]{3,2,1,0:T(8,128)S(1)} %get-tuple-element.17.w, f32[12,24,128]{2,1,0:T(8,128)S(1)} %get-tuple-element.18.coef, f32[44,8,128]{2,1,0:T(8,128)S(1)} %collective-permute-done.4.outer, f32[44,8,128]{2,1,0:T(8,128)S(1)} %collective-permute-done.5.inner, ...), custom_call_target="tpu_custom_call" | custom-call | tf_op jit(solution)/shard_map/image_and_gram/pallas_call | solution.py:372
  39.0 16.1 %all_to_all.10.parts = f32[32,8,128]{2,1,0:T(8,128)S(1)} all-to-all(f32[32,8,128]{2,1,0:T(8,128)S(1)} %get-tuple-element.23), channel_id=1, replica_groups=mesh['z'=16,'core'=2,'gy'=16] {'core','gy'}, dimensions={0} | all-to-all | bytes 262144 | tf_op jit(solution)/shard_map/all_to_all | solution.py:534
  55.2 25.8 %all_to_all.11.parts = f32[16,8,128]{2,1,0:T(8,128)S(1)} all-to-all(f32[16,8,128]{2,1,0:T(8,128)S(1)} %sum_and_spread.1), channel_id=1, replica_groups=mesh['z'=16,'core'=2,'gy'=16] {'z'}, dimensions={0} | all-to-all | bytes 131072 | tf_op jit(solution)/shard_map/all_to_all | solution.py:535
  81.0 3.9 %finish.1 = f32[2,8,4,8,128]{4,3,2,1,0:T(8,128)} custom-call(f32[16,8,128]{2,1,0:T(8,128)S(1)} %all_to_all.11.parts, f32[4,200,128]{2,1,0:T(8,128)S(1)} %pad_maximum_fusion.own.start, f32[4,16,8,128]{3,2,1,0:T(8,128)S(1)} %get-tuple-element.17.w, f32[4,128,128]{2,1,0:T(8,128)S(1)} %old_images.1.old_image, f32[4,64,128]{2,1,0:T(8,128)S(1)} %get-tuple-element.24.w_image), custom_call_target="tpu_custom_call" | custom-call | tf_op jit(solution)/shard_map/finish/pallas_call | solution.py:493
  (7 shorter events, 0.2 us)
Async XLA Ops:
  1.3 0.7 copy-start
  2.0 7.5 %collective-permute-start = (f32[4,136,128]{2,1,0:T(8,128)S(1)}, f32[4,136,128]{2,1,0:T(8,128)S(1)}, u32[]{:S(2)}, u32[]{:S(2)}) collective-permute-start(f32[4,136,128]{2,1,0:T(8,128)S(1)} %pad_maximum_fusion.1), channel_id=1, source_target_pairs={{0,1},{1,2},{2,3},{3,4},{4,5},{5,6},{6,7},{7,8},{8,9},{9,10},{10,1... | collective-permute-start | bytes 835592 | tf_op jit(solution)/shard_map/ppermute | solution.py:508
  6.1 7.3 %collective-permute-start.1 = (f32[4,136,128]{2,1,0:T(8,128)S(1)}, f32[4,136,128]{2,1,0:T(8,128)S(1)}, u32[]{:S(2)}, u32[]{:S(2)}) collective-permute-start(f32[4,136,128]{2,1,0:T(8,128)S(1)} %pad_maximum_fusion.2), channel_id=1, source_target_pairs={{1,0},{2,1},{3,2},{4,3},{5,4},{6,5},{7,6},{8,7},{9,8},{10,9},{11,1... | collective-permute-start | bytes 835592 | tf_op jit(solution)/shard_map/ppermute | solution.py:509
  13.5 14.9 %collective-permute-start.2 = (f32[94,8,128]{2,1,0:T(8,128)S(1)}, f32[94,8,128]{2,1,0:T(8,128)S(1)}, u32[]{:S(2)}, u32[]{:S(2)}) collective-permute-start(f32[94,8,128]{2,1,0:T(8,128)S(1)} %get-tuple-element.15), channel_id=1, source_target_pairs={{16,32},{32,16},{48,64},{64,48},{80,96},{96,80},{112,128},{128,112... | collective-permute-start | bytes 1155080 | tf_op jit(solution)/shard_map/ppermute | solution.py:516
  20.6 7.8 %collective-permute-start.3 = (f32[94,8,128]{2,1,0:T(8,128)S(1)}, f32[94,8,128]{2,1,0:T(8,128)S(1)}, u32[]{:S(2)}, u32[]{:S(2)}) collective-permute-start(f32[94,8,128]{2,1,0:T(8,128)S(1)} %get-tuple-element.16), channel_id=1, source_target_pairs={{0,16},{16,0},{32,48},{48,32},{64,80},{80,64},{96,112},{112,96},{1... | collective-permute-start | bytes 1155080 | tf_op jit(solution)/shard_map/ppermute | solution.py:516
  22.6 13.3 %collective-permute-start.6 = (f32[80,8,128]{2,1,0:T(8,128)S(1)}, f32[80,8,128]{2,1,0:T(8,128)S(1)}, u32[]{:S(2)}, u32[]{:S(2)}) collective-permute-start(f32[80,8,128]{2,1,0:T(8,128)S(1)} %get-tuple-element.21), channel_id=1, source_target_pairs={{16,32},{32,16},{48,64},{64,48},{80,96},{96,80},{112,128},{128,112... | collective-permute-start | bytes 983048 | tf_op jit(solution)/shard_map/ppermute | solution.py:516
  26.5 9.4 %collective-permute-start.7 = (f32[80,8,128]{2,1,0:T(8,128)S(1)}, f32[80,8,128]{2,1,0:T(8,128)S(1)}, u32[]{:S(2)}, u32[]{:S(2)}) collective-permute-start(f32[80,8,128]{2,1,0:T(8,128)S(1)} %get-tuple-element.22), channel_id=1, source_target_pairs={{0,16},{16,0},{32,48},{48,32},{64,80},{80,64},{96,112},{112,96},{1... | collective-permute-start | bytes 983048 | tf_op jit(solution)/shard_map/ppermute | solution.py:516
  30.0 7.4 %collective-permute-start.4 = (f32[44,8,128]{2,1,0:T(8,128)S(1)}, f32[44,8,128]{2,1,0:T(8,128)S(1)}, u32[]{:S(2)}, u32[]{:S(2)}) collective-permute-start(f32[44,8,128]{2,1,0:T(8,128)S(1)} %get-tuple-element.19), channel_id=1, source_target_pairs={{16,32},{32,16},{48,64},{64,48},{80,96},{96,80},{112,128},{128,112... | collective-permute-start | bytes 540680 | tf_op jit(solution)/shard_map/ppermute | solution.py:516
  34.0 3.5 %collective-permute-start.5 = (f32[44,8,128]{2,1,0:T(8,128)S(1)}, f32[44,8,128]{2,1,0:T(8,128)S(1)}, u32[]{:S(2)}, u32[]{:S(2)}) collective-permute-start(f32[44,8,128]{2,1,0:T(8,128)S(1)} %get-tuple-element.20), channel_id=1, source_target_pairs={{0,16},{16,0},{32,48},{48,32},{64,80},{80,64},{96,112},{112,96},{1... | collective-permute-start | bytes 540680 | tf_op jit(solution)/shard_map/ppermute | solution.py:516

commit v13 on v12

--- a/solution.py
+++ b/solution.py
@@ -75,39 +75,39 @@
             out[start + spot // 8, pl.ds(spot % 8, 1), :] = ref[x, pl.ds(row, 1), :]
 
 
-def column_kernel(own, below, above, outward, inward, old_outward, old_inward):
-    for first, second, inner in ((outward, old_outward, False), (inward, old_inward, True)):
+def column_kernel(own, below, above, outward, inward, old_outward):
+    for first, second, later, inner in ((outward, old_outward, 0, False), (inward, inward, FIRST_TILES, True)):
         rows = [(below, 2 * HALF), (own, 2 * BLOCK), (above, 2 * HALF)]
         pack_columns(first, 0, SIDE_SPANS, inner, rows, FAR)
         if SIDE_SIZE % 8:
             first[SIDE_SIZE + FLAT_TILES - 1] = jnp.zeros((8, NZ), F32)
         pack_coefficient(first, SIDE_SIZE, SIDE_SPANS, inner, below, own, above)
         rows = [(below, 0), (own, 0), (above, 0)]
-        pack_columns(second, 0, NEAR_SPANS[:-1], inner, rows, NEAR)
+        pack_columns(second, later, NEAR_SPANS[:-1], inner, rows, NEAR)
         pack_columns(first, SIDE_SIZE + FLAT_TILES - SPLIT, NEAR_SPANS[-1:], inner, rows, NEAR)
         rows = [(below, HALF), (own, BLOCK), (above, HALF)]
-        pack_columns(second, SPLIT, NEAR_SPANS, inner, rows, NEAR)
+        pack_columns(second, later + SPLIT, NEAR_SPANS, inner, rows, NEAR)
 
 
 def pack_all(*args):
-    shapes = tuple(jax.ShapeDtypeStruct((size, 8, NZ), F32) for size in [FIRST_TILES] * 2 + [SECOND_TILES] * 2)
+    shapes = tuple(jax.ShapeDtypeStruct((size, 8, NZ), F32) for size in (FIRST_TILES, FIRST_TILES + SECOND_TILES, SECOND_TILES))
     return pl.pallas_call(
         column_kernel,
         out_shape=shapes,
         in_specs=[VMEM] * 3,
-        out_specs=(VMEM,) * 4,
+        out_specs=(VMEM,) * 3,
         compiler_params=pltpu.CompilerParams(vmem_limit_bytes=1 << 20),
         name="pack_all",
     )(*args)
 
 
 def fill_sides(wide, halo, sides):
-    for outer, inner, start, found in sides:
+    for outer, inner, start, inner_start, found in sides:
         for d, more, place in found:
             count = LY + 2 * more
             begin = halo - more
             wide[halo_plane(False, d), begin:begin + count] = outer[pl.ds(start + place, count)]
-            wide[halo_plane(True, d), begin:begin + count] = inner[pl.ds(start + place, count)]
+            wide[halo_plane(True, d), begin:begin + count] = inner[pl.ds(inner_start + place, count)]
 
 
 def fill_block(wide, halo, rows, reach, sides):
@@ -219,7 +219,7 @@
     fill_flat(coef, below, own, above, outer, inner)
     fill_tables(coef, 0, table_re, table_im, diag_re, diag_im)
     rows = [(below, 2 * HALF), (own, 2 * BLOCK), (above, 2 * HALF)]
-    fill_block(block, FAR, rows, FAR, [(outer, inner, 0, SIDE_SPANS)])
+    fill_block(block, FAR, rows, FAR, [(outer, inner, 0, 0, SIDE_SPANS)])
 
     def store(x, y, value):
         w[x, y] = value
@@ -246,16 +246,17 @@
     )(*args)
 
 
-def old_kernel(coef, own, below, above, outer, inner, first_outer, first_inner, out, block, first, second,
+def old_kernel(coef, own, below, above, outer, first_outer, inner, out, block, first, second,
                table_re, table_im, diag_re, diag_im):
     fill_tables(coef, FAR - NEAR, table_re, table_im, diag_re, diag_im)
     for group in range(2):
         rows = [(below, group * HALF), (own, group * BLOCK), (above, group * HALF)]
         if group == 0:
-            sides = [(outer, inner, 0, NEAR_SPANS[:-1]),
-                     (first_outer, first_inner, SIDE_SIZE + FLAT_TILES - SPLIT, NEAR_SPANS[-1:])]
+            last = SIDE_SIZE + FLAT_TILES - SPLIT
+            sides = [(outer, inner, 0, FIRST_TILES, NEAR_SPANS[:-1]),
+                     (first_outer, inner, last, last, NEAR_SPANS[-1:])]
         else:
-            sides = [(outer, inner, SPLIT, NEAR_SPANS)]
+            sides = [(outer, inner, SPLIT, FIRST_TILES + SPLIT, NEAR_SPANS)]
         fill_block(block, NEAR, rows, NEAR, sides)
 
         def store(x, y, value, group=group):
@@ -268,7 +269,7 @@
     return pl.pallas_call(
         old_kernel,
         out_shape=jax.ShapeDtypeStruct((LX, 2 * BLOCK, NZ), F32),
-        in_specs=[VMEM] * 8,
+        in_specs=[VMEM] * 7,
         out_specs=VMEM,
         scratch_shapes=smooth_scratch(NEAR),
         compiler_params=pltpu.CompilerParams(vmem_limit_bytes=16 << 20),
@@ -348,7 +349,7 @@
     block[...] = jnp.zeros(block.shape, F32)
     for x in range(LX):
         block[NEAR + x] = w[x]
-    fill_sides(block, NEAR, [(outer, inner, 0, NEAR_SPANS)])
+    fill_sides(block, NEAR, [(outer, inner, 0, 0, NEAR_SPANS)])
 
     def store(x, y, value):
         w_image[x, pl.ds(y * 8, 8), :] = value
@@ -510,10 +511,12 @@
     )
 
 
-def exchange(count, outward, inward):
-    inner = [(i, i ^ 1) for i in range(count)]
-    outer = [(i, i + 1 if i % 2 else i - 1) for i in range(1, count - 1)]
-    return lax.ppermute(outward, GX, outer), lax.ppermute(inward, GX, inner)
+def swap_chips(count, value):
+    return lax.ppermute(value, GX, [(i, i + 1 if i % 2 else i - 1) for i in range(1, count - 1)])
+
+
+def swap_cores(count, value):
+    return lax.ppermute(value, GX, [(i, i ^ 1) for i in range(count)])
 
 
 def per_device(nx, ny, nz, prior, coefficient):
@@ -523,12 +526,13 @@
     up = jnp.concatenate([start[:, HALF:BLOCK], start[:, BLOCK + HALF:]], axis=1)
     down = jnp.concatenate([start[:, :HALF], start[:, BLOCK:BLOCK + HALF], start[:, 2 * BLOCK:]], axis=1)
     rims = from_both("gy", ny, up, down)
-    outward, inward, old_outward, old_inward = pack_all(start, *rims)
-    sides = exchange(nx, outward, inward)
-    old_sides = exchange(nx, old_outward, old_inward)
-    w, coef, w_outward, w_inward = first_image(start, *rims, *sides)
-    w_sides = exchange(nx, w_outward, w_inward)
-    old_image = old_images(coef, start, *rims, *old_sides, *sides)
+    outward, inward, old_outward = pack_all(start, *rims)
+    outer = swap_chips(nx, outward)
+    inner = swap_cores(nx, inward)
+    old_outer = swap_chips(nx, old_outward)
+    w, coef, w_outward, w_inward = first_image(start, *rims, outer, inner)
+    w_sides = swap_chips(nx, w_outward), swap_cores(nx, w_inward)
+    old_image = old_images(coef, start, *rims, old_outer, outer, inner)
 
     w_image, spread = image_and_gram(2 * ny, w, coef, *w_sides, start, old_image)
     got = lax.all_to_all(spread, ("core", "gy"), 0, 0)

time: 85.4 us -> 86.8 us (1.016)
  waiting for transfers between devices: 5.97 us -> 10.8 us
  starting transfers between devices: 26.1 us -> 21.9 us
    ppermute x6 -> x5, waiting for transfers between devices: 0.02 us -> 4.85 us  [the longest x3 4.85 us: swap_chips(): lax.ppermute(value, GX, [(i, i + 1 if i % 2 else i - 1) for i in range(1,...]
    ppermute x6 -> x5, starting transfers between devices: 20.7 us -> 16.6 us  [the longest x2 9.12 us: swap_cores(): return lax.ppermute(value, GX, [(i, i ^ 1) for i in range(count)])]
    all_to_all x1, blocking collectives: 25.8 us -> 28.1 us  [per_device(): got = lax.all_to_all(sum_and_spread(got, nz), 'z', 0, 0)]
    all_to_all x1, blocking collectives: 16.1 us -> 14.6 us  [per_device(): got = lax.all_to_all(spread, ('core', 'gy'), 0, 0)]
  transfers between devices with their start and end apart: 8 -> 7, of which waited for: 2 -> 4; matrix products, arithmetic and copies ran while one was open for 0% -> 0% of each run, Pallas kernels for 4% -> 4%
where the time goes in v13:
time: 86.8 us; the launch traced here: 86.4 us
  blocking collectives  42.7 us (49%)
  starting transfers between devices  21.9 us (25%)
  waiting for transfers between devices  10.8 us (12%)
  Pallas kernels  8.7 us (10%)
  local copies, waits for them, and re-layouts  1.96 us (2%)
    all_to_all x1, blocking collectives, per_device(): got = lax.all_to_all(sum_and_spread(got, nz), 'z', 0, 0)  28.1 us
    all_to_all x1, blocking collectives, per_device(): got = lax.all_to_all(spread, ('core', 'gy'), 0, 0)  14.6 us
    ppermute x2, starting transfers between devices, swap_cores(): return lax.ppermute(value, GX, [(i, i ^ 1) for i in range(count)])  9.12 us
    ppermute x3, starting transfers between devices, swap_chips(): lax.ppermute(value, GX, [(i, i + 1 if i % 2 else i - 1) for i in range(1,...  7.48 us
    ppermute x3, waiting for transfers between devices, swap_chips(): lax.ppermute(value, GX, [(i, i + 1 if i % 2 else i - 1) for i in range(1,...  4.85 us
    ppermute x1, starting transfers between devices, from_both(): lax.ppermute(to_higher, axis, [(i, i + 1) for i in range(count - 1)])  4.05 us
    pallas_call x1, Pallas kernels, finish(): pl.pallas_call(functools.partial(final_kernel, cells), out_shape=jax.Shap...  3.93 us
    ppermute x1, waiting for transfers between devices, from_both(): lax.ppermute(to_lower, axis, [(i + 1, i) for i in range(count - 1)])  3.88 us
  transfers between devices with their start and end apart: 7, of which 4 were waited for; matrix products, arithmetic and copies ran while one was open for 0% of the time, Pallas kernels for 4%

profile of v13, /device:TPU:1, one launch (start us, length us, event | category | flops | bytes accessed | tf_op | source)
XLA Modules:
  0.0 86.4 jit_solution(12752933798589598359)
XLA Ops:
  0.0 1.3 %copy.3 = f32[4,3,8,2,4,128]{5,4,3,2,1,0:T(4,128)S(1)} copy(f32[4,3,8,2,4,128]{5,2,0,4,3,1:T(8,128)} %bitcast.7) | data formatting | bytes 786432 | tf_op jit(solution)/shard_map/transpose | solution.py:524
  1.3 0.0 copy-start
  1.3 0.7 copy-done
  2.0 4.0 %collective-permute-start = (f32[4,136,128]{2,1,0:T(8,128)S(1)}, f32[4,136,128]{2,1,0:T(8,128)S(1)}, u32[]{:S(2)}, u32[]{:S(2)}) collective-permute-start(f32[4,136,128]{2,1,0:T(8,128)S(1)} %pad_maximum_fusion.1), channel_id=1, source_target_pairs={{0,1},{1,2},{2,3},{3,4},{4,5},{5,6},{6,7},{7,8},{8,9},{9,10},{10,1... | collective-permute-start | bytes 835592 | tf_op jit(solution)/shard_map/ppermute | solution.py:509
  6.1 1.3 %collective-permute-start.1 = (f32[4,136,128]{2,1,0:T(8,128)S(1)}, f32[4,136,128]{2,1,0:T(8,128)S(1)}, u32[]{:S(2)}, u32[]{:S(2)}) collective-permute-start(f32[4,136,128]{2,1,0:T(8,128)S(1)} %pad_maximum_fusion.2), channel_id=1, source_target_pairs={{1,0},{2,1},{3,2},{4,3},{5,4},{6,5},{7,6},{8,7},{9,8},{10,9},{11,1... | collective-permute-start | bytes 835592 | tf_op jit(solution)/shard_map/ppermute | solution.py:510
  7.5 2.1 %collective-permute-done.below = f32[4,136,128]{2,1,0:T(8,128)S(1)} collective-permute-done((f32[4,136,128]{2,1,0:T(8,128)S(1)}, f32[4,136,128]{2,1,0:T(8,128)S(1)}, u32[]{:S(2)}, u32[]{:S(2)}) %collective-permute-start) | collective-permute-done | bytes 278560 | tf_op jit(solution)/shard_map/ppermute | solution.py:509
  9.5 3.9 %collective-permute-done.1.above = f32[4,136,128]{2,1,0:T(8,128)S(1)} collective-permute-done((f32[4,136,128]{2,1,0:T(8,128)S(1)}, f32[4,136,128]{2,1,0:T(8,128)S(1)}, u32[]{:S(2)}, u32[]{:S(2)}) %collective-permute-start.1) | collective-permute-done | bytes 278560 | tf_op jit(solution)/shard_map/ppermute | solution.py:510
  13.4 0.1 pack_all.1
  13.5 7.2 %collective-permute-start.3 = (f32[174,8,128]{2,1,0:T(8,128)S(1)}, f32[174,8,128]{2,1,0:T(8,128)S(1)}, u32[]{:S(2)}, u32[]{:S(2)}) collective-permute-start(f32[174,8,128]{2,1,0:T(8,128)S(1)} %get-tuple-element.15), channel_id=1, source_target_pairs={{0,16},{16,0},{32,48},{48,32},{64,80},{80,64},{96,112},{112,96},{1... | collective-permute-start | bytes 2138120 | tf_op jit(solution)/shard_map/ppermute | solution.py:519
  20.7 1.9 %collective-permute-start.2 = (f32[94,8,128]{2,1,0:T(8,128)S(1)}, f32[94,8,128]{2,1,0:T(8,128)S(1)}, u32[]{:S(2)}, u32[]{:S(2)}) collective-permute-start(f32[94,8,128]{2,1,0:T(8,128)S(1)} %get-tuple-element.14), channel_id=1, source_target_pairs={{16,32},{32,16},{48,64},{64,48},{80,96},{96,80},{112,128},{128,112... | collective-permute-start | bytes 1155080 | tf_op jit(solution)/shard_map/ppermute | solution.py:515
  22.7 3.6 %collective-permute-start.6 = (f32[80,8,128]{2,1,0:T(8,128)S(1)}, f32[80,8,128]{2,1,0:T(8,128)S(1)}, u32[]{:S(2)}, u32[]{:S(2)}) collective-permute-start(f32[80,8,128]{2,1,0:T(8,128)S(1)} %get-tuple-element.20), channel_id=1, source_target_pairs={{16,32},{32,16},{48,64},{64,48},{80,96},{96,80},{112,128},{128,112... | collective-permute-start | bytes 983048 | tf_op jit(solution)/shard_map/ppermute | solution.py:515
  26.3 3.4 %collective-permute-done.2.outer.first_outer = f32[94,8,128]{2,1,0:T(8,128)S(1)} collective-permute-done((f32[94,8,128]{2,1,0:T(8,128)S(1)}, f32[94,8,128]{2,1,0:T(8,128)S(1)}, u32[]{:S(2)}, u32[]{:S(2)}) %collective-permute-start.2) | collective-permute-done | bytes 385056 | tf_op jit(solution)/shard_map/ppermute | solution.py:515
  29.7 0.0 collective-permute-done.3.inner
  29.8 1.6 %first_image.1 = (f32[4,16,8,128]{3,2,1,0:T(8,128)S(1)}, f32[12,24,128]{2,1,0:T(8,128)S(1)}, f32[44,8,128]{2,1,0:T(8,128)S(1)}, f32[44,8,128]{2,1,0:T(8,128)S(1)}) custom-call(f32[4,200,128]{2,1,0:T(8,128)S(1)} %pad_maximum_fusion.own.start, f32[4,136,128]{2,1,0:T(8,128)S(1)} %collective-permute-done.below, f32[4,136,128]{2,1,0:T(8,128)S(1)} %collective-permute-done.1.above, ...), custom_call_target="tpu_custom_call" | custom-call | flops 12000000 | bytes 18000000 | tf_op jit(solution)/shard_map/first_image/pallas_call | solution.py:236
  31.3 1.9 %collective-permute-start.4 = (f32[44,8,128]{2,1,0:T(8,128)S(1)}, f32[44,8,128]{2,1,0:T(8,128)S(1)}, u32[]{:S(2)}, u32[]{:S(2)}) collective-permute-start(f32[44,8,128]{2,1,0:T(8,128)S(1)} %get-tuple-element.18), channel_id=1, source_target_pairs={{16,32},{32,16},{48,64},{64,48},{80,96},{96,80},{112,128},{128,112... | collective-permute-start | bytes 540680 | tf_op jit(solution)/shard_map/ppermute | solution.py:515
  33.2 1.9 %collective-permute-start.5 = (f32[44,8,128]{2,1,0:T(8,128)S(1)}, f32[44,8,128]{2,1,0:T(8,128)S(1)}, u32[]{:S(2)}, u32[]{:S(2)}) collective-permute-start(f32[44,8,128]{2,1,0:T(8,128)S(1)} %get-tuple-element.19), channel_id=1, source_target_pairs={{0,16},{16,0},{32,48},{48,32},{64,80},{80,64},{96,112},{112,96},{1... | collective-permute-start | bytes 540680 | tf_op jit(solution)/shard_map/ppermute | solution.py:519
  35.2 0.0 collective-permute-done.6.outer
  35.2 1.5 %old_images.1.old_image = f32[4,128,128]{2,1,0:T(8,128)S(1)} custom-call(f32[12,24,128]{2,1,0:T(8,128)S(1)} %get-tuple-element.17.coef, f32[4,200,128]{2,1,0:T(8,128)S(1)} %pad_maximum_fusion.own.start, f32[4,136,128]{2,1,0:T(8,128)S(1)} %collective-permute-done.below, f32[4,136,128]{2,1,0:T(8,128)S(1)} %collective-permute-done.1.above, ...), custom_call_target="tpu_custom_call" | custom-call | flops 12000000 | bytes 24000000 | tf_op jit(solution)/shard_map/old_images/pallas_call | solution.py:269
  36.7 1.4 %collective-permute-done.4.outer = f32[44,8,128]{2,1,0:T(8,128)S(1)} collective-permute-done((f32[44,8,128]{2,1,0:T(8,128)S(1)}, f32[44,8,128]{2,1,0:T(8,128)S(1)}, u32[]{:S(2)}, u32[]{:S(2)}) %collective-permute-start.4) | collective-permute-done | bytes 180256 | tf_op jit(solution)/shard_map/ppermute | solution.py:515
  38.1 0.0 collective-permute-done.5.inner
  38.1 1.5 %image_and_gram.1 = (f32[4,64,128]{2,1,0:T(8,128)S(1)}, f32[32,8,128]{2,1,0:T(8,128)S(1)}) custom-call(f32[4,16,8,128]{3,2,1,0:T(8,128)S(1)} %get-tuple-element.16.w, f32[12,24,128]{2,1,0:T(8,128)S(1)} %get-tuple-element.17.coef, f32[44,8,128]{2,1,0:T(8,128)S(1)} %collective-permute-done.4.outer, f32[44,8,128]{2,1,0:T(8,128)S(1)} %collective-permute-done.5.inner, ...), custom_call_target="tpu_custom_call" | custom-call | tf_op jit(solution)/shard_map/image_and_gram/pallas_call | solution.py:373
  39.7 14.6 %all_to_all.10.parts = f32[32,8,128]{2,1,0:T(8,128)S(1)} all-to-all(f32[32,8,128]{2,1,0:T(8,128)S(1)} %get-tuple-element.21), channel_id=1, replica_groups=mesh['z'=16,'core'=2,'gy'=16] {'core','gy'}, dimensions={0} | all-to-all | bytes 262144 | tf_op jit(solution)/shard_map/all_to_all | solution.py:538
  54.3 28.1 %all_to_all.11.parts = f32[16,8,128]{2,1,0:T(8,128)S(1)} all-to-all(f32[16,8,128]{2,1,0:T(8,128)S(1)} %sum_and_spread.1), channel_id=1, replica_groups=mesh['z'=16,'core'=2,'gy'=16] {'z'}, dimensions={0} | all-to-all | bytes 131072 | tf_op jit(solution)/shard_map/all_to_all | solution.py:539
  82.4 3.9 %finish.1 = f32[2,8,4,8,128]{4,3,2,1,0:T(8,128)} custom-call(f32[16,8,128]{2,1,0:T(8,128)S(1)} %all_to_all.11.parts, f32[4,200,128]{2,1,0:T(8,128)S(1)} %pad_maximum_fusion.own.start, f32[4,16,8,128]{3,2,1,0:T(8,128)S(1)} %get-tuple-element.16.w, f32[4,128,128]{2,1,0:T(8,128)S(1)} %old_images.1.old_image, f32[4,64,128]{2,1,0:T(8,128)S(1)} %get-tuple-element.22.w_image), custom_call_target="tpu_custom_call" | custom-call | tf_op jit(solution)/shard_map/finish/pallas_call | solution.py:494
  (7 shorter events, 0.2 us)
Async XLA Ops:
  1.3 0.7 copy-start
  2.0 7.5 %collective-permute-start = (f32[4,136,128]{2,1,0:T(8,128)S(1)}, f32[4,136,128]{2,1,0:T(8,128)S(1)}, u32[]{:S(2)}, u32[]{:S(2)}) collective-permute-start(f32[4,136,128]{2,1,0:T(8,128)S(1)} %pad_maximum_fusion.1), channel_id=1, source_target_pairs={{0,1},{1,2},{2,3},{3,4},{4,5},{5,6},{6,7},{7,8},{8,9},{9,10},{10,1... | collective-permute-start | bytes 835592 | tf_op jit(solution)/shard_map/ppermute | solution.py:509
  6.1 7.3 %collective-permute-start.1 = (f32[4,136,128]{2,1,0:T(8,128)S(1)}, f32[4,136,128]{2,1,0:T(8,128)S(1)}, u32[]{:S(2)}, u32[]{:S(2)}) collective-permute-start(f32[4,136,128]{2,1,0:T(8,128)S(1)} %pad_maximum_fusion.2), channel_id=1, source_target_pairs={{1,0},{2,1},{3,2},{4,3},{5,4},{6,5},{7,6},{8,7},{9,8},{10,9},{11,1... | collective-permute-start | bytes 835592 | tf_op jit(solution)/shard_map/ppermute | solution.py:510
  13.5 16.2 %collective-permute-start.3 = (f32[174,8,128]{2,1,0:T(8,128)S(1)}, f32[174,8,128]{2,1,0:T(8,128)S(1)}, u32[]{:S(2)}, u32[]{:S(2)}) collective-permute-start(f32[174,8,128]{2,1,0:T(8,128)S(1)} %get-tuple-element.15), channel_id=1, source_target_pairs={{0,16},{16,0},{32,48},{48,32},{64,80},{80,64},{96,112},{112,96},{1... | collective-permute-start | bytes 2138120 | tf_op jit(solution)/shard_map/ppermute | solution.py:519
  20.7 9.0 %collective-permute-start.2 = (f32[94,8,128]{2,1,0:T(8,128)S(1)}, f32[94,8,128]{2,1,0:T(8,128)S(1)}, u32[]{:S(2)}, u32[]{:S(2)}) collective-permute-start(f32[94,8,128]{2,1,0:T(8,128)S(1)} %get-tuple-element.14), channel_id=1, source_target_pairs={{16,32},{32,16},{48,64},{64,48},{80,96},{96,80},{112,128},{128,112... | collective-permute-start | bytes 1155080 | tf_op jit(solution)/shard_map/ppermute | solution.py:515
  22.7 12.5 %collective-permute-start.6 = (f32[80,8,128]{2,1,0:T(8,128)S(1)}, f32[80,8,128]{2,1,0:T(8,128)S(1)}, u32[]{:S(2)}, u32[]{:S(2)}) collective-permute-start(f32[80,8,128]{2,1,0:T(8,128)S(1)} %get-tuple-element.20), channel_id=1, source_target_pairs={{16,32},{32,16},{48,64},{64,48},{80,96},{96,80},{112,128},{128,112... | collective-permute-start | bytes 983048 | tf_op jit(solution)/shard_map/ppermute | solution.py:515
  31.3 6.8 %collective-permute-start.4 = (f32[44,8,128]{2,1,0:T(8,128)S(1)}, f32[44,8,128]{2,1,0:T(8,128)S(1)}, u32[]{:S(2)}, u32[]{:S(2)}) collective-permute-start(f32[44,8,128]{2,1,0:T(8,128)S(1)} %get-tuple-element.18), channel_id=1, source_target_pairs={{16,32},{32,16},{48,64},{64,48},{80,96},{96,80},{112,128},{128,112... | collective-permute-start | bytes 540680 | tf_op jit(solution)/shard_map/ppermute | solution.py:515
  33.2 4.9 %collective-permute-start.5 = (f32[44,8,128]{2,1,0:T(8,128)S(1)}, f32[44,8,128]{2,1,0:T(8,128)S(1)}, u32[]{:S(2)}, u32[]{:S(2)}) collective-permute-start(f32[44,8,128]{2,1,0:T(8,128)S(1)} %get-tuple-element.19), channel_id=1, source_target_pairs={{0,16},{16,0},{32,48},{48,32},{64,80},{80,64},{96,112},{112,96},{1... | collective-permute-start | bytes 540680 | tf_op jit(solution)/shard_map/ppermute | solution.py:519

commit v14 on v12

--- a/solution.py
+++ b/solution.py
@@ -503,6 +503,35 @@
 GX = ("z", "core")
 
 
+def turn_kernel(prior, coefficient, start, up, down):
+    for x in range(LX):
+        for k in range(3):
+            block = jnp.swapaxes(prior[k, :, :, x].reshape(8, LY, NZ), 0, 1).reshape(BLOCK, NZ)
+            start[x, pl.ds(k * BLOCK, BLOCK), :] = block
+            if k < 2:
+                up[x, pl.ds(k * HALF, HALF), :] = block[HALF:]
+                down[x, pl.ds(k * HALF, HALF), :] = block[:HALF]
+            else:
+                up[x, pl.ds(2 * HALF, BLOCK), :] = block
+                down[x, pl.ds(2 * HALF, BLOCK), :] = block
+        value = coefficient[x]
+        start[x, pl.ds(3 * BLOCK, LY), :] = value
+        up[x, pl.ds(2 * HALF + BLOCK, LY), :] = value
+        down[x, pl.ds(2 * HALF + BLOCK, LY), :] = value
+
+
+def turn(prior, coefficient):
+    message = jax.ShapeDtypeStruct((LX, 2 * HALF + BLOCK + LY, NZ), F32)
+    return pl.pallas_call(
+        turn_kernel,
+        out_shape=(jax.ShapeDtypeStruct((LX, 3 * BLOCK + LY, NZ), F32), message, message),
+        in_specs=[VMEM] * 2,
+        out_specs=(VMEM,) * 3,
+        compiler_params=pltpu.CompilerParams(vmem_limit_bytes=1 << 20),
+        name="turn",
+    )(prior, coefficient)
+
+
 def from_both(axis, count, to_higher, to_lower):
     return (
         lax.ppermute(to_higher, axis, [(i, i + 1) for i in range(count - 1)]),
@@ -518,10 +547,7 @@
 
 def per_device(nx, ny, nz, prior, coefficient):
     cells = coefficient.size * nx * ny
-    by_cell = prior.transpose(3, 0, 4, 1, 2, 5).reshape(LX, 3 * LY * 8, NZ)
-    start = jnp.concatenate([by_cell, coefficient], axis=1)
-    up = jnp.concatenate([start[:, HALF:BLOCK], start[:, BLOCK + HALF:]], axis=1)
-    down = jnp.concatenate([start[:, :HALF], start[:, BLOCK:BLOCK + HALF], start[:, 2 * BLOCK:]], axis=1)
+    start, up, down = turn(prior, coefficient)
     rims = from_both("gy", ny, up, down)
     outward, inward, old_outward, old_inward = pack_all(start, *rims)
     sides = exchange(nx, outward, inward)

time: 85.4 us -> 85.1 us (level)
    transpose x1 -> x0, local copies, waits for them, and re-layouts: 1.25 us -> none  [per_device(): by_cell = prior.transpose(3, 0, 4, 1, 2, 5).reshape(LX, 3 * LY * 8, NZ)]
    unnamed x2 -> x4, local copies, waits for them, and re-layouts: 0.69 us -> 1.71 us
where the time goes in v14:
time: 85.1 us; the launch traced here: 84.6 us
  blocking collectives  41.9 us (49%)
  starting transfers between devices  26.1 us (31%)
  Pallas kernels  8.8 us (10%)
  waiting for transfers between devices  6.01 us (7%)
  local copies, waits for them, and re-layouts  1.71 us (2%)
    all_to_all x1, blocking collectives, per_device(): got = lax.all_to_all(sum_and_spread(got, nz), 'z', 0, 0)  25.8 us
    ppermute x6, starting transfers between devices, exchange(): return (lax.ppermute(outward, GX, outer), lax.ppermute(inward, GX, inner))  20.7 us
    all_to_all x1, blocking collectives, per_device(): got = lax.all_to_all(spread, ('core', 'gy'), 0, 0)  16.1 us
    ppermute x1, starting transfers between devices, from_both(): lax.ppermute(to_higher, axis, [(i, i + 1) for i in range(count - 1)])  4.05 us
    pallas_call x1, Pallas kernels, finish(): pl.pallas_call(functools.partial(final_kernel, cells), out_shape=jax.Shap...  3.93 us
    ppermute x1, waiting for transfers between devices, from_both(): lax.ppermute(to_lower, axis, [(i + 1, i) for i in range(count - 1)])  3.83 us
    ppermute x1, waiting for transfers between devices, from_both(): lax.ppermute(to_higher, axis, [(i, i + 1) for i in range(count - 1)])  2.16 us
    unnamed x4, local copies, waits for them, and re-layouts  1.71 us
  transfers between devices with their start and end apart: 8, of which 2 were waited for; matrix products, arithmetic and copies ran while one was open for 0% of the time, Pallas kernels for 4%

profile of v14, /device:TPU:1, one launch (start us, length us, event | category | flops | bytes accessed | tf_op | source)
XLA Modules:
  0.0 84.6 jit_solution(272360033814642009)
XLA Ops:
  0.0 0.0 copy-start
  0.0 1.0 %copy-done = f32[3,2,4,4,8,128]{5,4,3,2,1,0:T(8,128)S(1)} copy-done((f32[3,2,4,4,8,128]{5,4,3,2,1,0:T(8,128)S(1)}, f32[3,2,4,4,8,128]{5,4,3,2,1,0:T(8,128)}, u32[]{:S(2)}) %copy-start) | copy-done | bytes 393240
  1.0 0.0 copy-start.1
  1.0 0.7 copy-done.1
  1.7 0.1 turn.1
  1.8 4.0 %collective-permute-start = (f32[4,136,128]{2,1,0:T(8,128)S(1)}, f32[4,136,128]{2,1,0:T(8,128)S(1)}, u32[]{:S(2)}, u32[]{:S(2)}) collective-permute-start(f32[4,136,128]{2,1,0:T(8,128)S(1)} %get-tuple-element.19), channel_id=1, source_target_pairs={{0,1},{1,2},{2,3},{3,4},{4,5},{5,6},{6,7},{7,8},{8,9},{9,10},{10,1... | collective-permute-start | bytes 835592 | tf_op jit(solution)/shard_map/ppermute | solution.py:537
  5.9 1.3 %collective-permute-start.1 = (f32[4,136,128]{2,1,0:T(8,128)S(1)}, f32[4,136,128]{2,1,0:T(8,128)S(1)}, u32[]{:S(2)}, u32[]{:S(2)}) collective-permute-start(f32[4,136,128]{2,1,0:T(8,128)S(1)} %get-tuple-element.20), channel_id=1, source_target_pairs={{1,0},{2,1},{3,2},{4,3},{5,4},{6,5},{7,6},{8,7},{9,8},{10,9},{11,1... | collective-permute-start | bytes 835592 | tf_op jit(solution)/shard_map/ppermute | solution.py:538
  7.2 2.2 %collective-permute-done.below = f32[4,136,128]{2,1,0:T(8,128)S(1)} collective-permute-done((f32[4,136,128]{2,1,0:T(8,128)S(1)}, f32[4,136,128]{2,1,0:T(8,128)S(1)}, u32[]{:S(2)}, u32[]{:S(2)}) %collective-permute-start) | collective-permute-done | bytes 278560 | tf_op jit(solution)/shard_map/ppermute | solution.py:537
  9.3 3.8 %collective-permute-done.1.above = f32[4,136,128]{2,1,0:T(8,128)S(1)} collective-permute-done((f32[4,136,128]{2,1,0:T(8,128)S(1)}, f32[4,136,128]{2,1,0:T(8,128)S(1)}, u32[]{:S(2)}, u32[]{:S(2)}) %collective-permute-start.1) | collective-permute-done | bytes 278560 | tf_op jit(solution)/shard_map/ppermute | solution.py:538
  13.2 0.1 pack_all.1
  13.3 7.1 %collective-permute-start.2 = (f32[94,8,128]{2,1,0:T(8,128)S(1)}, f32[94,8,128]{2,1,0:T(8,128)S(1)}, u32[]{:S(2)}, u32[]{:S(2)}) collective-permute-start(f32[94,8,128]{2,1,0:T(8,128)S(1)} %get-tuple-element.21), channel_id=1, source_target_pairs={{16,32},{32,16},{48,64},{64,48},{80,96},{96,80},{112,128},{128,112... | collective-permute-start | bytes 1155080 | tf_op jit(solution)/shard_map/ppermute | solution.py:545
  20.4 1.9 %collective-permute-start.3 = (f32[94,8,128]{2,1,0:T(8,128)S(1)}, f32[94,8,128]{2,1,0:T(8,128)S(1)}, u32[]{:S(2)}, u32[]{:S(2)}) collective-permute-start(f32[94,8,128]{2,1,0:T(8,128)S(1)} %get-tuple-element.22), channel_id=1, source_target_pairs={{0,16},{16,0},{32,48},{48,32},{64,80},{80,64},{96,112},{112,96},{1... | collective-permute-start | bytes 1155080 | tf_op jit(solution)/shard_map/ppermute | solution.py:545
  22.3 3.9 %collective-permute-start.6 = (f32[80,8,128]{2,1,0:T(8,128)S(1)}, f32[80,8,128]{2,1,0:T(8,128)S(1)}, u32[]{:S(2)}, u32[]{:S(2)}) collective-permute-start(f32[80,8,128]{2,1,0:T(8,128)S(1)} %get-tuple-element.27), channel_id=1, source_target_pairs={{16,32},{32,16},{48,64},{64,48},{80,96},{96,80},{112,128},{128,112... | collective-permute-start | bytes 983048 | tf_op jit(solution)/shard_map/ppermute | solution.py:545
  26.2 1.9 %collective-permute-start.7 = (f32[80,8,128]{2,1,0:T(8,128)S(1)}, f32[80,8,128]{2,1,0:T(8,128)S(1)}, u32[]{:S(2)}, u32[]{:S(2)}) collective-permute-start(f32[80,8,128]{2,1,0:T(8,128)S(1)} %get-tuple-element.28), channel_id=1, source_target_pairs={{0,16},{16,0},{32,48},{48,32},{64,80},{80,64},{96,112},{112,96},{1... | collective-permute-start | bytes 983048 | tf_op jit(solution)/shard_map/ppermute | solution.py:545
  28.2 0.0 collective-permute-done.2.outer.first_outer
  28.2 0.0 collective-permute-done.3.inner.first_inner
  28.2 1.6 %first_image.1 = (f32[4,16,8,128]{3,2,1,0:T(8,128)S(1)}, f32[12,24,128]{2,1,0:T(8,128)S(1)}, f32[44,8,128]{2,1,0:T(8,128)S(1)}, f32[44,8,128]{2,1,0:T(8,128)S(1)}) custom-call(f32[4,200,128]{2,1,0:T(8,128)S(1)} %get-tuple-element.18.own.start, f32[4,136,128]{2,1,0:T(8,128)S(1)} %collective-permute-done.below, ...), custom_call_target="tpu_custom_call" | custom-call | flops 12000000 | bytes 18000000 | tf_op jit(solution)/shard_map/first_image/pallas_call | solution.py:236
  29.8 3.9 %collective-permute-start.4 = (f32[44,8,128]{2,1,0:T(8,128)S(1)}, f32[44,8,128]{2,1,0:T(8,128)S(1)}, u32[]{:S(2)}, u32[]{:S(2)}) collective-permute-start(f32[44,8,128]{2,1,0:T(8,128)S(1)} %get-tuple-element.25), channel_id=1, source_target_pairs={{16,32},{32,16},{48,64},{64,48},{80,96},{96,80},{112,128},{128,112... | collective-permute-start | bytes 540680 | tf_op jit(solution)/shard_map/ppermute | solution.py:545
  33.7 1.9 %collective-permute-start.5 = (f32[44,8,128]{2,1,0:T(8,128)S(1)}, f32[44,8,128]{2,1,0:T(8,128)S(1)}, u32[]{:S(2)}, u32[]{:S(2)}) collective-permute-start(f32[44,8,128]{2,1,0:T(8,128)S(1)} %get-tuple-element.26), channel_id=1, source_target_pairs={{0,16},{16,0},{32,48},{48,32},{64,80},{80,64},{96,112},{112,96},{1... | collective-permute-start | bytes 540680 | tf_op jit(solution)/shard_map/ppermute | solution.py:545
  35.6 0.0 collective-permute-done.6.outer
  35.6 0.0 collective-permute-done.7.inner
  35.7 1.5 %old_images.1.old_image = f32[4,128,128]{2,1,0:T(8,128)S(1)} custom-call(f32[12,24,128]{2,1,0:T(8,128)S(1)} %get-tuple-element.24.coef, f32[4,200,128]{2,1,0:T(8,128)S(1)} %get-tuple-element.18.own.start, f32[4,136,128]{2,1,0:T(8,128)S(1)} %collective-permute-done.below, f32[4,136,128]{2,1,0:T(8,128)S(1)} %collective-permute-done.1.above, ...), custom_call_target="tpu_custom_call" | custom-call | flops 12000000 | bytes 24000000 | tf_op jit(solution)/shard_map/old_images/pallas_call | solution.py:268
  37.2 0.0 collective-permute-done.4.outer
  37.2 0.0 collective-permute-done.5.inner
  37.2 1.5 %image_and_gram.1 = (f32[4,64,128]{2,1,0:T(8,128)S(1)}, f32[32,8,128]{2,1,0:T(8,128)S(1)}) custom-call(f32[4,16,8,128]{3,2,1,0:T(8,128)S(1)} %get-tuple-element.23.w, f32[12,24,128]{2,1,0:T(8,128)S(1)} %get-tuple-element.24.coef, f32[44,8,128]{2,1,0:T(8,128)S(1)} %collective-permute-done.4.outer, f32[44,8,128]{2,1,0:T(8,128)S(1)} %collective-permute-done.5.inner, ...), custom_call_target="tpu_custom_call" | custom-call | tf_op jit(solution)/shard_map/image_and_gram/pallas_call | solution.py:372
  38.8 16.1 %all_to_all.10.parts = f32[32,8,128]{2,1,0:T(8,128)S(1)} all-to-all(f32[32,8,128]{2,1,0:T(8,128)S(1)} %get-tuple-element.29), channel_id=1, replica_groups=mesh['z'=16,'core'=2,'gy'=16] {'core','gy'}, dimensions={0} | all-to-all | bytes 262144 | tf_op jit(solution)/shard_map/all_to_all | solution.py:560
  54.9 25.8 %all_to_all.11.parts = f32[16,8,128]{2,1,0:T(8,128)S(1)} all-to-all(f32[16,8,128]{2,1,0:T(8,128)S(1)} %sum_and_spread.1), channel_id=1, replica_groups=mesh['z'=16,'core'=2,'gy'=16] {'z'}, dimensions={0} | all-to-all | bytes 131072 | tf_op jit(solution)/shard_map/all_to_all | solution.py:561
  80.7 3.9 %finish.1 = f32[2,8,4,8,128]{4,3,2,1,0:T(8,128)} custom-call(f32[16,8,128]{2,1,0:T(8,128)S(1)} %all_to_all.11.parts, f32[4,200,128]{2,1,0:T(8,128)S(1)} %get-tuple-element.18.own.start, f32[4,16,8,128]{3,2,1,0:T(8,128)S(1)} %get-tuple-element.23.w, f32[4,128,128]{2,1,0:T(8,128)S(1)} %old_images.1.old_image, f32[4,64,128]{2,1,0:T(8,128)S(1)} %get-tuple-element.30.w_image), custom_call_target="tpu_custom_call" | custom-call | tf_op jit(solution)/shard_map/finish/pallas_call | solution.py:493
  (1 shorter events, 0.0 us)
Async XLA Ops:
  0.0 1.0 %copy-start = (f32[3,2,4,4,8,128]{5,4,3,2,1,0:T(8,128)S(1)}, f32[3,2,4,4,8,128]{5,4,3,2,1,0:T(8,128)}, u32[]{:S(2)}) copy-start(f32[3,2,4,4,8,128]{5,4,3,2,1,0:T(8,128)} %prior.1) | copy-start | bytes 1179652
  1.0 0.7 copy-start.1
  1.8 7.5 %collective-permute-start = (f32[4,136,128]{2,1,0:T(8,128)S(1)}, f32[4,136,128]{2,1,0:T(8,128)S(1)}, u32[]{:S(2)}, u32[]{:S(2)}) collective-permute-start(f32[4,136,128]{2,1,0:T(8,128)S(1)} %get-tuple-element.19), channel_id=1, source_target_pairs={{0,1},{1,2},{2,3},{3,4},{4,5},{5,6},{6,7},{7,8},{8,9},{9,10},{10,1... | collective-permute-start | bytes 835592 | tf_op jit(solution)/shard_map/ppermute | solution.py:537
  5.9 7.3 %collective-permute-start.1 = (f32[4,136,128]{2,1,0:T(8,128)S(1)}, f32[4,136,128]{2,1,0:T(8,128)S(1)}, u32[]{:S(2)}, u32[]{:S(2)}) collective-permute-start(f32[4,136,128]{2,1,0:T(8,128)S(1)} %get-tuple-element.20), channel_id=1, source_target_pairs={{1,0},{2,1},{3,2},{4,3},{5,4},{6,5},{7,6},{8,7},{9,8},{10,9},{11,1... | collective-permute-start | bytes 835592 | tf_op jit(solution)/shard_map/ppermute | solution.py:538
  13.3 14.9 %collective-permute-start.2 = (f32[94,8,128]{2,1,0:T(8,128)S(1)}, f32[94,8,128]{2,1,0:T(8,128)S(1)}, u32[]{:S(2)}, u32[]{:S(2)}) collective-permute-start(f32[94,8,128]{2,1,0:T(8,128)S(1)} %get-tuple-element.21), channel_id=1, source_target_pairs={{16,32},{32,16},{48,64},{64,48},{80,96},{96,80},{112,128},{128,112... | collective-permute-start | bytes 1155080 | tf_op jit(solution)/shard_map/ppermute | solution.py:545
  20.4 7.8 %collective-permute-start.3 = (f32[94,8,128]{2,1,0:T(8,128)S(1)}, f32[94,8,128]{2,1,0:T(8,128)S(1)}, u32[]{:S(2)}, u32[]{:S(2)}) collective-permute-start(f32[94,8,128]{2,1,0:T(8,128)S(1)} %get-tuple-element.22), channel_id=1, source_target_pairs={{0,16},{16,0},{32,48},{48,32},{64,80},{80,64},{96,112},{112,96},{1... | collective-permute-start | bytes 1155080 | tf_op jit(solution)/shard_map/ppermute | solution.py:545
  22.3 13.3 %collective-permute-start.6 = (f32[80,8,128]{2,1,0:T(8,128)S(1)}, f32[80,8,128]{2,1,0:T(8,128)S(1)}, u32[]{:S(2)}, u32[]{:S(2)}) collective-permute-start(f32[80,8,128]{2,1,0:T(8,128)S(1)} %get-tuple-element.27), channel_id=1, source_target_pairs={{16,32},{32,16},{48,64},{64,48},{80,96},{96,80},{112,128},{128,112... | collective-permute-start | bytes 983048 | tf_op jit(solution)/shard_map/ppermute | solution.py:545
  26.2 9.4 %collective-permute-start.7 = (f32[80,8,128]{2,1,0:T(8,128)S(1)}, f32[80,8,128]{2,1,0:T(8,128)S(1)}, u32[]{:S(2)}, u32[]{:S(2)}) collective-permute-start(f32[80,8,128]{2,1,0:T(8,128)S(1)} %get-tuple-element.28), channel_id=1, source_target_pairs={{0,16},{16,0},{32,48},{48,32},{64,80},{80,64},{96,112},{112,96},{1... | collective-permute-start | bytes 983048 | tf_op jit(solution)/shard_map/ppermute | solution.py:545
  29.8 7.4 %collective-permute-start.4 = (f32[44,8,128]{2,1,0:T(8,128)S(1)}, f32[44,8,128]{2,1,0:T(8,128)S(1)}, u32[]{:S(2)}, u32[]{:S(2)}) collective-permute-start(f32[44,8,128]{2,1,0:T(8,128)S(1)} %get-tuple-element.25), channel_id=1, source_target_pairs={{16,32},{32,16},{48,64},{64,48},{80,96},{96,80},{112,128},{128,112... | collective-permute-start | bytes 540680 | tf_op jit(solution)/shard_map/ppermute | solution.py:545
  33.7 3.5 %collective-permute-start.5 = (f32[44,8,128]{2,1,0:T(8,128)S(1)}, f32[44,8,128]{2,1,0:T(8,128)S(1)}, u32[]{:S(2)}, u32[]{:S(2)}) collective-permute-start(f32[44,8,128]{2,1,0:T(8,128)S(1)} %get-tuple-element.26), channel_id=1, source_target_pairs={{0,16},{16,0},{32,48},{48,32},{64,80},{80,64},{96,112},{112,96},{1... | collective-permute-start | bytes 540680 | tf_op jit(solution)/shard_map/ppermute | solution.py:545

commit v15 on v14

--- a/solution.py
+++ b/solution.py
@@ -503,7 +503,13 @@
 GX = ("z", "core")
 
 
-def turn_kernel(prior, coefficient, start, up, down):
+def turn_kernel(prior_hbm, coefficient_hbm, start, up, down, prior, coefficient, arrived):
+    copies = (pltpu.make_async_copy(prior_hbm, prior, arrived.at[0]),
+              pltpu.make_async_copy(coefficient_hbm, coefficient, arrived.at[1]))
+    for copy in copies:
+        copy.start()
+    for copy in copies:
+        copy.wait()
     for x in range(LX):
         for k in range(3):
             block = jnp.swapaxes(prior[k, :, :, x].reshape(8, LY, NZ), 0, 1).reshape(BLOCK, NZ)
@@ -525,8 +531,10 @@
     return pl.pallas_call(
         turn_kernel,
         out_shape=(jax.ShapeDtypeStruct((LX, 3 * BLOCK + LY, NZ), F32), message, message),
-        in_specs=[VMEM] * 2,
+        in_specs=[pl.BlockSpec(memory_space=pl.ANY)] * 2,
         out_specs=(VMEM,) * 3,
+        scratch_shapes=[pltpu.VMEM(prior.shape, F32), pltpu.VMEM(coefficient.shape, F32),
+                        pltpu.SemaphoreType.DMA((2,))],
         compiler_params=pltpu.CompilerParams(vmem_limit_bytes=1 << 20),
         name="turn",
     )(prior, coefficient)

time: 85.1 us -> 85.3 us (level)
  no operation moved by 1% of the time
where the time goes in v15:
time: 85.3 us; the launch traced here: 84.8 us
  blocking collectives  41.9 us (49%)
  starting transfers between devices  26.1 us (31%)
  Pallas kernels  9.02 us (11%)
  waiting for transfers between devices  6.01 us (7%)
  local copies, waits for them, and re-layouts  1.71 us (2%)
    all_to_all x1, blocking collectives, per_device(): got = lax.all_to_all(sum_and_spread(got, nz), 'z', 0, 0)  25.8 us
    ppermute x6, starting transfers between devices, exchange(): return (lax.ppermute(outward, GX, outer), lax.ppermute(inward, GX, inner))  20.7 us
    all_to_all x1, blocking collectives, per_device(): got = lax.all_to_all(spread, ('core', 'gy'), 0, 0)  16.1 us
    ppermute x1, starting transfers between devices, from_both(): lax.ppermute(to_higher, axis, [(i, i + 1) for i in range(count - 1)])  4.05 us
    pallas_call x1, Pallas kernels, finish(): pl.pallas_call(functools.partial(final_kernel, cells), out_shape=jax.Shap...  3.93 us
    ppermute x1, waiting for transfers between devices, from_both(): lax.ppermute(to_lower, axis, [(i + 1, i) for i in range(count - 1)])  3.83 us
    ppermute x1, waiting for transfers between devices, from_both(): lax.ppermute(to_higher, axis, [(i, i + 1) for i in range(count - 1)])  2.16 us
    unnamed x4, local copies, waits for them, and re-layouts  1.71 us
  transfers between devices with their start and end apart: 8, of which 2 were waited for; matrix products, arithmetic and copies ran while one was open for 0% of the time, Pallas kernels for 4%

profile of v15, /device:TPU:1, one launch (start us, length us, event | category | flops | bytes accessed | tf_op | source)
XLA Modules:
  0.0 84.8 jit_solution(7840739452814056604)
XLA Ops:
  0.0 0.0 copy-start
  0.0 1.0 %copy-done = f32[3,2,4,4,8,128]{5,4,3,2,1,0:T(8,128)S(1)} copy-done((f32[3,2,4,4,8,128]{5,4,3,2,1,0:T(8,128)S(1)}, f32[3,2,4,4,8,128]{5,4,3,2,1,0:T(8,128)}, u32[]{:S(2)}) %copy-start) | copy-done | bytes 393240
  1.0 0.0 copy-start.1
  1.0 0.7 copy-done.1
  1.7 0.3 turn.1
  2.0 4.0 %collective-permute-start = (f32[4,136,128]{2,1,0:T(8,128)S(1)}, f32[4,136,128]{2,1,0:T(8,128)S(1)}, u32[]{:S(2)}, u32[]{:S(2)}) collective-permute-start(f32[4,136,128]{2,1,0:T(8,128)S(1)} %get-tuple-element.19), channel_id=1, source_target_pairs={{0,1},{1,2},{2,3},{3,4},{4,5},{5,6},{6,7},{7,8},{8,9},{9,10},{10,1... | collective-permute-start | bytes 835592 | tf_op jit(solution)/shard_map/ppermute | solution.py:545
  6.1 1.3 %collective-permute-start.1 = (f32[4,136,128]{2,1,0:T(8,128)S(1)}, f32[4,136,128]{2,1,0:T(8,128)S(1)}, u32[]{:S(2)}, u32[]{:S(2)}) collective-permute-start(f32[4,136,128]{2,1,0:T(8,128)S(1)} %get-tuple-element.20), channel_id=1, source_target_pairs={{1,0},{2,1},{3,2},{4,3},{5,4},{6,5},{7,6},{8,7},{9,8},{10,9},{11,1... | collective-permute-start | bytes 835592 | tf_op jit(solution)/shard_map/ppermute | solution.py:546
  7.4 2.2 %collective-permute-done.below = f32[4,136,128]{2,1,0:T(8,128)S(1)} collective-permute-done((f32[4,136,128]{2,1,0:T(8,128)S(1)}, f32[4,136,128]{2,1,0:T(8,128)S(1)}, u32[]{:S(2)}, u32[]{:S(2)}) %collective-permute-start) | collective-permute-done | bytes 278560 | tf_op jit(solution)/shard_map/ppermute | solution.py:545
  9.5 3.8 %collective-permute-done.1.above = f32[4,136,128]{2,1,0:T(8,128)S(1)} collective-permute-done((f32[4,136,128]{2,1,0:T(8,128)S(1)}, f32[4,136,128]{2,1,0:T(8,128)S(1)}, u32[]{:S(2)}, u32[]{:S(2)}) %collective-permute-start.1) | collective-permute-done | bytes 278560 | tf_op jit(solution)/shard_map/ppermute | solution.py:546
  13.4 0.1 pack_all.1
  13.5 7.1 %collective-permute-start.2 = (f32[94,8,128]{2,1,0:T(8,128)S(1)}, f32[94,8,128]{2,1,0:T(8,128)S(1)}, u32[]{:S(2)}, u32[]{:S(2)}) collective-permute-start(f32[94,8,128]{2,1,0:T(8,128)S(1)} %get-tuple-element.21), channel_id=1, source_target_pairs={{16,32},{32,16},{48,64},{64,48},{80,96},{96,80},{112,128},{128,112... | collective-permute-start | bytes 1155080 | tf_op jit(solution)/shard_map/ppermute | solution.py:553
  20.6 1.9 %collective-permute-start.3 = (f32[94,8,128]{2,1,0:T(8,128)S(1)}, f32[94,8,128]{2,1,0:T(8,128)S(1)}, u32[]{:S(2)}, u32[]{:S(2)}) collective-permute-start(f32[94,8,128]{2,1,0:T(8,128)S(1)} %get-tuple-element.22), channel_id=1, source_target_pairs={{0,16},{16,0},{32,48},{48,32},{64,80},{80,64},{96,112},{112,96},{1... | collective-permute-start | bytes 1155080 | tf_op jit(solution)/shard_map/ppermute | solution.py:553
  22.5 3.9 %collective-permute-start.6 = (f32[80,8,128]{2,1,0:T(8,128)S(1)}, f32[80,8,128]{2,1,0:T(8,128)S(1)}, u32[]{:S(2)}, u32[]{:S(2)}) collective-permute-start(f32[80,8,128]{2,1,0:T(8,128)S(1)} %get-tuple-element.27), channel_id=1, source_target_pairs={{16,32},{32,16},{48,64},{64,48},{80,96},{96,80},{112,128},{128,112... | collective-permute-start | bytes 983048 | tf_op jit(solution)/shard_map/ppermute | solution.py:553
  26.5 1.9 %collective-permute-start.7 = (f32[80,8,128]{2,1,0:T(8,128)S(1)}, f32[80,8,128]{2,1,0:T(8,128)S(1)}, u32[]{:S(2)}, u32[]{:S(2)}) collective-permute-start(f32[80,8,128]{2,1,0:T(8,128)S(1)} %get-tuple-element.28), channel_id=1, source_target_pairs={{0,16},{16,0},{32,48},{48,32},{64,80},{80,64},{96,112},{112,96},{1... | collective-permute-start | bytes 983048 | tf_op jit(solution)/shard_map/ppermute | solution.py:553
  28.4 0.0 collective-permute-done.2.outer.first_outer
  28.4 0.0 collective-permute-done.3.inner.first_inner
  28.4 1.6 %first_image.1 = (f32[4,16,8,128]{3,2,1,0:T(8,128)S(1)}, f32[12,24,128]{2,1,0:T(8,128)S(1)}, f32[44,8,128]{2,1,0:T(8,128)S(1)}, f32[44,8,128]{2,1,0:T(8,128)S(1)}) custom-call(f32[4,200,128]{2,1,0:T(8,128)S(1)} %get-tuple-element.18.own.start, f32[4,136,128]{2,1,0:T(8,128)S(1)} %collective-permute-done.below, ...), custom_call_target="tpu_custom_call" | custom-call | flops 12000000 | bytes 18000000 | tf_op jit(solution)/shard_map/first_image/pallas_call | solution.py:236
  30.0 3.9 %collective-permute-start.4 = (f32[44,8,128]{2,1,0:T(8,128)S(1)}, f32[44,8,128]{2,1,0:T(8,128)S(1)}, u32[]{:S(2)}, u32[]{:S(2)}) collective-permute-start(f32[44,8,128]{2,1,0:T(8,128)S(1)} %get-tuple-element.25), channel_id=1, source_target_pairs={{16,32},{32,16},{48,64},{64,48},{80,96},{96,80},{112,128},{128,112... | collective-permute-start | bytes 540680 | tf_op jit(solution)/shard_map/ppermute | solution.py:553
  33.9 1.9 %collective-permute-start.5 = (f32[44,8,128]{2,1,0:T(8,128)S(1)}, f32[44,8,128]{2,1,0:T(8,128)S(1)}, u32[]{:S(2)}, u32[]{:S(2)}) collective-permute-start(f32[44,8,128]{2,1,0:T(8,128)S(1)} %get-tuple-element.26), channel_id=1, source_target_pairs={{0,16},{16,0},{32,48},{48,32},{64,80},{80,64},{96,112},{112,96},{1... | collective-permute-start | bytes 540680 | tf_op jit(solution)/shard_map/ppermute | solution.py:553
  35.9 0.0 collective-permute-done.6.outer
  35.9 0.0 collective-permute-done.7.inner
  35.9 1.5 %old_images.1.old_image = f32[4,128,128]{2,1,0:T(8,128)S(1)} custom-call(f32[12,24,128]{2,1,0:T(8,128)S(1)} %get-tuple-element.24.coef, f32[4,200,128]{2,1,0:T(8,128)S(1)} %get-tuple-element.18.own.start, f32[4,136,128]{2,1,0:T(8,128)S(1)} %collective-permute-done.below, f32[4,136,128]{2,1,0:T(8,128)S(1)} %collective-permute-done.1.above, ...), custom_call_target="tpu_custom_call" | custom-call | flops 12000000 | bytes 24000000 | tf_op jit(solution)/shard_map/old_images/pallas_call | solution.py:268
  37.4 0.0 collective-permute-done.4.outer
  37.4 0.0 collective-permute-done.5.inner
  37.4 1.5 %image_and_gram.1 = (f32[4,64,128]{2,1,0:T(8,128)S(1)}, f32[32,8,128]{2,1,0:T(8,128)S(1)}) custom-call(f32[4,16,8,128]{3,2,1,0:T(8,128)S(1)} %get-tuple-element.23.w, f32[12,24,128]{2,1,0:T(8,128)S(1)} %get-tuple-element.24.coef, f32[44,8,128]{2,1,0:T(8,128)S(1)} %collective-permute-done.4.outer, f32[44,8,128]{2,1,0:T(8,128)S(1)} %collective-permute-done.5.inner, ...), custom_call_target="tpu_custom_call" | custom-call | tf_op jit(solution)/shard_map/image_and_gram/pallas_call | solution.py:372
  39.0 16.1 %all_to_all.10.parts = f32[32,8,128]{2,1,0:T(8,128)S(1)} all-to-all(f32[32,8,128]{2,1,0:T(8,128)S(1)} %get-tuple-element.29), channel_id=1, replica_groups=mesh['z'=16,'core'=2,'gy'=16] {'core','gy'}, dimensions={0} | all-to-all | bytes 262144 | tf_op jit(solution)/shard_map/all_to_all | solution.py:568
  55.1 25.8 %all_to_all.11.parts = f32[16,8,128]{2,1,0:T(8,128)S(1)} all-to-all(f32[16,8,128]{2,1,0:T(8,128)S(1)} %sum_and_spread.1), channel_id=1, replica_groups=mesh['z'=16,'core'=2,'gy'=16] {'z'}, dimensions={0} | all-to-all | bytes 131072 | tf_op jit(solution)/shard_map/all_to_all | solution.py:569
  80.9 3.9 %finish.1 = f32[2,8,4,8,128]{4,3,2,1,0:T(8,128)} custom-call(f32[16,8,128]{2,1,0:T(8,128)S(1)} %all_to_all.11.parts, f32[4,200,128]{2,1,0:T(8,128)S(1)} %get-tuple-element.18.own.start, f32[4,16,8,128]{3,2,1,0:T(8,128)S(1)} %get-tuple-element.23.w, f32[4,128,128]{2,1,0:T(8,128)S(1)} %old_images.1.old_image, f32[4,64,128]{2,1,0:T(8,128)S(1)} %get-tuple-element.30.w_image), custom_call_target="tpu_custom_call" | custom-call | tf_op jit(solution)/shard_map/finish/pallas_call | solution.py:493
  (1 shorter events, 0.0 us)
Async XLA Ops:
  0.0 1.0 %copy-start = (f32[3,2,4,4,8,128]{5,4,3,2,1,0:T(8,128)S(1)}, f32[3,2,4,4,8,128]{5,4,3,2,1,0:T(8,128)}, u32[]{:S(2)}) copy-start(f32[3,2,4,4,8,128]{5,4,3,2,1,0:T(8,128)} %prior_hbm.1) | copy-start | bytes 1179652
  1.0 0.7 copy-start.1
  2.0 7.5 %collective-permute-start = (f32[4,136,128]{2,1,0:T(8,128)S(1)}, f32[4,136,128]{2,1,0:T(8,128)S(1)}, u32[]{:S(2)}, u32[]{:S(2)}) collective-permute-start(f32[4,136,128]{2,1,0:T(8,128)S(1)} %get-tuple-element.19), channel_id=1, source_target_pairs={{0,1},{1,2},{2,3},{3,4},{4,5},{5,6},{6,7},{7,8},{8,9},{9,10},{10,1... | collective-permute-start | bytes 835592 | tf_op jit(solution)/shard_map/ppermute | solution.py:545
  6.1 7.3 %collective-permute-start.1 = (f32[4,136,128]{2,1,0:T(8,128)S(1)}, f32[4,136,128]{2,1,0:T(8,128)S(1)}, u32[]{:S(2)}, u32[]{:S(2)}) collective-permute-start(f32[4,136,128]{2,1,0:T(8,128)S(1)} %get-tuple-element.20), channel_id=1, source_target_pairs={{1,0},{2,1},{3,2},{4,3},{5,4},{6,5},{7,6},{8,7},{9,8},{10,9},{11,1... | collective-permute-start | bytes 835592 | tf_op jit(solution)/shard_map/ppermute | solution.py:546
  13.5 14.9 %collective-permute-start.2 = (f32[94,8,128]{2,1,0:T(8,128)S(1)}, f32[94,8,128]{2,1,0:T(8,128)S(1)}, u32[]{:S(2)}, u32[]{:S(2)}) collective-permute-start(f32[94,8,128]{2,1,0:T(8,128)S(1)} %get-tuple-element.21), channel_id=1, source_target_pairs={{16,32},{32,16},{48,64},{64,48},{80,96},{96,80},{112,128},{128,112... | collective-permute-start | bytes 1155080 | tf_op jit(solution)/shard_map/ppermute | solution.py:553
  20.6 7.8 %collective-permute-start.3 = (f32[94,8,128]{2,1,0:T(8,128)S(1)}, f32[94,8,128]{2,1,0:T(8,128)S(1)}, u32[]{:S(2)}, u32[]{:S(2)}) collective-permute-start(f32[94,8,128]{2,1,0:T(8,128)S(1)} %get-tuple-element.22), channel_id=1, source_target_pairs={{0,16},{16,0},{32,48},{48,32},{64,80},{80,64},{96,112},{112,96},{1... | collective-permute-start | bytes 1155080 | tf_op jit(solution)/shard_map/ppermute | solution.py:553
  22.5 13.3 %collective-permute-start.6 = (f32[80,8,128]{2,1,0:T(8,128)S(1)}, f32[80,8,128]{2,1,0:T(8,128)S(1)}, u32[]{:S(2)}, u32[]{:S(2)}) collective-permute-start(f32[80,8,128]{2,1,0:T(8,128)S(1)} %get-tuple-element.27), channel_id=1, source_target_pairs={{16,32},{32,16},{48,64},{64,48},{80,96},{96,80},{112,128},{128,112... | collective-permute-start | bytes 983048 | tf_op jit(solution)/shard_map/ppermute | solution.py:553
  26.5 9.4 %collective-permute-start.7 = (f32[80,8,128]{2,1,0:T(8,128)S(1)}, f32[80,8,128]{2,1,0:T(8,128)S(1)}, u32[]{:S(2)}, u32[]{:S(2)}) collective-permute-start(f32[80,8,128]{2,1,0:T(8,128)S(1)} %get-tuple-element.28), channel_id=1, source_target_pairs={{0,16},{16,0},{32,48},{48,32},{64,80},{80,64},{96,112},{112,96},{1... | collective-permute-start | bytes 983048 | tf_op jit(solution)/shard_map/ppermute | solution.py:553
  30.0 7.4 %collective-permute-start.4 = (f32[44,8,128]{2,1,0:T(8,128)S(1)}, f32[44,8,128]{2,1,0:T(8,128)S(1)}, u32[]{:S(2)}, u32[]{:S(2)}) collective-permute-start(f32[44,8,128]{2,1,0:T(8,128)S(1)} %get-tuple-element.25), channel_id=1, source_target_pairs={{16,32},{32,16},{48,64},{64,48},{80,96},{96,80},{112,128},{128,112... | collective-permute-start | bytes 540680 | tf_op jit(solution)/shard_map/ppermute | solution.py:553
  33.9 3.5 %collective-permute-start.5 = (f32[44,8,128]{2,1,0:T(8,128)S(1)}, f32[44,8,128]{2,1,0:T(8,128)S(1)}, u32[]{:S(2)}, u32[]{:S(2)}) collective-permute-start(f32[44,8,128]{2,1,0:T(8,128)S(1)} %get-tuple-element.26), channel_id=1, source_target_pairs={{0,16},{16,0},{32,48},{48,32},{64,80},{80,64},{96,112},{112,96},{1... | collective-permute-start | bytes 540680 | tf_op jit(solution)/shard_map/ppermute | solution.py:553

commit v16 on v14

--- a/solution.py
+++ b/solution.py
@@ -556,9 +556,9 @@
     w_sides = exchange(nx, w_outward, w_inward)
     old_image = old_images(coef, start, *rims, *old_sides, *sides)
 
-    w_image, spread = image_and_gram(2 * ny, w, coef, *w_sides, start, old_image)
-    got = lax.all_to_all(spread, ("core", "gy"), 0, 0)
-    got = lax.all_to_all(sum_and_spread(got, nz), "z", 0, 0)
+    w_image, spread = image_and_gram(nz, w, coef, *w_sides, start, old_image)
+    got = lax.all_to_all(spread, "z", 0, 0)
+    got = lax.all_to_all(sum_and_spread(got, 2 * ny), ("core", "gy"), 0, 0)
     out = finish(cells, got, start, w, old_image, w_image)
     return out.reshape(2, 2, 4, LX, LY, NZ)
 

time: 85.1 us -> 86.5 us (1.016)
  blocking collectives: 41.9 us -> 43.3 us
    all_to_all x2, blocking collectives: 41.9 us -> 43.3 us  [the longest x1 25.4 us: per_device(): got = lax.all_to_all(spread, 'z', 0, 0)]
where the time goes in v16:
time: 86.5 us; the launch traced here: 86.1 us
  blocking collectives  43.3 us (50%)
  starting transfers between devices  26.1 us (30%)
  Pallas kernels  8.8 us (10%)
  waiting for transfers between devices  6.01 us (7%)
  local copies, waits for them, and re-layouts  1.71 us (2%)
    all_to_all x1, blocking collectives, per_device(): got = lax.all_to_all(spread, 'z', 0, 0)  25.4 us
    ppermute x6, starting transfers between devices, exchange(): return (lax.ppermute(outward, GX, outer), lax.ppermute(inward, GX, inner))  20.7 us
    all_to_all x1, blocking collectives, per_device(): got = lax.all_to_all(sum_and_spread(got, 2 * ny), ('core', 'gy'), 0, 0)  18 us
    ppermute x1, starting transfers between devices, from_both(): lax.ppermute(to_higher, axis, [(i, i + 1) for i in range(count - 1)])  4.05 us
    pallas_call x1, Pallas kernels, finish(): pl.pallas_call(functools.partial(final_kernel, cells), out_shape=jax.Shap...  3.94 us
    ppermute x1, waiting for transfers between devices, from_both(): lax.ppermute(to_lower, axis, [(i + 1, i) for i in range(count - 1)])  3.83 us
    ppermute x1, waiting for transfers between devices, from_both(): lax.ppermute(to_higher, axis, [(i, i + 1) for i in range(count - 1)])  2.16 us
  transfers between devices with their start and end apart: 8, of which 2 were waited for; matrix products, arithmetic and copies ran while one was open for 0% of the time, Pallas kernels for 4%

profile of v16, /device:TPU:1, one launch (start us, length us, event | category | flops | bytes accessed | tf_op | source)
XLA Modules:
  0.0 86.1 jit_solution(282901129765331229)
XLA Ops:
  0.0 0.0 copy-start
  0.0 1.0 %copy-done = f32[3,2,4,4,8,128]{5,4,3,2,1,0:T(8,128)S(1)} copy-done((f32[3,2,4,4,8,128]{5,4,3,2,1,0:T(8,128)S(1)}, f32[3,2,4,4,8,128]{5,4,3,2,1,0:T(8,128)}, u32[]{:S(2)}) %copy-start) | copy-done | bytes 393240
  1.0 0.0 copy-start.1
  1.0 0.7 copy-done.1
  1.7 0.1 turn.1
  1.8 4.0 %collective-permute-start = (f32[4,136,128]{2,1,0:T(8,128)S(1)}, f32[4,136,128]{2,1,0:T(8,128)S(1)}, u32[]{:S(2)}, u32[]{:S(2)}) collective-permute-start(f32[4,136,128]{2,1,0:T(8,128)S(1)} %get-tuple-element.19), channel_id=1, source_target_pairs={{0,1},{1,2},{2,3},{3,4},{4,5},{5,6},{6,7},{7,8},{8,9},{9,10},{10,1... | collective-permute-start | bytes 835592 | tf_op jit(solution)/shard_map/ppermute | solution.py:537
  5.9 1.3 %collective-permute-start.1 = (f32[4,136,128]{2,1,0:T(8,128)S(1)}, f32[4,136,128]{2,1,0:T(8,128)S(1)}, u32[]{:S(2)}, u32[]{:S(2)}) collective-permute-start(f32[4,136,128]{2,1,0:T(8,128)S(1)} %get-tuple-element.20), channel_id=1, source_target_pairs={{1,0},{2,1},{3,2},{4,3},{5,4},{6,5},{7,6},{8,7},{9,8},{10,9},{11,1... | collective-permute-start | bytes 835592 | tf_op jit(solution)/shard_map/ppermute | solution.py:538
  7.2 2.2 %collective-permute-done.below = f32[4,136,128]{2,1,0:T(8,128)S(1)} collective-permute-done((f32[4,136,128]{2,1,0:T(8,128)S(1)}, f32[4,136,128]{2,1,0:T(8,128)S(1)}, u32[]{:S(2)}, u32[]{:S(2)}) %collective-permute-start) | collective-permute-done | bytes 278560 | tf_op jit(solution)/shard_map/ppermute | solution.py:537
  9.3 3.8 %collective-permute-done.1.above = f32[4,136,128]{2,1,0:T(8,128)S(1)} collective-permute-done((f32[4,136,128]{2,1,0:T(8,128)S(1)}, f32[4,136,128]{2,1,0:T(8,128)S(1)}, u32[]{:S(2)}, u32[]{:S(2)}) %collective-permute-start.1) | collective-permute-done | bytes 278560 | tf_op jit(solution)/shard_map/ppermute | solution.py:538
  13.2 0.1 pack_all.1
  13.3 7.1 %collective-permute-start.2 = (f32[94,8,128]{2,1,0:T(8,128)S(1)}, f32[94,8,128]{2,1,0:T(8,128)S(1)}, u32[]{:S(2)}, u32[]{:S(2)}) collective-permute-start(f32[94,8,128]{2,1,0:T(8,128)S(1)} %get-tuple-element.21), channel_id=1, source_target_pairs={{16,32},{32,16},{48,64},{64,48},{80,96},{96,80},{112,128},{128,112... | collective-permute-start | bytes 1155080 | tf_op jit(solution)/shard_map/ppermute | solution.py:545
  20.4 1.9 %collective-permute-start.3 = (f32[94,8,128]{2,1,0:T(8,128)S(1)}, f32[94,8,128]{2,1,0:T(8,128)S(1)}, u32[]{:S(2)}, u32[]{:S(2)}) collective-permute-start(f32[94,8,128]{2,1,0:T(8,128)S(1)} %get-tuple-element.22), channel_id=1, source_target_pairs={{0,16},{16,0},{32,48},{48,32},{64,80},{80,64},{96,112},{112,96},{1... | collective-permute-start | bytes 1155080 | tf_op jit(solution)/shard_map/ppermute | solution.py:545
  22.3 3.9 %collective-permute-start.6 = (f32[80,8,128]{2,1,0:T(8,128)S(1)}, f32[80,8,128]{2,1,0:T(8,128)S(1)}, u32[]{:S(2)}, u32[]{:S(2)}) collective-permute-start(f32[80,8,128]{2,1,0:T(8,128)S(1)} %get-tuple-element.27), channel_id=1, source_target_pairs={{16,32},{32,16},{48,64},{64,48},{80,96},{96,80},{112,128},{128,112... | collective-permute-start | bytes 983048 | tf_op jit(solution)/shard_map/ppermute | solution.py:545
  26.2 1.9 %collective-permute-start.7 = (f32[80,8,128]{2,1,0:T(8,128)S(1)}, f32[80,8,128]{2,1,0:T(8,128)S(1)}, u32[]{:S(2)}, u32[]{:S(2)}) collective-permute-start(f32[80,8,128]{2,1,0:T(8,128)S(1)} %get-tuple-element.28), channel_id=1, source_target_pairs={{0,16},{16,0},{32,48},{48,32},{64,80},{80,64},{96,112},{112,96},{1... | collective-permute-start | bytes 983048 | tf_op jit(solution)/shard_map/ppermute | solution.py:545
  28.2 0.0 collective-permute-done.2.outer.first_outer
  28.2 0.0 collective-permute-done.3.inner.first_inner
  28.2 1.6 %first_image.1 = (f32[4,16,8,128]{3,2,1,0:T(8,128)S(1)}, f32[12,24,128]{2,1,0:T(8,128)S(1)}, f32[44,8,128]{2,1,0:T(8,128)S(1)}, f32[44,8,128]{2,1,0:T(8,128)S(1)}) custom-call(f32[4,200,128]{2,1,0:T(8,128)S(1)} %get-tuple-element.18.own.start, f32[4,136,128]{2,1,0:T(8,128)S(1)} %collective-permute-done.below, ...), custom_call_target="tpu_custom_call" | custom-call | flops 12000000 | bytes 18000000 | tf_op jit(solution)/shard_map/first_image/pallas_call | solution.py:236
  29.8 3.9 %collective-permute-start.4 = (f32[44,8,128]{2,1,0:T(8,128)S(1)}, f32[44,8,128]{2,1,0:T(8,128)S(1)}, u32[]{:S(2)}, u32[]{:S(2)}) collective-permute-start(f32[44,8,128]{2,1,0:T(8,128)S(1)} %get-tuple-element.25), channel_id=1, source_target_pairs={{16,32},{32,16},{48,64},{64,48},{80,96},{96,80},{112,128},{128,112... | collective-permute-start | bytes 540680 | tf_op jit(solution)/shard_map/ppermute | solution.py:545
  33.7 1.9 %collective-permute-start.5 = (f32[44,8,128]{2,1,0:T(8,128)S(1)}, f32[44,8,128]{2,1,0:T(8,128)S(1)}, u32[]{:S(2)}, u32[]{:S(2)}) collective-permute-start(f32[44,8,128]{2,1,0:T(8,128)S(1)} %get-tuple-element.26), channel_id=1, source_target_pairs={{0,16},{16,0},{32,48},{48,32},{64,80},{80,64},{96,112},{112,96},{1... | collective-permute-start | bytes 540680 | tf_op jit(solution)/shard_map/ppermute | solution.py:545
  35.6 0.0 collective-permute-done.6.outer
  35.6 0.0 collective-permute-done.7.inner
  35.7 1.5 %old_images.1.old_image = f32[4,128,128]{2,1,0:T(8,128)S(1)} custom-call(f32[12,24,128]{2,1,0:T(8,128)S(1)} %get-tuple-element.24.coef, f32[4,200,128]{2,1,0:T(8,128)S(1)} %get-tuple-element.18.own.start, f32[4,136,128]{2,1,0:T(8,128)S(1)} %collective-permute-done.below, f32[4,136,128]{2,1,0:T(8,128)S(1)} %collective-permute-done.1.above, ...), custom_call_target="tpu_custom_call" | custom-call | flops 12000000 | bytes 24000000 | tf_op jit(solution)/shard_map/old_images/pallas_call | solution.py:268
  37.2 0.0 collective-permute-done.4.outer
  37.2 0.0 collective-permute-done.5.inner
  37.2 1.5 %image_and_gram.1 = (f32[4,64,128]{2,1,0:T(8,128)S(1)}, f32[16,8,128]{2,1,0:T(8,128)S(1)}) custom-call(f32[4,16,8,128]{3,2,1,0:T(8,128)S(1)} %get-tuple-element.23.w, f32[12,24,128]{2,1,0:T(8,128)S(1)} %get-tuple-element.24.coef, f32[44,8,128]{2,1,0:T(8,128)S(1)} %collective-permute-done.4.outer, f32[44,8,128]{2,1,0:T(8,128)S(1)} %collective-permute-done.5.inner, ...), custom_call_target="tpu_custom_call" | custom-call | tf_op jit(solution)/shard_map/image_and_gram/pallas_call | solution.py:372
  38.8 25.4 %all_to_all.10.parts = f32[16,8,128]{2,1,0:T(8,128)S(1)} all-to-all(f32[16,8,128]{2,1,0:T(8,128)S(1)} %get-tuple-element.29), channel_id=1, replica_groups=mesh['z'=16,'core'=2,'gy'=16] {'z'}, dimensions={0} | all-to-all | bytes 131072 | tf_op jit(solution)/shard_map/all_to_all | solution.py:560
  64.2 18.0 %all_to_all.11.parts = f32[32,8,128]{2,1,0:T(8,128)S(1)} all-to-all(f32[32,8,128]{2,1,0:T(8,128)S(1)} %sum_and_spread.1), channel_id=1, replica_groups=mesh['z'=16,'core'=2,'gy'=16] {'core','gy'}, dimensions={0} | all-to-all | bytes 262144 | tf_op jit(solution)/shard_map/all_to_all | solution.py:561
  82.1 3.9 %finish.1 = f32[2,8,4,8,128]{4,3,2,1,0:T(8,128)} custom-call(f32[32,8,128]{2,1,0:T(8,128)S(1)} %all_to_all.11.parts, f32[4,200,128]{2,1,0:T(8,128)S(1)} %get-tuple-element.18.own.start, f32[4,16,8,128]{3,2,1,0:T(8,128)S(1)} %get-tuple-element.23.w, f32[4,128,128]{2,1,0:T(8,128)S(1)} %old_images.1.old_image, f32[4,64,128]{2,1,0:T(8,128)S(1)} %get-tuple-element.30.w_image), custom_call_target="tpu_custom_call" | custom-call | tf_op jit(solution)/shard_map/finish/pallas_call | solution.py:493
  (1 shorter events, 0.0 us)
Async XLA Ops:
  0.0 1.0 %copy-start = (f32[3,2,4,4,8,128]{5,4,3,2,1,0:T(8,128)S(1)}, f32[3,2,4,4,8,128]{5,4,3,2,1,0:T(8,128)}, u32[]{:S(2)}) copy-start(f32[3,2,4,4,8,128]{5,4,3,2,1,0:T(8,128)} %prior.1) | copy-start | bytes 1179652
  1.0 0.7 copy-start.1
  1.8 7.5 %collective-permute-start = (f32[4,136,128]{2,1,0:T(8,128)S(1)}, f32[4,136,128]{2,1,0:T(8,128)S(1)}, u32[]{:S(2)}, u32[]{:S(2)}) collective-permute-start(f32[4,136,128]{2,1,0:T(8,128)S(1)} %get-tuple-element.19), channel_id=1, source_target_pairs={{0,1},{1,2},{2,3},{3,4},{4,5},{5,6},{6,7},{7,8},{8,9},{9,10},{10,1... | collective-permute-start | bytes 835592 | tf_op jit(solution)/shard_map/ppermute | solution.py:537
  5.9 7.3 %collective-permute-start.1 = (f32[4,136,128]{2,1,0:T(8,128)S(1)}, f32[4,136,128]{2,1,0:T(8,128)S(1)}, u32[]{:S(2)}, u32[]{:S(2)}) collective-permute-start(f32[4,136,128]{2,1,0:T(8,128)S(1)} %get-tuple-element.20), channel_id=1, source_target_pairs={{1,0},{2,1},{3,2},{4,3},{5,4},{6,5},{7,6},{8,7},{9,8},{10,9},{11,1... | collective-permute-start | bytes 835592 | tf_op jit(solution)/shard_map/ppermute | solution.py:538
  13.3 14.9 %collective-permute-start.2 = (f32[94,8,128]{2,1,0:T(8,128)S(1)}, f32[94,8,128]{2,1,0:T(8,128)S(1)}, u32[]{:S(2)}, u32[]{:S(2)}) collective-permute-start(f32[94,8,128]{2,1,0:T(8,128)S(1)} %get-tuple-element.21), channel_id=1, source_target_pairs={{16,32},{32,16},{48,64},{64,48},{80,96},{96,80},{112,128},{128,112... | collective-permute-start | bytes 1155080 | tf_op jit(solution)/shard_map/ppermute | solution.py:545
  20.4 7.8 %collective-permute-start.3 = (f32[94,8,128]{2,1,0:T(8,128)S(1)}, f32[94,8,128]{2,1,0:T(8,128)S(1)}, u32[]{:S(2)}, u32[]{:S(2)}) collective-permute-start(f32[94,8,128]{2,1,0:T(8,128)S(1)} %get-tuple-element.22), channel_id=1, source_target_pairs={{0,16},{16,0},{32,48},{48,32},{64,80},{80,64},{96,112},{112,96},{1... | collective-permute-start | bytes 1155080 | tf_op jit(solution)/shard_map/ppermute | solution.py:545
  22.3 13.3 %collective-permute-start.6 = (f32[80,8,128]{2,1,0:T(8,128)S(1)}, f32[80,8,128]{2,1,0:T(8,128)S(1)}, u32[]{:S(2)}, u32[]{:S(2)}) collective-permute-start(f32[80,8,128]{2,1,0:T(8,128)S(1)} %get-tuple-element.27), channel_id=1, source_target_pairs={{16,32},{32,16},{48,64},{64,48},{80,96},{96,80},{112,128},{128,112... | collective-permute-start | bytes 983048 | tf_op jit(solution)/shard_map/ppermute | solution.py:545
  26.2 9.4 %collective-permute-start.7 = (f32[80,8,128]{2,1,0:T(8,128)S(1)}, f32[80,8,128]{2,1,0:T(8,128)S(1)}, u32[]{:S(2)}, u32[]{:S(2)}) collective-permute-start(f32[80,8,128]{2,1,0:T(8,128)S(1)} %get-tuple-element.28), channel_id=1, source_target_pairs={{0,16},{16,0},{32,48},{48,32},{64,80},{80,64},{96,112},{112,96},{1... | collective-permute-start | bytes 983048 | tf_op jit(solution)/shard_map/ppermute | solution.py:545
  29.8 7.4 %collective-permute-start.4 = (f32[44,8,128]{2,1,0:T(8,128)S(1)}, f32[44,8,128]{2,1,0:T(8,128)S(1)}, u32[]{:S(2)}, u32[]{:S(2)}) collective-permute-start(f32[44,8,128]{2,1,0:T(8,128)S(1)} %get-tuple-element.25), channel_id=1, source_target_pairs={{16,32},{32,16},{48,64},{64,48},{80,96},{96,80},{112,128},{128,112... | collective-permute-start | bytes 540680 | tf_op jit(solution)/shard_map/ppermute | solution.py:545
  33.7 3.5 %collective-permute-start.5 = (f32[44,8,128]{2,1,0:T(8,128)S(1)}, f32[44,8,128]{2,1,0:T(8,128)S(1)}, u32[]{:S(2)}, u32[]{:S(2)}) collective-permute-start(f32[44,8,128]{2,1,0:T(8,128)S(1)} %get-tuple-element.26), channel_id=1, source_target_pairs={{0,16},{16,0},{32,48},{48,32},{64,80},{80,64},{96,112},{112,96},{1... | collective-permute-start | bytes 540680 | tf_op jit(solution)/shard_map/ppermute | solution.py:545
